TPU v7x, 256 devices: a whole 4x4x8 slice. The times are simulated.
256 devices in a mesh: ta: 32 (over y, z), gz: 8 (over x, core).
Axes of the slice: x: 4, y: 4, z: 8, core: 2. Of those that a mesh axis runs over, the one named last changes fastest.
Arguments:
- level2_residual: bfloat16 [32, 8, 3, 4, 48, 1536], P('ta', 'gz'), may hold values from -6 to 6
- prolongator: bfloat16 [32, 8, 3, 4, 1536, 128], P('ta', 'gz'), may hold values from -0.15625 to 0.15625
- coarse_links: bfloat16 [9, 32, 8, 3, 4, 128, 128], P(None, 'ta', 'gz'), may hold values from -0.15625 to 0.15625
Outputs:
- correction: bfloat16 [32, 8, 3, 4, 48, 1536], P('ta', 'gz')
All inputs are finite; a program needn't handle non-finite values.
Results may differ from a plain program's by a relative error of at most 0.034.
Values may be sent and summed in bfloat16 or wider, within the bound.
No kernel may reach another device: no remote copies, remote signals or barrier semaphores. Data moves between devices by JAX's collectives and lax.ppermute only.
A program may use at most 64 MiB of HBM per device.

v0:
```python
import functools

import jax
import jax.numpy as jnp
from jax import lax
from jax.experimental import pallas as pl
from jax.experimental.pallas import tpu as pltpu
from jax.sharding import PartitionSpec as P

ITERS = 16
LIMIT = 16 * 2**20
VMEM = pl.BlockSpec(memory_space=pltpu.VMEM)
HBM = pl.BlockSpec(memory_space=pltpu.HBM)
SMEM = pl.BlockSpec(memory_space=pltpu.SMEM)
NN = (((1,), (0,)), ((), ()))
NT = (((1,), (1,)), ((), ()))


def call(kernel, ins, outs, scratch=(), in_specs=None, out_specs=None, flops=0):
    in_specs = in_specs or [VMEM] * len(ins)
    out_specs = out_specs or [VMEM] * len(outs)
    ins = [
        x if spec is SMEM else pltpu.with_memory_space_constraint(x, spec.memory_space)
        for x, spec in zip(ins, in_specs)
    ]
    return pl.pallas_call(
        kernel,
        in_specs=in_specs,
        out_specs=out_specs,
        out_shape=[
            pltpu.VMEM(o.shape, o.dtype) if spec is VMEM else o for o, spec in zip(outs, out_specs)
        ],
        scratch_shapes=list(scratch),
        compiler_params=pltpu.CompilerParams(vmem_limit_bytes=LIMIT),
        cost_estimate=pl.CostEstimate(flops=flops, bytes_accessed=0, transcendentals=0),
    )(*ins)


def shape(dims, dtype=jnp.bfloat16):
    return jax.ShapeDtypeStruct(dims, dtype)


def dot(a, b, dims=NN):
    return lax.dot_general(a, b, dims, preferred_element_type=jnp.float32)


def restrict_kernel(residual, prolongator, rhs, buffer, held, sems):
    sites = rhs.shape[0]
    copies = []
    for s in range(sites):
        copies.append(
            (
                pltpu.make_async_copy(residual.at[s], buffer.at[s], sems.at[0, s]),
                pltpu.make_async_copy(prolongator.at[s], held.at[s], sems.at[1, s]),
            )
        )
        for c in copies[-1]:
            c.start()
    for s in range(sites):
        for c in copies[s]:
            c.wait()
        rhs[s] = dot(buffer[s], held[s]).astype(rhs.dtype)


def links_kernel(slots, links, remote, buffer, sems):
    sites, _, wide = remote.shape
    for i in range(4):
        pltpu.make_async_copy(links.at[slots[i]], buffer.at[i], sems.at[i]).start()
    for i in range(4):
        pltpu.make_async_copy(links.at[slots[i]], buffer.at[i], sems.at[i]).wait()
        for s in range(sites):
            remote[s, i * wide : (i + 1) * wide, :] = buffer[i, s].T

    @pl.when(slots[4] < 0)
    def _():
        remote[:, :wide, :] = -remote[:, :wide, :]


def local_kernel(ny, nx, rhs, value, links, out, buffer, sems):
    copies = []
    for y in range(ny):
        row = pl.ds(y * nx, nx)
        copies.append(pltpu.make_async_copy(links.at[:5, row], buffer.at[:, row], sems.at[y]))
        copies[-1].start()
    for y in range(ny):
        copies[y].wait()
        for x in range(nx):
            s = y * nx + x
            near = [
                s,
                y * nx + (x + 1) % nx,
                y * nx + (x - 1) % nx,
                (y + 1) % ny * nx + x,
                (y - 1) % ny * nx + x,
            ]
            lhs = jnp.concatenate([value[n] for n in near], 1)
            rows = jnp.concatenate([buffer[d, s] for d in range(5)], 1)
            out[s] = rhs[s].astype(jnp.float32) - dot(lhs, rows, NT)


def remote_kernel(part, a, b, c, d, weights, token, out):
    for s in range(part.shape[0]):
        lhs = jnp.concatenate([a[s], b[s], c[s], d[s]], 1)
        out[s] = (part[s] - dot(lhs, weights[s])).astype(out.dtype)


def after_kernel(earlier, arrived, token):
    token[...] = jnp.zeros_like(token)


def transpose_kernel(prolongator, earlier, out, buffer, sems):
    sites = out.shape[0]

    def fetch(s):
        return pltpu.make_async_copy(prolongator.at[s], buffer.at[s], sems.at[s])

    for s in range(sites):
        fetch(s).start()

    def turn(s, _):
        fetch(s).wait()
        out[s] = buffer[s].T
        return 0

    lax.fori_loop(0, sites, turn, 0)


def prolong_kernel(value, weights, out, buffer, sems):
    copies = []
    for s in range(value.shape[0]):
        buffer[s] = dot(value[s], weights[s]).astype(buffer.dtype)
        copies.append(pltpu.make_async_copy(buffer.at[s], out.at[s], sems.at[s]))
        copies[-1].start()
    for c in copies:
        c.wait()


def swap(count, first):
    pairs = [((i + first) % count, (i + first + 1) % count) for i in range(0, count, 2)]
    return pairs + [(b, a) for a, b in pairs]


def per_device(level2_residual, prolongator, coarse_links):
    nt, nz = lax.axis_size("ta"), lax.axis_size("gz")
    t, z = lax.axis_index("ta"), lax.axis_index("gz")
    ny, nx, rhs_count, fine = level2_residual.shape[2:]
    wide = prolongator.shape[-1]
    sites = ny * nx
    residual = level2_residual.reshape(sites, rhs_count, fine)
    prolong = prolongator.reshape(sites, fine, wide)
    links = coarse_links.reshape(9, sites, wide, wide)
    field = (sites, rhs_count, wide)
    flops = 2 * sites * rhs_count * wide * wide

    (rhs,) = call(
        restrict_kernel,
        [residual, prolong],
        [shape(field)],
        [
            pltpu.VMEM(residual.shape, residual.dtype),
            pltpu.VMEM(prolong.shape, prolong.dtype),
            pltpu.SemaphoreType.DMA((2, sites)),
        ],
        in_specs=[HBM, HBM],
    )
    t_odd, z_odd = t % 2, z % 2
    edge = (t == 0) | (t == nt - 1)
    slots = jnp.stack([8 - t_odd, 7 + t_odd, 6 - z_odd, 5 + z_odd, jnp.where(edge, -1, 1)]).astype(
        jnp.int32
    )
    (remote_weights,) = call(
        links_kernel,
        [slots, links],
        [shape((sites, 4 * wide, wide))],
        [pltpu.VMEM((4, *links.shape[1:]), links.dtype), pltpu.SemaphoreType.DMA((4,))],
        in_specs=[SMEM, HBM],
    )

    def sweep(value):
        z_near = lax.ppermute(value, "gz", swap(nz, 0))
        z_far = lax.ppermute(value, "gz", swap(nz, 1))
        t_near = lax.ppermute(value, "ta", swap(nt, 0))
        t_far = lax.ppermute(value, "ta", swap(nt, 1))
        (part,) = call(
            functools.partial(local_kernel, ny, nx),
            [rhs, value, links],
            [shape(field, jnp.float32)],
            [pltpu.VMEM((5, *links.shape[1:]), links.dtype), pltpu.SemaphoreType.DMA((ny,))],
            in_specs=[VMEM, VMEM, HBM],
            flops=5 * flops,
        )
        token = value
        for arrived in (t_far, t_near, z_far):
            (token,) = call(after_kernel, [token, arrived], [shape((8, 128), jnp.float32)])
        (value,) = call(
            remote_kernel,
            [part, t_far, t_near, z_far, z_near, remote_weights, token],
            [shape(field)],
            flops=4 * flops,
        )
        return value

    last = lax.fori_loop(1, ITERS - 1, lambda _, v: sweep(v), sweep(rhs))
    value = sweep(last)

    (weights,) = call(
        transpose_kernel,
        [prolong, last],
        [shape((sites, wide, fine))],
        [pltpu.VMEM(prolong.shape, prolong.dtype), pltpu.SemaphoreType.DMA((sites,))],
        in_specs=[HBM, VMEM],
    )
    (out,) = call(
        prolong_kernel,
        [value, weights],
        [shape((sites, rhs_count, fine))],
        [pltpu.VMEM((sites, rhs_count, fine), jnp.bfloat16), pltpu.SemaphoreType.DMA((sites,))],
        out_specs=[HBM],
    )
    return out.reshape(level2_residual.shape)


def solution(mesh):
    placed = (
        P("ta", "gz", None, None, None, None),
        P("ta", "gz", None, None, None, None),
        P(None, "ta", "gz", None, None, None, None),
    )
    return jax.shard_map(
        per_device,
        mesh=mesh,
        in_specs=placed,
        out_specs=P("ta", "gz", None, None, None, None),
        check_vma=False,
    )
```

profile of v0, /device:TPU:1, one launch (start us, length us, event | category | flops | bytes accessed | tf_op | source)
XLA Modules:
  0.0 157.8 jit_solution(7685109789939649131)
XLA Ops:
  0.0 3.7 %shard_map.37.rhs.value.earlier = bf16[12,48,128]{2,1,0:T(8,128)(2,1)S(1)} custom-call(bf16[12,48,1536]{2,1,0:T(8,128)(2,1)} %bitcast.14, bf16[12,1536,128]{2,1,0:T(8,128)(2,1)} %bitcast.12), custom_call_target="tpu_custom_call" | custom-call | tf_op jit(solution)/shard_map/pallas_call | solution.py:26
  3.7 8.9 %collective-permute-start.4 = (bf16[12,48,128]{2,1,0:T(8,128)(2,1)S(1)}, bf16[12,48,128]{2,1,0:T(8,128)(2,1)S(1)}, u32[]{:S(2)}, u32[]{:S(2)}) collective-permute-start(bf16[12,48,128]{2,1,0:T(8,128)(2,1)S(1)} %shard_map.37.rhs.value.earlier), channel_id=1, source_target_pairs={{8,16},{24,32},{40,48},{56,64},{72,80},{88,96},{104,112},{120,128}... | collective-permute-start | bytes 442376 | tf_op jit(solution)/shard_map/ppermute | solution.py:183
  12.6 2.1 %collective-permute-start.6 = (bf16[12,48,128]{2,1,0:T(8,128)(2,1)S(1)}, bf16[12,48,128]{2,1,0:T(8,128)(2,1)S(1)}, u32[]{:S(2)}, u32[]{:S(2)}) collective-permute-start(bf16[12,48,128]{2,1,0:T(8,128)(2,1)S(1)} %shard_map.37.rhs.value.earlier), channel_id=1, source_target_pairs={{1,2},{3,4},{5,6},{7,0},{2,1},{4,3},{6,5},{0,7},{9,10},{11,12},{13... | collective-permute-start | bytes 442376 | tf_op jit(solution)/shard_map/ppermute | solution.py:181
  14.7 0.8 collective-permute-start.7
  15.6 2.3 %shard_map.39.weights = bf16[12,512,128]{2,1,0:T(8,128)(2,1)S(1)} custom-call(s32[5]{0:T(128)S(1)} %stack.23.slots, bf16[9,12,128,128]{3,2,1,0:T(8,128)(2,1)} %bitcast.9), custom_call_target="tpu_custom_call" | custom-call | tf_op jit(solution)/shard_map/pallas_call | solution.py:26
  17.8 2.2 %shard_map.38.part = f32[12,48,128]{2,1,0:T(8,128)S(1)} custom-call(bf16[12,48,128]{2,1,0:T(8,128)(2,1)S(1)} %shard_map.37.rhs.value.earlier, bf16[12,48,128]{2,1,0:T(8,128)(2,1)S(1)} %shard_map.37.rhs.value.earlier, bf16[9,12,128,128]{3,2,1,0:T(8,128)(2,1)} %bitcast.10), custom_call_target="tpu_custom_call" | custom-call | flops 94371840 | tf_op jit(solution)/shard_map/pallas_call | solution.py:26
  20.5 123.8 %while.10 = (s32[]{:T(128)}, bf16[12,48,128]{2,1,0:T(8,128)(2,1)S(1)}, bf16[12,48,128]{2,1,0:T(8,128)(2,1)S(1)}, bf16[9,12,128,128]{3,2,1,0:T(8,128)(2,1)}, bf16[12,512,128]{2,1,0:T(8,128)(2,1)S(1)}, /*index=5*/s32[]{:T(128)}) while((s32[]{:T(128)}, bf16[12,48,128]{2,1,0:T(8,128)(2,1)S(1)}, bf16[12,48,128]{2,1,0:T(8,128)(2,1)S(1)}, ...), condition=%wide.region_1.2_spmd, body=%wide.region_0.1_spmd.sunk | while | flops 169869312 | bytes 2359525 | solution.py:203
  20.6 1.5 collective-permute-start
  22.2 1.9 %collective-permute-start.2 = (bf16[12,48,128]{2,1,0:T(8,128)(2,1)S(1)}, bf16[12,48,128]{2,1,0:T(8,128)(2,1)S(1)}, u32[]{:S(2)}, u32[]{:S(2)}) collective-permute-start(bf16[12,48,128]{2,1,0:T(8,128)(2,1)S(1)} %get-tuple-element.81.value.earlier), channel_id=1, source_target_pairs={{1,2},{3,4},{5,6},{7,0},{2,1},{4,3},{6,5},{0,7},{9,10},{11,12},{13... | collective-permute-start | bytes 442376 | tf_op jit(solution)/shard_map/while/body/eval_jaxpr/ppermute | solution.py:181
  24.1 2.2 %eval_jaxpr.5.part = f32[12,48,128]{2,1,0:T(8,128)S(1)} custom-call(bf16[12,48,128]{2,1,0:T(8,128)(2,1)S(1)} %get-tuple-element.88.rhs, bf16[12,48,128]{2,1,0:T(8,128)(2,1)S(1)} %get-tuple-element.81.value.earlier, bf16[9,12,128,128]{3,2,1,0:T(8,128)(2,1)} %get-tuple-element.89.links), custom_call_target="tpu_custom_call" | custom-call | flops 94371840 | tf_op jit(solution)/shard_map/while/body/eval_jaxpr/pallas_call | solution.py:26
  26.4 3.1 %collective-permute-done.arrived.a = bf16[12,48,128]{2,1,0:T(8,128)(2,1)S(1)} collective-permute-done((bf16[12,48,128]{2,1,0:T(8,128)(2,1)S(1)}, bf16[12,48,128]{2,1,0:T(8,128)(2,1)S(1)}, u32[]{:S(2)}, u32[]{:S(2)}) %collective-permute-start) | collective-permute-done | bytes 147488 | tf_op jit(solution)/shard_map/while/body/eval_jaxpr/ppermute | solution.py:183
  29.9 1.2 collective-permute-start
  31.1 2.0 %collective-permute-start.2 = (bf16[12,48,128]{2,1,0:T(8,128)(2,1)S(1)}, bf16[12,48,128]{2,1,0:T(8,128)(2,1)S(1)}, u32[]{:S(2)}, u32[]{:S(2)}) collective-permute-start(bf16[12,48,128]{2,1,0:T(8,128)(2,1)S(1)} %get-tuple-element.81.value.earlier), channel_id=1, source_target_pairs={{1,2},{3,4},{5,6},{7,0},{2,1},{4,3},{6,5},{0,7},{9,10},{11,12},{13... | collective-permute-start | bytes 442376 | tf_op jit(solution)/shard_map/while/body/eval_jaxpr/ppermute | solution.py:181
  33.1 2.2 %eval_jaxpr.5.part = f32[12,48,128]{2,1,0:T(8,128)S(1)} custom-call(bf16[12,48,128]{2,1,0:T(8,128)(2,1)S(1)} %get-tuple-element.88.rhs, bf16[12,48,128]{2,1,0:T(8,128)(2,1)S(1)} %get-tuple-element.81.value.earlier, bf16[9,12,128,128]{3,2,1,0:T(8,128)(2,1)} %get-tuple-element.89.links), custom_call_target="tpu_custom_call" | custom-call | flops 94371840 | tf_op jit(solution)/shard_map/while/body/eval_jaxpr/pallas_call | solution.py:26
  35.4 2.5 %collective-permute-done.arrived.a = bf16[12,48,128]{2,1,0:T(8,128)(2,1)S(1)} collective-permute-done((bf16[12,48,128]{2,1,0:T(8,128)(2,1)S(1)}, bf16[12,48,128]{2,1,0:T(8,128)(2,1)S(1)}, u32[]{:S(2)}, u32[]{:S(2)}) %collective-permute-start) | collective-permute-done | bytes 147488 | tf_op jit(solution)/shard_map/while/body/eval_jaxpr/ppermute | solution.py:183
  38.3 1.8 %collective-permute-start = (bf16[12,48,128]{2,1,0:T(8,128)(2,1)S(1)}, bf16[12,48,128]{2,1,0:T(8,128)(2,1)S(1)}, u32[]{:S(2)}, u32[]{:S(2)}) collective-permute-start(bf16[12,48,128]{2,1,0:T(8,128)(2,1)S(1)} %get-tuple-element.81.value.earlier), channel_id=1, source_target_pairs={{8,16},{24,32},{40,48},{56,64},{72,80},{88,96},{104,112},{120,128}... | collective-permute-start | bytes 442376 | tf_op jit(solution)/shard_map/while/body/eval_jaxpr/ppermute | solution.py:183
  40.1 2.0 %collective-permute-start.2 = (bf16[12,48,128]{2,1,0:T(8,128)(2,1)S(1)}, bf16[12,48,128]{2,1,0:T(8,128)(2,1)S(1)}, u32[]{:S(2)}, u32[]{:S(2)}) collective-permute-start(bf16[12,48,128]{2,1,0:T(8,128)(2,1)S(1)} %get-tuple-element.81.value.earlier), channel_id=1, source_target_pairs={{1,2},{3,4},{5,6},{7,0},{2,1},{4,3},{6,5},{0,7},{9,10},{11,12},{13... | collective-permute-start | bytes 442376 | tf_op jit(solution)/shard_map/while/body/eval_jaxpr/ppermute | solution.py:181
  42.4 2.2 %eval_jaxpr.5.part = f32[12,48,128]{2,1,0:T(8,128)S(1)} custom-call(bf16[12,48,128]{2,1,0:T(8,128)(2,1)S(1)} %get-tuple-element.88.rhs, bf16[12,48,128]{2,1,0:T(8,128)(2,1)S(1)} %get-tuple-element.81.value.earlier, bf16[9,12,128,128]{3,2,1,0:T(8,128)(2,1)} %get-tuple-element.89.links), custom_call_target="tpu_custom_call" | custom-call | flops 94371840 | tf_op jit(solution)/shard_map/while/body/eval_jaxpr/pallas_call | solution.py:26
  44.6 1.1 collective-permute-done.arrived.a
  46.2 2.2 %collective-permute-start = (bf16[12,48,128]{2,1,0:T(8,128)(2,1)S(1)}, bf16[12,48,128]{2,1,0:T(8,128)(2,1)S(1)}, u32[]{:S(2)}, u32[]{:S(2)}) collective-permute-start(bf16[12,48,128]{2,1,0:T(8,128)(2,1)S(1)} %get-tuple-element.81.value.earlier), channel_id=1, source_target_pairs={{8,16},{24,32},{40,48},{56,64},{72,80},{88,96},{104,112},{120,128}... | collective-permute-start | bytes 442376 | tf_op jit(solution)/shard_map/while/body/eval_jaxpr/ppermute | solution.py:183
  48.4 2.6 %collective-permute-start.2 = (bf16[12,48,128]{2,1,0:T(8,128)(2,1)S(1)}, bf16[12,48,128]{2,1,0:T(8,128)(2,1)S(1)}, u32[]{:S(2)}, u32[]{:S(2)}) collective-permute-start(bf16[12,48,128]{2,1,0:T(8,128)(2,1)S(1)} %get-tuple-element.81.value.earlier), channel_id=1, source_target_pairs={{1,2},{3,4},{5,6},{7,0},{2,1},{4,3},{6,5},{0,7},{9,10},{11,12},{13... | collective-permute-start | bytes 442376 | tf_op jit(solution)/shard_map/while/body/eval_jaxpr/ppermute | solution.py:181
  51.7 2.2 %eval_jaxpr.5.part = f32[12,48,128]{2,1,0:T(8,128)S(1)} custom-call(bf16[12,48,128]{2,1,0:T(8,128)(2,1)S(1)} %get-tuple-element.88.rhs, bf16[12,48,128]{2,1,0:T(8,128)(2,1)S(1)} %get-tuple-element.81.value.earlier, bf16[9,12,128,128]{3,2,1,0:T(8,128)(2,1)} %get-tuple-element.89.links), custom_call_target="tpu_custom_call" | custom-call | flops 94371840 | tf_op jit(solution)/shard_map/while/body/eval_jaxpr/pallas_call | solution.py:26
  54.5 3.0 %collective-permute-start = (bf16[12,48,128]{2,1,0:T(8,128)(2,1)S(1)}, bf16[12,48,128]{2,1,0:T(8,128)(2,1)S(1)}, u32[]{:S(2)}, u32[]{:S(2)}) collective-permute-start(bf16[12,48,128]{2,1,0:T(8,128)(2,1)S(1)} %get-tuple-element.81.value.earlier), channel_id=1, source_target_pairs={{8,16},{24,32},{40,48},{56,64},{72,80},{88,96},{104,112},{120,128}... | collective-permute-start | bytes 442376 | tf_op jit(solution)/shard_map/while/body/eval_jaxpr/ppermute | solution.py:183
  57.4 2.6 %collective-permute-start.2 = (bf16[12,48,128]{2,1,0:T(8,128)(2,1)S(1)}, bf16[12,48,128]{2,1,0:T(8,128)(2,1)S(1)}, u32[]{:S(2)}, u32[]{:S(2)}) collective-permute-start(bf16[12,48,128]{2,1,0:T(8,128)(2,1)S(1)} %get-tuple-element.81.value.earlier), channel_id=1, source_target_pairs={{1,2},{3,4},{5,6},{7,0},{2,1},{4,3},{6,5},{0,7},{9,10},{11,12},{13... | collective-permute-start | bytes 442376 | tf_op jit(solution)/shard_map/while/body/eval_jaxpr/ppermute | solution.py:181
  60.7 2.2 %eval_jaxpr.5.part = f32[12,48,128]{2,1,0:T(8,128)S(1)} custom-call(bf16[12,48,128]{2,1,0:T(8,128)(2,1)S(1)} %get-tuple-element.88.rhs, bf16[12,48,128]{2,1,0:T(8,128)(2,1)S(1)} %get-tuple-element.81.value.earlier, bf16[9,12,128,128]{3,2,1,0:T(8,128)(2,1)} %get-tuple-element.89.links), custom_call_target="tpu_custom_call" | custom-call | flops 94371840 | tf_op jit(solution)/shard_map/while/body/eval_jaxpr/pallas_call | solution.py:26
  63.4 3.0 %collective-permute-start = (bf16[12,48,128]{2,1,0:T(8,128)(2,1)S(1)}, bf16[12,48,128]{2,1,0:T(8,128)(2,1)S(1)}, u32[]{:S(2)}, u32[]{:S(2)}) collective-permute-start(bf16[12,48,128]{2,1,0:T(8,128)(2,1)S(1)} %get-tuple-element.81.value.earlier), channel_id=1, source_target_pairs={{8,16},{24,32},{40,48},{56,64},{72,80},{88,96},{104,112},{120,128}... | collective-permute-start | bytes 442376 | tf_op jit(solution)/shard_map/while/body/eval_jaxpr/ppermute | solution.py:183
  66.4 2.6 %collective-permute-start.2 = (bf16[12,48,128]{2,1,0:T(8,128)(2,1)S(1)}, bf16[12,48,128]{2,1,0:T(8,128)(2,1)S(1)}, u32[]{:S(2)}, u32[]{:S(2)}) collective-permute-start(bf16[12,48,128]{2,1,0:T(8,128)(2,1)S(1)} %get-tuple-element.81.value.earlier), channel_id=1, source_target_pairs={{1,2},{3,4},{5,6},{7,0},{2,1},{4,3},{6,5},{0,7},{9,10},{11,12},{13... | collective-permute-start | bytes 442376 | tf_op jit(solution)/shard_map/while/body/eval_jaxpr/ppermute | solution.py:181
  69.7 2.2 %eval_jaxpr.5.part = f32[12,48,128]{2,1,0:T(8,128)S(1)} custom-call(bf16[12,48,128]{2,1,0:T(8,128)(2,1)S(1)} %get-tuple-element.88.rhs, bf16[12,48,128]{2,1,0:T(8,128)(2,1)S(1)} %get-tuple-element.81.value.earlier, bf16[9,12,128,128]{3,2,1,0:T(8,128)(2,1)} %get-tuple-element.89.links), custom_call_target="tpu_custom_call" | custom-call | flops 94371840 | tf_op jit(solution)/shard_map/while/body/eval_jaxpr/pallas_call | solution.py:26
  72.4 3.0 %collective-permute-start = (bf16[12,48,128]{2,1,0:T(8,128)(2,1)S(1)}, bf16[12,48,128]{2,1,0:T(8,128)(2,1)S(1)}, u32[]{:S(2)}, u32[]{:S(2)}) collective-permute-start(bf16[12,48,128]{2,1,0:T(8,128)(2,1)S(1)} %get-tuple-element.81.value.earlier), channel_id=1, source_target_pairs={{8,16},{24,32},{40,48},{56,64},{72,80},{88,96},{104,112},{120,128}... | collective-permute-start | bytes 442376 | tf_op jit(solution)/shard_map/while/body/eval_jaxpr/ppermute | solution.py:183
  75.4 2.6 %collective-permute-start.2 = (bf16[12,48,128]{2,1,0:T(8,128)(2,1)S(1)}, bf16[12,48,128]{2,1,0:T(8,128)(2,1)S(1)}, u32[]{:S(2)}, u32[]{:S(2)}) collective-permute-start(bf16[12,48,128]{2,1,0:T(8,128)(2,1)S(1)} %get-tuple-element.81.value.earlier), channel_id=1, source_target_pairs={{1,2},{3,4},{5,6},{7,0},{2,1},{4,3},{6,5},{0,7},{9,10},{11,12},{13... | collective-permute-start | bytes 442376 | tf_op jit(solution)/shard_map/while/body/eval_jaxpr/ppermute | solution.py:181
  78.7 2.2 %eval_jaxpr.5.part = f32[12,48,128]{2,1,0:T(8,128)S(1)} custom-call(bf16[12,48,128]{2,1,0:T(8,128)(2,1)S(1)} %get-tuple-element.88.rhs, bf16[12,48,128]{2,1,0:T(8,128)(2,1)S(1)} %get-tuple-element.81.value.earlier, bf16[9,12,128,128]{3,2,1,0:T(8,128)(2,1)} %get-tuple-element.89.links), custom_call_target="tpu_custom_call" | custom-call | flops 94371840 | tf_op jit(solution)/shard_map/while/body/eval_jaxpr/pallas_call | solution.py:26
  81.4 3.0 %collective-permute-start = (bf16[12,48,128]{2,1,0:T(8,128)(2,1)S(1)}, bf16[12,48,128]{2,1,0:T(8,128)(2,1)S(1)}, u32[]{:S(2)}, u32[]{:S(2)}) collective-permute-start(bf16[12,48,128]{2,1,0:T(8,128)(2,1)S(1)} %get-tuple-element.81.value.earlier), channel_id=1, source_target_pairs={{8,16},{24,32},{40,48},{56,64},{72,80},{88,96},{104,112},{120,128}... | collective-permute-start | bytes 442376 | tf_op jit(solution)/shard_map/while/body/eval_jaxpr/ppermute | solution.py:183
  84.4 2.6 %collective-permute-start.2 = (bf16[12,48,128]{2,1,0:T(8,128)(2,1)S(1)}, bf16[12,48,128]{2,1,0:T(8,128)(2,1)S(1)}, u32[]{:S(2)}, u32[]{:S(2)}) collective-permute-start(bf16[12,48,128]{2,1,0:T(8,128)(2,1)S(1)} %get-tuple-element.81.value.earlier), channel_id=1, source_target_pairs={{1,2},{3,4},{5,6},{7,0},{2,1},{4,3},{6,5},{0,7},{9,10},{11,12},{13... | collective-permute-start | bytes 442376 | tf_op jit(solution)/shard_map/while/body/eval_jaxpr/ppermute | solution.py:181
  87.0 0.7 collective-permute-start.3
  87.7 2.2 %eval_jaxpr.5.part = f32[12,48,128]{2,1,0:T(8,128)S(1)} custom-call(bf16[12,48,128]{2,1,0:T(8,128)(2,1)S(1)} %get-tuple-element.88.rhs, bf16[12,48,128]{2,1,0:T(8,128)(2,1)S(1)} %get-tuple-element.81.value.earlier, bf16[9,12,128,128]{3,2,1,0:T(8,128)(2,1)} %get-tuple-element.89.links), custom_call_target="tpu_custom_call" | custom-call | flops 94371840 | tf_op jit(solution)/shard_map/while/body/eval_jaxpr/pallas_call | solution.py:26
  90.4 3.0 %collective-permute-start = (bf16[12,48,128]{2,1,0:T(8,128)(2,1)S(1)}, bf16[12,48,128]{2,1,0:T(8,128)(2,1)S(1)}, u32[]{:S(2)}, u32[]{:S(2)}) collective-permute-start(bf16[12,48,128]{2,1,0:T(8,128)(2,1)S(1)} %get-tuple-element.81.value.earlier), channel_id=1, source_target_pairs={{8,16},{24,32},{40,48},{56,64},{72,80},{88,96},{104,112},{120,128}... | collective-permute-start | bytes 442376 | tf_op jit(solution)/shard_map/while/body/eval_jaxpr/ppermute | solution.py:183
  93.4 2.6 %collective-permute-start.2 = (bf16[12,48,128]{2,1,0:T(8,128)(2,1)S(1)}, bf16[12,48,128]{2,1,0:T(8,128)(2,1)S(1)}, u32[]{:S(2)}, u32[]{:S(2)}) collective-permute-start(bf16[12,48,128]{2,1,0:T(8,128)(2,1)S(1)} %get-tuple-element.81.value.earlier), channel_id=1, source_target_pairs={{1,2},{3,4},{5,6},{7,0},{2,1},{4,3},{6,5},{0,7},{9,10},{11,12},{13... | collective-permute-start | bytes 442376 | tf_op jit(solution)/shard_map/while/body/eval_jaxpr/ppermute | solution.py:181
  96.7 2.2 %eval_jaxpr.5.part = f32[12,48,128]{2,1,0:T(8,128)S(1)} custom-call(bf16[12,48,128]{2,1,0:T(8,128)(2,1)S(1)} %get-tuple-element.88.rhs, bf16[12,48,128]{2,1,0:T(8,128)(2,1)S(1)} %get-tuple-element.81.value.earlier, bf16[9,12,128,128]{3,2,1,0:T(8,128)(2,1)} %get-tuple-element.89.links), custom_call_target="tpu_custom_call" | custom-call | flops 94371840 | tf_op jit(solution)/shard_map/while/body/eval_jaxpr/pallas_call | solution.py:26
  99.4 3.0 %collective-permute-start = (bf16[12,48,128]{2,1,0:T(8,128)(2,1)S(1)}, bf16[12,48,128]{2,1,0:T(8,128)(2,1)S(1)}, u32[]{:S(2)}, u32[]{:S(2)}) collective-permute-start(bf16[12,48,128]{2,1,0:T(8,128)(2,1)S(1)} %get-tuple-element.81.value.earlier), channel_id=1, source_target_pairs={{8,16},{24,32},{40,48},{56,64},{72,80},{88,96},{104,112},{120,128}... | collective-permute-start | bytes 442376 | tf_op jit(solution)/shard_map/while/body/eval_jaxpr/ppermute | solution.py:183
  102.4 2.6 %collective-permute-start.2 = (bf16[12,48,128]{2,1,0:T(8,128)(2,1)S(1)}, bf16[12,48,128]{2,1,0:T(8,128)(2,1)S(1)}, u32[]{:S(2)}, u32[]{:S(2)}) collective-permute-start(bf16[12,48,128]{2,1,0:T(8,128)(2,1)S(1)} %get-tuple-element.81.value.earlier), channel_id=1, source_target_pairs={{1,2},{3,4},{5,6},{7,0},{2,1},{4,3},{6,5},{0,7},{9,10},{11,12},{13... | collective-permute-start | bytes 442376 | tf_op jit(solution)/shard_map/while/body/eval_jaxpr/ppermute | solution.py:181
  105.0 0.7 collective-permute-start.3
  105.7 2.2 %eval_jaxpr.5.part = f32[12,48,128]{2,1,0:T(8,128)S(1)} custom-call(bf16[12,48,128]{2,1,0:T(8,128)(2,1)S(1)} %get-tuple-element.88.rhs, bf16[12,48,128]{2,1,0:T(8,128)(2,1)S(1)} %get-tuple-element.81.value.earlier, bf16[9,12,128,128]{3,2,1,0:T(8,128)(2,1)} %get-tuple-element.89.links), custom_call_target="tpu_custom_call" | custom-call | flops 94371840 | tf_op jit(solution)/shard_map/while/body/eval_jaxpr/pallas_call | solution.py:26
  108.4 3.0 %collective-permute-start = (bf16[12,48,128]{2,1,0:T(8,128)(2,1)S(1)}, bf16[12,48,128]{2,1,0:T(8,128)(2,1)S(1)}, u32[]{:S(2)}, u32[]{:S(2)}) collective-permute-start(bf16[12,48,128]{2,1,0:T(8,128)(2,1)S(1)} %get-tuple-element.81.value.earlier), channel_id=1, source_target_pairs={{8,16},{24,32},{40,48},{56,64},{72,80},{88,96},{104,112},{120,128}... | collective-permute-start | bytes 442376 | tf_op jit(solution)/shard_map/while/body/eval_jaxpr/ppermute | solution.py:183
  111.4 2.6 %collective-permute-start.2 = (bf16[12,48,128]{2,1,0:T(8,128)(2,1)S(1)}, bf16[12,48,128]{2,1,0:T(8,128)(2,1)S(1)}, u32[]{:S(2)}, u32[]{:S(2)}) collective-permute-start(bf16[12,48,128]{2,1,0:T(8,128)(2,1)S(1)} %get-tuple-element.81.value.earlier), channel_id=1, source_target_pairs={{1,2},{3,4},{5,6},{7,0},{2,1},{4,3},{6,5},{0,7},{9,10},{11,12},{13... | collective-permute-start | bytes 442376 | tf_op jit(solution)/shard_map/while/body/eval_jaxpr/ppermute | solution.py:181
  114.0 0.7 collective-permute-start.3
  114.7 2.2 %eval_jaxpr.5.part = f32[12,48,128]{2,1,0:T(8,128)S(1)} custom-call(bf16[12,48,128]{2,1,0:T(8,128)(2,1)S(1)} %get-tuple-element.88.rhs, bf16[12,48,128]{2,1,0:T(8,128)(2,1)S(1)} %get-tuple-element.81.value.earlier, bf16[9,12,128,128]{3,2,1,0:T(8,128)(2,1)} %get-tuple-element.89.links), custom_call_target="tpu_custom_call" | custom-call | flops 94371840 | tf_op jit(solution)/shard_map/while/body/eval_jaxpr/pallas_call | solution.py:26
  117.4 3.0 %collective-permute-start = (bf16[12,48,128]{2,1,0:T(8,128)(2,1)S(1)}, bf16[12,48,128]{2,1,0:T(8,128)(2,1)S(1)}, u32[]{:S(2)}, u32[]{:S(2)}) collective-permute-start(bf16[12,48,128]{2,1,0:T(8,128)(2,1)S(1)} %get-tuple-element.81.value.earlier), channel_id=1, source_target_pairs={{8,16},{24,32},{40,48},{56,64},{72,80},{88,96},{104,112},{120,128}... | collective-permute-start | bytes 442376 | tf_op jit(solution)/shard_map/while/body/eval_jaxpr/ppermute | solution.py:183
  120.3 2.6 %collective-permute-start.2 = (bf16[12,48,128]{2,1,0:T(8,128)(2,1)S(1)}, bf16[12,48,128]{2,1,0:T(8,128)(2,1)S(1)}, u32[]{:S(2)}, u32[]{:S(2)}) collective-permute-start(bf16[12,48,128]{2,1,0:T(8,128)(2,1)S(1)} %get-tuple-element.81.value.earlier), channel_id=1, source_target_pairs={{1,2},{3,4},{5,6},{7,0},{2,1},{4,3},{6,5},{0,7},{9,10},{11,12},{13... | collective-permute-start | bytes 442376 | tf_op jit(solution)/shard_map/while/body/eval_jaxpr/ppermute | solution.py:181
  123.0 0.7 collective-permute-start.3
  123.7 2.2 %eval_jaxpr.5.part = f32[12,48,128]{2,1,0:T(8,128)S(1)} custom-call(bf16[12,48,128]{2,1,0:T(8,128)(2,1)S(1)} %get-tuple-element.88.rhs, bf16[12,48,128]{2,1,0:T(8,128)(2,1)S(1)} %get-tuple-element.81.value.earlier, bf16[9,12,128,128]{3,2,1,0:T(8,128)(2,1)} %get-tuple-element.89.links), custom_call_target="tpu_custom_call" | custom-call | flops 94371840 | tf_op jit(solution)/shard_map/while/body/eval_jaxpr/pallas_call | solution.py:26
  126.4 3.0 %collective-permute-start = (bf16[12,48,128]{2,1,0:T(8,128)(2,1)S(1)}, bf16[12,48,128]{2,1,0:T(8,128)(2,1)S(1)}, u32[]{:S(2)}, u32[]{:S(2)}) collective-permute-start(bf16[12,48,128]{2,1,0:T(8,128)(2,1)S(1)} %get-tuple-element.81.value.earlier), channel_id=1, source_target_pairs={{8,16},{24,32},{40,48},{56,64},{72,80},{88,96},{104,112},{120,128}... | collective-permute-start | bytes 442376 | tf_op jit(solution)/shard_map/while/body/eval_jaxpr/ppermute | solution.py:183
  129.3 2.6 %collective-permute-start.2 = (bf16[12,48,128]{2,1,0:T(8,128)(2,1)S(1)}, bf16[12,48,128]{2,1,0:T(8,128)(2,1)S(1)}, u32[]{:S(2)}, u32[]{:S(2)}) collective-permute-start(bf16[12,48,128]{2,1,0:T(8,128)(2,1)S(1)} %get-tuple-element.81.value.earlier), channel_id=1, source_target_pairs={{1,2},{3,4},{5,6},{7,0},{2,1},{4,3},{6,5},{0,7},{9,10},{11,12},{13... | collective-permute-start | bytes 442376 | tf_op jit(solution)/shard_map/while/body/eval_jaxpr/ppermute | solution.py:181
  132.0 0.7 collective-permute-start.3
  132.6 2.2 %eval_jaxpr.5.part = f32[12,48,128]{2,1,0:T(8,128)S(1)} custom-call(bf16[12,48,128]{2,1,0:T(8,128)(2,1)S(1)} %get-tuple-element.88.rhs, bf16[12,48,128]{2,1,0:T(8,128)(2,1)S(1)} %get-tuple-element.81.value.earlier, bf16[9,12,128,128]{3,2,1,0:T(8,128)(2,1)} %get-tuple-element.89.links), custom_call_target="tpu_custom_call" | custom-call | flops 94371840 | tf_op jit(solution)/shard_map/while/body/eval_jaxpr/pallas_call | solution.py:26
  135.4 3.0 %collective-permute-start = (bf16[12,48,128]{2,1,0:T(8,128)(2,1)S(1)}, bf16[12,48,128]{2,1,0:T(8,128)(2,1)S(1)}, u32[]{:S(2)}, u32[]{:S(2)}) collective-permute-start(bf16[12,48,128]{2,1,0:T(8,128)(2,1)S(1)} %get-tuple-element.81.value.earlier), channel_id=1, source_target_pairs={{8,16},{24,32},{40,48},{56,64},{72,80},{88,96},{104,112},{120,128}... | collective-permute-start | bytes 442376 | tf_op jit(solution)/shard_map/while/body/eval_jaxpr/ppermute | solution.py:183
  138.3 2.6 %collective-permute-start.2 = (bf16[12,48,128]{2,1,0:T(8,128)(2,1)S(1)}, bf16[12,48,128]{2,1,0:T(8,128)(2,1)S(1)}, u32[]{:S(2)}, u32[]{:S(2)}) collective-permute-start(bf16[12,48,128]{2,1,0:T(8,128)(2,1)S(1)} %get-tuple-element.81.value.earlier), channel_id=1, source_target_pairs={{1,2},{3,4},{5,6},{7,0},{2,1},{4,3},{6,5},{0,7},{9,10},{11,12},{13... | collective-permute-start | bytes 442376 | tf_op jit(solution)/shard_map/while/body/eval_jaxpr/ppermute | solution.py:181
  141.0 0.7 collective-permute-start.3
  141.6 2.2 %eval_jaxpr.5.part = f32[12,48,128]{2,1,0:T(8,128)S(1)} custom-call(bf16[12,48,128]{2,1,0:T(8,128)(2,1)S(1)} %get-tuple-element.88.rhs, bf16[12,48,128]{2,1,0:T(8,128)(2,1)S(1)} %get-tuple-element.81.value.earlier, bf16[9,12,128,128]{3,2,1,0:T(8,128)(2,1)} %get-tuple-element.89.links), custom_call_target="tpu_custom_call" | custom-call | flops 94371840 | tf_op jit(solution)/shard_map/while/body/eval_jaxpr/pallas_call | solution.py:26
  144.3 3.0 %collective-permute-start.8 = (bf16[12,48,128]{2,1,0:T(8,128)(2,1)S(1)}, bf16[12,48,128]{2,1,0:T(8,128)(2,1)S(1)}, u32[]{:S(2)}, u32[]{:S(2)}) collective-permute-start(bf16[12,48,128]{2,1,0:T(8,128)(2,1)S(1)} %get-tuple-element.32.value.earlier), channel_id=1, source_target_pairs={{8,16},{24,32},{40,48},{56,64},{72,80},{88,96},{104,112},{120,128}... | collective-permute-start | bytes 442376 | tf_op jit(solution)/shard_map/ppermute | solution.py:183
  147.3 2.6 %collective-permute-start.10 = (bf16[12,48,128]{2,1,0:T(8,128)(2,1)S(1)}, bf16[12,48,128]{2,1,0:T(8,128)(2,1)S(1)}, u32[]{:S(2)}, u32[]{:S(2)}) collective-permute-start(bf16[12,48,128]{2,1,0:T(8,128)(2,1)S(1)} %get-tuple-element.32.value.earlier), channel_id=1, source_target_pairs={{1,2},{3,4},{5,6},{7,0},{2,1},{4,3},{6,5},{0,7},{9,10},{11,12},{13... | collective-permute-start | bytes 442376 | tf_op jit(solution)/shard_map/ppermute | solution.py:181
  149.9 0.7 collective-permute-start.11
  150.6 3.0 %shard_map.49.weights = bf16[12,128,1536]{2,1,0:T(8,128)(2,1)S(1)} custom-call(bf16[12,1536,128]{2,1,0:T(8,128)(2,1)} %bitcast.13, bf16[12,48,128]{2,1,0:T(8,128)(2,1)S(1)} %get-tuple-element.32.value.earlier), custom_call_target="tpu_custom_call" | custom-call | tf_op jit(solution)/shard_map/pallas_call | solution.py:26
  153.6 2.2 %shard_map.44.part = f32[12,48,128]{2,1,0:T(8,128)S(1)} custom-call(bf16[12,48,128]{2,1,0:T(8,128)(2,1)S(1)} %get-tuple-element.105, bf16[12,48,128]{2,1,0:T(8,128)(2,1)S(1)} %get-tuple-element.32.value.earlier, bf16[9,12,128,128]{3,2,1,0:T(8,128)(2,1)} %get-tuple-element.118), custom_call_target="tpu_custom_call" | custom-call | flops 94371840 | tf_op jit(solution)/shard_map/pallas_call | solution.py:26
  156.3 1.5 shard_map.50
  (150 shorter events, 10.2 us)
Async XLA Ops:
  3.7 16.4 %collective-permute-start.4 = (bf16[12,48,128]{2,1,0:T(8,128)(2,1)S(1)}, bf16[12,48,128]{2,1,0:T(8,128)(2,1)S(1)}, u32[]{:S(2)}, u32[]{:S(2)}) collective-permute-start(bf16[12,48,128]{2,1,0:T(8,128)(2,1)S(1)} %shard_map.37.rhs.value.earlier), channel_id=1, source_target_pairs={{8,16},{24,32},{40,48},{56,64},{72,80},{88,96},{104,112},{120,128}... | collective-permute-start | bytes 442376 | tf_op jit(solution)/shard_map/ppermute | solution.py:183
  12.6 7.5 %collective-permute-start.5 = (bf16[12,48,128]{2,1,0:T(8,128)(2,1)S(1)}, bf16[12,48,128]{2,1,0:T(8,128)(2,1)S(1)}, u32[]{:S(2)}, u32[]{:S(2)}) collective-permute-start(bf16[12,48,128]{2,1,0:T(8,128)(2,1)S(1)} %shard_map.37.rhs.value.earlier), channel_id=1, source_target_pairs={{0,8},{16,24},{32,40},{48,56},{64,72},{80,88},{96,104},{112,120},{... | collective-permute-start | bytes 442376 | tf_op jit(solution)/shard_map/ppermute | solution.py:182
  12.6 7.5 %collective-permute-start.6 = (bf16[12,48,128]{2,1,0:T(8,128)(2,1)S(1)}, bf16[12,48,128]{2,1,0:T(8,128)(2,1)S(1)}, u32[]{:S(2)}, u32[]{:S(2)}) collective-permute-start(bf16[12,48,128]{2,1,0:T(8,128)(2,1)S(1)} %shard_map.37.rhs.value.earlier), channel_id=1, source_target_pairs={{1,2},{3,4},{5,6},{7,0},{2,1},{4,3},{6,5},{0,7},{9,10},{11,12},{13... | collective-permute-start | bytes 442376 | tf_op jit(solution)/shard_map/ppermute | solution.py:181
  14.7 5.5 %collective-permute-start.7 = (bf16[12,48,128]{2,1,0:T(8,128)(2,1)S(1)}, bf16[12,48,128]{2,1,0:T(8,128)(2,1)S(1)}, u32[]{:S(2)}, u32[]{:S(2)}) collective-permute-start(bf16[12,48,128]{2,1,0:T(8,128)(2,1)S(1)} %shard_map.37.rhs.value.earlier), channel_id=1, source_target_pairs={{0,1},{2,3},{4,5},{6,7},{1,0},{3,2},{5,4},{7,6},{8,9},{10,11},{12,... | collective-permute-start | bytes 442376 | tf_op jit(solution)/shard_map/ppermute | solution.py:180
  20.6 8.9 %collective-permute-start = (bf16[12,48,128]{2,1,0:T(8,128)(2,1)S(1)}, bf16[12,48,128]{2,1,0:T(8,128)(2,1)S(1)}, u32[]{:S(2)}, u32[]{:S(2)}) collective-permute-start(bf16[12,48,128]{2,1,0:T(8,128)(2,1)S(1)} %get-tuple-element.81.value.earlier), channel_id=1, source_target_pairs={{8,16},{24,32},{40,48},{56,64},{72,80},{88,96},{104,112},{120,128}... | collective-permute-start | bytes 442376 | tf_op jit(solution)/shard_map/while/body/eval_jaxpr/ppermute | solution.py:183
  22.1 7.4 %collective-permute-start.1 = (bf16[12,48,128]{2,1,0:T(8,128)(2,1)S(1)}, bf16[12,48,128]{2,1,0:T(8,128)(2,1)S(1)}, u32[]{:S(2)}, u32[]{:S(2)}) collective-permute-start(bf16[12,48,128]{2,1,0:T(8,128)(2,1)S(1)} %get-tuple-element.81.value.earlier), channel_id=1, source_target_pairs={{0,8},{16,24},{32,40},{48,56},{64,72},{80,88},{96,104},{112,120},{... | collective-permute-start | bytes 442376 | tf_op jit(solution)/shard_map/while/body/eval_jaxpr/ppermute | solution.py:182
  22.2 7.3 %collective-permute-start.2 = (bf16[12,48,128]{2,1,0:T(8,128)(2,1)S(1)}, bf16[12,48,128]{2,1,0:T(8,128)(2,1)S(1)}, u32[]{:S(2)}, u32[]{:S(2)}) collective-permute-start(bf16[12,48,128]{2,1,0:T(8,128)(2,1)S(1)} %get-tuple-element.81.value.earlier), channel_id=1, source_target_pairs={{1,2},{3,4},{5,6},{7,0},{2,1},{4,3},{6,5},{0,7},{9,10},{11,12},{13... | collective-permute-start | bytes 442376 | tf_op jit(solution)/shard_map/while/body/eval_jaxpr/ppermute | solution.py:181
  24.1 5.4 %collective-permute-start.3 = (bf16[12,48,128]{2,1,0:T(8,128)(2,1)S(1)}, bf16[12,48,128]{2,1,0:T(8,128)(2,1)S(1)}, u32[]{:S(2)}, u32[]{:S(2)}) collective-permute-start(bf16[12,48,128]{2,1,0:T(8,128)(2,1)S(1)} %get-tuple-element.81.value.earlier), channel_id=1, source_target_pairs={{0,1},{2,3},{4,5},{6,7},{1,0},{3,2},{5,4},{7,6},{8,9},{10,11},{12,... | collective-permute-start | bytes 442376 | tf_op jit(solution)/shard_map/while/body/eval_jaxpr/ppermute | solution.py:180
  29.9 8.0 %collective-permute-start = (bf16[12,48,128]{2,1,0:T(8,128)(2,1)S(1)}, bf16[12,48,128]{2,1,0:T(8,128)(2,1)S(1)}, u32[]{:S(2)}, u32[]{:S(2)}) collective-permute-start(bf16[12,48,128]{2,1,0:T(8,128)(2,1)S(1)} %get-tuple-element.81.value.earlier), channel_id=1, source_target_pairs={{8,16},{24,32},{40,48},{56,64},{72,80},{88,96},{104,112},{120,128}... | collective-permute-start | bytes 442376 | tf_op jit(solution)/shard_map/while/body/eval_jaxpr/ppermute | solution.py:183
  31.1 6.8 %collective-permute-start.1 = (bf16[12,48,128]{2,1,0:T(8,128)(2,1)S(1)}, bf16[12,48,128]{2,1,0:T(8,128)(2,1)S(1)}, u32[]{:S(2)}, u32[]{:S(2)}) collective-permute-start(bf16[12,48,128]{2,1,0:T(8,128)(2,1)S(1)} %get-tuple-element.81.value.earlier), channel_id=1, source_target_pairs={{0,8},{16,24},{32,40},{48,56},{64,72},{80,88},{96,104},{112,120},{... | collective-permute-start | bytes 442376 | tf_op jit(solution)/shard_map/while/body/eval_jaxpr/ppermute | solution.py:182
  31.1 6.8 %collective-permute-start.2 = (bf16[12,48,128]{2,1,0:T(8,128)(2,1)S(1)}, bf16[12,48,128]{2,1,0:T(8,128)(2,1)S(1)}, u32[]{:S(2)}, u32[]{:S(2)}) collective-permute-start(bf16[12,48,128]{2,1,0:T(8,128)(2,1)S(1)} %get-tuple-element.81.value.earlier), channel_id=1, source_target_pairs={{1,2},{3,4},{5,6},{7,0},{2,1},{4,3},{6,5},{0,7},{9,10},{11,12},{13... | collective-permute-start | bytes 442376 | tf_op jit(solution)/shard_map/while/body/eval_jaxpr/ppermute | solution.py:181
  33.1 4.8 %collective-permute-start.3 = (bf16[12,48,128]{2,1,0:T(8,128)(2,1)S(1)}, bf16[12,48,128]{2,1,0:T(8,128)(2,1)S(1)}, u32[]{:S(2)}, u32[]{:S(2)}) collective-permute-start(bf16[12,48,128]{2,1,0:T(8,128)(2,1)S(1)} %get-tuple-element.81.value.earlier), channel_id=1, source_target_pairs={{0,1},{2,3},{4,5},{6,7},{1,0},{3,2},{5,4},{7,6},{8,9},{10,11},{12,... | collective-permute-start | bytes 442376 | tf_op jit(solution)/shard_map/while/body/eval_jaxpr/ppermute | solution.py:180
  38.3 7.4 %collective-permute-start = (bf16[12,48,128]{2,1,0:T(8,128)(2,1)S(1)}, bf16[12,48,128]{2,1,0:T(8,128)(2,1)S(1)}, u32[]{:S(2)}, u32[]{:S(2)}) collective-permute-start(bf16[12,48,128]{2,1,0:T(8,128)(2,1)S(1)} %get-tuple-element.81.value.earlier), channel_id=1, source_target_pairs={{8,16},{24,32},{40,48},{56,64},{72,80},{88,96},{104,112},{120,128}... | collective-permute-start | bytes 442376 | tf_op jit(solution)/shard_map/while/body/eval_jaxpr/ppermute | solution.py:183
  40.1 5.6 %collective-permute-start.1 = (bf16[12,48,128]{2,1,0:T(8,128)(2,1)S(1)}, bf16[12,48,128]{2,1,0:T(8,128)(2,1)S(1)}, u32[]{:S(2)}, u32[]{:S(2)}) collective-permute-start(bf16[12,48,128]{2,1,0:T(8,128)(2,1)S(1)} %get-tuple-element.81.value.earlier), channel_id=1, source_target_pairs={{0,8},{16,24},{32,40},{48,56},{64,72},{80,88},{96,104},{112,120},{... | collective-permute-start | bytes 442376 | tf_op jit(solution)/shard_map/while/body/eval_jaxpr/ppermute | solution.py:182
  40.1 5.6 %collective-permute-start.2 = (bf16[12,48,128]{2,1,0:T(8,128)(2,1)S(1)}, bf16[12,48,128]{2,1,0:T(8,128)(2,1)S(1)}, u32[]{:S(2)}, u32[]{:S(2)}) collective-permute-start(bf16[12,48,128]{2,1,0:T(8,128)(2,1)S(1)} %get-tuple-element.81.value.earlier), channel_id=1, source_target_pairs={{1,2},{3,4},{5,6},{7,0},{2,1},{4,3},{6,5},{0,7},{9,10},{11,12},{13... | collective-permute-start | bytes 442376 | tf_op jit(solution)/shard_map/while/body/eval_jaxpr/ppermute | solution.py:181
  42.1 3.7 %collective-permute-start.3 = (bf16[12,48,128]{2,1,0:T(8,128)(2,1)S(1)}, bf16[12,48,128]{2,1,0:T(8,128)(2,1)S(1)}, u32[]{:S(2)}, u32[]{:S(2)}) collective-permute-start(bf16[12,48,128]{2,1,0:T(8,128)(2,1)S(1)} %get-tuple-element.81.value.earlier), channel_id=1, source_target_pairs={{0,1},{2,3},{4,5},{6,7},{1,0},{3,2},{5,4},{7,6},{8,9},{10,11},{12,... | collective-permute-start | bytes 442376 | tf_op jit(solution)/shard_map/while/body/eval_jaxpr/ppermute | solution.py:180
  46.2 7.8 %collective-permute-start = (bf16[12,48,128]{2,1,0:T(8,128)(2,1)S(1)}, bf16[12,48,128]{2,1,0:T(8,128)(2,1)S(1)}, u32[]{:S(2)}, u32[]{:S(2)}) collective-permute-start(bf16[12,48,128]{2,1,0:T(8,128)(2,1)S(1)} %get-tuple-element.81.value.earlier), channel_id=1, source_target_pairs={{8,16},{24,32},{40,48},{56,64},{72,80},{88,96},{104,112},{120,128}... | collective-permute-start | bytes 442376 | tf_op jit(solution)/shard_map/while/body/eval_jaxpr/ppermute | solution.py:183
  48.4 5.6 %collective-permute-start.1 = (bf16[12,48,128]{2,1,0:T(8,128)(2,1)S(1)}, bf16[12,48,128]{2,1,0:T(8,128)(2,1)S(1)}, u32[]{:S(2)}, u32[]{:S(2)}) collective-permute-start(bf16[12,48,128]{2,1,0:T(8,128)(2,1)S(1)} %get-tuple-element.81.value.earlier), channel_id=1, source_target_pairs={{0,8},{16,24},{32,40},{48,56},{64,72},{80,88},{96,104},{112,120},{... | collective-permute-start | bytes 442376 | tf_op jit(solution)/shard_map/while/body/eval_jaxpr/ppermute | solution.py:182
  48.4 5.6 %collective-permute-start.2 = (bf16[12,48,128]{2,1,0:T(8,128)(2,1)S(1)}, bf16[12,48,128]{2,1,0:T(8,128)(2,1)S(1)}, u32[]{:S(2)}, u32[]{:S(2)}) collective-permute-start(bf16[12,48,128]{2,1,0:T(8,128)(2,1)S(1)} %get-tuple-element.81.value.earlier), channel_id=1, source_target_pairs={{1,2},{3,4},{5,6},{7,0},{2,1},{4,3},{6,5},{0,7},{9,10},{11,12},{13... | collective-permute-start | bytes 442376 | tf_op jit(solution)/shard_map/while/body/eval_jaxpr/ppermute | solution.py:181
  51.1 3.0 %collective-permute-start.3 = (bf16[12,48,128]{2,1,0:T(8,128)(2,1)S(1)}, bf16[12,48,128]{2,1,0:T(8,128)(2,1)S(1)}, u32[]{:S(2)}, u32[]{:S(2)}) collective-permute-start(bf16[12,48,128]{2,1,0:T(8,128)(2,1)S(1)} %get-tuple-element.81.value.earlier), channel_id=1, source_target_pairs={{0,1},{2,3},{4,5},{6,7},{1,0},{3,2},{5,4},{7,6},{8,9},{10,11},{12,... | collective-permute-start | bytes 442376 | tf_op jit(solution)/shard_map/while/body/eval_jaxpr/ppermute | solution.py:180
  54.5 8.5 %collective-permute-start = (bf16[12,48,128]{2,1,0:T(8,128)(2,1)S(1)}, bf16[12,48,128]{2,1,0:T(8,128)(2,1)S(1)}, u32[]{:S(2)}, u32[]{:S(2)}) collective-permute-start(bf16[12,48,128]{2,1,0:T(8,128)(2,1)S(1)} %get-tuple-element.81.value.earlier), channel_id=1, source_target_pairs={{8,16},{24,32},{40,48},{56,64},{72,80},{88,96},{104,112},{120,128}... | collective-permute-start | bytes 442376 | tf_op jit(solution)/shard_map/while/body/eval_jaxpr/ppermute | solution.py:183
  57.4 5.6 %collective-permute-start.1 = (bf16[12,48,128]{2,1,0:T(8,128)(2,1)S(1)}, bf16[12,48,128]{2,1,0:T(8,128)(2,1)S(1)}, u32[]{:S(2)}, u32[]{:S(2)}) collective-permute-start(bf16[12,48,128]{2,1,0:T(8,128)(2,1)S(1)} %get-tuple-element.81.value.earlier), channel_id=1, source_target_pairs={{0,8},{16,24},{32,40},{48,56},{64,72},{80,88},{96,104},{112,120},{... | collective-permute-start | bytes 442376 | tf_op jit(solution)/shard_map/while/body/eval_jaxpr/ppermute | solution.py:182
  57.4 5.6 %collective-permute-start.2 = (bf16[12,48,128]{2,1,0:T(8,128)(2,1)S(1)}, bf16[12,48,128]{2,1,0:T(8,128)(2,1)S(1)}, u32[]{:S(2)}, u32[]{:S(2)}) collective-permute-start(bf16[12,48,128]{2,1,0:T(8,128)(2,1)S(1)} %get-tuple-element.81.value.earlier), channel_id=1, source_target_pairs={{1,2},{3,4},{5,6},{7,0},{2,1},{4,3},{6,5},{0,7},{9,10},{11,12},{13... | collective-permute-start | bytes 442376 | tf_op jit(solution)/shard_map/while/body/eval_jaxpr/ppermute | solution.py:181
  60.1 3.0 %collective-permute-start.3 = (bf16[12,48,128]{2,1,0:T(8,128)(2,1)S(1)}, bf16[12,48,128]{2,1,0:T(8,128)(2,1)S(1)}, u32[]{:S(2)}, u32[]{:S(2)}) collective-permute-start(bf16[12,48,128]{2,1,0:T(8,128)(2,1)S(1)} %get-tuple-element.81.value.earlier), channel_id=1, source_target_pairs={{0,1},{2,3},{4,5},{6,7},{1,0},{3,2},{5,4},{7,6},{8,9},{10,11},{12,... | collective-permute-start | bytes 442376 | tf_op jit(solution)/shard_map/while/body/eval_jaxpr/ppermute | solution.py:180
  63.4 8.5 %collective-permute-start = (bf16[12,48,128]{2,1,0:T(8,128)(2,1)S(1)}, bf16[12,48,128]{2,1,0:T(8,128)(2,1)S(1)}, u32[]{:S(2)}, u32[]{:S(2)}) collective-permute-start(bf16[12,48,128]{2,1,0:T(8,128)(2,1)S(1)} %get-tuple-element.81.value.earlier), channel_id=1, source_target_pairs={{8,16},{24,32},{40,48},{56,64},{72,80},{88,96},{104,112},{120,128}... | collective-permute-start | bytes 442376 | tf_op jit(solution)/shard_map/while/body/eval_jaxpr/ppermute | solution.py:183
  66.4 5.6 %collective-permute-start.1 = (bf16[12,48,128]{2,1,0:T(8,128)(2,1)S(1)}, bf16[12,48,128]{2,1,0:T(8,128)(2,1)S(1)}, u32[]{:S(2)}, u32[]{:S(2)}) collective-permute-start(bf16[12,48,128]{2,1,0:T(8,128)(2,1)S(1)} %get-tuple-element.81.value.earlier), channel_id=1, source_target_pairs={{0,8},{16,24},{32,40},{48,56},{64,72},{80,88},{96,104},{112,120},{... | collective-permute-start | bytes 442376 | tf_op jit(solution)/shard_map/while/body/eval_jaxpr/ppermute | solution.py:182
  66.4 5.6 %collective-permute-start.2 = (bf16[12,48,128]{2,1,0:T(8,128)(2,1)S(1)}, bf16[12,48,128]{2,1,0:T(8,128)(2,1)S(1)}, u32[]{:S(2)}, u32[]{:S(2)}) collective-permute-start(bf16[12,48,128]{2,1,0:T(8,128)(2,1)S(1)} %get-tuple-element.81.value.earlier), channel_id=1, source_target_pairs={{1,2},{3,4},{5,6},{7,0},{2,1},{4,3},{6,5},{0,7},{9,10},{11,12},{13... | collective-permute-start | bytes 442376 | tf_op jit(solution)/shard_map/while/body/eval_jaxpr/ppermute | solution.py:181
  69.1 3.0 %collective-permute-start.3 = (bf16[12,48,128]{2,1,0:T(8,128)(2,1)S(1)}, bf16[12,48,128]{2,1,0:T(8,128)(2,1)S(1)}, u32[]{:S(2)}, u32[]{:S(2)}) collective-permute-start(bf16[12,48,128]{2,1,0:T(8,128)(2,1)S(1)} %get-tuple-element.81.value.earlier), channel_id=1, source_target_pairs={{0,1},{2,3},{4,5},{6,7},{1,0},{3,2},{5,4},{7,6},{8,9},{10,11},{12,... | collective-permute-start | bytes 442376 | tf_op jit(solution)/shard_map/while/body/eval_jaxpr/ppermute | solution.py:180
  72.4 8.5 %collective-permute-start = (bf16[12,48,128]{2,1,0:T(8,128)(2,1)S(1)}, bf16[12,48,128]{2,1,0:T(8,128)(2,1)S(1)}, u32[]{:S(2)}, u32[]{:S(2)}) collective-permute-start(bf16[12,48,128]{2,1,0:T(8,128)(2,1)S(1)} %get-tuple-element.81.value.earlier), channel_id=1, source_target_pairs={{8,16},{24,32},{40,48},{56,64},{72,80},{88,96},{104,112},{120,128}... | collective-permute-start | bytes 442376 | tf_op jit(solution)/shard_map/while/body/eval_jaxpr/ppermute | solution.py:183
  75.4 5.6 %collective-permute-start.1 = (bf16[12,48,128]{2,1,0:T(8,128)(2,1)S(1)}, bf16[12,48,128]{2,1,0:T(8,128)(2,1)S(1)}, u32[]{:S(2)}, u32[]{:S(2)}) collective-permute-start(bf16[12,48,128]{2,1,0:T(8,128)(2,1)S(1)} %get-tuple-element.81.value.earlier), channel_id=1, source_target_pairs={{0,8},{16,24},{32,40},{48,56},{64,72},{80,88},{96,104},{112,120},{... | collective-permute-start | bytes 442376 | tf_op jit(solution)/shard_map/while/body/eval_jaxpr/ppermute | solution.py:182
  75.4 5.6 %collective-permute-start.2 = (bf16[12,48,128]{2,1,0:T(8,128)(2,1)S(1)}, bf16[12,48,128]{2,1,0:T(8,128)(2,1)S(1)}, u32[]{:S(2)}, u32[]{:S(2)}) collective-permute-start(bf16[12,48,128]{2,1,0:T(8,128)(2,1)S(1)} %get-tuple-element.81.value.earlier), channel_id=1, source_target_pairs={{1,2},{3,4},{5,6},{7,0},{2,1},{4,3},{6,5},{0,7},{9,10},{11,12},{13... | collective-permute-start | bytes 442376 | tf_op jit(solution)/shard_map/while/body/eval_jaxpr/ppermute | solution.py:181
  78.0 3.0 %collective-permute-start.3 = (bf16[12,48,128]{2,1,0:T(8,128)(2,1)S(1)}, bf16[12,48,128]{2,1,0:T(8,128)(2,1)S(1)}, u32[]{:S(2)}, u32[]{:S(2)}) collective-permute-start(bf16[12,48,128]{2,1,0:T(8,128)(2,1)S(1)} %get-tuple-element.81.value.earlier), channel_id=1, source_target_pairs={{0,1},{2,3},{4,5},{6,7},{1,0},{3,2},{5,4},{7,6},{8,9},{10,11},{12,... | collective-permute-start | bytes 442376 | tf_op jit(solution)/shard_map/while/body/eval_jaxpr/ppermute | solution.py:180
  81.4 8.5 %collective-permute-start = (bf16[12,48,128]{2,1,0:T(8,128)(2,1)S(1)}, bf16[12,48,128]{2,1,0:T(8,128)(2,1)S(1)}, u32[]{:S(2)}, u32[]{:S(2)}) collective-permute-start(bf16[12,48,128]{2,1,0:T(8,128)(2,1)S(1)} %get-tuple-element.81.value.earlier), channel_id=1, source_target_pairs={{8,16},{24,32},{40,48},{56,64},{72,80},{88,96},{104,112},{120,128}... | collective-permute-start | bytes 442376 | tf_op jit(solution)/shard_map/while/body/eval_jaxpr/ppermute | solution.py:183
  84.4 5.6 %collective-permute-start.1 = (bf16[12,48,128]{2,1,0:T(8,128)(2,1)S(1)}, bf16[12,48,128]{2,1,0:T(8,128)(2,1)S(1)}, u32[]{:S(2)}, u32[]{:S(2)}) collective-permute-start(bf16[12,48,128]{2,1,0:T(8,128)(2,1)S(1)} %get-tuple-element.81.value.earlier), channel_id=1, source_target_pairs={{0,8},{16,24},{32,40},{48,56},{64,72},{80,88},{96,104},{112,120},{... | collective-permute-start | bytes 442376 | tf_op jit(solution)/shard_map/while/body/eval_jaxpr/ppermute | solution.py:182
  84.4 5.6 %collective-permute-start.2 = (bf16[12,48,128]{2,1,0:T(8,128)(2,1)S(1)}, bf16[12,48,128]{2,1,0:T(8,128)(2,1)S(1)}, u32[]{:S(2)}, u32[]{:S(2)}) collective-permute-start(bf16[12,48,128]{2,1,0:T(8,128)(2,1)S(1)} %get-tuple-element.81.value.earlier), channel_id=1, source_target_pairs={{1,2},{3,4},{5,6},{7,0},{2,1},{4,3},{6,5},{0,7},{9,10},{11,12},{13... | collective-permute-start | bytes 442376 | tf_op jit(solution)/shard_map/while/body/eval_jaxpr/ppermute | solution.py:181
  87.0 3.0 %collective-permute-start.3 = (bf16[12,48,128]{2,1,0:T(8,128)(2,1)S(1)}, bf16[12,48,128]{2,1,0:T(8,128)(2,1)S(1)}, u32[]{:S(2)}, u32[]{:S(2)}) collective-permute-start(bf16[12,48,128]{2,1,0:T(8,128)(2,1)S(1)} %get-tuple-element.81.value.earlier), channel_id=1, source_target_pairs={{0,1},{2,3},{4,5},{6,7},{1,0},{3,2},{5,4},{7,6},{8,9},{10,11},{12,... | collective-permute-start | bytes 442376 | tf_op jit(solution)/shard_map/while/body/eval_jaxpr/ppermute | solution.py:180
  90.4 8.5 %collective-permute-start = (bf16[12,48,128]{2,1,0:T(8,128)(2,1)S(1)}, bf16[12,48,128]{2,1,0:T(8,128)(2,1)S(1)}, u32[]{:S(2)}, u32[]{:S(2)}) collective-permute-start(bf16[12,48,128]{2,1,0:T(8,128)(2,1)S(1)} %get-tuple-element.81.value.earlier), channel_id=1, source_target_pairs={{8,16},{24,32},{40,48},{56,64},{72,80},{88,96},{104,112},{120,128}... | collective-permute-start | bytes 442376 | tf_op jit(solution)/shard_map/while/body/eval_jaxpr/ppermute | solution.py:183
  93.4 5.6 %collective-permute-start.1 = (bf16[12,48,128]{2,1,0:T(8,128)(2,1)S(1)}, bf16[12,48,128]{2,1,0:T(8,128)(2,1)S(1)}, u32[]{:S(2)}, u32[]{:S(2)}) collective-permute-start(bf16[12,48,128]{2,1,0:T(8,128)(2,1)S(1)} %get-tuple-element.81.value.earlier), channel_id=1, source_target_pairs={{0,8},{16,24},{32,40},{48,56},{64,72},{80,88},{96,104},{112,120},{... | collective-permute-start | bytes 442376 | tf_op jit(solution)/shard_map/while/body/eval_jaxpr/ppermute | solution.py:182
  93.4 5.6 %collective-permute-start.2 = (bf16[12,48,128]{2,1,0:T(8,128)(2,1)S(1)}, bf16[12,48,128]{2,1,0:T(8,128)(2,1)S(1)}, u32[]{:S(2)}, u32[]{:S(2)}) collective-permute-start(bf16[12,48,128]{2,1,0:T(8,128)(2,1)S(1)} %get-tuple-element.81.value.earlier), channel_id=1, source_target_pairs={{1,2},{3,4},{5,6},{7,0},{2,1},{4,3},{6,5},{0,7},{9,10},{11,12},{13... | collective-permute-start | bytes 442376 | tf_op jit(solution)/shard_map/while/body/eval_jaxpr/ppermute | solution.py:181
  96.0 3.0 %collective-permute-start.3 = (bf16[12,48,128]{2,1,0:T(8,128)(2,1)S(1)}, bf16[12,48,128]{2,1,0:T(8,128)(2,1)S(1)}, u32[]{:S(2)}, u32[]{:S(2)}) collective-permute-start(bf16[12,48,128]{2,1,0:T(8,128)(2,1)S(1)} %get-tuple-element.81.value.earlier), channel_id=1, source_target_pairs={{0,1},{2,3},{4,5},{6,7},{1,0},{3,2},{5,4},{7,6},{8,9},{10,11},{12,... | collective-permute-start | bytes 442376 | tf_op jit(solution)/shard_map/while/body/eval_jaxpr/ppermute | solution.py:180
  99.4 8.5 %collective-permute-start = (bf16[12,48,128]{2,1,0:T(8,128)(2,1)S(1)}, bf16[12,48,128]{2,1,0:T(8,128)(2,1)S(1)}, u32[]{:S(2)}, u32[]{:S(2)}) collective-permute-start(bf16[12,48,128]{2,1,0:T(8,128)(2,1)S(1)} %get-tuple-element.81.value.earlier), channel_id=1, source_target_pairs={{8,16},{24,32},{40,48},{56,64},{72,80},{88,96},{104,112},{120,128}... | collective-permute-start | bytes 442376 | tf_op jit(solution)/shard_map/while/body/eval_jaxpr/ppermute | solution.py:183
  102.4 5.6 %collective-permute-start.1 = (bf16[12,48,128]{2,1,0:T(8,128)(2,1)S(1)}, bf16[12,48,128]{2,1,0:T(8,128)(2,1)S(1)}, u32[]{:S(2)}, u32[]{:S(2)}) collective-permute-start(bf16[12,48,128]{2,1,0:T(8,128)(2,1)S(1)} %get-tuple-element.81.value.earlier), channel_id=1, source_target_pairs={{0,8},{16,24},{32,40},{48,56},{64,72},{80,88},{96,104},{112,120},{... | collective-permute-start | bytes 442376 | tf_op jit(solution)/shard_map/while/body/eval_jaxpr/ppermute | solution.py:182
  102.4 5.6 %collective-permute-start.2 = (bf16[12,48,128]{2,1,0:T(8,128)(2,1)S(1)}, bf16[12,48,128]{2,1,0:T(8,128)(2,1)S(1)}, u32[]{:S(2)}, u32[]{:S(2)}) collective-permute-start(bf16[12,48,128]{2,1,0:T(8,128)(2,1)S(1)} %get-tuple-element.81.value.earlier), channel_id=1, source_target_pairs={{1,2},{3,4},{5,6},{7,0},{2,1},{4,3},{6,5},{0,7},{9,10},{11,12},{13... | collective-permute-start | bytes 442376 | tf_op jit(solution)/shard_map/while/body/eval_jaxpr/ppermute | solution.py:181
  105.0 3.0 %collective-permute-start.3 = (bf16[12,48,128]{2,1,0:T(8,128)(2,1)S(1)}, bf16[12,48,128]{2,1,0:T(8,128)(2,1)S(1)}, u32[]{:S(2)}, u32[]{:S(2)}) collective-permute-start(bf16[12,48,128]{2,1,0:T(8,128)(2,1)S(1)} %get-tuple-element.81.value.earlier), channel_id=1, source_target_pairs={{0,1},{2,3},{4,5},{6,7},{1,0},{3,2},{5,4},{7,6},{8,9},{10,11},{12,... | collective-permute-start | bytes 442376 | tf_op jit(solution)/shard_map/while/body/eval_jaxpr/ppermute | solution.py:180
  108.4 8.5 %collective-permute-start = (bf16[12,48,128]{2,1,0:T(8,128)(2,1)S(1)}, bf16[12,48,128]{2,1,0:T(8,128)(2,1)S(1)}, u32[]{:S(2)}, u32[]{:S(2)}) collective-permute-start(bf16[12,48,128]{2,1,0:T(8,128)(2,1)S(1)} %get-tuple-element.81.value.earlier), channel_id=1, source_target_pairs={{8,16},{24,32},{40,48},{56,64},{72,80},{88,96},{104,112},{120,128}... | collective-permute-start | bytes 442376 | tf_op jit(solution)/shard_map/while/body/eval_jaxpr/ppermute | solution.py:183
  111.3 5.6 %collective-permute-start.1 = (bf16[12,48,128]{2,1,0:T(8,128)(2,1)S(1)}, bf16[12,48,128]{2,1,0:T(8,128)(2,1)S(1)}, u32[]{:S(2)}, u32[]{:S(2)}) collective-permute-start(bf16[12,48,128]{2,1,0:T(8,128)(2,1)S(1)} %get-tuple-element.81.value.earlier), channel_id=1, source_target_pairs={{0,8},{16,24},{32,40},{48,56},{64,72},{80,88},{96,104},{112,120},{... | collective-permute-start | bytes 442376 | tf_op jit(solution)/shard_map/while/body/eval_jaxpr/ppermute | solution.py:182
  111.4 5.6 %collective-permute-start.2 = (bf16[12,48,128]{2,1,0:T(8,128)(2,1)S(1)}, bf16[12,48,128]{2,1,0:T(8,128)(2,1)S(1)}, u32[]{:S(2)}, u32[]{:S(2)}) collective-permute-start(bf16[12,48,128]{2,1,0:T(8,128)(2,1)S(1)} %get-tuple-element.81.value.earlier), channel_id=1, source_target_pairs={{1,2},{3,4},{5,6},{7,0},{2,1},{4,3},{6,5},{0,7},{9,10},{11,12},{13... | collective-permute-start | bytes 442376 | tf_op jit(solution)/shard_map/while/body/eval_jaxpr/ppermute | solution.py:181
  114.0 3.0 %collective-permute-start.3 = (bf16[12,48,128]{2,1,0:T(8,128)(2,1)S(1)}, bf16[12,48,128]{2,1,0:T(8,128)(2,1)S(1)}, u32[]{:S(2)}, u32[]{:S(2)}) collective-permute-start(bf16[12,48,128]{2,1,0:T(8,128)(2,1)S(1)} %get-tuple-element.81.value.earlier), channel_id=1, source_target_pairs={{0,1},{2,3},{4,5},{6,7},{1,0},{3,2},{5,4},{7,6},{8,9},{10,11},{12,... | collective-permute-start | bytes 442376 | tf_op jit(solution)/shard_map/while/body/eval_jaxpr/ppermute | solution.py:180
  117.4 8.5 %collective-permute-start = (bf16[12,48,128]{2,1,0:T(8,128)(2,1)S(1)}, bf16[12,48,128]{2,1,0:T(8,128)(2,1)S(1)}, u32[]{:S(2)}, u32[]{:S(2)}) collective-permute-start(bf16[12,48,128]{2,1,0:T(8,128)(2,1)S(1)} %get-tuple-element.81.value.earlier), channel_id=1, source_target_pairs={{8,16},{24,32},{40,48},{56,64},{72,80},{88,96},{104,112},{120,128}... | collective-permute-start | bytes 442376 | tf_op jit(solution)/shard_map/while/body/eval_jaxpr/ppermute | solution.py:183
  120.3 5.6 %collective-permute-start.1 = (bf16[12,48,128]{2,1,0:T(8,128)(2,1)S(1)}, bf16[12,48,128]{2,1,0:T(8,128)(2,1)S(1)}, u32[]{:S(2)}, u32[]{:S(2)}) collective-permute-start(bf16[12,48,128]{2,1,0:T(8,128)(2,1)S(1)} %get-tuple-element.81.value.earlier), channel_id=1, source_target_pairs={{0,8},{16,24},{32,40},{48,56},{64,72},{80,88},{96,104},{112,120},{... | collective-permute-start | bytes 442376 | tf_op jit(solution)/shard_map/while/body/eval_jaxpr/ppermute | solution.py:182
  120.3 5.6 %collective-permute-start.2 = (bf16[12,48,128]{2,1,0:T(8,128)(2,1)S(1)}, bf16[12,48,128]{2,1,0:T(8,128)(2,1)S(1)}, u32[]{:S(2)}, u32[]{:S(2)}) collective-permute-start(bf16[12,48,128]{2,1,0:T(8,128)(2,1)S(1)} %get-tuple-element.81.value.earlier), channel_id=1, source_target_pairs={{1,2},{3,4},{5,6},{7,0},{2,1},{4,3},{6,5},{0,7},{9,10},{11,12},{13... | collective-permute-start | bytes 442376 | tf_op jit(solution)/shard_map/while/body/eval_jaxpr/ppermute | solution.py:181
  123.0 3.0 %collective-permute-start.3 = (bf16[12,48,128]{2,1,0:T(8,128)(2,1)S(1)}, bf16[12,48,128]{2,1,0:T(8,128)(2,1)S(1)}, u32[]{:S(2)}, u32[]{:S(2)}) collective-permute-start(bf16[12,48,128]{2,1,0:T(8,128)(2,1)S(1)} %get-tuple-element.81.value.earlier), channel_id=1, source_target_pairs={{0,1},{2,3},{4,5},{6,7},{1,0},{3,2},{5,4},{7,6},{8,9},{10,11},{12,... | collective-permute-start | bytes 442376 | tf_op jit(solution)/shard_map/while/body/eval_jaxpr/ppermute | solution.py:180
  126.4 8.5 %collective-permute-start = (bf16[12,48,128]{2,1,0:T(8,128)(2,1)S(1)}, bf16[12,48,128]{2,1,0:T(8,128)(2,1)S(1)}, u32[]{:S(2)}, u32[]{:S(2)}) collective-permute-start(bf16[12,48,128]{2,1,0:T(8,128)(2,1)S(1)} %get-tuple-element.81.value.earlier), channel_id=1, source_target_pairs={{8,16},{24,32},{40,48},{56,64},{72,80},{88,96},{104,112},{120,128}... | collective-permute-start | bytes 442376 | tf_op jit(solution)/shard_map/while/body/eval_jaxpr/ppermute | solution.py:183
  129.3 5.6 %collective-permute-start.1 = (bf16[12,48,128]{2,1,0:T(8,128)(2,1)S(1)}, bf16[12,48,128]{2,1,0:T(8,128)(2,1)S(1)}, u32[]{:S(2)}, u32[]{:S(2)}) collective-permute-start(bf16[12,48,128]{2,1,0:T(8,128)(2,1)S(1)} %get-tuple-element.81.value.earlier), channel_id=1, source_target_pairs={{0,8},{16,24},{32,40},{48,56},{64,72},{80,88},{96,104},{112,120},{... | collective-permute-start | bytes 442376 | tf_op jit(solution)/shard_map/while/body/eval_jaxpr/ppermute | solution.py:182
  129.3 5.6 %collective-permute-start.2 = (bf16[12,48,128]{2,1,0:T(8,128)(2,1)S(1)}, bf16[12,48,128]{2,1,0:T(8,128)(2,1)S(1)}, u32[]{:S(2)}, u32[]{:S(2)}) collective-permute-start(bf16[12,48,128]{2,1,0:T(8,128)(2,1)S(1)} %get-tuple-element.81.value.earlier), channel_id=1, source_target_pairs={{1,2},{3,4},{5,6},{7,0},{2,1},{4,3},{6,5},{0,7},{9,10},{11,12},{13... | collective-permute-start | bytes 442376 | tf_op jit(solution)/shard_map/while/body/eval_jaxpr/ppermute | solution.py:181
  132.0 3.0 %collective-permute-start.3 = (bf16[12,48,128]{2,1,0:T(8,128)(2,1)S(1)}, bf16[12,48,128]{2,1,0:T(8,128)(2,1)S(1)}, u32[]{:S(2)}, u32[]{:S(2)}) collective-permute-start(bf16[12,48,128]{2,1,0:T(8,128)(2,1)S(1)} %get-tuple-element.81.value.earlier), channel_id=1, source_target_pairs={{0,1},{2,3},{4,5},{6,7},{1,0},{3,2},{5,4},{7,6},{8,9},{10,11},{12,... | collective-permute-start | bytes 442376 | tf_op jit(solution)/shard_map/while/body/eval_jaxpr/ppermute | solution.py:180
  135.4 8.5 %collective-permute-start = (bf16[12,48,128]{2,1,0:T(8,128)(2,1)S(1)}, bf16[12,48,128]{2,1,0:T(8,128)(2,1)S(1)}, u32[]{:S(2)}, u32[]{:S(2)}) collective-permute-start(bf16[12,48,128]{2,1,0:T(8,128)(2,1)S(1)} %get-tuple-element.81.value.earlier), channel_id=1, source_target_pairs={{8,16},{24,32},{40,48},{56,64},{72,80},{88,96},{104,112},{120,128}... | collective-permute-start | bytes 442376 | tf_op jit(solution)/shard_map/while/body/eval_jaxpr/ppermute | solution.py:183
  138.3 5.6 %collective-permute-start.1 = (bf16[12,48,128]{2,1,0:T(8,128)(2,1)S(1)}, bf16[12,48,128]{2,1,0:T(8,128)(2,1)S(1)}, u32[]{:S(2)}, u32[]{:S(2)}) collective-permute-start(bf16[12,48,128]{2,1,0:T(8,128)(2,1)S(1)} %get-tuple-element.81.value.earlier), channel_id=1, source_target_pairs={{0,8},{16,24},{32,40},{48,56},{64,72},{80,88},{96,104},{112,120},{... | collective-permute-start | bytes 442376 | tf_op jit(solution)/shard_map/while/body/eval_jaxpr/ppermute | solution.py:182
  138.3 5.6 %collective-permute-start.2 = (bf16[12,48,128]{2,1,0:T(8,128)(2,1)S(1)}, bf16[12,48,128]{2,1,0:T(8,128)(2,1)S(1)}, u32[]{:S(2)}, u32[]{:S(2)}) collective-permute-start(bf16[12,48,128]{2,1,0:T(8,128)(2,1)S(1)} %get-tuple-element.81.value.earlier), channel_id=1, source_target_pairs={{1,2},{3,4},{5,6},{7,0},{2,1},{4,3},{6,5},{0,7},{9,10},{11,12},{13... | collective-permute-start | bytes 442376 | tf_op jit(solution)/shard_map/while/body/eval_jaxpr/ppermute | solution.py:181
  141.0 3.0 %collective-permute-start.3 = (bf16[12,48,128]{2,1,0:T(8,128)(2,1)S(1)}, bf16[12,48,128]{2,1,0:T(8,128)(2,1)S(1)}, u32[]{:S(2)}, u32[]{:S(2)}) collective-permute-start(bf16[12,48,128]{2,1,0:T(8,128)(2,1)S(1)} %get-tuple-element.81.value.earlier), channel_id=1, source_target_pairs={{0,1},{2,3},{4,5},{6,7},{1,0},{3,2},{5,4},{7,6},{8,9},{10,11},{12,... | collective-permute-start | bytes 442376 | tf_op jit(solution)/shard_map/while/body/eval_jaxpr/ppermute | solution.py:180
  144.3 11.5 %collective-permute-start.8 = (bf16[12,48,128]{2,1,0:T(8,128)(2,1)S(1)}, bf16[12,48,128]{2,1,0:T(8,128)(2,1)S(1)}, u32[]{:S(2)}, u32[]{:S(2)}) collective-permute-start(bf16[12,48,128]{2,1,0:T(8,128)(2,1)S(1)} %get-tuple-element.32.value.earlier), channel_id=1, source_target_pairs={{8,16},{24,32},{40,48},{56,64},{72,80},{88,96},{104,112},{120,128}... | collective-permute-start | bytes 442376 | tf_op jit(solution)/shard_map/ppermute | solution.py:183
  147.3 8.6 %collective-permute-start.9 = (bf16[12,48,128]{2,1,0:T(8,128)(2,1)S(1)}, bf16[12,48,128]{2,1,0:T(8,128)(2,1)S(1)}, u32[]{:S(2)}, u32[]{:S(2)}) collective-permute-start(bf16[12,48,128]{2,1,0:T(8,128)(2,1)S(1)} %get-tuple-element.32.value.earlier), channel_id=1, source_target_pairs={{0,8},{16,24},{32,40},{48,56},{64,72},{80,88},{96,104},{112,120},{... | collective-permute-start | bytes 442376 | tf_op jit(solution)/shard_map/ppermute | solution.py:182
  147.3 8.6 %collective-permute-start.10 = (bf16[12,48,128]{2,1,0:T(8,128)(2,1)S(1)}, bf16[12,48,128]{2,1,0:T(8,128)(2,1)S(1)}, u32[]{:S(2)}, u32[]{:S(2)}) collective-permute-start(bf16[12,48,128]{2,1,0:T(8,128)(2,1)S(1)} %get-tuple-element.32.value.earlier), channel_id=1, source_target_pairs={{1,2},{3,4},{5,6},{7,0},{2,1},{4,3},{6,5},{0,7},{9,10},{11,12},{13... | collective-permute-start | bytes 442376 | tf_op jit(solution)/shard_map/ppermute | solution.py:181
  149.9 6.0 %collective-permute-start.11 = (bf16[12,48,128]{2,1,0:T(8,128)(2,1)S(1)}, bf16[12,48,128]{2,1,0:T(8,128)(2,1)S(1)}, u32[]{:S(2)}, u32[]{:S(2)}) collective-permute-start(bf16[12,48,128]{2,1,0:T(8,128)(2,1)S(1)} %get-tuple-element.32.value.earlier), channel_id=1, source_target_pairs={{0,1},{2,3},{4,5},{6,7},{1,0},{3,2},{5,4},{7,6},{8,9},{10,11},{12,... | collective-permute-start | bytes 442376 | tf_op jit(solution)/shard_map/ppermute | solution.py:180
where the time goes:
time: 158 us
  starting transfers between devices  97.2 us (62%)
  Pallas kernels  52.3 us (33%)
  waiting for transfers between devices  6.88 us (4%)
    pallas_call x84, Pallas kernels, call(): pl.pallas_call(kernel, in_specs=in_specs, out_specs=out_specs, out_shape=...  52.3 us
    ppermute x16, starting transfers between devices, sweep(): t_far = lax.ppermute(value, 'ta', swap(nt, 1))  48.3 us
    ppermute x16, starting transfers between devices, sweep(): z_far = lax.ppermute(value, 'gz', swap(nz, 1))  39.6 us
    ppermute x16, starting transfers between devices, sweep(): z_near = lax.ppermute(value, 'gz', swap(nz, 0))  9.15 us
    ppermute x16, waiting for transfers between devices, sweep(): t_far = lax.ppermute(value, 'ta', swap(nt, 1))  6.76 us
  transfers between devices with their start and end apart: 64, of which 3 were waited for; matrix products, arithmetic and copies ran while one was open for 0% of the time, Pallas kernels for 26%

commit v1 on v0

--- a/solution.py
+++ b/solution.py
@@ -62,26 +62,16 @@
         rhs[s] = dot(buffer[s], held[s]).astype(rhs.dtype)
 
 
-def links_kernel(slots, links, remote, buffer, sems):
-    sites, _, wide = remote.shape
-    for i in range(4):
-        pltpu.make_async_copy(links.at[slots[i]], buffer.at[i], sems.at[i]).start()
-    for i in range(4):
-        pltpu.make_async_copy(links.at[slots[i]], buffer.at[i], sems.at[i]).wait()
-        for s in range(sites):
-            remote[s, i * wide : (i + 1) * wide, :] = buffer[i, s].T
-
-    @pl.when(slots[4] < 0)
-    def _():
-        remote[:, :wide, :] = -remote[:, :wide, :]
-
-
-def local_kernel(ny, nx, rhs, value, links, out, buffer, sems):
+def fetch_rows(ny, nx, links, buffer, sems):
     copies = []
     for y in range(ny):
         row = pl.ds(y * nx, nx)
         copies.append(pltpu.make_async_copy(links.at[:5, row], buffer.at[:, row], sems.at[y]))
         copies[-1].start()
+    return copies
+
+
+def local_rows(ny, nx, rhs, value, buffer, out, copies):
     for y in range(ny):
         copies[y].wait()
         for x in range(nx):
@@ -98,6 +88,50 @@
             out[s] = rhs[s].astype(jnp.float32) - dot(lhs, rows, NT)
 
 
+def local_kernel(ny, nx, rhs, value, links, out, buffer, sems):
+    copies = fetch_rows(ny, nx, links, buffer, sems)
+    local_rows(ny, nx, rhs, value, buffer, out, copies)
+
+
+def first_kernel(ny, nx, slots, rhs, links, out, remote, buffer, sems, others, other_sems):
+    sites, _, wide = remote.shape
+    copies = fetch_rows(ny, nx, links, buffer, sems)
+
+    def fetch(i):
+        return pltpu.make_async_copy(links.at[slots[i]], others.at[i], other_sems.at[i])
+
+    for i in range(4):
+        fetch(i).start()
+    local_rows(ny, nx, rhs, rhs, buffer, out, copies)
+    for i in range(4):
+        fetch(i).wait()
+        for s in range(sites):
+            remote[s, i * wide : (i + 1) * wide, :] = others[i, s].T
+
+    @pl.when(slots[4] < 0)
+    def _():
+        remote[:, :wide, :] = -remote[:, :wide, :]
+
+
+def last_kernel(ny, nx, rhs, value, links, prolongator, out, turned, buffer, sems, held, held_sems):
+    copies = fetch_rows(ny, nx, links, buffer, sems)
+    sites = held.shape[0]
+
+    def fetch(s):
+        return pltpu.make_async_copy(prolongator.at[s], held.at[s], held_sems.at[s])
+
+    for s in range(sites):
+        fetch(s).start()
+    local_rows(ny, nx, rhs, value, buffer, out, copies)
+
+    def turn(s, _):
+        fetch(s).wait()
+        turned[s] = held[s].T
+        return 0
+
+    lax.fori_loop(0, sites, turn, 0)
+
+
 def remote_kernel(part, a, b, c, d, weights, token, out):
     for s in range(part.shape[0]):
         lhs = jnp.concatenate([a[s], b[s], c[s], d[s]], 1)
@@ -108,27 +142,10 @@
     token[...] = jnp.zeros_like(token)
 
 
-def transpose_kernel(prolongator, earlier, out, buffer, sems):
-    sites = out.shape[0]
-
-    def fetch(s):
-        return pltpu.make_async_copy(prolongator.at[s], buffer.at[s], sems.at[s])
-
-    for s in range(sites):
-        fetch(s).start()
-
-    def turn(s, _):
-        fetch(s).wait()
-        out[s] = buffer[s].T
-        return 0
-
-    lax.fori_loop(0, sites, turn, 0)
-
-
-def prolong_kernel(value, weights, out, buffer, sems):
+def prolong_kernel(value, turned, out, buffer, sems):
     copies = []
     for s in range(value.shape[0]):
-        buffer[s] = dot(value[s], weights[s]).astype(buffer.dtype)
+        buffer[s] = dot(value[s], turned[s]).astype(buffer.dtype)
         copies.append(pltpu.make_async_copy(buffer.at[s], out.at[s], sems.at[s]))
         copies[-1].start()
     for c in copies:
@@ -168,51 +185,76 @@
     slots = jnp.stack([8 - t_odd, 7 + t_odd, 6 - z_odd, 5 + z_odd, jnp.where(edge, -1, 1)]).astype(
         jnp.int32
     )
-    (remote_weights,) = call(
-        links_kernel,
-        [slots, links],
-        [shape((sites, 4 * wide, wide))],
-        [pltpu.VMEM((4, *links.shape[1:]), links.dtype), pltpu.SemaphoreType.DMA((4,))],
-        in_specs=[SMEM, HBM],
-    )
-
-    def sweep(value):
+    local_scratch = [
+        pltpu.VMEM((5, *links.shape[1:]), links.dtype),
+        pltpu.SemaphoreType.DMA((ny,)),
+    ]
+
+    def swaps(value):
         z_near = lax.ppermute(value, "gz", swap(nz, 0))
         z_far = lax.ppermute(value, "gz", swap(nz, 1))
         t_near = lax.ppermute(value, "ta", swap(nt, 0))
         t_far = lax.ppermute(value, "ta", swap(nt, 1))
+        return t_far, t_near, z_far, z_near
+
+    def finish(value, part, arrivals, remote_weights):
+        token = value
+        for arrived in arrivals[:3]:
+            (token,) = call(after_kernel, [token, arrived], [shape((8, 128), jnp.float32)])
+        (value,) = call(
+            remote_kernel,
+            [part, *arrivals, remote_weights, token],
+            [shape(field)],
+            flops=4 * flops,
+        )
+        return value
+
+    arrivals = swaps(rhs)
+    part, remote_weights = call(
+        functools.partial(first_kernel, ny, nx),
+        [slots, rhs, links],
+        [shape(field, jnp.float32), shape((sites, 4 * wide, wide))],
+        [
+            *local_scratch,
+            pltpu.VMEM((4, *links.shape[1:]), links.dtype),
+            pltpu.SemaphoreType.DMA((4,)),
+        ],
+        in_specs=[SMEM, VMEM, HBM],
+        flops=5 * flops,
+    )
+    value = finish(rhs, part, arrivals, remote_weights)
+
+    def sweep(_, value):
+        arrivals = swaps(value)
         (part,) = call(
             functools.partial(local_kernel, ny, nx),
             [rhs, value, links],
             [shape(field, jnp.float32)],
-            [pltpu.VMEM((5, *links.shape[1:]), links.dtype), pltpu.SemaphoreType.DMA((ny,))],
+            local_scratch,
             in_specs=[VMEM, VMEM, HBM],
             flops=5 * flops,
         )
-        token = value
-        for arrived in (t_far, t_near, z_far):
-            (token,) = call(after_kernel, [token, arrived], [shape((8, 128), jnp.float32)])
-        (value,) = call(
-            remote_kernel,
-            [part, t_far, t_near, z_far, z_near, remote_weights, token],
-            [shape(field)],
-            flops=4 * flops,
-        )
-        return value
-
-    last = lax.fori_loop(1, ITERS - 1, lambda _, v: sweep(v), sweep(rhs))
-    value = sweep(last)
-
-    (weights,) = call(
-        transpose_kernel,
-        [prolong, last],
-        [shape((sites, wide, fine))],
-        [pltpu.VMEM(prolong.shape, prolong.dtype), pltpu.SemaphoreType.DMA((sites,))],
-        in_specs=[HBM, VMEM],
-    )
+        return finish(value, part, arrivals, remote_weights)
+
+    value = lax.fori_loop(1, ITERS - 1, sweep, value)
+    arrivals = swaps(value)
+    part, turned = call(
+        functools.partial(last_kernel, ny, nx),
+        [rhs, value, links, prolong],
+        [shape(field, jnp.float32), shape((sites, wide, fine))],
+        [
+            *local_scratch,
+            pltpu.VMEM(prolong.shape, prolong.dtype),
+            pltpu.SemaphoreType.DMA((sites,)),
+        ],
+        in_specs=[VMEM, VMEM, HBM, HBM],
+        flops=5 * flops,
+    )
+    value = finish(value, part, arrivals, remote_weights)
+
     (out,) = call(
         prolong_kernel,
-        [value, weights],
+        [value, turned],
         [shape((sites, rhs_count, fine))],
         [pltpu.VMEM((sites, rhs_count, fine), jnp.bfloat16), pltpu.SemaphoreType.DMA((sites,))],
         out_specs=[HBM],

time: 158 us -> 158 us (level)
  waiting for transfers between devices: 6.88 us -> 13.4 us
  starting transfers between devices: 97.2 us -> 91.3 us
    ppermute x64, waiting for transfers between devices: 6.88 us -> 13.4 us  [the longest x16 10 us: swaps(): z_far = lax.ppermute(value, 'gz', swap(nz, 1))]
    ppermute x64, starting transfers between devices: 97.2 us -> 91.3 us  [the longest x16 50.6 us: swaps(): z_far = lax.ppermute(value, 'gz', swap(nz, 1))]
    pallas_call x84 -> x82, Pallas kernels: 52.3 us -> 51.4 us  [call(): pl.pallas_call(kernel, in_specs=in_specs, out_specs=out_specs, out_shape=...]
  transfers between devices with their start and end apart: 64 -> 64, of which waited for: 3 -> 15; matrix products, arithmetic and copies ran while one was open for 0% -> 0% of each run, Pallas kernels for 26% -> 26%
where the time goes in v1:
time: 158 us; the launch traced here: 157 us
  starting transfers between devices  91.3 us (58%)
  Pallas kernels  51.4 us (33%)
  waiting for transfers between devices  13.4 us (8%)
    pallas_call x82, Pallas kernels, call(): pl.pallas_call(kernel, in_specs=in_specs, out_specs=out_specs, out_shape=...  51.4 us
    ppermute x16, starting transfers between devices, swaps(): z_far = lax.ppermute(value, 'gz', swap(nz, 1))  50.6 us
    ppermute x16, starting transfers between devices, swaps(): t_far = lax.ppermute(value, 'ta', swap(nt, 1))  39.7 us
    ppermute x16, waiting for transfers between devices, swaps(): z_far = lax.ppermute(value, 'gz', swap(nz, 1))  10 us
    ppermute x16, waiting for transfers between devices, swaps(): t_far = lax.ppermute(value, 'ta', swap(nt, 1))  3.29 us
  transfers between devices with their start and end apart: 64, of which 15 were waited for; matrix products, arithmetic and copies ran while one was open for 0% of the time, Pallas kernels for 26%

profile of v1, /device:TPU:1, one launch (start us, length us, event | category | flops | bytes accessed | tf_op | source)
XLA Modules:
  0.0 157.2 jit_solution(7544532672158080392)
XLA Ops:
  0.0 3.7 %shard_map.37.rhs.earlier = bf16[12,48,128]{2,1,0:T(8,128)(2,1)S(1)} custom-call(bf16[12,48,1536]{2,1,0:T(8,128)(2,1)} %bitcast.13, bf16[12,1536,128]{2,1,0:T(8,128)(2,1)} %bitcast.11), custom_call_target="tpu_custom_call" | custom-call | tf_op jit(solution)/shard_map/pallas_call | solution.py:26
  3.7 8.9 %collective-permute-start.4 = (bf16[12,48,128]{2,1,0:T(8,128)(2,1)S(1)}, bf16[12,48,128]{2,1,0:T(8,128)(2,1)S(1)}, u32[]{:S(2)}, u32[]{:S(2)}) collective-permute-start(bf16[12,48,128]{2,1,0:T(8,128)(2,1)S(1)} %shard_map.37.rhs.earlier), channel_id=1, source_target_pairs={{8,16},{24,32},{40,48},{56,64},{72,80},{88,96},{104,112},{120,128}... | collective-permute-start | bytes 442376 | tf_op jit(solution)/shard_map/ppermute | solution.py:197
  12.6 2.1 %collective-permute-start.6 = (bf16[12,48,128]{2,1,0:T(8,128)(2,1)S(1)}, bf16[12,48,128]{2,1,0:T(8,128)(2,1)S(1)}, u32[]{:S(2)}, u32[]{:S(2)}) collective-permute-start(bf16[12,48,128]{2,1,0:T(8,128)(2,1)S(1)} %shard_map.37.rhs.earlier), channel_id=1, source_target_pairs={{1,2},{3,4},{5,6},{7,0},{2,1},{4,3},{6,5},{0,7},{9,10},{11,12},{13... | collective-permute-start | bytes 442376 | tf_op jit(solution)/shard_map/ppermute | solution.py:195
  15.6 3.5 %shard_map.38 = (f32[12,48,128]{2,1,0:T(8,128)S(1)}, bf16[12,512,128]{2,1,0:T(8,128)(2,1)S(1)}) custom-call(s32[5]{0:T(128)S(1)} %stack.23.slots, bf16[12,48,128]{2,1,0:T(8,128)(2,1)S(1)} %shard_map.37.rhs.earlier, bf16[9,12,128,128]{3,2,1,0:T(8,128)(2,1)} %bitcast.9), custom_call_target="tpu_custom_call" | custom-call | flops 94371840 | tf_op jit(solution)/shard_map/pallas_call | solution.py:26
  19.6 124.9 %while.10 = (s32[]{:T(128)}, bf16[12,48,128]{2,1,0:T(8,128)(2,1)S(1)}, bf16[12,48,128]{2,1,0:T(8,128)(2,1)S(1)}, bf16[9,12,128,128]{3,2,1,0:T(8,128)(2,1)}, bf16[12,512,128]{2,1,0:T(8,128)(2,1)S(1)}, /*index=5*/s32[]{:T(128)}) while((s32[]{:T(128)}, bf16[12,48,128]{2,1,0:T(8,128)(2,1)S(1)}, bf16[12,48,128]{2,1,0:T(8,128)(2,1)S(1)}, ...), condition=%wide.region_1.2_spmd, body=%wide.region_0.1_spmd.sunk | while | flops 169869312 | bytes 2359525 | solution.py:239
  19.6 1.6 collective-permute-start
  21.2 2.9 %collective-permute-start.2 = (bf16[12,48,128]{2,1,0:T(8,128)(2,1)S(1)}, bf16[12,48,128]{2,1,0:T(8,128)(2,1)S(1)}, u32[]{:S(2)}, u32[]{:S(2)}) collective-permute-start(bf16[12,48,128]{2,1,0:T(8,128)(2,1)S(1)} %get-tuple-element.89.value.earlier), channel_id=1, source_target_pairs={{1,2},{3,4},{5,6},{7,0},{2,1},{4,3},{6,5},{0,7},{9,10},{11,12},{13... | collective-permute-start | bytes 442376 | tf_op jit(solution)/shard_map/while/body/eval_jaxpr/ppermute | solution.py:195
  24.1 2.2 %eval_jaxpr.5.part = f32[12,48,128]{2,1,0:T(8,128)S(1)} custom-call(bf16[12,48,128]{2,1,0:T(8,128)(2,1)S(1)} %get-tuple-element.96.rhs, bf16[12,48,128]{2,1,0:T(8,128)(2,1)S(1)} %get-tuple-element.89.value.earlier, bf16[9,12,128,128]{3,2,1,0:T(8,128)(2,1)} %get-tuple-element.97.links), custom_call_target="tpu_custom_call" | custom-call | flops 94371840 | tf_op jit(solution)/shard_map/while/body/eval_jaxpr/pallas_call | solution.py:26
  26.4 2.0 %collective-permute-done.arrived.a = bf16[12,48,128]{2,1,0:T(8,128)(2,1)S(1)} collective-permute-done((bf16[12,48,128]{2,1,0:T(8,128)(2,1)S(1)}, bf16[12,48,128]{2,1,0:T(8,128)(2,1)S(1)}, u32[]{:S(2)}, u32[]{:S(2)}) %collective-permute-start) | collective-permute-done | bytes 147488 | tf_op jit(solution)/shard_map/while/body/eval_jaxpr/ppermute | solution.py:197
  28.8 1.2 collective-permute-start
  30.0 3.1 %collective-permute-start.2 = (bf16[12,48,128]{2,1,0:T(8,128)(2,1)S(1)}, bf16[12,48,128]{2,1,0:T(8,128)(2,1)S(1)}, u32[]{:S(2)}, u32[]{:S(2)}) collective-permute-start(bf16[12,48,128]{2,1,0:T(8,128)(2,1)S(1)} %get-tuple-element.89.value.earlier), channel_id=1, source_target_pairs={{1,2},{3,4},{5,6},{7,0},{2,1},{4,3},{6,5},{0,7},{9,10},{11,12},{13... | collective-permute-start | bytes 442376 | tf_op jit(solution)/shard_map/while/body/eval_jaxpr/ppermute | solution.py:195
  33.1 2.2 %eval_jaxpr.5.part = f32[12,48,128]{2,1,0:T(8,128)S(1)} custom-call(bf16[12,48,128]{2,1,0:T(8,128)(2,1)S(1)} %get-tuple-element.96.rhs, bf16[12,48,128]{2,1,0:T(8,128)(2,1)S(1)} %get-tuple-element.89.value.earlier, bf16[9,12,128,128]{3,2,1,0:T(8,128)(2,1)} %get-tuple-element.97.links), custom_call_target="tpu_custom_call" | custom-call | flops 94371840 | tf_op jit(solution)/shard_map/while/body/eval_jaxpr/pallas_call | solution.py:26
  35.4 1.2 collective-permute-done.arrived.a
  37.0 2.0 %collective-permute-start = (bf16[12,48,128]{2,1,0:T(8,128)(2,1)S(1)}, bf16[12,48,128]{2,1,0:T(8,128)(2,1)S(1)}, u32[]{:S(2)}, u32[]{:S(2)}) collective-permute-start(bf16[12,48,128]{2,1,0:T(8,128)(2,1)S(1)} %get-tuple-element.89.value.earlier), channel_id=1, source_target_pairs={{8,16},{24,32},{40,48},{56,64},{72,80},{88,96},{104,112},{120,128}... | collective-permute-start | bytes 442376 | tf_op jit(solution)/shard_map/while/body/eval_jaxpr/ppermute | solution.py:197
  39.0 3.1 %collective-permute-start.2 = (bf16[12,48,128]{2,1,0:T(8,128)(2,1)S(1)}, bf16[12,48,128]{2,1,0:T(8,128)(2,1)S(1)}, u32[]{:S(2)}, u32[]{:S(2)}) collective-permute-start(bf16[12,48,128]{2,1,0:T(8,128)(2,1)S(1)} %get-tuple-element.89.value.earlier), channel_id=1, source_target_pairs={{1,2},{3,4},{5,6},{7,0},{2,1},{4,3},{6,5},{0,7},{9,10},{11,12},{13... | collective-permute-start | bytes 442376 | tf_op jit(solution)/shard_map/while/body/eval_jaxpr/ppermute | solution.py:195
  42.1 2.2 %eval_jaxpr.5.part = f32[12,48,128]{2,1,0:T(8,128)S(1)} custom-call(bf16[12,48,128]{2,1,0:T(8,128)(2,1)S(1)} %get-tuple-element.96.rhs, bf16[12,48,128]{2,1,0:T(8,128)(2,1)S(1)} %get-tuple-element.89.value.earlier, bf16[9,12,128,128]{3,2,1,0:T(8,128)(2,1)} %get-tuple-element.97.links), custom_call_target="tpu_custom_call" | custom-call | flops 94371840 | tf_op jit(solution)/shard_map/while/body/eval_jaxpr/pallas_call | solution.py:26
  45.6 2.2 %collective-permute-start = (bf16[12,48,128]{2,1,0:T(8,128)(2,1)S(1)}, bf16[12,48,128]{2,1,0:T(8,128)(2,1)S(1)}, u32[]{:S(2)}, u32[]{:S(2)}) collective-permute-start(bf16[12,48,128]{2,1,0:T(8,128)(2,1)S(1)} %get-tuple-element.89.value.earlier), channel_id=1, source_target_pairs={{8,16},{24,32},{40,48},{56,64},{72,80},{88,96},{104,112},{120,128}... | collective-permute-start | bytes 442376 | tf_op jit(solution)/shard_map/while/body/eval_jaxpr/ppermute | solution.py:197
  47.8 3.3 %collective-permute-start.2 = (bf16[12,48,128]{2,1,0:T(8,128)(2,1)S(1)}, bf16[12,48,128]{2,1,0:T(8,128)(2,1)S(1)}, u32[]{:S(2)}, u32[]{:S(2)}) collective-permute-start(bf16[12,48,128]{2,1,0:T(8,128)(2,1)S(1)} %get-tuple-element.89.value.earlier), channel_id=1, source_target_pairs={{1,2},{3,4},{5,6},{7,0},{2,1},{4,3},{6,5},{0,7},{9,10},{11,12},{13... | collective-permute-start | bytes 442376 | tf_op jit(solution)/shard_map/while/body/eval_jaxpr/ppermute | solution.py:195
  51.1 2.2 %eval_jaxpr.5.part = f32[12,48,128]{2,1,0:T(8,128)S(1)} custom-call(bf16[12,48,128]{2,1,0:T(8,128)(2,1)S(1)} %get-tuple-element.96.rhs, bf16[12,48,128]{2,1,0:T(8,128)(2,1)S(1)} %get-tuple-element.89.value.earlier, bf16[9,12,128,128]{3,2,1,0:T(8,128)(2,1)} %get-tuple-element.97.links), custom_call_target="tpu_custom_call" | custom-call | flops 94371840 | tf_op jit(solution)/shard_map/while/body/eval_jaxpr/pallas_call | solution.py:26
  53.4 0.8 collective-permute-done.2.arrived.c
  54.6 2.2 %collective-permute-start = (bf16[12,48,128]{2,1,0:T(8,128)(2,1)S(1)}, bf16[12,48,128]{2,1,0:T(8,128)(2,1)S(1)}, u32[]{:S(2)}, u32[]{:S(2)}) collective-permute-start(bf16[12,48,128]{2,1,0:T(8,128)(2,1)S(1)} %get-tuple-element.89.value.earlier), channel_id=1, source_target_pairs={{8,16},{24,32},{40,48},{56,64},{72,80},{88,96},{104,112},{120,128}... | collective-permute-start | bytes 442376 | tf_op jit(solution)/shard_map/while/body/eval_jaxpr/ppermute | solution.py:197
  56.8 3.3 %collective-permute-start.2 = (bf16[12,48,128]{2,1,0:T(8,128)(2,1)S(1)}, bf16[12,48,128]{2,1,0:T(8,128)(2,1)S(1)}, u32[]{:S(2)}, u32[]{:S(2)}) collective-permute-start(bf16[12,48,128]{2,1,0:T(8,128)(2,1)S(1)} %get-tuple-element.89.value.earlier), channel_id=1, source_target_pairs={{1,2},{3,4},{5,6},{7,0},{2,1},{4,3},{6,5},{0,7},{9,10},{11,12},{13... | collective-permute-start | bytes 442376 | tf_op jit(solution)/shard_map/while/body/eval_jaxpr/ppermute | solution.py:195
  60.1 2.2 %eval_jaxpr.5.part = f32[12,48,128]{2,1,0:T(8,128)S(1)} custom-call(bf16[12,48,128]{2,1,0:T(8,128)(2,1)S(1)} %get-tuple-element.96.rhs, bf16[12,48,128]{2,1,0:T(8,128)(2,1)S(1)} %get-tuple-element.89.value.earlier, bf16[9,12,128,128]{3,2,1,0:T(8,128)(2,1)} %get-tuple-element.97.links), custom_call_target="tpu_custom_call" | custom-call | flops 94371840 | tf_op jit(solution)/shard_map/while/body/eval_jaxpr/pallas_call | solution.py:26
  62.3 0.8 collective-permute-done.2.arrived.c
  63.6 2.2 %collective-permute-start = (bf16[12,48,128]{2,1,0:T(8,128)(2,1)S(1)}, bf16[12,48,128]{2,1,0:T(8,128)(2,1)S(1)}, u32[]{:S(2)}, u32[]{:S(2)}) collective-permute-start(bf16[12,48,128]{2,1,0:T(8,128)(2,1)S(1)} %get-tuple-element.89.value.earlier), channel_id=1, source_target_pairs={{8,16},{24,32},{40,48},{56,64},{72,80},{88,96},{104,112},{120,128}... | collective-permute-start | bytes 442376 | tf_op jit(solution)/shard_map/while/body/eval_jaxpr/ppermute | solution.py:197
  65.8 3.3 %collective-permute-start.2 = (bf16[12,48,128]{2,1,0:T(8,128)(2,1)S(1)}, bf16[12,48,128]{2,1,0:T(8,128)(2,1)S(1)}, u32[]{:S(2)}, u32[]{:S(2)}) collective-permute-start(bf16[12,48,128]{2,1,0:T(8,128)(2,1)S(1)} %get-tuple-element.89.value.earlier), channel_id=1, source_target_pairs={{1,2},{3,4},{5,6},{7,0},{2,1},{4,3},{6,5},{0,7},{9,10},{11,12},{13... | collective-permute-start | bytes 442376 | tf_op jit(solution)/shard_map/while/body/eval_jaxpr/ppermute | solution.py:195
  69.1 2.2 %eval_jaxpr.5.part = f32[12,48,128]{2,1,0:T(8,128)S(1)} custom-call(bf16[12,48,128]{2,1,0:T(8,128)(2,1)S(1)} %get-tuple-element.96.rhs, bf16[12,48,128]{2,1,0:T(8,128)(2,1)S(1)} %get-tuple-element.89.value.earlier, bf16[9,12,128,128]{3,2,1,0:T(8,128)(2,1)} %get-tuple-element.97.links), custom_call_target="tpu_custom_call" | custom-call | flops 94371840 | tf_op jit(solution)/shard_map/while/body/eval_jaxpr/pallas_call | solution.py:26
  71.3 0.8 collective-permute-done.2.arrived.c
  72.6 2.2 %collective-permute-start = (bf16[12,48,128]{2,1,0:T(8,128)(2,1)S(1)}, bf16[12,48,128]{2,1,0:T(8,128)(2,1)S(1)}, u32[]{:S(2)}, u32[]{:S(2)}) collective-permute-start(bf16[12,48,128]{2,1,0:T(8,128)(2,1)S(1)} %get-tuple-element.89.value.earlier), channel_id=1, source_target_pairs={{8,16},{24,32},{40,48},{56,64},{72,80},{88,96},{104,112},{120,128}... | collective-permute-start | bytes 442376 | tf_op jit(solution)/shard_map/while/body/eval_jaxpr/ppermute | solution.py:197
  74.7 3.3 %collective-permute-start.2 = (bf16[12,48,128]{2,1,0:T(8,128)(2,1)S(1)}, bf16[12,48,128]{2,1,0:T(8,128)(2,1)S(1)}, u32[]{:S(2)}, u32[]{:S(2)}) collective-permute-start(bf16[12,48,128]{2,1,0:T(8,128)(2,1)S(1)} %get-tuple-element.89.value.earlier), channel_id=1, source_target_pairs={{1,2},{3,4},{5,6},{7,0},{2,1},{4,3},{6,5},{0,7},{9,10},{11,12},{13... | collective-permute-start | bytes 442376 | tf_op jit(solution)/shard_map/while/body/eval_jaxpr/ppermute | solution.py:195
  78.0 2.2 %eval_jaxpr.5.part = f32[12,48,128]{2,1,0:T(8,128)S(1)} custom-call(bf16[12,48,128]{2,1,0:T(8,128)(2,1)S(1)} %get-tuple-element.96.rhs, bf16[12,48,128]{2,1,0:T(8,128)(2,1)S(1)} %get-tuple-element.89.value.earlier, bf16[9,12,128,128]{3,2,1,0:T(8,128)(2,1)} %get-tuple-element.97.links), custom_call_target="tpu_custom_call" | custom-call | flops 94371840 | tf_op jit(solution)/shard_map/while/body/eval_jaxpr/pallas_call | solution.py:26
  80.3 0.8 collective-permute-done.2.arrived.c
  81.6 2.2 %collective-permute-start = (bf16[12,48,128]{2,1,0:T(8,128)(2,1)S(1)}, bf16[12,48,128]{2,1,0:T(8,128)(2,1)S(1)}, u32[]{:S(2)}, u32[]{:S(2)}) collective-permute-start(bf16[12,48,128]{2,1,0:T(8,128)(2,1)S(1)} %get-tuple-element.89.value.earlier), channel_id=1, source_target_pairs={{8,16},{24,32},{40,48},{56,64},{72,80},{88,96},{104,112},{120,128}... | collective-permute-start | bytes 442376 | tf_op jit(solution)/shard_map/while/body/eval_jaxpr/ppermute | solution.py:197
  83.7 3.3 %collective-permute-start.2 = (bf16[12,48,128]{2,1,0:T(8,128)(2,1)S(1)}, bf16[12,48,128]{2,1,0:T(8,128)(2,1)S(1)}, u32[]{:S(2)}, u32[]{:S(2)}) collective-permute-start(bf16[12,48,128]{2,1,0:T(8,128)(2,1)S(1)} %get-tuple-element.89.value.earlier), channel_id=1, source_target_pairs={{1,2},{3,4},{5,6},{7,0},{2,1},{4,3},{6,5},{0,7},{9,10},{11,12},{13... | collective-permute-start | bytes 442376 | tf_op jit(solution)/shard_map/while/body/eval_jaxpr/ppermute | solution.py:195
  87.0 2.2 %eval_jaxpr.5.part = f32[12,48,128]{2,1,0:T(8,128)S(1)} custom-call(bf16[12,48,128]{2,1,0:T(8,128)(2,1)S(1)} %get-tuple-element.96.rhs, bf16[12,48,128]{2,1,0:T(8,128)(2,1)S(1)} %get-tuple-element.89.value.earlier, bf16[9,12,128,128]{3,2,1,0:T(8,128)(2,1)} %get-tuple-element.97.links), custom_call_target="tpu_custom_call" | custom-call | flops 94371840 | tf_op jit(solution)/shard_map/while/body/eval_jaxpr/pallas_call | solution.py:26
  89.3 0.8 collective-permute-done.2.arrived.c
  90.6 2.2 %collective-permute-start = (bf16[12,48,128]{2,1,0:T(8,128)(2,1)S(1)}, bf16[12,48,128]{2,1,0:T(8,128)(2,1)S(1)}, u32[]{:S(2)}, u32[]{:S(2)}) collective-permute-start(bf16[12,48,128]{2,1,0:T(8,128)(2,1)S(1)} %get-tuple-element.89.value.earlier), channel_id=1, source_target_pairs={{8,16},{24,32},{40,48},{56,64},{72,80},{88,96},{104,112},{120,128}... | collective-permute-start | bytes 442376 | tf_op jit(solution)/shard_map/while/body/eval_jaxpr/ppermute | solution.py:197
  92.7 3.3 %collective-permute-start.2 = (bf16[12,48,128]{2,1,0:T(8,128)(2,1)S(1)}, bf16[12,48,128]{2,1,0:T(8,128)(2,1)S(1)}, u32[]{:S(2)}, u32[]{:S(2)}) collective-permute-start(bf16[12,48,128]{2,1,0:T(8,128)(2,1)S(1)} %get-tuple-element.89.value.earlier), channel_id=1, source_target_pairs={{1,2},{3,4},{5,6},{7,0},{2,1},{4,3},{6,5},{0,7},{9,10},{11,12},{13... | collective-permute-start | bytes 442376 | tf_op jit(solution)/shard_map/while/body/eval_jaxpr/ppermute | solution.py:195
  96.0 2.2 %eval_jaxpr.5.part = f32[12,48,128]{2,1,0:T(8,128)S(1)} custom-call(bf16[12,48,128]{2,1,0:T(8,128)(2,1)S(1)} %get-tuple-element.96.rhs, bf16[12,48,128]{2,1,0:T(8,128)(2,1)S(1)} %get-tuple-element.89.value.earlier, bf16[9,12,128,128]{3,2,1,0:T(8,128)(2,1)} %get-tuple-element.97.links), custom_call_target="tpu_custom_call" | custom-call | flops 94371840 | tf_op jit(solution)/shard_map/while/body/eval_jaxpr/pallas_call | solution.py:26
  98.3 0.8 collective-permute-done.2.arrived.c
  99.5 2.2 %collective-permute-start = (bf16[12,48,128]{2,1,0:T(8,128)(2,1)S(1)}, bf16[12,48,128]{2,1,0:T(8,128)(2,1)S(1)}, u32[]{:S(2)}, u32[]{:S(2)}) collective-permute-start(bf16[12,48,128]{2,1,0:T(8,128)(2,1)S(1)} %get-tuple-element.89.value.earlier), channel_id=1, source_target_pairs={{8,16},{24,32},{40,48},{56,64},{72,80},{88,96},{104,112},{120,128}... | collective-permute-start | bytes 442376 | tf_op jit(solution)/shard_map/while/body/eval_jaxpr/ppermute | solution.py:197
  101.7 3.3 %collective-permute-start.2 = (bf16[12,48,128]{2,1,0:T(8,128)(2,1)S(1)}, bf16[12,48,128]{2,1,0:T(8,128)(2,1)S(1)}, u32[]{:S(2)}, u32[]{:S(2)}) collective-permute-start(bf16[12,48,128]{2,1,0:T(8,128)(2,1)S(1)} %get-tuple-element.89.value.earlier), channel_id=1, source_target_pairs={{1,2},{3,4},{5,6},{7,0},{2,1},{4,3},{6,5},{0,7},{9,10},{11,12},{13... | collective-permute-start | bytes 442376 | tf_op jit(solution)/shard_map/while/body/eval_jaxpr/ppermute | solution.py:195
  105.0 2.2 %eval_jaxpr.5.part = f32[12,48,128]{2,1,0:T(8,128)S(1)} custom-call(bf16[12,48,128]{2,1,0:T(8,128)(2,1)S(1)} %get-tuple-element.96.rhs, bf16[12,48,128]{2,1,0:T(8,128)(2,1)S(1)} %get-tuple-element.89.value.earlier, bf16[9,12,128,128]{3,2,1,0:T(8,128)(2,1)} %get-tuple-element.97.links), custom_call_target="tpu_custom_call" | custom-call | flops 94371840 | tf_op jit(solution)/shard_map/while/body/eval_jaxpr/pallas_call | solution.py:26
  107.3 0.8 collective-permute-done.2.arrived.c
  108.5 2.2 %collective-permute-start = (bf16[12,48,128]{2,1,0:T(8,128)(2,1)S(1)}, bf16[12,48,128]{2,1,0:T(8,128)(2,1)S(1)}, u32[]{:S(2)}, u32[]{:S(2)}) collective-permute-start(bf16[12,48,128]{2,1,0:T(8,128)(2,1)S(1)} %get-tuple-element.89.value.earlier), channel_id=1, source_target_pairs={{8,16},{24,32},{40,48},{56,64},{72,80},{88,96},{104,112},{120,128}... | collective-permute-start | bytes 442376 | tf_op jit(solution)/shard_map/while/body/eval_jaxpr/ppermute | solution.py:197
  110.7 3.3 %collective-permute-start.2 = (bf16[12,48,128]{2,1,0:T(8,128)(2,1)S(1)}, bf16[12,48,128]{2,1,0:T(8,128)(2,1)S(1)}, u32[]{:S(2)}, u32[]{:S(2)}) collective-permute-start(bf16[12,48,128]{2,1,0:T(8,128)(2,1)S(1)} %get-tuple-element.89.value.earlier), channel_id=1, source_target_pairs={{1,2},{3,4},{5,6},{7,0},{2,1},{4,3},{6,5},{0,7},{9,10},{11,12},{13... | collective-permute-start | bytes 442376 | tf_op jit(solution)/shard_map/while/body/eval_jaxpr/ppermute | solution.py:195
  114.0 2.2 %eval_jaxpr.5.part = f32[12,48,128]{2,1,0:T(8,128)S(1)} custom-call(bf16[12,48,128]{2,1,0:T(8,128)(2,1)S(1)} %get-tuple-element.96.rhs, bf16[12,48,128]{2,1,0:T(8,128)(2,1)S(1)} %get-tuple-element.89.value.earlier, bf16[9,12,128,128]{3,2,1,0:T(8,128)(2,1)} %get-tuple-element.97.links), custom_call_target="tpu_custom_call" | custom-call | flops 94371840 | tf_op jit(solution)/shard_map/while/body/eval_jaxpr/pallas_call | solution.py:26
  116.3 0.8 collective-permute-done.2.arrived.c
  117.5 2.2 %collective-permute-start = (bf16[12,48,128]{2,1,0:T(8,128)(2,1)S(1)}, bf16[12,48,128]{2,1,0:T(8,128)(2,1)S(1)}, u32[]{:S(2)}, u32[]{:S(2)}) collective-permute-start(bf16[12,48,128]{2,1,0:T(8,128)(2,1)S(1)} %get-tuple-element.89.value.earlier), channel_id=1, source_target_pairs={{8,16},{24,32},{40,48},{56,64},{72,80},{88,96},{104,112},{120,128}... | collective-permute-start | bytes 442376 | tf_op jit(solution)/shard_map/while/body/eval_jaxpr/ppermute | solution.py:197
  119.7 3.3 %collective-permute-start.2 = (bf16[12,48,128]{2,1,0:T(8,128)(2,1)S(1)}, bf16[12,48,128]{2,1,0:T(8,128)(2,1)S(1)}, u32[]{:S(2)}, u32[]{:S(2)}) collective-permute-start(bf16[12,48,128]{2,1,0:T(8,128)(2,1)S(1)} %get-tuple-element.89.value.earlier), channel_id=1, source_target_pairs={{1,2},{3,4},{5,6},{7,0},{2,1},{4,3},{6,5},{0,7},{9,10},{11,12},{13... | collective-permute-start | bytes 442376 | tf_op jit(solution)/shard_map/while/body/eval_jaxpr/ppermute | solution.py:195
  123.0 2.2 %eval_jaxpr.5.part = f32[12,48,128]{2,1,0:T(8,128)S(1)} custom-call(bf16[12,48,128]{2,1,0:T(8,128)(2,1)S(1)} %get-tuple-element.96.rhs, bf16[12,48,128]{2,1,0:T(8,128)(2,1)S(1)} %get-tuple-element.89.value.earlier, bf16[9,12,128,128]{3,2,1,0:T(8,128)(2,1)} %get-tuple-element.97.links), custom_call_target="tpu_custom_call" | custom-call | flops 94371840 | tf_op jit(solution)/shard_map/while/body/eval_jaxpr/pallas_call | solution.py:26
  125.3 0.8 collective-permute-done.2.arrived.c
  126.5 2.2 %collective-permute-start = (bf16[12,48,128]{2,1,0:T(8,128)(2,1)S(1)}, bf16[12,48,128]{2,1,0:T(8,128)(2,1)S(1)}, u32[]{:S(2)}, u32[]{:S(2)}) collective-permute-start(bf16[12,48,128]{2,1,0:T(8,128)(2,1)S(1)} %get-tuple-element.89.value.earlier), channel_id=1, source_target_pairs={{8,16},{24,32},{40,48},{56,64},{72,80},{88,96},{104,112},{120,128}... | collective-permute-start | bytes 442376 | tf_op jit(solution)/shard_map/while/body/eval_jaxpr/ppermute | solution.py:197
  128.7 3.3 %collective-permute-start.2 = (bf16[12,48,128]{2,1,0:T(8,128)(2,1)S(1)}, bf16[12,48,128]{2,1,0:T(8,128)(2,1)S(1)}, u32[]{:S(2)}, u32[]{:S(2)}) collective-permute-start(bf16[12,48,128]{2,1,0:T(8,128)(2,1)S(1)} %get-tuple-element.89.value.earlier), channel_id=1, source_target_pairs={{1,2},{3,4},{5,6},{7,0},{2,1},{4,3},{6,5},{0,7},{9,10},{11,12},{13... | collective-permute-start | bytes 442376 | tf_op jit(solution)/shard_map/while/body/eval_jaxpr/ppermute | solution.py:195
  132.0 2.2 %eval_jaxpr.5.part = f32[12,48,128]{2,1,0:T(8,128)S(1)} custom-call(bf16[12,48,128]{2,1,0:T(8,128)(2,1)S(1)} %get-tuple-element.96.rhs, bf16[12,48,128]{2,1,0:T(8,128)(2,1)S(1)} %get-tuple-element.89.value.earlier, bf16[9,12,128,128]{3,2,1,0:T(8,128)(2,1)} %get-tuple-element.97.links), custom_call_target="tpu_custom_call" | custom-call | flops 94371840 | tf_op jit(solution)/shard_map/while/body/eval_jaxpr/pallas_call | solution.py:26
  134.2 0.8 collective-permute-done.2.arrived.c
  135.5 2.2 %collective-permute-start = (bf16[12,48,128]{2,1,0:T(8,128)(2,1)S(1)}, bf16[12,48,128]{2,1,0:T(8,128)(2,1)S(1)}, u32[]{:S(2)}, u32[]{:S(2)}) collective-permute-start(bf16[12,48,128]{2,1,0:T(8,128)(2,1)S(1)} %get-tuple-element.89.value.earlier), channel_id=1, source_target_pairs={{8,16},{24,32},{40,48},{56,64},{72,80},{88,96},{104,112},{120,128}... | collective-permute-start | bytes 442376 | tf_op jit(solution)/shard_map/while/body/eval_jaxpr/ppermute | solution.py:197
  137.7 3.3 %collective-permute-start.2 = (bf16[12,48,128]{2,1,0:T(8,128)(2,1)S(1)}, bf16[12,48,128]{2,1,0:T(8,128)(2,1)S(1)}, u32[]{:S(2)}, u32[]{:S(2)}) collective-permute-start(bf16[12,48,128]{2,1,0:T(8,128)(2,1)S(1)} %get-tuple-element.89.value.earlier), channel_id=1, source_target_pairs={{1,2},{3,4},{5,6},{7,0},{2,1},{4,3},{6,5},{0,7},{9,10},{11,12},{13... | collective-permute-start | bytes 442376 | tf_op jit(solution)/shard_map/while/body/eval_jaxpr/ppermute | solution.py:195
  141.0 2.2 %eval_jaxpr.5.part = f32[12,48,128]{2,1,0:T(8,128)S(1)} custom-call(bf16[12,48,128]{2,1,0:T(8,128)(2,1)S(1)} %get-tuple-element.96.rhs, bf16[12,48,128]{2,1,0:T(8,128)(2,1)S(1)} %get-tuple-element.89.value.earlier, bf16[9,12,128,128]{3,2,1,0:T(8,128)(2,1)} %get-tuple-element.97.links), custom_call_target="tpu_custom_call" | custom-call | flops 94371840 | tf_op jit(solution)/shard_map/while/body/eval_jaxpr/pallas_call | solution.py:26
  143.2 0.8 collective-permute-done.2.arrived.c
  144.5 2.2 %collective-permute-start.8 = (bf16[12,48,128]{2,1,0:T(8,128)(2,1)S(1)}, bf16[12,48,128]{2,1,0:T(8,128)(2,1)S(1)}, u32[]{:S(2)}, u32[]{:S(2)}) collective-permute-start(bf16[12,48,128]{2,1,0:T(8,128)(2,1)S(1)} %get-tuple-element.38.value.earlier), channel_id=1, source_target_pairs={{8,16},{24,32},{40,48},{56,64},{72,80},{88,96},{104,112},{120,128}... | collective-permute-start | bytes 442376 | tf_op jit(solution)/shard_map/ppermute | solution.py:197
  146.7 3.3 %collective-permute-start.10 = (bf16[12,48,128]{2,1,0:T(8,128)(2,1)S(1)}, bf16[12,48,128]{2,1,0:T(8,128)(2,1)S(1)}, u32[]{:S(2)}, u32[]{:S(2)}) collective-permute-start(bf16[12,48,128]{2,1,0:T(8,128)(2,1)S(1)} %get-tuple-element.38.value.earlier), channel_id=1, source_target_pairs={{1,2},{3,4},{5,6},{7,0},{2,1},{4,3},{6,5},{0,7},{9,10},{11,12},{13... | collective-permute-start | bytes 442376 | tf_op jit(solution)/shard_map/ppermute | solution.py:195
  149.9 5.3 %shard_map.43 = (f32[12,48,128]{2,1,0:T(8,128)S(1)}, bf16[12,128,1536]{2,1,0:T(8,128)(2,1)S(1)}) custom-call(bf16[12,48,128]{2,1,0:T(8,128)(2,1)S(1)} %get-tuple-element.116, bf16[12,48,128]{2,1,0:T(8,128)(2,1)S(1)} %get-tuple-element.38.value.earlier, bf16[9,12,128,128]{3,2,1,0:T(8,128)(2,1)} %get-tuple-element.126, bf16[12,1536,128]{2,1,0:T(8,128)(2,1)} %bitcast.12), custom_call_target="tpu_custom_call" | custom-call | flops 94371840 | tf_op jit(solution)/shard_map/pallas_call | solution.py:26
  155.7 1.5 shard_map.48
  (148 shorter events, 8.2 us)
Async XLA Ops:
  3.7 15.5 %collective-permute-start.4 = (bf16[12,48,128]{2,1,0:T(8,128)(2,1)S(1)}, bf16[12,48,128]{2,1,0:T(8,128)(2,1)S(1)}, u32[]{:S(2)}, u32[]{:S(2)}) collective-permute-start(bf16[12,48,128]{2,1,0:T(8,128)(2,1)S(1)} %shard_map.37.rhs.earlier), channel_id=1, source_target_pairs={{8,16},{24,32},{40,48},{56,64},{72,80},{88,96},{104,112},{120,128}... | collective-permute-start | bytes 442376 | tf_op jit(solution)/shard_map/ppermute | solution.py:197
  12.6 6.5 %collective-permute-start.5 = (bf16[12,48,128]{2,1,0:T(8,128)(2,1)S(1)}, bf16[12,48,128]{2,1,0:T(8,128)(2,1)S(1)}, u32[]{:S(2)}, u32[]{:S(2)}) collective-permute-start(bf16[12,48,128]{2,1,0:T(8,128)(2,1)S(1)} %shard_map.37.rhs.earlier), channel_id=1, source_target_pairs={{0,8},{16,24},{32,40},{48,56},{64,72},{80,88},{96,104},{112,120},{... | collective-permute-start | bytes 442376 | tf_op jit(solution)/shard_map/ppermute | solution.py:196
  12.6 6.6 %collective-permute-start.6 = (bf16[12,48,128]{2,1,0:T(8,128)(2,1)S(1)}, bf16[12,48,128]{2,1,0:T(8,128)(2,1)S(1)}, u32[]{:S(2)}, u32[]{:S(2)}) collective-permute-start(bf16[12,48,128]{2,1,0:T(8,128)(2,1)S(1)} %shard_map.37.rhs.earlier), channel_id=1, source_target_pairs={{1,2},{3,4},{5,6},{7,0},{2,1},{4,3},{6,5},{0,7},{9,10},{11,12},{13... | collective-permute-start | bytes 442376 | tf_op jit(solution)/shard_map/ppermute | solution.py:195
  14.7 4.5 %collective-permute-start.7 = (bf16[12,48,128]{2,1,0:T(8,128)(2,1)S(1)}, bf16[12,48,128]{2,1,0:T(8,128)(2,1)S(1)}, u32[]{:S(2)}, u32[]{:S(2)}) collective-permute-start(bf16[12,48,128]{2,1,0:T(8,128)(2,1)S(1)} %shard_map.37.rhs.earlier), channel_id=1, source_target_pairs={{0,1},{2,3},{4,5},{6,7},{1,0},{3,2},{5,4},{7,6},{8,9},{10,11},{12,... | collective-permute-start | bytes 442376 | tf_op jit(solution)/shard_map/ppermute | solution.py:194
  19.6 8.7 %collective-permute-start = (bf16[12,48,128]{2,1,0:T(8,128)(2,1)S(1)}, bf16[12,48,128]{2,1,0:T(8,128)(2,1)S(1)}, u32[]{:S(2)}, u32[]{:S(2)}) collective-permute-start(bf16[12,48,128]{2,1,0:T(8,128)(2,1)S(1)} %get-tuple-element.89.value.earlier), channel_id=1, source_target_pairs={{8,16},{24,32},{40,48},{56,64},{72,80},{88,96},{104,112},{120,128}... | collective-permute-start | bytes 442376 | tf_op jit(solution)/shard_map/while/body/eval_jaxpr/ppermute | solution.py:197
  21.2 7.2 %collective-permute-start.1 = (bf16[12,48,128]{2,1,0:T(8,128)(2,1)S(1)}, bf16[12,48,128]{2,1,0:T(8,128)(2,1)S(1)}, u32[]{:S(2)}, u32[]{:S(2)}) collective-permute-start(bf16[12,48,128]{2,1,0:T(8,128)(2,1)S(1)} %get-tuple-element.89.value.earlier), channel_id=1, source_target_pairs={{0,8},{16,24},{32,40},{48,56},{64,72},{80,88},{96,104},{112,120},{... | collective-permute-start | bytes 442376 | tf_op jit(solution)/shard_map/while/body/eval_jaxpr/ppermute | solution.py:196
  21.2 7.1 %collective-permute-start.2 = (bf16[12,48,128]{2,1,0:T(8,128)(2,1)S(1)}, bf16[12,48,128]{2,1,0:T(8,128)(2,1)S(1)}, u32[]{:S(2)}, u32[]{:S(2)}) collective-permute-start(bf16[12,48,128]{2,1,0:T(8,128)(2,1)S(1)} %get-tuple-element.89.value.earlier), channel_id=1, source_target_pairs={{1,2},{3,4},{5,6},{7,0},{2,1},{4,3},{6,5},{0,7},{9,10},{11,12},{13... | collective-permute-start | bytes 442376 | tf_op jit(solution)/shard_map/while/body/eval_jaxpr/ppermute | solution.py:195
  24.1 4.2 %collective-permute-start.3 = (bf16[12,48,128]{2,1,0:T(8,128)(2,1)S(1)}, bf16[12,48,128]{2,1,0:T(8,128)(2,1)S(1)}, u32[]{:S(2)}, u32[]{:S(2)}) collective-permute-start(bf16[12,48,128]{2,1,0:T(8,128)(2,1)S(1)} %get-tuple-element.89.value.earlier), channel_id=1, source_target_pairs={{0,1},{2,3},{4,5},{6,7},{1,0},{3,2},{5,4},{7,6},{8,9},{10,11},{12,... | collective-permute-start | bytes 442376 | tf_op jit(solution)/shard_map/while/body/eval_jaxpr/ppermute | solution.py:194
  28.8 7.8 %collective-permute-start = (bf16[12,48,128]{2,1,0:T(8,128)(2,1)S(1)}, bf16[12,48,128]{2,1,0:T(8,128)(2,1)S(1)}, u32[]{:S(2)}, u32[]{:S(2)}) collective-permute-start(bf16[12,48,128]{2,1,0:T(8,128)(2,1)S(1)} %get-tuple-element.89.value.earlier), channel_id=1, source_target_pairs={{8,16},{24,32},{40,48},{56,64},{72,80},{88,96},{104,112},{120,128}... | collective-permute-start | bytes 442376 | tf_op jit(solution)/shard_map/while/body/eval_jaxpr/ppermute | solution.py:197
  30.0 6.6 %collective-permute-start.1 = (bf16[12,48,128]{2,1,0:T(8,128)(2,1)S(1)}, bf16[12,48,128]{2,1,0:T(8,128)(2,1)S(1)}, u32[]{:S(2)}, u32[]{:S(2)}) collective-permute-start(bf16[12,48,128]{2,1,0:T(8,128)(2,1)S(1)} %get-tuple-element.89.value.earlier), channel_id=1, source_target_pairs={{0,8},{16,24},{32,40},{48,56},{64,72},{80,88},{96,104},{112,120},{... | collective-permute-start | bytes 442376 | tf_op jit(solution)/shard_map/while/body/eval_jaxpr/ppermute | solution.py:196
  30.0 6.6 %collective-permute-start.2 = (bf16[12,48,128]{2,1,0:T(8,128)(2,1)S(1)}, bf16[12,48,128]{2,1,0:T(8,128)(2,1)S(1)}, u32[]{:S(2)}, u32[]{:S(2)}) collective-permute-start(bf16[12,48,128]{2,1,0:T(8,128)(2,1)S(1)} %get-tuple-element.89.value.earlier), channel_id=1, source_target_pairs={{1,2},{3,4},{5,6},{7,0},{2,1},{4,3},{6,5},{0,7},{9,10},{11,12},{13... | collective-permute-start | bytes 442376 | tf_op jit(solution)/shard_map/while/body/eval_jaxpr/ppermute | solution.py:195
  33.1 3.5 %collective-permute-start.3 = (bf16[12,48,128]{2,1,0:T(8,128)(2,1)S(1)}, bf16[12,48,128]{2,1,0:T(8,128)(2,1)S(1)}, u32[]{:S(2)}, u32[]{:S(2)}) collective-permute-start(bf16[12,48,128]{2,1,0:T(8,128)(2,1)S(1)} %get-tuple-element.89.value.earlier), channel_id=1, source_target_pairs={{0,1},{2,3},{4,5},{6,7},{1,0},{3,2},{5,4},{7,6},{8,9},{10,11},{12,... | collective-permute-start | bytes 442376 | tf_op jit(solution)/shard_map/while/body/eval_jaxpr/ppermute | solution.py:194
  37.0 7.4 %collective-permute-start = (bf16[12,48,128]{2,1,0:T(8,128)(2,1)S(1)}, bf16[12,48,128]{2,1,0:T(8,128)(2,1)S(1)}, u32[]{:S(2)}, u32[]{:S(2)}) collective-permute-start(bf16[12,48,128]{2,1,0:T(8,128)(2,1)S(1)} %get-tuple-element.89.value.earlier), channel_id=1, source_target_pairs={{8,16},{24,32},{40,48},{56,64},{72,80},{88,96},{104,112},{120,128}... | collective-permute-start | bytes 442376 | tf_op jit(solution)/shard_map/while/body/eval_jaxpr/ppermute | solution.py:197
  39.0 5.4 %collective-permute-start.1 = (bf16[12,48,128]{2,1,0:T(8,128)(2,1)S(1)}, bf16[12,48,128]{2,1,0:T(8,128)(2,1)S(1)}, u32[]{:S(2)}, u32[]{:S(2)}) collective-permute-start(bf16[12,48,128]{2,1,0:T(8,128)(2,1)S(1)} %get-tuple-element.89.value.earlier), channel_id=1, source_target_pairs={{0,8},{16,24},{32,40},{48,56},{64,72},{80,88},{96,104},{112,120},{... | collective-permute-start | bytes 442376 | tf_op jit(solution)/shard_map/while/body/eval_jaxpr/ppermute | solution.py:196
  39.0 6.2 %collective-permute-start.2 = (bf16[12,48,128]{2,1,0:T(8,128)(2,1)S(1)}, bf16[12,48,128]{2,1,0:T(8,128)(2,1)S(1)}, u32[]{:S(2)}, u32[]{:S(2)}) collective-permute-start(bf16[12,48,128]{2,1,0:T(8,128)(2,1)S(1)} %get-tuple-element.89.value.earlier), channel_id=1, source_target_pairs={{1,2},{3,4},{5,6},{7,0},{2,1},{4,3},{6,5},{0,7},{9,10},{11,12},{13... | collective-permute-start | bytes 442376 | tf_op jit(solution)/shard_map/while/body/eval_jaxpr/ppermute | solution.py:195
  42.1 3.1 %collective-permute-start.3 = (bf16[12,48,128]{2,1,0:T(8,128)(2,1)S(1)}, bf16[12,48,128]{2,1,0:T(8,128)(2,1)S(1)}, u32[]{:S(2)}, u32[]{:S(2)}) collective-permute-start(bf16[12,48,128]{2,1,0:T(8,128)(2,1)S(1)} %get-tuple-element.89.value.earlier), channel_id=1, source_target_pairs={{0,1},{2,3},{4,5},{6,7},{1,0},{3,2},{5,4},{7,6},{8,9},{10,11},{12,... | collective-permute-start | bytes 442376 | tf_op jit(solution)/shard_map/while/body/eval_jaxpr/ppermute | solution.py:194
  45.6 7.7 %collective-permute-start = (bf16[12,48,128]{2,1,0:T(8,128)(2,1)S(1)}, bf16[12,48,128]{2,1,0:T(8,128)(2,1)S(1)}, u32[]{:S(2)}, u32[]{:S(2)}) collective-permute-start(bf16[12,48,128]{2,1,0:T(8,128)(2,1)S(1)} %get-tuple-element.89.value.earlier), channel_id=1, source_target_pairs={{8,16},{24,32},{40,48},{56,64},{72,80},{88,96},{104,112},{120,128}... | collective-permute-start | bytes 442376 | tf_op jit(solution)/shard_map/while/body/eval_jaxpr/ppermute | solution.py:197
  47.8 5.6 %collective-permute-start.1 = (bf16[12,48,128]{2,1,0:T(8,128)(2,1)S(1)}, bf16[12,48,128]{2,1,0:T(8,128)(2,1)S(1)}, u32[]{:S(2)}, u32[]{:S(2)}) collective-permute-start(bf16[12,48,128]{2,1,0:T(8,128)(2,1)S(1)} %get-tuple-element.89.value.earlier), channel_id=1, source_target_pairs={{0,8},{16,24},{32,40},{48,56},{64,72},{80,88},{96,104},{112,120},{... | collective-permute-start | bytes 442376 | tf_op jit(solution)/shard_map/while/body/eval_jaxpr/ppermute | solution.py:196
  47.8 6.4 %collective-permute-start.2 = (bf16[12,48,128]{2,1,0:T(8,128)(2,1)S(1)}, bf16[12,48,128]{2,1,0:T(8,128)(2,1)S(1)}, u32[]{:S(2)}, u32[]{:S(2)}) collective-permute-start(bf16[12,48,128]{2,1,0:T(8,128)(2,1)S(1)} %get-tuple-element.89.value.earlier), channel_id=1, source_target_pairs={{1,2},{3,4},{5,6},{7,0},{2,1},{4,3},{6,5},{0,7},{9,10},{11,12},{13... | collective-permute-start | bytes 442376 | tf_op jit(solution)/shard_map/while/body/eval_jaxpr/ppermute | solution.py:195
  51.1 3.1 %collective-permute-start.3 = (bf16[12,48,128]{2,1,0:T(8,128)(2,1)S(1)}, bf16[12,48,128]{2,1,0:T(8,128)(2,1)S(1)}, u32[]{:S(2)}, u32[]{:S(2)}) collective-permute-start(bf16[12,48,128]{2,1,0:T(8,128)(2,1)S(1)} %get-tuple-element.89.value.earlier), channel_id=1, source_target_pairs={{0,1},{2,3},{4,5},{6,7},{1,0},{3,2},{5,4},{7,6},{8,9},{10,11},{12,... | collective-permute-start | bytes 442376 | tf_op jit(solution)/shard_map/while/body/eval_jaxpr/ppermute | solution.py:194
  54.6 7.7 %collective-permute-start = (bf16[12,48,128]{2,1,0:T(8,128)(2,1)S(1)}, bf16[12,48,128]{2,1,0:T(8,128)(2,1)S(1)}, u32[]{:S(2)}, u32[]{:S(2)}) collective-permute-start(bf16[12,48,128]{2,1,0:T(8,128)(2,1)S(1)} %get-tuple-element.89.value.earlier), channel_id=1, source_target_pairs={{8,16},{24,32},{40,48},{56,64},{72,80},{88,96},{104,112},{120,128}... | collective-permute-start | bytes 442376 | tf_op jit(solution)/shard_map/while/body/eval_jaxpr/ppermute | solution.py:197
  56.8 5.6 %collective-permute-start.1 = (bf16[12,48,128]{2,1,0:T(8,128)(2,1)S(1)}, bf16[12,48,128]{2,1,0:T(8,128)(2,1)S(1)}, u32[]{:S(2)}, u32[]{:S(2)}) collective-permute-start(bf16[12,48,128]{2,1,0:T(8,128)(2,1)S(1)} %get-tuple-element.89.value.earlier), channel_id=1, source_target_pairs={{0,8},{16,24},{32,40},{48,56},{64,72},{80,88},{96,104},{112,120},{... | collective-permute-start | bytes 442376 | tf_op jit(solution)/shard_map/while/body/eval_jaxpr/ppermute | solution.py:196
  56.8 6.4 %collective-permute-start.2 = (bf16[12,48,128]{2,1,0:T(8,128)(2,1)S(1)}, bf16[12,48,128]{2,1,0:T(8,128)(2,1)S(1)}, u32[]{:S(2)}, u32[]{:S(2)}) collective-permute-start(bf16[12,48,128]{2,1,0:T(8,128)(2,1)S(1)} %get-tuple-element.89.value.earlier), channel_id=1, source_target_pairs={{1,2},{3,4},{5,6},{7,0},{2,1},{4,3},{6,5},{0,7},{9,10},{11,12},{13... | collective-permute-start | bytes 442376 | tf_op jit(solution)/shard_map/while/body/eval_jaxpr/ppermute | solution.py:195
  60.1 3.1 %collective-permute-start.3 = (bf16[12,48,128]{2,1,0:T(8,128)(2,1)S(1)}, bf16[12,48,128]{2,1,0:T(8,128)(2,1)S(1)}, u32[]{:S(2)}, u32[]{:S(2)}) collective-permute-start(bf16[12,48,128]{2,1,0:T(8,128)(2,1)S(1)} %get-tuple-element.89.value.earlier), channel_id=1, source_target_pairs={{0,1},{2,3},{4,5},{6,7},{1,0},{3,2},{5,4},{7,6},{8,9},{10,11},{12,... | collective-permute-start | bytes 442376 | tf_op jit(solution)/shard_map/while/body/eval_jaxpr/ppermute | solution.py:194
  63.6 7.7 %collective-permute-start = (bf16[12,48,128]{2,1,0:T(8,128)(2,1)S(1)}, bf16[12,48,128]{2,1,0:T(8,128)(2,1)S(1)}, u32[]{:S(2)}, u32[]{:S(2)}) collective-permute-start(bf16[12,48,128]{2,1,0:T(8,128)(2,1)S(1)} %get-tuple-element.89.value.earlier), channel_id=1, source_target_pairs={{8,16},{24,32},{40,48},{56,64},{72,80},{88,96},{104,112},{120,128}... | collective-permute-start | bytes 442376 | tf_op jit(solution)/shard_map/while/body/eval_jaxpr/ppermute | solution.py:197
  65.8 5.6 %collective-permute-start.1 = (bf16[12,48,128]{2,1,0:T(8,128)(2,1)S(1)}, bf16[12,48,128]{2,1,0:T(8,128)(2,1)S(1)}, u32[]{:S(2)}, u32[]{:S(2)}) collective-permute-start(bf16[12,48,128]{2,1,0:T(8,128)(2,1)S(1)} %get-tuple-element.89.value.earlier), channel_id=1, source_target_pairs={{0,8},{16,24},{32,40},{48,56},{64,72},{80,88},{96,104},{112,120},{... | collective-permute-start | bytes 442376 | tf_op jit(solution)/shard_map/while/body/eval_jaxpr/ppermute | solution.py:196
  65.8 6.4 %collective-permute-start.2 = (bf16[12,48,128]{2,1,0:T(8,128)(2,1)S(1)}, bf16[12,48,128]{2,1,0:T(8,128)(2,1)S(1)}, u32[]{:S(2)}, u32[]{:S(2)}) collective-permute-start(bf16[12,48,128]{2,1,0:T(8,128)(2,1)S(1)} %get-tuple-element.89.value.earlier), channel_id=1, source_target_pairs={{1,2},{3,4},{5,6},{7,0},{2,1},{4,3},{6,5},{0,7},{9,10},{11,12},{13... | collective-permute-start | bytes 442376 | tf_op jit(solution)/shard_map/while/body/eval_jaxpr/ppermute | solution.py:195
  69.1 3.1 %collective-permute-start.3 = (bf16[12,48,128]{2,1,0:T(8,128)(2,1)S(1)}, bf16[12,48,128]{2,1,0:T(8,128)(2,1)S(1)}, u32[]{:S(2)}, u32[]{:S(2)}) collective-permute-start(bf16[12,48,128]{2,1,0:T(8,128)(2,1)S(1)} %get-tuple-element.89.value.earlier), channel_id=1, source_target_pairs={{0,1},{2,3},{4,5},{6,7},{1,0},{3,2},{5,4},{7,6},{8,9},{10,11},{12,... | collective-permute-start | bytes 442376 | tf_op jit(solution)/shard_map/while/body/eval_jaxpr/ppermute | solution.py:194
  72.6 7.7 %collective-permute-start = (bf16[12,48,128]{2,1,0:T(8,128)(2,1)S(1)}, bf16[12,48,128]{2,1,0:T(8,128)(2,1)S(1)}, u32[]{:S(2)}, u32[]{:S(2)}) collective-permute-start(bf16[12,48,128]{2,1,0:T(8,128)(2,1)S(1)} %get-tuple-element.89.value.earlier), channel_id=1, source_target_pairs={{8,16},{24,32},{40,48},{56,64},{72,80},{88,96},{104,112},{120,128}... | collective-permute-start | bytes 442376 | tf_op jit(solution)/shard_map/while/body/eval_jaxpr/ppermute | solution.py:197
  74.7 5.6 %collective-permute-start.1 = (bf16[12,48,128]{2,1,0:T(8,128)(2,1)S(1)}, bf16[12,48,128]{2,1,0:T(8,128)(2,1)S(1)}, u32[]{:S(2)}, u32[]{:S(2)}) collective-permute-start(bf16[12,48,128]{2,1,0:T(8,128)(2,1)S(1)} %get-tuple-element.89.value.earlier), channel_id=1, source_target_pairs={{0,8},{16,24},{32,40},{48,56},{64,72},{80,88},{96,104},{112,120},{... | collective-permute-start | bytes 442376 | tf_op jit(solution)/shard_map/while/body/eval_jaxpr/ppermute | solution.py:196
  74.7 6.4 %collective-permute-start.2 = (bf16[12,48,128]{2,1,0:T(8,128)(2,1)S(1)}, bf16[12,48,128]{2,1,0:T(8,128)(2,1)S(1)}, u32[]{:S(2)}, u32[]{:S(2)}) collective-permute-start(bf16[12,48,128]{2,1,0:T(8,128)(2,1)S(1)} %get-tuple-element.89.value.earlier), channel_id=1, source_target_pairs={{1,2},{3,4},{5,6},{7,0},{2,1},{4,3},{6,5},{0,7},{9,10},{11,12},{13... | collective-permute-start | bytes 442376 | tf_op jit(solution)/shard_map/while/body/eval_jaxpr/ppermute | solution.py:195
  78.0 3.1 %collective-permute-start.3 = (bf16[12,48,128]{2,1,0:T(8,128)(2,1)S(1)}, bf16[12,48,128]{2,1,0:T(8,128)(2,1)S(1)}, u32[]{:S(2)}, u32[]{:S(2)}) collective-permute-start(bf16[12,48,128]{2,1,0:T(8,128)(2,1)S(1)} %get-tuple-element.89.value.earlier), channel_id=1, source_target_pairs={{0,1},{2,3},{4,5},{6,7},{1,0},{3,2},{5,4},{7,6},{8,9},{10,11},{12,... | collective-permute-start | bytes 442376 | tf_op jit(solution)/shard_map/while/body/eval_jaxpr/ppermute | solution.py:194
  81.6 7.7 %collective-permute-start = (bf16[12,48,128]{2,1,0:T(8,128)(2,1)S(1)}, bf16[12,48,128]{2,1,0:T(8,128)(2,1)S(1)}, u32[]{:S(2)}, u32[]{:S(2)}) collective-permute-start(bf16[12,48,128]{2,1,0:T(8,128)(2,1)S(1)} %get-tuple-element.89.value.earlier), channel_id=1, source_target_pairs={{8,16},{24,32},{40,48},{56,64},{72,80},{88,96},{104,112},{120,128}... | collective-permute-start | bytes 442376 | tf_op jit(solution)/shard_map/while/body/eval_jaxpr/ppermute | solution.py:197
  83.7 5.6 %collective-permute-start.1 = (bf16[12,48,128]{2,1,0:T(8,128)(2,1)S(1)}, bf16[12,48,128]{2,1,0:T(8,128)(2,1)S(1)}, u32[]{:S(2)}, u32[]{:S(2)}) collective-permute-start(bf16[12,48,128]{2,1,0:T(8,128)(2,1)S(1)} %get-tuple-element.89.value.earlier), channel_id=1, source_target_pairs={{0,8},{16,24},{32,40},{48,56},{64,72},{80,88},{96,104},{112,120},{... | collective-permute-start | bytes 442376 | tf_op jit(solution)/shard_map/while/body/eval_jaxpr/ppermute | solution.py:196
  83.7 6.4 %collective-permute-start.2 = (bf16[12,48,128]{2,1,0:T(8,128)(2,1)S(1)}, bf16[12,48,128]{2,1,0:T(8,128)(2,1)S(1)}, u32[]{:S(2)}, u32[]{:S(2)}) collective-permute-start(bf16[12,48,128]{2,1,0:T(8,128)(2,1)S(1)} %get-tuple-element.89.value.earlier), channel_id=1, source_target_pairs={{1,2},{3,4},{5,6},{7,0},{2,1},{4,3},{6,5},{0,7},{9,10},{11,12},{13... | collective-permute-start | bytes 442376 | tf_op jit(solution)/shard_map/while/body/eval_jaxpr/ppermute | solution.py:195
  87.0 3.1 %collective-permute-start.3 = (bf16[12,48,128]{2,1,0:T(8,128)(2,1)S(1)}, bf16[12,48,128]{2,1,0:T(8,128)(2,1)S(1)}, u32[]{:S(2)}, u32[]{:S(2)}) collective-permute-start(bf16[12,48,128]{2,1,0:T(8,128)(2,1)S(1)} %get-tuple-element.89.value.earlier), channel_id=1, source_target_pairs={{0,1},{2,3},{4,5},{6,7},{1,0},{3,2},{5,4},{7,6},{8,9},{10,11},{12,... | collective-permute-start | bytes 442376 | tf_op jit(solution)/shard_map/while/body/eval_jaxpr/ppermute | solution.py:194
  90.6 7.7 %collective-permute-start = (bf16[12,48,128]{2,1,0:T(8,128)(2,1)S(1)}, bf16[12,48,128]{2,1,0:T(8,128)(2,1)S(1)}, u32[]{:S(2)}, u32[]{:S(2)}) collective-permute-start(bf16[12,48,128]{2,1,0:T(8,128)(2,1)S(1)} %get-tuple-element.89.value.earlier), channel_id=1, source_target_pairs={{8,16},{24,32},{40,48},{56,64},{72,80},{88,96},{104,112},{120,128}... | collective-permute-start | bytes 442376 | tf_op jit(solution)/shard_map/while/body/eval_jaxpr/ppermute | solution.py:197
  92.7 5.6 %collective-permute-start.1 = (bf16[12,48,128]{2,1,0:T(8,128)(2,1)S(1)}, bf16[12,48,128]{2,1,0:T(8,128)(2,1)S(1)}, u32[]{:S(2)}, u32[]{:S(2)}) collective-permute-start(bf16[12,48,128]{2,1,0:T(8,128)(2,1)S(1)} %get-tuple-element.89.value.earlier), channel_id=1, source_target_pairs={{0,8},{16,24},{32,40},{48,56},{64,72},{80,88},{96,104},{112,120},{... | collective-permute-start | bytes 442376 | tf_op jit(solution)/shard_map/while/body/eval_jaxpr/ppermute | solution.py:196
  92.7 6.4 %collective-permute-start.2 = (bf16[12,48,128]{2,1,0:T(8,128)(2,1)S(1)}, bf16[12,48,128]{2,1,0:T(8,128)(2,1)S(1)}, u32[]{:S(2)}, u32[]{:S(2)}) collective-permute-start(bf16[12,48,128]{2,1,0:T(8,128)(2,1)S(1)} %get-tuple-element.89.value.earlier), channel_id=1, source_target_pairs={{1,2},{3,4},{5,6},{7,0},{2,1},{4,3},{6,5},{0,7},{9,10},{11,12},{13... | collective-permute-start | bytes 442376 | tf_op jit(solution)/shard_map/while/body/eval_jaxpr/ppermute | solution.py:195
  96.0 3.1 %collective-permute-start.3 = (bf16[12,48,128]{2,1,0:T(8,128)(2,1)S(1)}, bf16[12,48,128]{2,1,0:T(8,128)(2,1)S(1)}, u32[]{:S(2)}, u32[]{:S(2)}) collective-permute-start(bf16[12,48,128]{2,1,0:T(8,128)(2,1)S(1)} %get-tuple-element.89.value.earlier), channel_id=1, source_target_pairs={{0,1},{2,3},{4,5},{6,7},{1,0},{3,2},{5,4},{7,6},{8,9},{10,11},{12,... | collective-permute-start | bytes 442376 | tf_op jit(solution)/shard_map/while/body/eval_jaxpr/ppermute | solution.py:194
  99.5 7.7 %collective-permute-start = (bf16[12,48,128]{2,1,0:T(8,128)(2,1)S(1)}, bf16[12,48,128]{2,1,0:T(8,128)(2,1)S(1)}, u32[]{:S(2)}, u32[]{:S(2)}) collective-permute-start(bf16[12,48,128]{2,1,0:T(8,128)(2,1)S(1)} %get-tuple-element.89.value.earlier), channel_id=1, source_target_pairs={{8,16},{24,32},{40,48},{56,64},{72,80},{88,96},{104,112},{120,128}... | collective-permute-start | bytes 442376 | tf_op jit(solution)/shard_map/while/body/eval_jaxpr/ppermute | solution.py:197
  101.7 5.6 %collective-permute-start.1 = (bf16[12,48,128]{2,1,0:T(8,128)(2,1)S(1)}, bf16[12,48,128]{2,1,0:T(8,128)(2,1)S(1)}, u32[]{:S(2)}, u32[]{:S(2)}) collective-permute-start(bf16[12,48,128]{2,1,0:T(8,128)(2,1)S(1)} %get-tuple-element.89.value.earlier), channel_id=1, source_target_pairs={{0,8},{16,24},{32,40},{48,56},{64,72},{80,88},{96,104},{112,120},{... | collective-permute-start | bytes 442376 | tf_op jit(solution)/shard_map/while/body/eval_jaxpr/ppermute | solution.py:196
  101.7 6.4 %collective-permute-start.2 = (bf16[12,48,128]{2,1,0:T(8,128)(2,1)S(1)}, bf16[12,48,128]{2,1,0:T(8,128)(2,1)S(1)}, u32[]{:S(2)}, u32[]{:S(2)}) collective-permute-start(bf16[12,48,128]{2,1,0:T(8,128)(2,1)S(1)} %get-tuple-element.89.value.earlier), channel_id=1, source_target_pairs={{1,2},{3,4},{5,6},{7,0},{2,1},{4,3},{6,5},{0,7},{9,10},{11,12},{13... | collective-permute-start | bytes 442376 | tf_op jit(solution)/shard_map/while/body/eval_jaxpr/ppermute | solution.py:195
  105.0 3.1 %collective-permute-start.3 = (bf16[12,48,128]{2,1,0:T(8,128)(2,1)S(1)}, bf16[12,48,128]{2,1,0:T(8,128)(2,1)S(1)}, u32[]{:S(2)}, u32[]{:S(2)}) collective-permute-start(bf16[12,48,128]{2,1,0:T(8,128)(2,1)S(1)} %get-tuple-element.89.value.earlier), channel_id=1, source_target_pairs={{0,1},{2,3},{4,5},{6,7},{1,0},{3,2},{5,4},{7,6},{8,9},{10,11},{12,... | collective-permute-start | bytes 442376 | tf_op jit(solution)/shard_map/while/body/eval_jaxpr/ppermute | solution.py:194
  108.5 7.7 %collective-permute-start = (bf16[12,48,128]{2,1,0:T(8,128)(2,1)S(1)}, bf16[12,48,128]{2,1,0:T(8,128)(2,1)S(1)}, u32[]{:S(2)}, u32[]{:S(2)}) collective-permute-start(bf16[12,48,128]{2,1,0:T(8,128)(2,1)S(1)} %get-tuple-element.89.value.earlier), channel_id=1, source_target_pairs={{8,16},{24,32},{40,48},{56,64},{72,80},{88,96},{104,112},{120,128}... | collective-permute-start | bytes 442376 | tf_op jit(solution)/shard_map/while/body/eval_jaxpr/ppermute | solution.py:197
  110.7 5.6 %collective-permute-start.1 = (bf16[12,48,128]{2,1,0:T(8,128)(2,1)S(1)}, bf16[12,48,128]{2,1,0:T(8,128)(2,1)S(1)}, u32[]{:S(2)}, u32[]{:S(2)}) collective-permute-start(bf16[12,48,128]{2,1,0:T(8,128)(2,1)S(1)} %get-tuple-element.89.value.earlier), channel_id=1, source_target_pairs={{0,8},{16,24},{32,40},{48,56},{64,72},{80,88},{96,104},{112,120},{... | collective-permute-start | bytes 442376 | tf_op jit(solution)/shard_map/while/body/eval_jaxpr/ppermute | solution.py:196
  110.7 6.4 %collective-permute-start.2 = (bf16[12,48,128]{2,1,0:T(8,128)(2,1)S(1)}, bf16[12,48,128]{2,1,0:T(8,128)(2,1)S(1)}, u32[]{:S(2)}, u32[]{:S(2)}) collective-permute-start(bf16[12,48,128]{2,1,0:T(8,128)(2,1)S(1)} %get-tuple-element.89.value.earlier), channel_id=1, source_target_pairs={{1,2},{3,4},{5,6},{7,0},{2,1},{4,3},{6,5},{0,7},{9,10},{11,12},{13... | collective-permute-start | bytes 442376 | tf_op jit(solution)/shard_map/while/body/eval_jaxpr/ppermute | solution.py:195
  114.0 3.1 %collective-permute-start.3 = (bf16[12,48,128]{2,1,0:T(8,128)(2,1)S(1)}, bf16[12,48,128]{2,1,0:T(8,128)(2,1)S(1)}, u32[]{:S(2)}, u32[]{:S(2)}) collective-permute-start(bf16[12,48,128]{2,1,0:T(8,128)(2,1)S(1)} %get-tuple-element.89.value.earlier), channel_id=1, source_target_pairs={{0,1},{2,3},{4,5},{6,7},{1,0},{3,2},{5,4},{7,6},{8,9},{10,11},{12,... | collective-permute-start | bytes 442376 | tf_op jit(solution)/shard_map/while/body/eval_jaxpr/ppermute | solution.py:194
  117.5 7.7 %collective-permute-start = (bf16[12,48,128]{2,1,0:T(8,128)(2,1)S(1)}, bf16[12,48,128]{2,1,0:T(8,128)(2,1)S(1)}, u32[]{:S(2)}, u32[]{:S(2)}) collective-permute-start(bf16[12,48,128]{2,1,0:T(8,128)(2,1)S(1)} %get-tuple-element.89.value.earlier), channel_id=1, source_target_pairs={{8,16},{24,32},{40,48},{56,64},{72,80},{88,96},{104,112},{120,128}... | collective-permute-start | bytes 442376 | tf_op jit(solution)/shard_map/while/body/eval_jaxpr/ppermute | solution.py:197
  119.7 5.5 %collective-permute-start.1 = (bf16[12,48,128]{2,1,0:T(8,128)(2,1)S(1)}, bf16[12,48,128]{2,1,0:T(8,128)(2,1)S(1)}, u32[]{:S(2)}, u32[]{:S(2)}) collective-permute-start(bf16[12,48,128]{2,1,0:T(8,128)(2,1)S(1)} %get-tuple-element.89.value.earlier), channel_id=1, source_target_pairs={{0,8},{16,24},{32,40},{48,56},{64,72},{80,88},{96,104},{112,120},{... | collective-permute-start | bytes 442376 | tf_op jit(solution)/shard_map/while/body/eval_jaxpr/ppermute | solution.py:196
  119.7 6.4 %collective-permute-start.2 = (bf16[12,48,128]{2,1,0:T(8,128)(2,1)S(1)}, bf16[12,48,128]{2,1,0:T(8,128)(2,1)S(1)}, u32[]{:S(2)}, u32[]{:S(2)}) collective-permute-start(bf16[12,48,128]{2,1,0:T(8,128)(2,1)S(1)} %get-tuple-element.89.value.earlier), channel_id=1, source_target_pairs={{1,2},{3,4},{5,6},{7,0},{2,1},{4,3},{6,5},{0,7},{9,10},{11,12},{13... | collective-permute-start | bytes 442376 | tf_op jit(solution)/shard_map/while/body/eval_jaxpr/ppermute | solution.py:195
  123.0 3.1 %collective-permute-start.3 = (bf16[12,48,128]{2,1,0:T(8,128)(2,1)S(1)}, bf16[12,48,128]{2,1,0:T(8,128)(2,1)S(1)}, u32[]{:S(2)}, u32[]{:S(2)}) collective-permute-start(bf16[12,48,128]{2,1,0:T(8,128)(2,1)S(1)} %get-tuple-element.89.value.earlier), channel_id=1, source_target_pairs={{0,1},{2,3},{4,5},{6,7},{1,0},{3,2},{5,4},{7,6},{8,9},{10,11},{12,... | collective-permute-start | bytes 442376 | tf_op jit(solution)/shard_map/while/body/eval_jaxpr/ppermute | solution.py:194
  126.5 7.7 %collective-permute-start = (bf16[12,48,128]{2,1,0:T(8,128)(2,1)S(1)}, bf16[12,48,128]{2,1,0:T(8,128)(2,1)S(1)}, u32[]{:S(2)}, u32[]{:S(2)}) collective-permute-start(bf16[12,48,128]{2,1,0:T(8,128)(2,1)S(1)} %get-tuple-element.89.value.earlier), channel_id=1, source_target_pairs={{8,16},{24,32},{40,48},{56,64},{72,80},{88,96},{104,112},{120,128}... | collective-permute-start | bytes 442376 | tf_op jit(solution)/shard_map/while/body/eval_jaxpr/ppermute | solution.py:197
  128.7 5.6 %collective-permute-start.1 = (bf16[12,48,128]{2,1,0:T(8,128)(2,1)S(1)}, bf16[12,48,128]{2,1,0:T(8,128)(2,1)S(1)}, u32[]{:S(2)}, u32[]{:S(2)}) collective-permute-start(bf16[12,48,128]{2,1,0:T(8,128)(2,1)S(1)} %get-tuple-element.89.value.earlier), channel_id=1, source_target_pairs={{0,8},{16,24},{32,40},{48,56},{64,72},{80,88},{96,104},{112,120},{... | collective-permute-start | bytes 442376 | tf_op jit(solution)/shard_map/while/body/eval_jaxpr/ppermute | solution.py:196
  128.7 6.4 %collective-permute-start.2 = (bf16[12,48,128]{2,1,0:T(8,128)(2,1)S(1)}, bf16[12,48,128]{2,1,0:T(8,128)(2,1)S(1)}, u32[]{:S(2)}, u32[]{:S(2)}) collective-permute-start(bf16[12,48,128]{2,1,0:T(8,128)(2,1)S(1)} %get-tuple-element.89.value.earlier), channel_id=1, source_target_pairs={{1,2},{3,4},{5,6},{7,0},{2,1},{4,3},{6,5},{0,7},{9,10},{11,12},{13... | collective-permute-start | bytes 442376 | tf_op jit(solution)/shard_map/while/body/eval_jaxpr/ppermute | solution.py:195
  132.0 3.1 %collective-permute-start.3 = (bf16[12,48,128]{2,1,0:T(8,128)(2,1)S(1)}, bf16[12,48,128]{2,1,0:T(8,128)(2,1)S(1)}, u32[]{:S(2)}, u32[]{:S(2)}) collective-permute-start(bf16[12,48,128]{2,1,0:T(8,128)(2,1)S(1)} %get-tuple-element.89.value.earlier), channel_id=1, source_target_pairs={{0,1},{2,3},{4,5},{6,7},{1,0},{3,2},{5,4},{7,6},{8,9},{10,11},{12,... | collective-permute-start | bytes 442376 | tf_op jit(solution)/shard_map/while/body/eval_jaxpr/ppermute | solution.py:194
  135.5 7.7 %collective-permute-start = (bf16[12,48,128]{2,1,0:T(8,128)(2,1)S(1)}, bf16[12,48,128]{2,1,0:T(8,128)(2,1)S(1)}, u32[]{:S(2)}, u32[]{:S(2)}) collective-permute-start(bf16[12,48,128]{2,1,0:T(8,128)(2,1)S(1)} %get-tuple-element.89.value.earlier), channel_id=1, source_target_pairs={{8,16},{24,32},{40,48},{56,64},{72,80},{88,96},{104,112},{120,128}... | collective-permute-start | bytes 442376 | tf_op jit(solution)/shard_map/while/body/eval_jaxpr/ppermute | solution.py:197
  137.7 5.5 %collective-permute-start.1 = (bf16[12,48,128]{2,1,0:T(8,128)(2,1)S(1)}, bf16[12,48,128]{2,1,0:T(8,128)(2,1)S(1)}, u32[]{:S(2)}, u32[]{:S(2)}) collective-permute-start(bf16[12,48,128]{2,1,0:T(8,128)(2,1)S(1)} %get-tuple-element.89.value.earlier), channel_id=1, source_target_pairs={{0,8},{16,24},{32,40},{48,56},{64,72},{80,88},{96,104},{112,120},{... | collective-permute-start | bytes 442376 | tf_op jit(solution)/shard_map/while/body/eval_jaxpr/ppermute | solution.py:196
  137.7 6.4 %collective-permute-start.2 = (bf16[12,48,128]{2,1,0:T(8,128)(2,1)S(1)}, bf16[12,48,128]{2,1,0:T(8,128)(2,1)S(1)}, u32[]{:S(2)}, u32[]{:S(2)}) collective-permute-start(bf16[12,48,128]{2,1,0:T(8,128)(2,1)S(1)} %get-tuple-element.89.value.earlier), channel_id=1, source_target_pairs={{1,2},{3,4},{5,6},{7,0},{2,1},{4,3},{6,5},{0,7},{9,10},{11,12},{13... | collective-permute-start | bytes 442376 | tf_op jit(solution)/shard_map/while/body/eval_jaxpr/ppermute | solution.py:195
  141.0 3.1 %collective-permute-start.3 = (bf16[12,48,128]{2,1,0:T(8,128)(2,1)S(1)}, bf16[12,48,128]{2,1,0:T(8,128)(2,1)S(1)}, u32[]{:S(2)}, u32[]{:S(2)}) collective-permute-start(bf16[12,48,128]{2,1,0:T(8,128)(2,1)S(1)} %get-tuple-element.89.value.earlier), channel_id=1, source_target_pairs={{0,1},{2,3},{4,5},{6,7},{1,0},{3,2},{5,4},{7,6},{8,9},{10,11},{12,... | collective-permute-start | bytes 442376 | tf_op jit(solution)/shard_map/while/body/eval_jaxpr/ppermute | solution.py:194
  144.5 10.8 %collective-permute-start.8 = (bf16[12,48,128]{2,1,0:T(8,128)(2,1)S(1)}, bf16[12,48,128]{2,1,0:T(8,128)(2,1)S(1)}, u32[]{:S(2)}, u32[]{:S(2)}) collective-permute-start(bf16[12,48,128]{2,1,0:T(8,128)(2,1)S(1)} %get-tuple-element.38.value.earlier), channel_id=1, source_target_pairs={{8,16},{24,32},{40,48},{56,64},{72,80},{88,96},{104,112},{120,128}... | collective-permute-start | bytes 442376 | tf_op jit(solution)/shard_map/ppermute | solution.py:197
  146.7 8.6 %collective-permute-start.9 = (bf16[12,48,128]{2,1,0:T(8,128)(2,1)S(1)}, bf16[12,48,128]{2,1,0:T(8,128)(2,1)S(1)}, u32[]{:S(2)}, u32[]{:S(2)}) collective-permute-start(bf16[12,48,128]{2,1,0:T(8,128)(2,1)S(1)} %get-tuple-element.38.value.earlier), channel_id=1, source_target_pairs={{0,8},{16,24},{32,40},{48,56},{64,72},{80,88},{96,104},{112,120},{... | collective-permute-start | bytes 442376 | tf_op jit(solution)/shard_map/ppermute | solution.py:196
  146.7 8.6 %collective-permute-start.10 = (bf16[12,48,128]{2,1,0:T(8,128)(2,1)S(1)}, bf16[12,48,128]{2,1,0:T(8,128)(2,1)S(1)}, u32[]{:S(2)}, u32[]{:S(2)}) collective-permute-start(bf16[12,48,128]{2,1,0:T(8,128)(2,1)S(1)} %get-tuple-element.38.value.earlier), channel_id=1, source_target_pairs={{1,2},{3,4},{5,6},{7,0},{2,1},{4,3},{6,5},{0,7},{9,10},{11,12},{13... | collective-permute-start | bytes 442376 | tf_op jit(solution)/shard_map/ppermute | solution.py:195
  149.9 5.4 %collective-permute-start.11 = (bf16[12,48,128]{2,1,0:T(8,128)(2,1)S(1)}, bf16[12,48,128]{2,1,0:T(8,128)(2,1)S(1)}, u32[]{:S(2)}, u32[]{:S(2)}) collective-permute-start(bf16[12,48,128]{2,1,0:T(8,128)(2,1)S(1)} %get-tuple-element.38.value.earlier), channel_id=1, source_target_pairs={{0,1},{2,3},{4,5},{6,7},{1,0},{3,2},{5,4},{7,6},{8,9},{10,11},{12,... | collective-permute-start | bytes 442376 | tf_op jit(solution)/shard_map/ppermute | solution.py:194

commit v2 on v1

--- a/solution.py
+++ b/solution.py
@@ -8,6 +8,7 @@
 from jax.sharding import PartitionSpec as P
 
 ITERS = 16
+KEPT = 1
 LIMIT = 16 * 2**20
 VMEM = pl.BlockSpec(memory_space=pltpu.VMEM)
 HBM = pl.BlockSpec(memory_space=pltpu.HBM)
@@ -56,53 +57,66 @@
         )
         for c in copies[-1]:
             c.start()
-    for s in range(sites):
-        for c in copies[s]:
-            c.wait()
-        rhs[s] = dot(buffer[s], held[s]).astype(rhs.dtype)
+    for first in range(0, sites, 2):
+        pair = range(first, min(first + 2, sites))
+        for s in pair:
+            for c in copies[s]:
+                c.wait()
+        for s in pair:
+            rhs[s] = dot(buffer[s], held[s]).astype(rhs.dtype)
 
 
 def fetch_rows(ny, nx, links, buffer, sems):
     copies = []
     for y in range(ny):
         row = pl.ds(y * nx, nx)
-        copies.append(pltpu.make_async_copy(links.at[:5, row], buffer.at[:, row], sems.at[y]))
+        copies.append(pltpu.make_async_copy(links.at[KEPT:5, row], buffer.at[:, row], sems.at[y]))
         copies[-1].start()
     return copies
 
 
-def local_rows(ny, nx, rhs, value, buffer, out, copies):
+def local_rows(ny, nx, rhs, value, kept, buffer, out, copies):
+    def near(s):
+        y, x = divmod(s, nx)
+        return [
+            s,
+            y * nx + (x + 1) % nx,
+            y * nx + (x - 1) % nx,
+            (y + 1) % ny * nx + x,
+            (y - 1) % ny * nx + x,
+        ]
+
+    for s in range(ny * nx):
+        lhs = jnp.concatenate([value[n] for n in near(s)[:KEPT]], 1)
+        out[s] = rhs[s].astype(jnp.float32) - dot(lhs, kept[s])
     for y in range(ny):
         copies[y].wait()
-        for x in range(nx):
-            s = y * nx + x
-            near = [
-                s,
-                y * nx + (x + 1) % nx,
-                y * nx + (x - 1) % nx,
-                (y + 1) % ny * nx + x,
-                (y - 1) % ny * nx + x,
-            ]
-            lhs = jnp.concatenate([value[n] for n in near], 1)
-            rows = jnp.concatenate([buffer[d, s] for d in range(5)], 1)
-            out[s] = rhs[s].astype(jnp.float32) - dot(lhs, rows, NT)
-
-
-def local_kernel(ny, nx, rhs, value, links, out, buffer, sems):
+        for s in range(y * nx, (y + 1) * nx):
+            lhs = jnp.concatenate([value[n] for n in near(s)[KEPT:]], 1)
+            rows = jnp.concatenate([buffer[d, s] for d in range(5 - KEPT)], 1)
+            out[s] = out[s] - dot(lhs, rows, NT)
+
+
+def local_kernel(ny, nx, rhs, value, kept, links, out, buffer, sems):
     copies = fetch_rows(ny, nx, links, buffer, sems)
-    local_rows(ny, nx, rhs, value, buffer, out, copies)
-
-
-def first_kernel(ny, nx, slots, rhs, links, out, remote, buffer, sems, others, other_sems):
+    local_rows(ny, nx, rhs, value, kept, buffer, out, copies)
+
+
+def first_kernel(ny, nx, slots, rhs, links, out, remote, kept, buffer, sems, others, other_sems):
     sites, _, wide = remote.shape
     copies = fetch_rows(ny, nx, links, buffer, sems)
 
     def fetch(i):
-        return pltpu.make_async_copy(links.at[slots[i]], others.at[i], other_sems.at[i])
-
-    for i in range(4):
+        source = slots[i] if i < 4 else i - 4
+        return pltpu.make_async_copy(links.at[source], others.at[i], other_sems.at[i])
+
+    for i in reversed(range(4 + KEPT)):
         fetch(i).start()
-    local_rows(ny, nx, rhs, rhs, buffer, out, copies)
+    for i in range(KEPT):
+        fetch(4 + i).wait()
+        for s in range(sites):
+            kept[s, i * wide : (i + 1) * wide, :] = others[4 + i, s].T
+    local_rows(ny, nx, rhs, rhs, kept, buffer, out, copies)
     for i in range(4):
         fetch(i).wait()
         for s in range(sites):
@@ -113,7 +127,7 @@
         remote[:, :wide, :] = -remote[:, :wide, :]
 
 
-def last_kernel(ny, nx, rhs, value, links, prolongator, out, turned, buffer, sems, held, held_sems):
+def last_kernel(ny, nx, rhs, value, kept, links, prolongator, out, turned, buffer, sems, held, held_sems):
     copies = fetch_rows(ny, nx, links, buffer, sems)
     sites = held.shape[0]
 
@@ -122,7 +136,7 @@
 
     for s in range(sites):
         fetch(s).start()
-    local_rows(ny, nx, rhs, value, buffer, out, copies)
+    local_rows(ny, nx, rhs, value, kept, buffer, out, copies)
 
     def turn(s, _):
         fetch(s).wait()
@@ -186,7 +200,7 @@
         jnp.int32
     )
     local_scratch = [
-        pltpu.VMEM((5, *links.shape[1:]), links.dtype),
+        pltpu.VMEM((5 - KEPT, *links.shape[1:]), links.dtype),
         pltpu.SemaphoreType.DMA((ny,)),
     ]
 
@@ -210,14 +224,18 @@
         return value
 
     arrivals = swaps(rhs)
-    part, remote_weights = call(
+    part, remote_weights, kept = call(
         functools.partial(first_kernel, ny, nx),
         [slots, rhs, links],
-        [shape(field, jnp.float32), shape((sites, 4 * wide, wide))],
+        [
+            shape(field, jnp.float32),
+            shape((sites, 4 * wide, wide)),
+            shape((sites, KEPT * wide, wide)),
+        ],
         [
             *local_scratch,
-            pltpu.VMEM((4, *links.shape[1:]), links.dtype),
-            pltpu.SemaphoreType.DMA((4,)),
+            pltpu.VMEM((4 + KEPT, *links.shape[1:]), links.dtype),
+            pltpu.SemaphoreType.DMA((4 + KEPT,)),
         ],
         in_specs=[SMEM, VMEM, HBM],
         flops=5 * flops,
@@ -228,10 +246,10 @@
         arrivals = swaps(value)
         (part,) = call(
             functools.partial(local_kernel, ny, nx),
-            [rhs, value, links],
+            [rhs, value, kept, links],
             [shape(field, jnp.float32)],
             local_scratch,
-            in_specs=[VMEM, VMEM, HBM],
+            in_specs=[VMEM, VMEM, VMEM, HBM],
             flops=5 * flops,
         )
         return finish(value, part, arrivals, remote_weights)
@@ -240,14 +258,14 @@
     arrivals = swaps(value)
     part, turned = call(
         functools.partial(last_kernel, ny, nx),
-        [rhs, value, links, prolong],
+        [rhs, value, kept, links, prolong],
         [shape(field, jnp.float32), shape((sites, wide, fine))],
         [
             *local_scratch,
             pltpu.VMEM(prolong.shape, prolong.dtype),
             pltpu.SemaphoreType.DMA((sites,)),
         ],
-        in_specs=[VMEM, VMEM, HBM, HBM],
+        in_specs=[VMEM, VMEM, VMEM, HBM, HBM],
         flops=5 * flops,
     )
     value = finish(value, part, arrivals, remote_weights)

time: 158 us -> 157 us (level)
  Pallas kernels: 51.4 us -> 46.7 us
  waiting for transfers between devices: 13.4 us -> 17.1 us
    pallas_call x82, Pallas kernels: 51.4 us -> 46.7 us  [call(): pl.pallas_call(kernel, in_specs=in_specs, out_specs=out_specs, out_shape=...]
    ppermute x16, waiting for transfers between devices: 10 us -> 13.3 us  [swaps(): z_far = lax.ppermute(value, 'gz', swap(nz, 1))]
  transfers between devices with their start and end apart: 64 -> 64, of which waited for: 15 -> 15; matrix products, arithmetic and copies ran while one was open for 0% -> 0% of each run, Pallas kernels for 26% -> 23%
where the time goes in v2:
time: 157 us
  starting transfers between devices  91.7 us (58%)
  Pallas kernels  46.7 us (30%)
  waiting for transfers between devices  17.1 us (11%)
    ppermute x16, starting transfers between devices, swaps(): z_far = lax.ppermute(value, 'gz', swap(nz, 1))  51.6 us
    pallas_call x82, Pallas kernels, call(): pl.pallas_call(kernel, in_specs=in_specs, out_specs=out_specs, out_shape=...  46.7 us
    ppermute x16, starting transfers between devices, swaps(): t_far = lax.ppermute(value, 'ta', swap(nt, 1))  39.1 us
    ppermute x16, waiting for transfers between devices, swaps(): z_far = lax.ppermute(value, 'gz', swap(nz, 1))  13.3 us
    ppermute x16, waiting for transfers between devices, swaps(): t_far = lax.ppermute(value, 'ta', swap(nt, 1))  3.66 us
  transfers between devices with their start and end apart: 64, of which 15 were waited for; matrix products, arithmetic and copies ran while one was open for 0% of the time, Pallas kernels for 23%

profile of v2, /device:TPU:1, one launch (start us, length us, event | category | flops | bytes accessed | tf_op | source)
XLA Modules:
  0.0 156.6 jit_solution(7538099253602360509)
XLA Ops:
  0.0 3.3 %shard_map.37.rhs.earlier = bf16[12,48,128]{2,1,0:T(8,128)(2,1)S(1)} custom-call(bf16[12,48,1536]{2,1,0:T(8,128)(2,1)} %bitcast.13, bf16[12,1536,128]{2,1,0:T(8,128)(2,1)} %bitcast.11), custom_call_target="tpu_custom_call" | custom-call | tf_op jit(solution)/shard_map/pallas_call | solution.py:27
  3.3 8.9 %collective-permute-start.4 = (bf16[12,48,128]{2,1,0:T(8,128)(2,1)S(1)}, bf16[12,48,128]{2,1,0:T(8,128)(2,1)S(1)}, u32[]{:S(2)}, u32[]{:S(2)}) collective-permute-start(bf16[12,48,128]{2,1,0:T(8,128)(2,1)S(1)} %shard_map.37.rhs.earlier), channel_id=1, source_target_pairs={{8,16},{24,32},{40,48},{56,64},{72,80},{88,96},{104,112},{120,128}... | collective-permute-start | bytes 442376 | tf_op jit(solution)/shard_map/ppermute | solution.py:211
  12.3 2.0 %collective-permute-start.6 = (bf16[12,48,128]{2,1,0:T(8,128)(2,1)S(1)}, bf16[12,48,128]{2,1,0:T(8,128)(2,1)S(1)}, u32[]{:S(2)}, u32[]{:S(2)}) collective-permute-start(bf16[12,48,128]{2,1,0:T(8,128)(2,1)S(1)} %shard_map.37.rhs.earlier), channel_id=1, source_target_pairs={{1,2},{3,4},{5,6},{7,0},{2,1},{4,3},{6,5},{0,7},{9,10},{11,12},{13... | collective-permute-start | bytes 442376 | tf_op jit(solution)/shard_map/ppermute | solution.py:209
  15.2 3.5 %shard_map.38 = (f32[12,48,128]{2,1,0:T(8,128)S(1)}, bf16[12,512,128]{2,1,0:T(8,128)(2,1)S(1)}, bf16[12,128,128]{2,1,0:T(8,128)(2,1)S(1)}) custom-call(s32[5]{0:T(128)S(1)} %stack.23.slots, bf16[12,48,128]{2,1,0:T(8,128)(2,1)S(1)} %shard_map.37.rhs.earlier, bf16[9,12,128,128]{3,2,1,0:T(8,128)(2,1)} %bitcast.9), custom_call_target="tpu_custom_call" | custom-call | flops 94371840 | tf_op jit(solution)/shard_map/pallas_call | solution.py:27
  19.2 124.9 %while.10 = (s32[]{:T(128)}, bf16[12,48,128]{2,1,0:T(8,128)(2,1)S(1)}, bf16[12,48,128]{2,1,0:T(8,128)(2,1)S(1)}, bf16[12,128,128]{2,1,0:T(8,128)(2,1)S(1)}, bf16...) while((s32[]{:T(128)}, bf16[12,48,128]{2,1,0:T(8,128)(2,1)S(1)}, ...), condition=%wide.region_1.2_spmd, body=%wide.region_0.1_spmd.sunk | while | flops 169869312 | bytes 2359533 | solution.py:257
  19.2 1.6 %collective-permute-start = (bf16[12,48,128]{2,1,0:T(8,128)(2,1)S(1)}, bf16[12,48,128]{2,1,0:T(8,128)(2,1)S(1)}, u32[]{:S(2)}, u32[]{:S(2)}) collective-permute-start(bf16[12,48,128]{2,1,0:T(8,128)(2,1)S(1)} %get-tuple-element.105.value.earlier), channel_id=1, source_target_pairs={{8,16},{24,32},{40,48},{56,64},{72,80},{88,96},{104,112},{120,128}... | collective-permute-start | bytes 442376 | tf_op jit(solution)/shard_map/while/body/eval_jaxpr/ppermute | solution.py:211
  20.8 2.9 %collective-permute-start.2 = (bf16[12,48,128]{2,1,0:T(8,128)(2,1)S(1)}, bf16[12,48,128]{2,1,0:T(8,128)(2,1)S(1)}, u32[]{:S(2)}, u32[]{:S(2)}) collective-permute-start(bf16[12,48,128]{2,1,0:T(8,128)(2,1)S(1)} %get-tuple-element.105.value.earlier), channel_id=1, source_target_pairs={{1,2},{3,4},{5,6},{7,0},{2,1},{4,3},{6,5},{0,7},{9,10},{11,12},{13... | collective-permute-start | bytes 442376 | tf_op jit(solution)/shard_map/while/body/eval_jaxpr/ppermute | solution.py:209
  23.8 1.9 %eval_jaxpr.5.part = f32[12,48,128]{2,1,0:T(8,128)S(1)} custom-call(bf16[12,48,128]{2,1,0:T(8,128)(2,1)S(1)} %get-tuple-element.113.rhs, bf16[12,48,128]{2,1,0:T(8,128)(2,1)S(1)} %get-tuple-element.105.value.earlier, bf16[12,128,128]{2,1,0:T(8,128)(2,1)S(1)} %get-tuple-element.114.kept, bf16[9,12,128,128]{3,2,1,0:T(8,128)(2,1)} %get-tuple-element.115.links), custom_call_target="tpu_custom_call" | custom-call | flops 94371840 | tf_op jit(solution)/shard_map/while/body/eval_jaxpr/pallas_call | solution.py:27
  25.7 2.1 %collective-permute-done.arrived.a = bf16[12,48,128]{2,1,0:T(8,128)(2,1)S(1)} collective-permute-done((bf16[12,48,128]{2,1,0:T(8,128)(2,1)S(1)}, bf16[12,48,128]{2,1,0:T(8,128)(2,1)S(1)}, u32[]{:S(2)}, u32[]{:S(2)}) %collective-permute-start) | collective-permute-done | bytes 147488 | tf_op jit(solution)/shard_map/while/body/eval_jaxpr/ppermute | solution.py:211
  28.3 1.2 collective-permute-start
  29.5 3.2 %collective-permute-start.2 = (bf16[12,48,128]{2,1,0:T(8,128)(2,1)S(1)}, bf16[12,48,128]{2,1,0:T(8,128)(2,1)S(1)}, u32[]{:S(2)}, u32[]{:S(2)}) collective-permute-start(bf16[12,48,128]{2,1,0:T(8,128)(2,1)S(1)} %get-tuple-element.105.value.earlier), channel_id=1, source_target_pairs={{1,2},{3,4},{5,6},{7,0},{2,1},{4,3},{6,5},{0,7},{9,10},{11,12},{13... | collective-permute-start | bytes 442376 | tf_op jit(solution)/shard_map/while/body/eval_jaxpr/ppermute | solution.py:209
  32.8 1.9 %eval_jaxpr.5.part = f32[12,48,128]{2,1,0:T(8,128)S(1)} custom-call(bf16[12,48,128]{2,1,0:T(8,128)(2,1)S(1)} %get-tuple-element.113.rhs, bf16[12,48,128]{2,1,0:T(8,128)(2,1)S(1)} %get-tuple-element.105.value.earlier, bf16[12,128,128]{2,1,0:T(8,128)(2,1)S(1)} %get-tuple-element.114.kept, bf16[9,12,128,128]{3,2,1,0:T(8,128)(2,1)} %get-tuple-element.115.links), custom_call_target="tpu_custom_call" | custom-call | flops 94371840 | tf_op jit(solution)/shard_map/while/body/eval_jaxpr/pallas_call | solution.py:27
  34.7 1.3 collective-permute-done.arrived.a
  36.5 2.1 %collective-permute-start = (bf16[12,48,128]{2,1,0:T(8,128)(2,1)S(1)}, bf16[12,48,128]{2,1,0:T(8,128)(2,1)S(1)}, u32[]{:S(2)}, u32[]{:S(2)}) collective-permute-start(bf16[12,48,128]{2,1,0:T(8,128)(2,1)S(1)} %get-tuple-element.105.value.earlier), channel_id=1, source_target_pairs={{8,16},{24,32},{40,48},{56,64},{72,80},{88,96},{104,112},{120,128}... | collective-permute-start | bytes 442376 | tf_op jit(solution)/shard_map/while/body/eval_jaxpr/ppermute | solution.py:211
  38.5 3.2 %collective-permute-start.2 = (bf16[12,48,128]{2,1,0:T(8,128)(2,1)S(1)}, bf16[12,48,128]{2,1,0:T(8,128)(2,1)S(1)}, u32[]{:S(2)}, u32[]{:S(2)}) collective-permute-start(bf16[12,48,128]{2,1,0:T(8,128)(2,1)S(1)} %get-tuple-element.105.value.earlier), channel_id=1, source_target_pairs={{1,2},{3,4},{5,6},{7,0},{2,1},{4,3},{6,5},{0,7},{9,10},{11,12},{13... | collective-permute-start | bytes 442376 | tf_op jit(solution)/shard_map/while/body/eval_jaxpr/ppermute | solution.py:209
  41.7 1.9 %eval_jaxpr.5.part = f32[12,48,128]{2,1,0:T(8,128)S(1)} custom-call(bf16[12,48,128]{2,1,0:T(8,128)(2,1)S(1)} %get-tuple-element.113.rhs, bf16[12,48,128]{2,1,0:T(8,128)(2,1)S(1)} %get-tuple-element.105.value.earlier, bf16[12,128,128]{2,1,0:T(8,128)(2,1)S(1)} %get-tuple-element.114.kept, bf16[9,12,128,128]{3,2,1,0:T(8,128)(2,1)} %get-tuple-element.115.links), custom_call_target="tpu_custom_call" | custom-call | flops 94371840 | tf_op jit(solution)/shard_map/while/body/eval_jaxpr/pallas_call | solution.py:27
  45.3 2.1 %collective-permute-start = (bf16[12,48,128]{2,1,0:T(8,128)(2,1)S(1)}, bf16[12,48,128]{2,1,0:T(8,128)(2,1)S(1)}, u32[]{:S(2)}, u32[]{:S(2)}) collective-permute-start(bf16[12,48,128]{2,1,0:T(8,128)(2,1)S(1)} %get-tuple-element.105.value.earlier), channel_id=1, source_target_pairs={{8,16},{24,32},{40,48},{56,64},{72,80},{88,96},{104,112},{120,128}... | collective-permute-start | bytes 442376 | tf_op jit(solution)/shard_map/while/body/eval_jaxpr/ppermute | solution.py:211
  47.4 3.4 %collective-permute-start.2 = (bf16[12,48,128]{2,1,0:T(8,128)(2,1)S(1)}, bf16[12,48,128]{2,1,0:T(8,128)(2,1)S(1)}, u32[]{:S(2)}, u32[]{:S(2)}) collective-permute-start(bf16[12,48,128]{2,1,0:T(8,128)(2,1)S(1)} %get-tuple-element.105.value.earlier), channel_id=1, source_target_pairs={{1,2},{3,4},{5,6},{7,0},{2,1},{4,3},{6,5},{0,7},{9,10},{11,12},{13... | collective-permute-start | bytes 442376 | tf_op jit(solution)/shard_map/while/body/eval_jaxpr/ppermute | solution.py:209
  50.7 1.9 %eval_jaxpr.5.part = f32[12,48,128]{2,1,0:T(8,128)S(1)} custom-call(bf16[12,48,128]{2,1,0:T(8,128)(2,1)S(1)} %get-tuple-element.113.rhs, bf16[12,48,128]{2,1,0:T(8,128)(2,1)S(1)} %get-tuple-element.105.value.earlier, bf16[12,128,128]{2,1,0:T(8,128)(2,1)S(1)} %get-tuple-element.114.kept, bf16[9,12,128,128]{3,2,1,0:T(8,128)(2,1)} %get-tuple-element.115.links), custom_call_target="tpu_custom_call" | custom-call | flops 94371840 | tf_op jit(solution)/shard_map/while/body/eval_jaxpr/pallas_call | solution.py:27
  52.7 1.1 collective-permute-done.2.arrived.c
  54.2 2.1 %collective-permute-start = (bf16[12,48,128]{2,1,0:T(8,128)(2,1)S(1)}, bf16[12,48,128]{2,1,0:T(8,128)(2,1)S(1)}, u32[]{:S(2)}, u32[]{:S(2)}) collective-permute-start(bf16[12,48,128]{2,1,0:T(8,128)(2,1)S(1)} %get-tuple-element.105.value.earlier), channel_id=1, source_target_pairs={{8,16},{24,32},{40,48},{56,64},{72,80},{88,96},{104,112},{120,128}... | collective-permute-start | bytes 442376 | tf_op jit(solution)/shard_map/while/body/eval_jaxpr/ppermute | solution.py:211
  56.3 3.4 %collective-permute-start.2 = (bf16[12,48,128]{2,1,0:T(8,128)(2,1)S(1)}, bf16[12,48,128]{2,1,0:T(8,128)(2,1)S(1)}, u32[]{:S(2)}, u32[]{:S(2)}) collective-permute-start(bf16[12,48,128]{2,1,0:T(8,128)(2,1)S(1)} %get-tuple-element.105.value.earlier), channel_id=1, source_target_pairs={{1,2},{3,4},{5,6},{7,0},{2,1},{4,3},{6,5},{0,7},{9,10},{11,12},{13... | collective-permute-start | bytes 442376 | tf_op jit(solution)/shard_map/while/body/eval_jaxpr/ppermute | solution.py:209
  59.7 1.9 %eval_jaxpr.5.part = f32[12,48,128]{2,1,0:T(8,128)S(1)} custom-call(bf16[12,48,128]{2,1,0:T(8,128)(2,1)S(1)} %get-tuple-element.113.rhs, bf16[12,48,128]{2,1,0:T(8,128)(2,1)S(1)} %get-tuple-element.105.value.earlier, bf16[12,128,128]{2,1,0:T(8,128)(2,1)S(1)} %get-tuple-element.114.kept, bf16[9,12,128,128]{3,2,1,0:T(8,128)(2,1)} %get-tuple-element.115.links), custom_call_target="tpu_custom_call" | custom-call | flops 94371840 | tf_op jit(solution)/shard_map/while/body/eval_jaxpr/pallas_call | solution.py:27
  61.7 1.1 collective-permute-done.2.arrived.c
  63.2 2.1 %collective-permute-start = (bf16[12,48,128]{2,1,0:T(8,128)(2,1)S(1)}, bf16[12,48,128]{2,1,0:T(8,128)(2,1)S(1)}, u32[]{:S(2)}, u32[]{:S(2)}) collective-permute-start(bf16[12,48,128]{2,1,0:T(8,128)(2,1)S(1)} %get-tuple-element.105.value.earlier), channel_id=1, source_target_pairs={{8,16},{24,32},{40,48},{56,64},{72,80},{88,96},{104,112},{120,128}... | collective-permute-start | bytes 442376 | tf_op jit(solution)/shard_map/while/body/eval_jaxpr/ppermute | solution.py:211
  65.3 3.4 %collective-permute-start.2 = (bf16[12,48,128]{2,1,0:T(8,128)(2,1)S(1)}, bf16[12,48,128]{2,1,0:T(8,128)(2,1)S(1)}, u32[]{:S(2)}, u32[]{:S(2)}) collective-permute-start(bf16[12,48,128]{2,1,0:T(8,128)(2,1)S(1)} %get-tuple-element.105.value.earlier), channel_id=1, source_target_pairs={{1,2},{3,4},{5,6},{7,0},{2,1},{4,3},{6,5},{0,7},{9,10},{11,12},{13... | collective-permute-start | bytes 442376 | tf_op jit(solution)/shard_map/while/body/eval_jaxpr/ppermute | solution.py:209
  68.7 1.9 %eval_jaxpr.5.part = f32[12,48,128]{2,1,0:T(8,128)S(1)} custom-call(bf16[12,48,128]{2,1,0:T(8,128)(2,1)S(1)} %get-tuple-element.113.rhs, bf16[12,48,128]{2,1,0:T(8,128)(2,1)S(1)} %get-tuple-element.105.value.earlier, bf16[12,128,128]{2,1,0:T(8,128)(2,1)S(1)} %get-tuple-element.114.kept, bf16[9,12,128,128]{3,2,1,0:T(8,128)(2,1)} %get-tuple-element.115.links), custom_call_target="tpu_custom_call" | custom-call | flops 94371840 | tf_op jit(solution)/shard_map/while/body/eval_jaxpr/pallas_call | solution.py:27
  70.7 1.1 collective-permute-done.2.arrived.c
  72.2 2.1 %collective-permute-start = (bf16[12,48,128]{2,1,0:T(8,128)(2,1)S(1)}, bf16[12,48,128]{2,1,0:T(8,128)(2,1)S(1)}, u32[]{:S(2)}, u32[]{:S(2)}) collective-permute-start(bf16[12,48,128]{2,1,0:T(8,128)(2,1)S(1)} %get-tuple-element.105.value.earlier), channel_id=1, source_target_pairs={{8,16},{24,32},{40,48},{56,64},{72,80},{88,96},{104,112},{120,128}... | collective-permute-start | bytes 442376 | tf_op jit(solution)/shard_map/while/body/eval_jaxpr/ppermute | solution.py:211
  74.3 3.4 %collective-permute-start.2 = (bf16[12,48,128]{2,1,0:T(8,128)(2,1)S(1)}, bf16[12,48,128]{2,1,0:T(8,128)(2,1)S(1)}, u32[]{:S(2)}, u32[]{:S(2)}) collective-permute-start(bf16[12,48,128]{2,1,0:T(8,128)(2,1)S(1)} %get-tuple-element.105.value.earlier), channel_id=1, source_target_pairs={{1,2},{3,4},{5,6},{7,0},{2,1},{4,3},{6,5},{0,7},{9,10},{11,12},{13... | collective-permute-start | bytes 442376 | tf_op jit(solution)/shard_map/while/body/eval_jaxpr/ppermute | solution.py:209
  77.7 1.9 %eval_jaxpr.5.part = f32[12,48,128]{2,1,0:T(8,128)S(1)} custom-call(bf16[12,48,128]{2,1,0:T(8,128)(2,1)S(1)} %get-tuple-element.113.rhs, bf16[12,48,128]{2,1,0:T(8,128)(2,1)S(1)} %get-tuple-element.105.value.earlier, bf16[12,128,128]{2,1,0:T(8,128)(2,1)S(1)} %get-tuple-element.114.kept, bf16[9,12,128,128]{3,2,1,0:T(8,128)(2,1)} %get-tuple-element.115.links), custom_call_target="tpu_custom_call" | custom-call | flops 94371840 | tf_op jit(solution)/shard_map/while/body/eval_jaxpr/pallas_call | solution.py:27
  79.7 1.1 collective-permute-done.2.arrived.c
  81.2 2.1 %collective-permute-start = (bf16[12,48,128]{2,1,0:T(8,128)(2,1)S(1)}, bf16[12,48,128]{2,1,0:T(8,128)(2,1)S(1)}, u32[]{:S(2)}, u32[]{:S(2)}) collective-permute-start(bf16[12,48,128]{2,1,0:T(8,128)(2,1)S(1)} %get-tuple-element.105.value.earlier), channel_id=1, source_target_pairs={{8,16},{24,32},{40,48},{56,64},{72,80},{88,96},{104,112},{120,128}... | collective-permute-start | bytes 442376 | tf_op jit(solution)/shard_map/while/body/eval_jaxpr/ppermute | solution.py:211
  83.3 3.4 %collective-permute-start.2 = (bf16[12,48,128]{2,1,0:T(8,128)(2,1)S(1)}, bf16[12,48,128]{2,1,0:T(8,128)(2,1)S(1)}, u32[]{:S(2)}, u32[]{:S(2)}) collective-permute-start(bf16[12,48,128]{2,1,0:T(8,128)(2,1)S(1)} %get-tuple-element.105.value.earlier), channel_id=1, source_target_pairs={{1,2},{3,4},{5,6},{7,0},{2,1},{4,3},{6,5},{0,7},{9,10},{11,12},{13... | collective-permute-start | bytes 442376 | tf_op jit(solution)/shard_map/while/body/eval_jaxpr/ppermute | solution.py:209
  86.7 1.9 %eval_jaxpr.5.part = f32[12,48,128]{2,1,0:T(8,128)S(1)} custom-call(bf16[12,48,128]{2,1,0:T(8,128)(2,1)S(1)} %get-tuple-element.113.rhs, bf16[12,48,128]{2,1,0:T(8,128)(2,1)S(1)} %get-tuple-element.105.value.earlier, bf16[12,128,128]{2,1,0:T(8,128)(2,1)S(1)} %get-tuple-element.114.kept, bf16[9,12,128,128]{3,2,1,0:T(8,128)(2,1)} %get-tuple-element.115.links), custom_call_target="tpu_custom_call" | custom-call | flops 94371840 | tf_op jit(solution)/shard_map/while/body/eval_jaxpr/pallas_call | solution.py:27
  88.7 1.1 collective-permute-done.2.arrived.c
  90.2 2.1 %collective-permute-start = (bf16[12,48,128]{2,1,0:T(8,128)(2,1)S(1)}, bf16[12,48,128]{2,1,0:T(8,128)(2,1)S(1)}, u32[]{:S(2)}, u32[]{:S(2)}) collective-permute-start(bf16[12,48,128]{2,1,0:T(8,128)(2,1)S(1)} %get-tuple-element.105.value.earlier), channel_id=1, source_target_pairs={{8,16},{24,32},{40,48},{56,64},{72,80},{88,96},{104,112},{120,128}... | collective-permute-start | bytes 442376 | tf_op jit(solution)/shard_map/while/body/eval_jaxpr/ppermute | solution.py:211
  92.3 3.4 %collective-permute-start.2 = (bf16[12,48,128]{2,1,0:T(8,128)(2,1)S(1)}, bf16[12,48,128]{2,1,0:T(8,128)(2,1)S(1)}, u32[]{:S(2)}, u32[]{:S(2)}) collective-permute-start(bf16[12,48,128]{2,1,0:T(8,128)(2,1)S(1)} %get-tuple-element.105.value.earlier), channel_id=1, source_target_pairs={{1,2},{3,4},{5,6},{7,0},{2,1},{4,3},{6,5},{0,7},{9,10},{11,12},{13... | collective-permute-start | bytes 442376 | tf_op jit(solution)/shard_map/while/body/eval_jaxpr/ppermute | solution.py:209
  95.7 1.9 %eval_jaxpr.5.part = f32[12,48,128]{2,1,0:T(8,128)S(1)} custom-call(bf16[12,48,128]{2,1,0:T(8,128)(2,1)S(1)} %get-tuple-element.113.rhs, bf16[12,48,128]{2,1,0:T(8,128)(2,1)S(1)} %get-tuple-element.105.value.earlier, bf16[12,128,128]{2,1,0:T(8,128)(2,1)S(1)} %get-tuple-element.114.kept, bf16[9,12,128,128]{3,2,1,0:T(8,128)(2,1)} %get-tuple-element.115.links), custom_call_target="tpu_custom_call" | custom-call | flops 94371840 | tf_op jit(solution)/shard_map/while/body/eval_jaxpr/pallas_call | solution.py:27
  97.7 1.1 collective-permute-done.2.arrived.c
  99.2 2.1 %collective-permute-start = (bf16[12,48,128]{2,1,0:T(8,128)(2,1)S(1)}, bf16[12,48,128]{2,1,0:T(8,128)(2,1)S(1)}, u32[]{:S(2)}, u32[]{:S(2)}) collective-permute-start(bf16[12,48,128]{2,1,0:T(8,128)(2,1)S(1)} %get-tuple-element.105.value.earlier), channel_id=1, source_target_pairs={{8,16},{24,32},{40,48},{56,64},{72,80},{88,96},{104,112},{120,128}... | collective-permute-start | bytes 442376 | tf_op jit(solution)/shard_map/while/body/eval_jaxpr/ppermute | solution.py:211
  101.3 3.4 %collective-permute-start.2 = (bf16[12,48,128]{2,1,0:T(8,128)(2,1)S(1)}, bf16[12,48,128]{2,1,0:T(8,128)(2,1)S(1)}, u32[]{:S(2)}, u32[]{:S(2)}) collective-permute-start(bf16[12,48,128]{2,1,0:T(8,128)(2,1)S(1)} %get-tuple-element.105.value.earlier), channel_id=1, source_target_pairs={{1,2},{3,4},{5,6},{7,0},{2,1},{4,3},{6,5},{0,7},{9,10},{11,12},{13... | collective-permute-start | bytes 442376 | tf_op jit(solution)/shard_map/while/body/eval_jaxpr/ppermute | solution.py:209
  104.7 1.9 %eval_jaxpr.5.part = f32[12,48,128]{2,1,0:T(8,128)S(1)} custom-call(bf16[12,48,128]{2,1,0:T(8,128)(2,1)S(1)} %get-tuple-element.113.rhs, bf16[12,48,128]{2,1,0:T(8,128)(2,1)S(1)} %get-tuple-element.105.value.earlier, bf16[12,128,128]{2,1,0:T(8,128)(2,1)S(1)} %get-tuple-element.114.kept, bf16[9,12,128,128]{3,2,1,0:T(8,128)(2,1)} %get-tuple-element.115.links), custom_call_target="tpu_custom_call" | custom-call | flops 94371840 | tf_op jit(solution)/shard_map/while/body/eval_jaxpr/pallas_call | solution.py:27
  106.6 1.1 collective-permute-done.2.arrived.c
  108.2 2.1 %collective-permute-start = (bf16[12,48,128]{2,1,0:T(8,128)(2,1)S(1)}, bf16[12,48,128]{2,1,0:T(8,128)(2,1)S(1)}, u32[]{:S(2)}, u32[]{:S(2)}) collective-permute-start(bf16[12,48,128]{2,1,0:T(8,128)(2,1)S(1)} %get-tuple-element.105.value.earlier), channel_id=1, source_target_pairs={{8,16},{24,32},{40,48},{56,64},{72,80},{88,96},{104,112},{120,128}... | collective-permute-start | bytes 442376 | tf_op jit(solution)/shard_map/while/body/eval_jaxpr/ppermute | solution.py:211
  110.3 3.4 %collective-permute-start.2 = (bf16[12,48,128]{2,1,0:T(8,128)(2,1)S(1)}, bf16[12,48,128]{2,1,0:T(8,128)(2,1)S(1)}, u32[]{:S(2)}, u32[]{:S(2)}) collective-permute-start(bf16[12,48,128]{2,1,0:T(8,128)(2,1)S(1)} %get-tuple-element.105.value.earlier), channel_id=1, source_target_pairs={{1,2},{3,4},{5,6},{7,0},{2,1},{4,3},{6,5},{0,7},{9,10},{11,12},{13... | collective-permute-start | bytes 442376 | tf_op jit(solution)/shard_map/while/body/eval_jaxpr/ppermute | solution.py:209
  113.6 1.9 %eval_jaxpr.5.part = f32[12,48,128]{2,1,0:T(8,128)S(1)} custom-call(bf16[12,48,128]{2,1,0:T(8,128)(2,1)S(1)} %get-tuple-element.113.rhs, bf16[12,48,128]{2,1,0:T(8,128)(2,1)S(1)} %get-tuple-element.105.value.earlier, bf16[12,128,128]{2,1,0:T(8,128)(2,1)S(1)} %get-tuple-element.114.kept, bf16[9,12,128,128]{3,2,1,0:T(8,128)(2,1)} %get-tuple-element.115.links), custom_call_target="tpu_custom_call" | custom-call | flops 94371840 | tf_op jit(solution)/shard_map/while/body/eval_jaxpr/pallas_call | solution.py:27
  115.6 1.1 collective-permute-done.2.arrived.c
  117.2 2.1 %collective-permute-start = (bf16[12,48,128]{2,1,0:T(8,128)(2,1)S(1)}, bf16[12,48,128]{2,1,0:T(8,128)(2,1)S(1)}, u32[]{:S(2)}, u32[]{:S(2)}) collective-permute-start(bf16[12,48,128]{2,1,0:T(8,128)(2,1)S(1)} %get-tuple-element.105.value.earlier), channel_id=1, source_target_pairs={{8,16},{24,32},{40,48},{56,64},{72,80},{88,96},{104,112},{120,128}... | collective-permute-start | bytes 442376 | tf_op jit(solution)/shard_map/while/body/eval_jaxpr/ppermute | solution.py:211
  119.3 3.4 %collective-permute-start.2 = (bf16[12,48,128]{2,1,0:T(8,128)(2,1)S(1)}, bf16[12,48,128]{2,1,0:T(8,128)(2,1)S(1)}, u32[]{:S(2)}, u32[]{:S(2)}) collective-permute-start(bf16[12,48,128]{2,1,0:T(8,128)(2,1)S(1)} %get-tuple-element.105.value.earlier), channel_id=1, source_target_pairs={{1,2},{3,4},{5,6},{7,0},{2,1},{4,3},{6,5},{0,7},{9,10},{11,12},{13... | collective-permute-start | bytes 442376 | tf_op jit(solution)/shard_map/while/body/eval_jaxpr/ppermute | solution.py:209
  122.6 1.9 %eval_jaxpr.5.part = f32[12,48,128]{2,1,0:T(8,128)S(1)} custom-call(bf16[12,48,128]{2,1,0:T(8,128)(2,1)S(1)} %get-tuple-element.113.rhs, bf16[12,48,128]{2,1,0:T(8,128)(2,1)S(1)} %get-tuple-element.105.value.earlier, bf16[12,128,128]{2,1,0:T(8,128)(2,1)S(1)} %get-tuple-element.114.kept, bf16[9,12,128,128]{3,2,1,0:T(8,128)(2,1)} %get-tuple-element.115.links), custom_call_target="tpu_custom_call" | custom-call | flops 94371840 | tf_op jit(solution)/shard_map/while/body/eval_jaxpr/pallas_call | solution.py:27
  124.6 1.1 collective-permute-done.2.arrived.c
  126.2 2.1 %collective-permute-start = (bf16[12,48,128]{2,1,0:T(8,128)(2,1)S(1)}, bf16[12,48,128]{2,1,0:T(8,128)(2,1)S(1)}, u32[]{:S(2)}, u32[]{:S(2)}) collective-permute-start(bf16[12,48,128]{2,1,0:T(8,128)(2,1)S(1)} %get-tuple-element.105.value.earlier), channel_id=1, source_target_pairs={{8,16},{24,32},{40,48},{56,64},{72,80},{88,96},{104,112},{120,128}... | collective-permute-start | bytes 442376 | tf_op jit(solution)/shard_map/while/body/eval_jaxpr/ppermute | solution.py:211
  128.3 3.4 %collective-permute-start.2 = (bf16[12,48,128]{2,1,0:T(8,128)(2,1)S(1)}, bf16[12,48,128]{2,1,0:T(8,128)(2,1)S(1)}, u32[]{:S(2)}, u32[]{:S(2)}) collective-permute-start(bf16[12,48,128]{2,1,0:T(8,128)(2,1)S(1)} %get-tuple-element.105.value.earlier), channel_id=1, source_target_pairs={{1,2},{3,4},{5,6},{7,0},{2,1},{4,3},{6,5},{0,7},{9,10},{11,12},{13... | collective-permute-start | bytes 442376 | tf_op jit(solution)/shard_map/while/body/eval_jaxpr/ppermute | solution.py:209
  131.6 1.9 %eval_jaxpr.5.part = f32[12,48,128]{2,1,0:T(8,128)S(1)} custom-call(bf16[12,48,128]{2,1,0:T(8,128)(2,1)S(1)} %get-tuple-element.113.rhs, bf16[12,48,128]{2,1,0:T(8,128)(2,1)S(1)} %get-tuple-element.105.value.earlier, bf16[12,128,128]{2,1,0:T(8,128)(2,1)S(1)} %get-tuple-element.114.kept, bf16[9,12,128,128]{3,2,1,0:T(8,128)(2,1)} %get-tuple-element.115.links), custom_call_target="tpu_custom_call" | custom-call | flops 94371840 | tf_op jit(solution)/shard_map/while/body/eval_jaxpr/pallas_call | solution.py:27
  133.6 1.1 collective-permute-done.2.arrived.c
  135.1 2.1 %collective-permute-start = (bf16[12,48,128]{2,1,0:T(8,128)(2,1)S(1)}, bf16[12,48,128]{2,1,0:T(8,128)(2,1)S(1)}, u32[]{:S(2)}, u32[]{:S(2)}) collective-permute-start(bf16[12,48,128]{2,1,0:T(8,128)(2,1)S(1)} %get-tuple-element.105.value.earlier), channel_id=1, source_target_pairs={{8,16},{24,32},{40,48},{56,64},{72,80},{88,96},{104,112},{120,128}... | collective-permute-start | bytes 442376 | tf_op jit(solution)/shard_map/while/body/eval_jaxpr/ppermute | solution.py:211
  137.3 3.3 %collective-permute-start.2 = (bf16[12,48,128]{2,1,0:T(8,128)(2,1)S(1)}, bf16[12,48,128]{2,1,0:T(8,128)(2,1)S(1)}, u32[]{:S(2)}, u32[]{:S(2)}) collective-permute-start(bf16[12,48,128]{2,1,0:T(8,128)(2,1)S(1)} %get-tuple-element.105.value.earlier), channel_id=1, source_target_pairs={{1,2},{3,4},{5,6},{7,0},{2,1},{4,3},{6,5},{0,7},{9,10},{11,12},{13... | collective-permute-start | bytes 442376 | tf_op jit(solution)/shard_map/while/body/eval_jaxpr/ppermute | solution.py:209
  140.6 1.9 %eval_jaxpr.5.part = f32[12,48,128]{2,1,0:T(8,128)S(1)} custom-call(bf16[12,48,128]{2,1,0:T(8,128)(2,1)S(1)} %get-tuple-element.113.rhs, bf16[12,48,128]{2,1,0:T(8,128)(2,1)S(1)} %get-tuple-element.105.value.earlier, bf16[12,128,128]{2,1,0:T(8,128)(2,1)S(1)} %get-tuple-element.114.kept, bf16[9,12,128,128]{3,2,1,0:T(8,128)(2,1)} %get-tuple-element.115.links), custom_call_target="tpu_custom_call" | custom-call | flops 94371840 | tf_op jit(solution)/shard_map/while/body/eval_jaxpr/pallas_call | solution.py:27
  142.6 1.1 collective-permute-done.2.arrived.c
  144.1 2.1 %collective-permute-start.8 = (bf16[12,48,128]{2,1,0:T(8,128)(2,1)S(1)}, bf16[12,48,128]{2,1,0:T(8,128)(2,1)S(1)}, u32[]{:S(2)}, u32[]{:S(2)}) collective-permute-start(bf16[12,48,128]{2,1,0:T(8,128)(2,1)S(1)} %get-tuple-element.45.value.earlier), channel_id=1, source_target_pairs={{8,16},{24,32},{40,48},{56,64},{72,80},{88,96},{104,112},{120,128}... | collective-permute-start | bytes 442376 | tf_op jit(solution)/shard_map/ppermute | solution.py:211
  146.2 3.3 %collective-permute-start.10 = (bf16[12,48,128]{2,1,0:T(8,128)(2,1)S(1)}, bf16[12,48,128]{2,1,0:T(8,128)(2,1)S(1)}, u32[]{:S(2)}, u32[]{:S(2)}) collective-permute-start(bf16[12,48,128]{2,1,0:T(8,128)(2,1)S(1)} %get-tuple-element.45.value.earlier), channel_id=1, source_target_pairs={{1,2},{3,4},{5,6},{7,0},{2,1},{4,3},{6,5},{0,7},{9,10},{11,12},{13... | collective-permute-start | bytes 442376 | tf_op jit(solution)/shard_map/ppermute | solution.py:209
  149.6 5.0 %shard_map.43 = (f32[12,48,128]{2,1,0:T(8,128)S(1)}, bf16[12,128,1536]{2,1,0:T(8,128)(2,1)S(1)}) custom-call(bf16[12,48,128]{2,1,0:T(8,128)(2,1)S(1)} %get-tuple-element.135, bf16[12,48,128]{2,1,0:T(8,128)(2,1)S(1)} %get-tuple-element.45.value.earlier, bf16[12,128,128]{2,1,0:T(8,128)(2,1)S(1)} %get-tuple-element.130, ...), custom_call_target="tpu_custom_call" | custom-call | flops 94371840 | tf_op jit(solution)/shard_map/pallas_call | solution.py:27
  155.1 1.5 shard_map.48
  (148 shorter events, 8.5 us)
Async XLA Ops:
  3.3 15.4 %collective-permute-start.4 = (bf16[12,48,128]{2,1,0:T(8,128)(2,1)S(1)}, bf16[12,48,128]{2,1,0:T(8,128)(2,1)S(1)}, u32[]{:S(2)}, u32[]{:S(2)}) collective-permute-start(bf16[12,48,128]{2,1,0:T(8,128)(2,1)S(1)} %shard_map.37.rhs.earlier), channel_id=1, source_target_pairs={{8,16},{24,32},{40,48},{56,64},{72,80},{88,96},{104,112},{120,128}... | collective-permute-start | bytes 442376 | tf_op jit(solution)/shard_map/ppermute | solution.py:211
  12.3 6.5 %collective-permute-start.5 = (bf16[12,48,128]{2,1,0:T(8,128)(2,1)S(1)}, bf16[12,48,128]{2,1,0:T(8,128)(2,1)S(1)}, u32[]{:S(2)}, u32[]{:S(2)}) collective-permute-start(bf16[12,48,128]{2,1,0:T(8,128)(2,1)S(1)} %shard_map.37.rhs.earlier), channel_id=1, source_target_pairs={{0,8},{16,24},{32,40},{48,56},{64,72},{80,88},{96,104},{112,120},{... | collective-permute-start | bytes 442376 | tf_op jit(solution)/shard_map/ppermute | solution.py:210
  12.3 6.5 %collective-permute-start.6 = (bf16[12,48,128]{2,1,0:T(8,128)(2,1)S(1)}, bf16[12,48,128]{2,1,0:T(8,128)(2,1)S(1)}, u32[]{:S(2)}, u32[]{:S(2)}) collective-permute-start(bf16[12,48,128]{2,1,0:T(8,128)(2,1)S(1)} %shard_map.37.rhs.earlier), channel_id=1, source_target_pairs={{1,2},{3,4},{5,6},{7,0},{2,1},{4,3},{6,5},{0,7},{9,10},{11,12},{13... | collective-permute-start | bytes 442376 | tf_op jit(solution)/shard_map/ppermute | solution.py:209
  14.3 4.5 %collective-permute-start.7 = (bf16[12,48,128]{2,1,0:T(8,128)(2,1)S(1)}, bf16[12,48,128]{2,1,0:T(8,128)(2,1)S(1)}, u32[]{:S(2)}, u32[]{:S(2)}) collective-permute-start(bf16[12,48,128]{2,1,0:T(8,128)(2,1)S(1)} %shard_map.37.rhs.earlier), channel_id=1, source_target_pairs={{0,1},{2,3},{4,5},{6,7},{1,0},{3,2},{5,4},{7,6},{8,9},{10,11},{12,... | collective-permute-start | bytes 442376 | tf_op jit(solution)/shard_map/ppermute | solution.py:208
  19.2 8.7 %collective-permute-start = (bf16[12,48,128]{2,1,0:T(8,128)(2,1)S(1)}, bf16[12,48,128]{2,1,0:T(8,128)(2,1)S(1)}, u32[]{:S(2)}, u32[]{:S(2)}) collective-permute-start(bf16[12,48,128]{2,1,0:T(8,128)(2,1)S(1)} %get-tuple-element.105.value.earlier), channel_id=1, source_target_pairs={{8,16},{24,32},{40,48},{56,64},{72,80},{88,96},{104,112},{120,128}... | collective-permute-start | bytes 442376 | tf_op jit(solution)/shard_map/while/body/eval_jaxpr/ppermute | solution.py:211
  20.8 7.0 %collective-permute-start.1 = (bf16[12,48,128]{2,1,0:T(8,128)(2,1)S(1)}, bf16[12,48,128]{2,1,0:T(8,128)(2,1)S(1)}, u32[]{:S(2)}, u32[]{:S(2)}) collective-permute-start(bf16[12,48,128]{2,1,0:T(8,128)(2,1)S(1)} %get-tuple-element.105.value.earlier), channel_id=1, source_target_pairs={{0,8},{16,24},{32,40},{48,56},{64,72},{80,88},{96,104},{112,120},{... | collective-permute-start | bytes 442376 | tf_op jit(solution)/shard_map/while/body/eval_jaxpr/ppermute | solution.py:210
  20.8 7.0 %collective-permute-start.2 = (bf16[12,48,128]{2,1,0:T(8,128)(2,1)S(1)}, bf16[12,48,128]{2,1,0:T(8,128)(2,1)S(1)}, u32[]{:S(2)}, u32[]{:S(2)}) collective-permute-start(bf16[12,48,128]{2,1,0:T(8,128)(2,1)S(1)} %get-tuple-element.105.value.earlier), channel_id=1, source_target_pairs={{1,2},{3,4},{5,6},{7,0},{2,1},{4,3},{6,5},{0,7},{9,10},{11,12},{13... | collective-permute-start | bytes 442376 | tf_op jit(solution)/shard_map/while/body/eval_jaxpr/ppermute | solution.py:209
  23.8 4.1 %collective-permute-start.3 = (bf16[12,48,128]{2,1,0:T(8,128)(2,1)S(1)}, bf16[12,48,128]{2,1,0:T(8,128)(2,1)S(1)}, u32[]{:S(2)}, u32[]{:S(2)}) collective-permute-start(bf16[12,48,128]{2,1,0:T(8,128)(2,1)S(1)} %get-tuple-element.105.value.earlier), channel_id=1, source_target_pairs={{0,1},{2,3},{4,5},{6,7},{1,0},{3,2},{5,4},{7,6},{8,9},{10,11},{12,... | collective-permute-start | bytes 442376 | tf_op jit(solution)/shard_map/while/body/eval_jaxpr/ppermute | solution.py:208
  28.3 7.7 %collective-permute-start = (bf16[12,48,128]{2,1,0:T(8,128)(2,1)S(1)}, bf16[12,48,128]{2,1,0:T(8,128)(2,1)S(1)}, u32[]{:S(2)}, u32[]{:S(2)}) collective-permute-start(bf16[12,48,128]{2,1,0:T(8,128)(2,1)S(1)} %get-tuple-element.105.value.earlier), channel_id=1, source_target_pairs={{8,16},{24,32},{40,48},{56,64},{72,80},{88,96},{104,112},{120,128}... | collective-permute-start | bytes 442376 | tf_op jit(solution)/shard_map/while/body/eval_jaxpr/ppermute | solution.py:211
  29.5 6.5 %collective-permute-start.1 = (bf16[12,48,128]{2,1,0:T(8,128)(2,1)S(1)}, bf16[12,48,128]{2,1,0:T(8,128)(2,1)S(1)}, u32[]{:S(2)}, u32[]{:S(2)}) collective-permute-start(bf16[12,48,128]{2,1,0:T(8,128)(2,1)S(1)} %get-tuple-element.105.value.earlier), channel_id=1, source_target_pairs={{0,8},{16,24},{32,40},{48,56},{64,72},{80,88},{96,104},{112,120},{... | collective-permute-start | bytes 442376 | tf_op jit(solution)/shard_map/while/body/eval_jaxpr/ppermute | solution.py:210
  29.5 6.5 %collective-permute-start.2 = (bf16[12,48,128]{2,1,0:T(8,128)(2,1)S(1)}, bf16[12,48,128]{2,1,0:T(8,128)(2,1)S(1)}, u32[]{:S(2)}, u32[]{:S(2)}) collective-permute-start(bf16[12,48,128]{2,1,0:T(8,128)(2,1)S(1)} %get-tuple-element.105.value.earlier), channel_id=1, source_target_pairs={{1,2},{3,4},{5,6},{7,0},{2,1},{4,3},{6,5},{0,7},{9,10},{11,12},{13... | collective-permute-start | bytes 442376 | tf_op jit(solution)/shard_map/while/body/eval_jaxpr/ppermute | solution.py:209
  32.7 3.3 %collective-permute-start.3 = (bf16[12,48,128]{2,1,0:T(8,128)(2,1)S(1)}, bf16[12,48,128]{2,1,0:T(8,128)(2,1)S(1)}, u32[]{:S(2)}, u32[]{:S(2)}) collective-permute-start(bf16[12,48,128]{2,1,0:T(8,128)(2,1)S(1)} %get-tuple-element.105.value.earlier), channel_id=1, source_target_pairs={{0,1},{2,3},{4,5},{6,7},{1,0},{3,2},{5,4},{7,6},{8,9},{10,11},{12,... | collective-permute-start | bytes 442376 | tf_op jit(solution)/shard_map/while/body/eval_jaxpr/ppermute | solution.py:208
  36.5 7.4 %collective-permute-start = (bf16[12,48,128]{2,1,0:T(8,128)(2,1)S(1)}, bf16[12,48,128]{2,1,0:T(8,128)(2,1)S(1)}, u32[]{:S(2)}, u32[]{:S(2)}) collective-permute-start(bf16[12,48,128]{2,1,0:T(8,128)(2,1)S(1)} %get-tuple-element.105.value.earlier), channel_id=1, source_target_pairs={{8,16},{24,32},{40,48},{56,64},{72,80},{88,96},{104,112},{120,128}... | collective-permute-start | bytes 442376 | tf_op jit(solution)/shard_map/while/body/eval_jaxpr/ppermute | solution.py:211
  38.5 5.3 %collective-permute-start.1 = (bf16[12,48,128]{2,1,0:T(8,128)(2,1)S(1)}, bf16[12,48,128]{2,1,0:T(8,128)(2,1)S(1)}, u32[]{:S(2)}, u32[]{:S(2)}) collective-permute-start(bf16[12,48,128]{2,1,0:T(8,128)(2,1)S(1)} %get-tuple-element.105.value.earlier), channel_id=1, source_target_pairs={{0,8},{16,24},{32,40},{48,56},{64,72},{80,88},{96,104},{112,120},{... | collective-permute-start | bytes 442376 | tf_op jit(solution)/shard_map/while/body/eval_jaxpr/ppermute | solution.py:210
  38.5 6.3 %collective-permute-start.2 = (bf16[12,48,128]{2,1,0:T(8,128)(2,1)S(1)}, bf16[12,48,128]{2,1,0:T(8,128)(2,1)S(1)}, u32[]{:S(2)}, u32[]{:S(2)}) collective-permute-start(bf16[12,48,128]{2,1,0:T(8,128)(2,1)S(1)} %get-tuple-element.105.value.earlier), channel_id=1, source_target_pairs={{1,2},{3,4},{5,6},{7,0},{2,1},{4,3},{6,5},{0,7},{9,10},{11,12},{13... | collective-permute-start | bytes 442376 | tf_op jit(solution)/shard_map/while/body/eval_jaxpr/ppermute | solution.py:209
  41.7 3.1 %collective-permute-start.3 = (bf16[12,48,128]{2,1,0:T(8,128)(2,1)S(1)}, bf16[12,48,128]{2,1,0:T(8,128)(2,1)S(1)}, u32[]{:S(2)}, u32[]{:S(2)}) collective-permute-start(bf16[12,48,128]{2,1,0:T(8,128)(2,1)S(1)} %get-tuple-element.105.value.earlier), channel_id=1, source_target_pairs={{0,1},{2,3},{4,5},{6,7},{1,0},{3,2},{5,4},{7,6},{8,9},{10,11},{12,... | collective-permute-start | bytes 442376 | tf_op jit(solution)/shard_map/while/body/eval_jaxpr/ppermute | solution.py:208
  45.3 7.4 %collective-permute-start = (bf16[12,48,128]{2,1,0:T(8,128)(2,1)S(1)}, bf16[12,48,128]{2,1,0:T(8,128)(2,1)S(1)}, u32[]{:S(2)}, u32[]{:S(2)}) collective-permute-start(bf16[12,48,128]{2,1,0:T(8,128)(2,1)S(1)} %get-tuple-element.105.value.earlier), channel_id=1, source_target_pairs={{8,16},{24,32},{40,48},{56,64},{72,80},{88,96},{104,112},{120,128}... | collective-permute-start | bytes 442376 | tf_op jit(solution)/shard_map/while/body/eval_jaxpr/ppermute | solution.py:211
  47.4 5.3 %collective-permute-start.1 = (bf16[12,48,128]{2,1,0:T(8,128)(2,1)S(1)}, bf16[12,48,128]{2,1,0:T(8,128)(2,1)S(1)}, u32[]{:S(2)}, u32[]{:S(2)}) collective-permute-start(bf16[12,48,128]{2,1,0:T(8,128)(2,1)S(1)} %get-tuple-element.105.value.earlier), channel_id=1, source_target_pairs={{0,8},{16,24},{32,40},{48,56},{64,72},{80,88},{96,104},{112,120},{... | collective-permute-start | bytes 442376 | tf_op jit(solution)/shard_map/while/body/eval_jaxpr/ppermute | solution.py:210
  47.4 6.5 %collective-permute-start.2 = (bf16[12,48,128]{2,1,0:T(8,128)(2,1)S(1)}, bf16[12,48,128]{2,1,0:T(8,128)(2,1)S(1)}, u32[]{:S(2)}, u32[]{:S(2)}) collective-permute-start(bf16[12,48,128]{2,1,0:T(8,128)(2,1)S(1)} %get-tuple-element.105.value.earlier), channel_id=1, source_target_pairs={{1,2},{3,4},{5,6},{7,0},{2,1},{4,3},{6,5},{0,7},{9,10},{11,12},{13... | collective-permute-start | bytes 442376 | tf_op jit(solution)/shard_map/while/body/eval_jaxpr/ppermute | solution.py:209
  50.7 3.1 %collective-permute-start.3 = (bf16[12,48,128]{2,1,0:T(8,128)(2,1)S(1)}, bf16[12,48,128]{2,1,0:T(8,128)(2,1)S(1)}, u32[]{:S(2)}, u32[]{:S(2)}) collective-permute-start(bf16[12,48,128]{2,1,0:T(8,128)(2,1)S(1)} %get-tuple-element.105.value.earlier), channel_id=1, source_target_pairs={{0,1},{2,3},{4,5},{6,7},{1,0},{3,2},{5,4},{7,6},{8,9},{10,11},{12,... | collective-permute-start | bytes 442376 | tf_op jit(solution)/shard_map/while/body/eval_jaxpr/ppermute | solution.py:208
  54.2 7.4 %collective-permute-start = (bf16[12,48,128]{2,1,0:T(8,128)(2,1)S(1)}, bf16[12,48,128]{2,1,0:T(8,128)(2,1)S(1)}, u32[]{:S(2)}, u32[]{:S(2)}) collective-permute-start(bf16[12,48,128]{2,1,0:T(8,128)(2,1)S(1)} %get-tuple-element.105.value.earlier), channel_id=1, source_target_pairs={{8,16},{24,32},{40,48},{56,64},{72,80},{88,96},{104,112},{120,128}... | collective-permute-start | bytes 442376 | tf_op jit(solution)/shard_map/while/body/eval_jaxpr/ppermute | solution.py:211
  56.3 5.3 %collective-permute-start.1 = (bf16[12,48,128]{2,1,0:T(8,128)(2,1)S(1)}, bf16[12,48,128]{2,1,0:T(8,128)(2,1)S(1)}, u32[]{:S(2)}, u32[]{:S(2)}) collective-permute-start(bf16[12,48,128]{2,1,0:T(8,128)(2,1)S(1)} %get-tuple-element.105.value.earlier), channel_id=1, source_target_pairs={{0,8},{16,24},{32,40},{48,56},{64,72},{80,88},{96,104},{112,120},{... | collective-permute-start | bytes 442376 | tf_op jit(solution)/shard_map/while/body/eval_jaxpr/ppermute | solution.py:210
  56.3 6.5 %collective-permute-start.2 = (bf16[12,48,128]{2,1,0:T(8,128)(2,1)S(1)}, bf16[12,48,128]{2,1,0:T(8,128)(2,1)S(1)}, u32[]{:S(2)}, u32[]{:S(2)}) collective-permute-start(bf16[12,48,128]{2,1,0:T(8,128)(2,1)S(1)} %get-tuple-element.105.value.earlier), channel_id=1, source_target_pairs={{1,2},{3,4},{5,6},{7,0},{2,1},{4,3},{6,5},{0,7},{9,10},{11,12},{13... | collective-permute-start | bytes 442376 | tf_op jit(solution)/shard_map/while/body/eval_jaxpr/ppermute | solution.py:209
  59.7 3.1 %collective-permute-start.3 = (bf16[12,48,128]{2,1,0:T(8,128)(2,1)S(1)}, bf16[12,48,128]{2,1,0:T(8,128)(2,1)S(1)}, u32[]{:S(2)}, u32[]{:S(2)}) collective-permute-start(bf16[12,48,128]{2,1,0:T(8,128)(2,1)S(1)} %get-tuple-element.105.value.earlier), channel_id=1, source_target_pairs={{0,1},{2,3},{4,5},{6,7},{1,0},{3,2},{5,4},{7,6},{8,9},{10,11},{12,... | collective-permute-start | bytes 442376 | tf_op jit(solution)/shard_map/while/body/eval_jaxpr/ppermute | solution.py:208
  63.2 7.4 %collective-permute-start = (bf16[12,48,128]{2,1,0:T(8,128)(2,1)S(1)}, bf16[12,48,128]{2,1,0:T(8,128)(2,1)S(1)}, u32[]{:S(2)}, u32[]{:S(2)}) collective-permute-start(bf16[12,48,128]{2,1,0:T(8,128)(2,1)S(1)} %get-tuple-element.105.value.earlier), channel_id=1, source_target_pairs={{8,16},{24,32},{40,48},{56,64},{72,80},{88,96},{104,112},{120,128}... | collective-permute-start | bytes 442376 | tf_op jit(solution)/shard_map/while/body/eval_jaxpr/ppermute | solution.py:211
  65.3 5.3 %collective-permute-start.1 = (bf16[12,48,128]{2,1,0:T(8,128)(2,1)S(1)}, bf16[12,48,128]{2,1,0:T(8,128)(2,1)S(1)}, u32[]{:S(2)}, u32[]{:S(2)}) collective-permute-start(bf16[12,48,128]{2,1,0:T(8,128)(2,1)S(1)} %get-tuple-element.105.value.earlier), channel_id=1, source_target_pairs={{0,8},{16,24},{32,40},{48,56},{64,72},{80,88},{96,104},{112,120},{... | collective-permute-start | bytes 442376 | tf_op jit(solution)/shard_map/while/body/eval_jaxpr/ppermute | solution.py:210
  65.3 6.5 %collective-permute-start.2 = (bf16[12,48,128]{2,1,0:T(8,128)(2,1)S(1)}, bf16[12,48,128]{2,1,0:T(8,128)(2,1)S(1)}, u32[]{:S(2)}, u32[]{:S(2)}) collective-permute-start(bf16[12,48,128]{2,1,0:T(8,128)(2,1)S(1)} %get-tuple-element.105.value.earlier), channel_id=1, source_target_pairs={{1,2},{3,4},{5,6},{7,0},{2,1},{4,3},{6,5},{0,7},{9,10},{11,12},{13... | collective-permute-start | bytes 442376 | tf_op jit(solution)/shard_map/while/body/eval_jaxpr/ppermute | solution.py:209
  68.7 3.1 %collective-permute-start.3 = (bf16[12,48,128]{2,1,0:T(8,128)(2,1)S(1)}, bf16[12,48,128]{2,1,0:T(8,128)(2,1)S(1)}, u32[]{:S(2)}, u32[]{:S(2)}) collective-permute-start(bf16[12,48,128]{2,1,0:T(8,128)(2,1)S(1)} %get-tuple-element.105.value.earlier), channel_id=1, source_target_pairs={{0,1},{2,3},{4,5},{6,7},{1,0},{3,2},{5,4},{7,6},{8,9},{10,11},{12,... | collective-permute-start | bytes 442376 | tf_op jit(solution)/shard_map/while/body/eval_jaxpr/ppermute | solution.py:208
  72.2 7.4 %collective-permute-start = (bf16[12,48,128]{2,1,0:T(8,128)(2,1)S(1)}, bf16[12,48,128]{2,1,0:T(8,128)(2,1)S(1)}, u32[]{:S(2)}, u32[]{:S(2)}) collective-permute-start(bf16[12,48,128]{2,1,0:T(8,128)(2,1)S(1)} %get-tuple-element.105.value.earlier), channel_id=1, source_target_pairs={{8,16},{24,32},{40,48},{56,64},{72,80},{88,96},{104,112},{120,128}... | collective-permute-start | bytes 442376 | tf_op jit(solution)/shard_map/while/body/eval_jaxpr/ppermute | solution.py:211
  74.3 5.3 %collective-permute-start.1 = (bf16[12,48,128]{2,1,0:T(8,128)(2,1)S(1)}, bf16[12,48,128]{2,1,0:T(8,128)(2,1)S(1)}, u32[]{:S(2)}, u32[]{:S(2)}) collective-permute-start(bf16[12,48,128]{2,1,0:T(8,128)(2,1)S(1)} %get-tuple-element.105.value.earlier), channel_id=1, source_target_pairs={{0,8},{16,24},{32,40},{48,56},{64,72},{80,88},{96,104},{112,120},{... | collective-permute-start | bytes 442376 | tf_op jit(solution)/shard_map/while/body/eval_jaxpr/ppermute | solution.py:210
  74.3 6.5 %collective-permute-start.2 = (bf16[12,48,128]{2,1,0:T(8,128)(2,1)S(1)}, bf16[12,48,128]{2,1,0:T(8,128)(2,1)S(1)}, u32[]{:S(2)}, u32[]{:S(2)}) collective-permute-start(bf16[12,48,128]{2,1,0:T(8,128)(2,1)S(1)} %get-tuple-element.105.value.earlier), channel_id=1, source_target_pairs={{1,2},{3,4},{5,6},{7,0},{2,1},{4,3},{6,5},{0,7},{9,10},{11,12},{13... | collective-permute-start | bytes 442376 | tf_op jit(solution)/shard_map/while/body/eval_jaxpr/ppermute | solution.py:209
  77.7 3.1 %collective-permute-start.3 = (bf16[12,48,128]{2,1,0:T(8,128)(2,1)S(1)}, bf16[12,48,128]{2,1,0:T(8,128)(2,1)S(1)}, u32[]{:S(2)}, u32[]{:S(2)}) collective-permute-start(bf16[12,48,128]{2,1,0:T(8,128)(2,1)S(1)} %get-tuple-element.105.value.earlier), channel_id=1, source_target_pairs={{0,1},{2,3},{4,5},{6,7},{1,0},{3,2},{5,4},{7,6},{8,9},{10,11},{12,... | collective-permute-start | bytes 442376 | tf_op jit(solution)/shard_map/while/body/eval_jaxpr/ppermute | solution.py:208
  81.2 7.4 %collective-permute-start = (bf16[12,48,128]{2,1,0:T(8,128)(2,1)S(1)}, bf16[12,48,128]{2,1,0:T(8,128)(2,1)S(1)}, u32[]{:S(2)}, u32[]{:S(2)}) collective-permute-start(bf16[12,48,128]{2,1,0:T(8,128)(2,1)S(1)} %get-tuple-element.105.value.earlier), channel_id=1, source_target_pairs={{8,16},{24,32},{40,48},{56,64},{72,80},{88,96},{104,112},{120,128}... | collective-permute-start | bytes 442376 | tf_op jit(solution)/shard_map/while/body/eval_jaxpr/ppermute | solution.py:211
  83.3 5.3 %collective-permute-start.1 = (bf16[12,48,128]{2,1,0:T(8,128)(2,1)S(1)}, bf16[12,48,128]{2,1,0:T(8,128)(2,1)S(1)}, u32[]{:S(2)}, u32[]{:S(2)}) collective-permute-start(bf16[12,48,128]{2,1,0:T(8,128)(2,1)S(1)} %get-tuple-element.105.value.earlier), channel_id=1, source_target_pairs={{0,8},{16,24},{32,40},{48,56},{64,72},{80,88},{96,104},{112,120},{... | collective-permute-start | bytes 442376 | tf_op jit(solution)/shard_map/while/body/eval_jaxpr/ppermute | solution.py:210
  83.3 6.5 %collective-permute-start.2 = (bf16[12,48,128]{2,1,0:T(8,128)(2,1)S(1)}, bf16[12,48,128]{2,1,0:T(8,128)(2,1)S(1)}, u32[]{:S(2)}, u32[]{:S(2)}) collective-permute-start(bf16[12,48,128]{2,1,0:T(8,128)(2,1)S(1)} %get-tuple-element.105.value.earlier), channel_id=1, source_target_pairs={{1,2},{3,4},{5,6},{7,0},{2,1},{4,3},{6,5},{0,7},{9,10},{11,12},{13... | collective-permute-start | bytes 442376 | tf_op jit(solution)/shard_map/while/body/eval_jaxpr/ppermute | solution.py:209
  86.7 3.1 %collective-permute-start.3 = (bf16[12,48,128]{2,1,0:T(8,128)(2,1)S(1)}, bf16[12,48,128]{2,1,0:T(8,128)(2,1)S(1)}, u32[]{:S(2)}, u32[]{:S(2)}) collective-permute-start(bf16[12,48,128]{2,1,0:T(8,128)(2,1)S(1)} %get-tuple-element.105.value.earlier), channel_id=1, source_target_pairs={{0,1},{2,3},{4,5},{6,7},{1,0},{3,2},{5,4},{7,6},{8,9},{10,11},{12,... | collective-permute-start | bytes 442376 | tf_op jit(solution)/shard_map/while/body/eval_jaxpr/ppermute | solution.py:208
  90.2 7.4 %collective-permute-start = (bf16[12,48,128]{2,1,0:T(8,128)(2,1)S(1)}, bf16[12,48,128]{2,1,0:T(8,128)(2,1)S(1)}, u32[]{:S(2)}, u32[]{:S(2)}) collective-permute-start(bf16[12,48,128]{2,1,0:T(8,128)(2,1)S(1)} %get-tuple-element.105.value.earlier), channel_id=1, source_target_pairs={{8,16},{24,32},{40,48},{56,64},{72,80},{88,96},{104,112},{120,128}... | collective-permute-start | bytes 442376 | tf_op jit(solution)/shard_map/while/body/eval_jaxpr/ppermute | solution.py:211
  92.3 5.3 %collective-permute-start.1 = (bf16[12,48,128]{2,1,0:T(8,128)(2,1)S(1)}, bf16[12,48,128]{2,1,0:T(8,128)(2,1)S(1)}, u32[]{:S(2)}, u32[]{:S(2)}) collective-permute-start(bf16[12,48,128]{2,1,0:T(8,128)(2,1)S(1)} %get-tuple-element.105.value.earlier), channel_id=1, source_target_pairs={{0,8},{16,24},{32,40},{48,56},{64,72},{80,88},{96,104},{112,120},{... | collective-permute-start | bytes 442376 | tf_op jit(solution)/shard_map/while/body/eval_jaxpr/ppermute | solution.py:210
  92.3 6.5 %collective-permute-start.2 = (bf16[12,48,128]{2,1,0:T(8,128)(2,1)S(1)}, bf16[12,48,128]{2,1,0:T(8,128)(2,1)S(1)}, u32[]{:S(2)}, u32[]{:S(2)}) collective-permute-start(bf16[12,48,128]{2,1,0:T(8,128)(2,1)S(1)} %get-tuple-element.105.value.earlier), channel_id=1, source_target_pairs={{1,2},{3,4},{5,6},{7,0},{2,1},{4,3},{6,5},{0,7},{9,10},{11,12},{13... | collective-permute-start | bytes 442376 | tf_op jit(solution)/shard_map/while/body/eval_jaxpr/ppermute | solution.py:209
  95.7 3.1 %collective-permute-start.3 = (bf16[12,48,128]{2,1,0:T(8,128)(2,1)S(1)}, bf16[12,48,128]{2,1,0:T(8,128)(2,1)S(1)}, u32[]{:S(2)}, u32[]{:S(2)}) collective-permute-start(bf16[12,48,128]{2,1,0:T(8,128)(2,1)S(1)} %get-tuple-element.105.value.earlier), channel_id=1, source_target_pairs={{0,1},{2,3},{4,5},{6,7},{1,0},{3,2},{5,4},{7,6},{8,9},{10,11},{12,... | collective-permute-start | bytes 442376 | tf_op jit(solution)/shard_map/while/body/eval_jaxpr/ppermute | solution.py:208
  99.2 7.4 %collective-permute-start = (bf16[12,48,128]{2,1,0:T(8,128)(2,1)S(1)}, bf16[12,48,128]{2,1,0:T(8,128)(2,1)S(1)}, u32[]{:S(2)}, u32[]{:S(2)}) collective-permute-start(bf16[12,48,128]{2,1,0:T(8,128)(2,1)S(1)} %get-tuple-element.105.value.earlier), channel_id=1, source_target_pairs={{8,16},{24,32},{40,48},{56,64},{72,80},{88,96},{104,112},{120,128}... | collective-permute-start | bytes 442376 | tf_op jit(solution)/shard_map/while/body/eval_jaxpr/ppermute | solution.py:211
  101.3 5.3 %collective-permute-start.1 = (bf16[12,48,128]{2,1,0:T(8,128)(2,1)S(1)}, bf16[12,48,128]{2,1,0:T(8,128)(2,1)S(1)}, u32[]{:S(2)}, u32[]{:S(2)}) collective-permute-start(bf16[12,48,128]{2,1,0:T(8,128)(2,1)S(1)} %get-tuple-element.105.value.earlier), channel_id=1, source_target_pairs={{0,8},{16,24},{32,40},{48,56},{64,72},{80,88},{96,104},{112,120},{... | collective-permute-start | bytes 442376 | tf_op jit(solution)/shard_map/while/body/eval_jaxpr/ppermute | solution.py:210
  101.3 6.5 %collective-permute-start.2 = (bf16[12,48,128]{2,1,0:T(8,128)(2,1)S(1)}, bf16[12,48,128]{2,1,0:T(8,128)(2,1)S(1)}, u32[]{:S(2)}, u32[]{:S(2)}) collective-permute-start(bf16[12,48,128]{2,1,0:T(8,128)(2,1)S(1)} %get-tuple-element.105.value.earlier), channel_id=1, source_target_pairs={{1,2},{3,4},{5,6},{7,0},{2,1},{4,3},{6,5},{0,7},{9,10},{11,12},{13... | collective-permute-start | bytes 442376 | tf_op jit(solution)/shard_map/while/body/eval_jaxpr/ppermute | solution.py:209
  104.6 3.1 %collective-permute-start.3 = (bf16[12,48,128]{2,1,0:T(8,128)(2,1)S(1)}, bf16[12,48,128]{2,1,0:T(8,128)(2,1)S(1)}, u32[]{:S(2)}, u32[]{:S(2)}) collective-permute-start(bf16[12,48,128]{2,1,0:T(8,128)(2,1)S(1)} %get-tuple-element.105.value.earlier), channel_id=1, source_target_pairs={{0,1},{2,3},{4,5},{6,7},{1,0},{3,2},{5,4},{7,6},{8,9},{10,11},{12,... | collective-permute-start | bytes 442376 | tf_op jit(solution)/shard_map/while/body/eval_jaxpr/ppermute | solution.py:208
  108.2 7.4 %collective-permute-start = (bf16[12,48,128]{2,1,0:T(8,128)(2,1)S(1)}, bf16[12,48,128]{2,1,0:T(8,128)(2,1)S(1)}, u32[]{:S(2)}, u32[]{:S(2)}) collective-permute-start(bf16[12,48,128]{2,1,0:T(8,128)(2,1)S(1)} %get-tuple-element.105.value.earlier), channel_id=1, source_target_pairs={{8,16},{24,32},{40,48},{56,64},{72,80},{88,96},{104,112},{120,128}... | collective-permute-start | bytes 442376 | tf_op jit(solution)/shard_map/while/body/eval_jaxpr/ppermute | solution.py:211
  110.3 5.3 %collective-permute-start.1 = (bf16[12,48,128]{2,1,0:T(8,128)(2,1)S(1)}, bf16[12,48,128]{2,1,0:T(8,128)(2,1)S(1)}, u32[]{:S(2)}, u32[]{:S(2)}) collective-permute-start(bf16[12,48,128]{2,1,0:T(8,128)(2,1)S(1)} %get-tuple-element.105.value.earlier), channel_id=1, source_target_pairs={{0,8},{16,24},{32,40},{48,56},{64,72},{80,88},{96,104},{112,120},{... | collective-permute-start | bytes 442376 | tf_op jit(solution)/shard_map/while/body/eval_jaxpr/ppermute | solution.py:210
  110.3 6.5 %collective-permute-start.2 = (bf16[12,48,128]{2,1,0:T(8,128)(2,1)S(1)}, bf16[12,48,128]{2,1,0:T(8,128)(2,1)S(1)}, u32[]{:S(2)}, u32[]{:S(2)}) collective-permute-start(bf16[12,48,128]{2,1,0:T(8,128)(2,1)S(1)} %get-tuple-element.105.value.earlier), channel_id=1, source_target_pairs={{1,2},{3,4},{5,6},{7,0},{2,1},{4,3},{6,5},{0,7},{9,10},{11,12},{13... | collective-permute-start | bytes 442376 | tf_op jit(solution)/shard_map/while/body/eval_jaxpr/ppermute | solution.py:209
  113.6 3.1 %collective-permute-start.3 = (bf16[12,48,128]{2,1,0:T(8,128)(2,1)S(1)}, bf16[12,48,128]{2,1,0:T(8,128)(2,1)S(1)}, u32[]{:S(2)}, u32[]{:S(2)}) collective-permute-start(bf16[12,48,128]{2,1,0:T(8,128)(2,1)S(1)} %get-tuple-element.105.value.earlier), channel_id=1, source_target_pairs={{0,1},{2,3},{4,5},{6,7},{1,0},{3,2},{5,4},{7,6},{8,9},{10,11},{12,... | collective-permute-start | bytes 442376 | tf_op jit(solution)/shard_map/while/body/eval_jaxpr/ppermute | solution.py:208
  117.2 7.4 %collective-permute-start = (bf16[12,48,128]{2,1,0:T(8,128)(2,1)S(1)}, bf16[12,48,128]{2,1,0:T(8,128)(2,1)S(1)}, u32[]{:S(2)}, u32[]{:S(2)}) collective-permute-start(bf16[12,48,128]{2,1,0:T(8,128)(2,1)S(1)} %get-tuple-element.105.value.earlier), channel_id=1, source_target_pairs={{8,16},{24,32},{40,48},{56,64},{72,80},{88,96},{104,112},{120,128}... | collective-permute-start | bytes 442376 | tf_op jit(solution)/shard_map/while/body/eval_jaxpr/ppermute | solution.py:211
  119.3 5.3 %collective-permute-start.1 = (bf16[12,48,128]{2,1,0:T(8,128)(2,1)S(1)}, bf16[12,48,128]{2,1,0:T(8,128)(2,1)S(1)}, u32[]{:S(2)}, u32[]{:S(2)}) collective-permute-start(bf16[12,48,128]{2,1,0:T(8,128)(2,1)S(1)} %get-tuple-element.105.value.earlier), channel_id=1, source_target_pairs={{0,8},{16,24},{32,40},{48,56},{64,72},{80,88},{96,104},{112,120},{... | collective-permute-start | bytes 442376 | tf_op jit(solution)/shard_map/while/body/eval_jaxpr/ppermute | solution.py:210
  119.3 6.5 %collective-permute-start.2 = (bf16[12,48,128]{2,1,0:T(8,128)(2,1)S(1)}, bf16[12,48,128]{2,1,0:T(8,128)(2,1)S(1)}, u32[]{:S(2)}, u32[]{:S(2)}) collective-permute-start(bf16[12,48,128]{2,1,0:T(8,128)(2,1)S(1)} %get-tuple-element.105.value.earlier), channel_id=1, source_target_pairs={{1,2},{3,4},{5,6},{7,0},{2,1},{4,3},{6,5},{0,7},{9,10},{11,12},{13... | collective-permute-start | bytes 442376 | tf_op jit(solution)/shard_map/while/body/eval_jaxpr/ppermute | solution.py:209
  122.6 3.1 %collective-permute-start.3 = (bf16[12,48,128]{2,1,0:T(8,128)(2,1)S(1)}, bf16[12,48,128]{2,1,0:T(8,128)(2,1)S(1)}, u32[]{:S(2)}, u32[]{:S(2)}) collective-permute-start(bf16[12,48,128]{2,1,0:T(8,128)(2,1)S(1)} %get-tuple-element.105.value.earlier), channel_id=1, source_target_pairs={{0,1},{2,3},{4,5},{6,7},{1,0},{3,2},{5,4},{7,6},{8,9},{10,11},{12,... | collective-permute-start | bytes 442376 | tf_op jit(solution)/shard_map/while/body/eval_jaxpr/ppermute | solution.py:208
  126.2 7.4 %collective-permute-start = (bf16[12,48,128]{2,1,0:T(8,128)(2,1)S(1)}, bf16[12,48,128]{2,1,0:T(8,128)(2,1)S(1)}, u32[]{:S(2)}, u32[]{:S(2)}) collective-permute-start(bf16[12,48,128]{2,1,0:T(8,128)(2,1)S(1)} %get-tuple-element.105.value.earlier), channel_id=1, source_target_pairs={{8,16},{24,32},{40,48},{56,64},{72,80},{88,96},{104,112},{120,128}... | collective-permute-start | bytes 442376 | tf_op jit(solution)/shard_map/while/body/eval_jaxpr/ppermute | solution.py:211
  128.3 5.3 %collective-permute-start.1 = (bf16[12,48,128]{2,1,0:T(8,128)(2,1)S(1)}, bf16[12,48,128]{2,1,0:T(8,128)(2,1)S(1)}, u32[]{:S(2)}, u32[]{:S(2)}) collective-permute-start(bf16[12,48,128]{2,1,0:T(8,128)(2,1)S(1)} %get-tuple-element.105.value.earlier), channel_id=1, source_target_pairs={{0,8},{16,24},{32,40},{48,56},{64,72},{80,88},{96,104},{112,120},{... | collective-permute-start | bytes 442376 | tf_op jit(solution)/shard_map/while/body/eval_jaxpr/ppermute | solution.py:210
  128.3 6.5 %collective-permute-start.2 = (bf16[12,48,128]{2,1,0:T(8,128)(2,1)S(1)}, bf16[12,48,128]{2,1,0:T(8,128)(2,1)S(1)}, u32[]{:S(2)}, u32[]{:S(2)}) collective-permute-start(bf16[12,48,128]{2,1,0:T(8,128)(2,1)S(1)} %get-tuple-element.105.value.earlier), channel_id=1, source_target_pairs={{1,2},{3,4},{5,6},{7,0},{2,1},{4,3},{6,5},{0,7},{9,10},{11,12},{13... | collective-permute-start | bytes 442376 | tf_op jit(solution)/shard_map/while/body/eval_jaxpr/ppermute | solution.py:209
  131.6 3.1 %collective-permute-start.3 = (bf16[12,48,128]{2,1,0:T(8,128)(2,1)S(1)}, bf16[12,48,128]{2,1,0:T(8,128)(2,1)S(1)}, u32[]{:S(2)}, u32[]{:S(2)}) collective-permute-start(bf16[12,48,128]{2,1,0:T(8,128)(2,1)S(1)} %get-tuple-element.105.value.earlier), channel_id=1, source_target_pairs={{0,1},{2,3},{4,5},{6,7},{1,0},{3,2},{5,4},{7,6},{8,9},{10,11},{12,... | collective-permute-start | bytes 442376 | tf_op jit(solution)/shard_map/while/body/eval_jaxpr/ppermute | solution.py:208
  135.1 7.4 %collective-permute-start = (bf16[12,48,128]{2,1,0:T(8,128)(2,1)S(1)}, bf16[12,48,128]{2,1,0:T(8,128)(2,1)S(1)}, u32[]{:S(2)}, u32[]{:S(2)}) collective-permute-start(bf16[12,48,128]{2,1,0:T(8,128)(2,1)S(1)} %get-tuple-element.105.value.earlier), channel_id=1, source_target_pairs={{8,16},{24,32},{40,48},{56,64},{72,80},{88,96},{104,112},{120,128}... | collective-permute-start | bytes 442376 | tf_op jit(solution)/shard_map/while/body/eval_jaxpr/ppermute | solution.py:211
  137.2 5.3 %collective-permute-start.1 = (bf16[12,48,128]{2,1,0:T(8,128)(2,1)S(1)}, bf16[12,48,128]{2,1,0:T(8,128)(2,1)S(1)}, u32[]{:S(2)}, u32[]{:S(2)}) collective-permute-start(bf16[12,48,128]{2,1,0:T(8,128)(2,1)S(1)} %get-tuple-element.105.value.earlier), channel_id=1, source_target_pairs={{0,8},{16,24},{32,40},{48,56},{64,72},{80,88},{96,104},{112,120},{... | collective-permute-start | bytes 442376 | tf_op jit(solution)/shard_map/while/body/eval_jaxpr/ppermute | solution.py:210
  137.3 6.5 %collective-permute-start.2 = (bf16[12,48,128]{2,1,0:T(8,128)(2,1)S(1)}, bf16[12,48,128]{2,1,0:T(8,128)(2,1)S(1)}, u32[]{:S(2)}, u32[]{:S(2)}) collective-permute-start(bf16[12,48,128]{2,1,0:T(8,128)(2,1)S(1)} %get-tuple-element.105.value.earlier), channel_id=1, source_target_pairs={{1,2},{3,4},{5,6},{7,0},{2,1},{4,3},{6,5},{0,7},{9,10},{11,12},{13... | collective-permute-start | bytes 442376 | tf_op jit(solution)/shard_map/while/body/eval_jaxpr/ppermute | solution.py:209
  140.6 3.1 %collective-permute-start.3 = (bf16[12,48,128]{2,1,0:T(8,128)(2,1)S(1)}, bf16[12,48,128]{2,1,0:T(8,128)(2,1)S(1)}, u32[]{:S(2)}, u32[]{:S(2)}) collective-permute-start(bf16[12,48,128]{2,1,0:T(8,128)(2,1)S(1)} %get-tuple-element.105.value.earlier), channel_id=1, source_target_pairs={{0,1},{2,3},{4,5},{6,7},{1,0},{3,2},{5,4},{7,6},{8,9},{10,11},{12,... | collective-permute-start | bytes 442376 | tf_op jit(solution)/shard_map/while/body/eval_jaxpr/ppermute | solution.py:208
  144.1 10.5 %collective-permute-start.8 = (bf16[12,48,128]{2,1,0:T(8,128)(2,1)S(1)}, bf16[12,48,128]{2,1,0:T(8,128)(2,1)S(1)}, u32[]{:S(2)}, u32[]{:S(2)}) collective-permute-start(bf16[12,48,128]{2,1,0:T(8,128)(2,1)S(1)} %get-tuple-element.45.value.earlier), channel_id=1, source_target_pairs={{8,16},{24,32},{40,48},{56,64},{72,80},{88,96},{104,112},{120,128}... | collective-permute-start | bytes 442376 | tf_op jit(solution)/shard_map/ppermute | solution.py:211
  146.2 8.4 %collective-permute-start.9 = (bf16[12,48,128]{2,1,0:T(8,128)(2,1)S(1)}, bf16[12,48,128]{2,1,0:T(8,128)(2,1)S(1)}, u32[]{:S(2)}, u32[]{:S(2)}) collective-permute-start(bf16[12,48,128]{2,1,0:T(8,128)(2,1)S(1)} %get-tuple-element.45.value.earlier), channel_id=1, source_target_pairs={{0,8},{16,24},{32,40},{48,56},{64,72},{80,88},{96,104},{112,120},{... | collective-permute-start | bytes 442376 | tf_op jit(solution)/shard_map/ppermute | solution.py:210
  146.2 8.4 %collective-permute-start.10 = (bf16[12,48,128]{2,1,0:T(8,128)(2,1)S(1)}, bf16[12,48,128]{2,1,0:T(8,128)(2,1)S(1)}, u32[]{:S(2)}, u32[]{:S(2)}) collective-permute-start(bf16[12,48,128]{2,1,0:T(8,128)(2,1)S(1)} %get-tuple-element.45.value.earlier), channel_id=1, source_target_pairs={{1,2},{3,4},{5,6},{7,0},{2,1},{4,3},{6,5},{0,7},{9,10},{11,12},{13... | collective-permute-start | bytes 442376 | tf_op jit(solution)/shard_map/ppermute | solution.py:209
  149.6 5.1 %collective-permute-start.11 = (bf16[12,48,128]{2,1,0:T(8,128)(2,1)S(1)}, bf16[12,48,128]{2,1,0:T(8,128)(2,1)S(1)}, u32[]{:S(2)}, u32[]{:S(2)}) collective-permute-start(bf16[12,48,128]{2,1,0:T(8,128)(2,1)S(1)} %get-tuple-element.45.value.earlier), channel_id=1, source_target_pairs={{0,1},{2,3},{4,5},{6,7},{1,0},{3,2},{5,4},{7,6},{8,9},{10,11},{12,... | collective-permute-start | bytes 442376 | tf_op jit(solution)/shard_map/ppermute | solution.py:208

commit v3 on v2

--- a/solution.py
+++ b/solution.py
@@ -9,6 +9,7 @@
 
 ITERS = 16
 KEPT = 1
+LATE = 3
 LIMIT = 16 * 2**20
 VMEM = pl.BlockSpec(memory_space=pltpu.VMEM)
 HBM = pl.BlockSpec(memory_space=pltpu.HBM)
@@ -127,23 +128,16 @@
         remote[:, :wide, :] = -remote[:, :wide, :]
 
 
-def last_kernel(ny, nx, rhs, value, kept, links, prolongator, out, turned, buffer, sems, held, held_sems):
+def last_kernel(ny, nx, first, rhs, value, kept, links, prolongator, out, turned, buffer, sems, held, held_sems):
     copies = fetch_rows(ny, nx, links, buffer, sems)
-    sites = held.shape[0]
-
-    def fetch(s):
-        return pltpu.make_async_copy(prolongator.at[s], held.at[s], held_sems.at[s])
-
-    for s in range(sites):
-        fetch(s).start()
+    fetched = []
+    for s in range(held.shape[0]):
+        fetched.append(pltpu.make_async_copy(prolongator.at[first + s], held.at[s], held_sems.at[s]))
+        fetched[-1].start()
     local_rows(ny, nx, rhs, value, kept, buffer, out, copies)
-
-    def turn(s, _):
-        fetch(s).wait()
+    for s in range(held.shape[0]):
+        fetched[s].wait()
         turned[s] = held[s].T
-        return 0
-
-    lax.fori_loop(0, sites, turn, 0)
 
 
 def remote_kernel(part, a, b, c, d, weights, token, out):
@@ -156,10 +150,13 @@
     token[...] = jnp.zeros_like(token)
 
 
-def prolong_kernel(value, turned, out, buffer, sems):
+def prolong_kernel(value, *refs):
+    *turned, out, buffer, sems = refs
+    share = turned[0].shape[0]
     copies = []
     for s in range(value.shape[0]):
-        buffer[s] = dot(value[s], turned[s]).astype(buffer.dtype)
+        weights = turned[s // share][s % share]
+        buffer[s] = dot(value[s], weights).astype(buffer.dtype)
         copies.append(pltpu.make_async_copy(buffer.at[s], out.at[s], sems.at[s]))
         copies[-1].start()
     for c in copies:
@@ -254,25 +251,29 @@
         )
         return finish(value, part, arrivals, remote_weights)
 
-    value = lax.fori_loop(1, ITERS - 1, sweep, value)
-    arrivals = swaps(value)
-    part, turned = call(
-        functools.partial(last_kernel, ny, nx),
-        [rhs, value, kept, links, prolong],
-        [shape(field, jnp.float32), shape((sites, wide, fine))],
-        [
-            *local_scratch,
-            pltpu.VMEM(prolong.shape, prolong.dtype),
-            pltpu.SemaphoreType.DMA((sites,)),
-        ],
-        in_specs=[VMEM, VMEM, VMEM, HBM, HBM],
-        flops=5 * flops,
-    )
-    value = finish(value, part, arrivals, remote_weights)
+    value = lax.fori_loop(1, ITERS - LATE, sweep, value)
+    share = sites // LATE
+    turned = []
+    for k in range(LATE):
+        arrivals = swaps(value)
+        part, some = call(
+            functools.partial(last_kernel, ny, nx, k * share),
+            [rhs, value, kept, links, prolong],
+            [shape(field, jnp.float32), shape((share, wide, fine))],
+            [
+                *local_scratch,
+                pltpu.VMEM((share, fine, wide), prolong.dtype),
+                pltpu.SemaphoreType.DMA((share,)),
+            ],
+            in_specs=[VMEM, VMEM, VMEM, HBM, HBM],
+            flops=5 * flops,
+        )
+        turned.append(some)
+        value = finish(value, part, arrivals, remote_weights)
 
     (out,) = call(
         prolong_kernel,
-        [value, turned],
+        [value, *turned],
         [shape((sites, rhs_count, fine))],
         [pltpu.VMEM((sites, rhs_count, fine), jnp.bfloat16), pltpu.SemaphoreType.DMA((sites,))],
         out_specs=[HBM],

time: 157 us -> 156 us (level)
  transfers between devices with their start and end apart: 64 -> 64, of which waited for: 15 -> 16; matrix products, arithmetic and copies ran while one was open for 0% -> 0% of each run, Pallas kernels for 23% -> 23%
where the time goes in v3:
time: 156 us; the launch traced here: 155 us
  starting transfers between devices  91.8 us (59%)
  Pallas kernels  45.9 us (29%)
  waiting for transfers between devices  16 us (10%)
    ppermute x16, starting transfers between devices, swaps(): z_far = lax.ppermute(value, 'gz', swap(nz, 1))  51.5 us
    pallas_call x82, Pallas kernels, call(): pl.pallas_call(kernel, in_specs=in_specs, out_specs=out_specs, out_shape=...  45.9 us
    ppermute x16, starting transfers between devices, swaps(): t_far = lax.ppermute(value, 'ta', swap(nt, 1))  39.4 us
    ppermute x16, waiting for transfers between devices, swaps(): z_far = lax.ppermute(value, 'gz', swap(nz, 1))  12.2 us
    ppermute x16, waiting for transfers between devices, swaps(): t_far = lax.ppermute(value, 'ta', swap(nt, 1))  3.72 us
  transfers between devices with their start and end apart: 64, of which 16 were waited for; matrix products, arithmetic and copies ran while one was open for 0% of the time, Pallas kernels for 23%

profile of v3, /device:TPU:1, one launch (start us, length us, event | category | flops | bytes accessed | tf_op | source)
XLA Modules:
  0.0 154.9 jit_solution(2110350142576864242)
XLA Ops:
  0.0 3.3 %shard_map.37.rhs.earlier = bf16[12,48,128]{2,1,0:T(8,128)(2,1)S(1)} custom-call(bf16[12,48,1536]{2,1,0:T(8,128)(2,1)} %bitcast.15, bf16[12,1536,128]{2,1,0:T(8,128)(2,1)} %bitcast.11), custom_call_target="tpu_custom_call" | custom-call | tf_op jit(solution)/shard_map/pallas_call | solution.py:28
  3.3 8.9 %collective-permute-start.4 = (bf16[12,48,128]{2,1,0:T(8,128)(2,1)S(1)}, bf16[12,48,128]{2,1,0:T(8,128)(2,1)S(1)}, u32[]{:S(2)}, u32[]{:S(2)}) collective-permute-start(bf16[12,48,128]{2,1,0:T(8,128)(2,1)S(1)} %shard_map.37.rhs.earlier), channel_id=1, source_target_pairs={{8,16},{24,32},{40,48},{56,64},{72,80},{88,96},{104,112},{120,128}... | collective-permute-start | bytes 442376 | tf_op jit(solution)/shard_map/ppermute | solution.py:208
  12.3 2.1 %collective-permute-start.6 = (bf16[12,48,128]{2,1,0:T(8,128)(2,1)S(1)}, bf16[12,48,128]{2,1,0:T(8,128)(2,1)S(1)}, u32[]{:S(2)}, u32[]{:S(2)}) collective-permute-start(bf16[12,48,128]{2,1,0:T(8,128)(2,1)S(1)} %shard_map.37.rhs.earlier), channel_id=1, source_target_pairs={{1,2},{3,4},{5,6},{7,0},{2,1},{4,3},{6,5},{0,7},{9,10},{11,12},{13... | collective-permute-start | bytes 442376 | tf_op jit(solution)/shard_map/ppermute | solution.py:206
  14.3 0.8 collective-permute-start.7
  15.2 3.5 %shard_map.38 = (f32[12,48,128]{2,1,0:T(8,128)S(1)}, bf16[12,512,128]{2,1,0:T(8,128)(2,1)S(1)}, bf16[12,128,128]{2,1,0:T(8,128)(2,1)S(1)}) custom-call(s32[5]{0:T(128)S(1)} %stack.23.slots, bf16[12,48,128]{2,1,0:T(8,128)(2,1)S(1)} %shard_map.37.rhs.earlier, bf16[9,12,128,128]{3,2,1,0:T(8,128)(2,1)} %bitcast.9), custom_call_target="tpu_custom_call" | custom-call | flops 94371840 | tf_op jit(solution)/shard_map/pallas_call | solution.py:28
  19.2 106.9 %while.10 = (s32[]{:T(128)}, bf16[12,48,128]{2,1,0:T(8,128)(2,1)S(1)}, bf16[12,48,128]{2,1,0:T(8,128)(2,1)S(1)}, bf16[12,128,128]{2,1,0:T(8,128)(2,1)S(1)}, bf16...) while((s32[]{:T(128)}, bf16[12,48,128]{2,1,0:T(8,128)(2,1)S(1)}, ...), condition=%wide.region_1.2_spmd, body=%wide.region_0.1_spmd.sunk | while | flops 169869312 | bytes 2359533 | solution.py:254
  19.2 1.6 %collective-permute-start = (bf16[12,48,128]{2,1,0:T(8,128)(2,1)S(1)}, bf16[12,48,128]{2,1,0:T(8,128)(2,1)S(1)}, u32[]{:S(2)}, u32[]{:S(2)}) collective-permute-start(bf16[12,48,128]{2,1,0:T(8,128)(2,1)S(1)} %get-tuple-element.113.value.earlier), channel_id=1, source_target_pairs={{8,16},{24,32},{40,48},{56,64},{72,80},{88,96},{104,112},{120,128}... | collective-permute-start | bytes 442376 | tf_op jit(solution)/shard_map/while/body/eval_jaxpr/ppermute | solution.py:208
  20.8 2.9 %collective-permute-start.2 = (bf16[12,48,128]{2,1,0:T(8,128)(2,1)S(1)}, bf16[12,48,128]{2,1,0:T(8,128)(2,1)S(1)}, u32[]{:S(2)}, u32[]{:S(2)}) collective-permute-start(bf16[12,48,128]{2,1,0:T(8,128)(2,1)S(1)} %get-tuple-element.113.value.earlier), channel_id=1, source_target_pairs={{1,2},{3,4},{5,6},{7,0},{2,1},{4,3},{6,5},{0,7},{9,10},{11,12},{13... | collective-permute-start | bytes 442376 | tf_op jit(solution)/shard_map/while/body/eval_jaxpr/ppermute | solution.py:206
  23.8 1.9 %eval_jaxpr.5.part = f32[12,48,128]{2,1,0:T(8,128)S(1)} custom-call(bf16[12,48,128]{2,1,0:T(8,128)(2,1)S(1)} %get-tuple-element.121.rhs, bf16[12,48,128]{2,1,0:T(8,128)(2,1)S(1)} %get-tuple-element.113.value.earlier, bf16[12,128,128]{2,1,0:T(8,128)(2,1)S(1)} %get-tuple-element.122.kept, bf16[9,12,128,128]{3,2,1,0:T(8,128)(2,1)} %get-tuple-element.123.links), custom_call_target="tpu_custom_call" | custom-call | flops 94371840 | tf_op jit(solution)/shard_map/while/body/eval_jaxpr/pallas_call | solution.py:28
  25.7 2.2 %collective-permute-done.arrived.a = bf16[12,48,128]{2,1,0:T(8,128)(2,1)S(1)} collective-permute-done((bf16[12,48,128]{2,1,0:T(8,128)(2,1)S(1)}, bf16[12,48,128]{2,1,0:T(8,128)(2,1)S(1)}, u32[]{:S(2)}, u32[]{:S(2)}) %collective-permute-start) | collective-permute-done | bytes 147488 | tf_op jit(solution)/shard_map/while/body/eval_jaxpr/ppermute | solution.py:208
  28.3 1.2 collective-permute-start
  29.5 3.2 %collective-permute-start.2 = (bf16[12,48,128]{2,1,0:T(8,128)(2,1)S(1)}, bf16[12,48,128]{2,1,0:T(8,128)(2,1)S(1)}, u32[]{:S(2)}, u32[]{:S(2)}) collective-permute-start(bf16[12,48,128]{2,1,0:T(8,128)(2,1)S(1)} %get-tuple-element.113.value.earlier), channel_id=1, source_target_pairs={{1,2},{3,4},{5,6},{7,0},{2,1},{4,3},{6,5},{0,7},{9,10},{11,12},{13... | collective-permute-start | bytes 442376 | tf_op jit(solution)/shard_map/while/body/eval_jaxpr/ppermute | solution.py:206
  32.8 1.9 %eval_jaxpr.5.part = f32[12,48,128]{2,1,0:T(8,128)S(1)} custom-call(bf16[12,48,128]{2,1,0:T(8,128)(2,1)S(1)} %get-tuple-element.121.rhs, bf16[12,48,128]{2,1,0:T(8,128)(2,1)S(1)} %get-tuple-element.113.value.earlier, bf16[12,128,128]{2,1,0:T(8,128)(2,1)S(1)} %get-tuple-element.122.kept, bf16[9,12,128,128]{3,2,1,0:T(8,128)(2,1)} %get-tuple-element.123.links), custom_call_target="tpu_custom_call" | custom-call | flops 94371840 | tf_op jit(solution)/shard_map/while/body/eval_jaxpr/pallas_call | solution.py:28
  34.7 1.3 collective-permute-done.arrived.a
  36.5 2.1 %collective-permute-start = (bf16[12,48,128]{2,1,0:T(8,128)(2,1)S(1)}, bf16[12,48,128]{2,1,0:T(8,128)(2,1)S(1)}, u32[]{:S(2)}, u32[]{:S(2)}) collective-permute-start(bf16[12,48,128]{2,1,0:T(8,128)(2,1)S(1)} %get-tuple-element.113.value.earlier), channel_id=1, source_target_pairs={{8,16},{24,32},{40,48},{56,64},{72,80},{88,96},{104,112},{120,128}... | collective-permute-start | bytes 442376 | tf_op jit(solution)/shard_map/while/body/eval_jaxpr/ppermute | solution.py:208
  38.5 3.2 %collective-permute-start.2 = (bf16[12,48,128]{2,1,0:T(8,128)(2,1)S(1)}, bf16[12,48,128]{2,1,0:T(8,128)(2,1)S(1)}, u32[]{:S(2)}, u32[]{:S(2)}) collective-permute-start(bf16[12,48,128]{2,1,0:T(8,128)(2,1)S(1)} %get-tuple-element.113.value.earlier), channel_id=1, source_target_pairs={{1,2},{3,4},{5,6},{7,0},{2,1},{4,3},{6,5},{0,7},{9,10},{11,12},{13... | collective-permute-start | bytes 442376 | tf_op jit(solution)/shard_map/while/body/eval_jaxpr/ppermute | solution.py:206
  41.7 1.9 %eval_jaxpr.5.part = f32[12,48,128]{2,1,0:T(8,128)S(1)} custom-call(bf16[12,48,128]{2,1,0:T(8,128)(2,1)S(1)} %get-tuple-element.121.rhs, bf16[12,48,128]{2,1,0:T(8,128)(2,1)S(1)} %get-tuple-element.113.value.earlier, bf16[12,128,128]{2,1,0:T(8,128)(2,1)S(1)} %get-tuple-element.122.kept, bf16[9,12,128,128]{3,2,1,0:T(8,128)(2,1)} %get-tuple-element.123.links), custom_call_target="tpu_custom_call" | custom-call | flops 94371840 | tf_op jit(solution)/shard_map/while/body/eval_jaxpr/pallas_call | solution.py:28
  43.9 1.0 collective-permute-done.2.arrived.c
  45.3 2.1 %collective-permute-start = (bf16[12,48,128]{2,1,0:T(8,128)(2,1)S(1)}, bf16[12,48,128]{2,1,0:T(8,128)(2,1)S(1)}, u32[]{:S(2)}, u32[]{:S(2)}) collective-permute-start(bf16[12,48,128]{2,1,0:T(8,128)(2,1)S(1)} %get-tuple-element.113.value.earlier), channel_id=1, source_target_pairs={{8,16},{24,32},{40,48},{56,64},{72,80},{88,96},{104,112},{120,128}... | collective-permute-start | bytes 442376 | tf_op jit(solution)/shard_map/while/body/eval_jaxpr/ppermute | solution.py:208
  47.4 3.4 %collective-permute-start.2 = (bf16[12,48,128]{2,1,0:T(8,128)(2,1)S(1)}, bf16[12,48,128]{2,1,0:T(8,128)(2,1)S(1)}, u32[]{:S(2)}, u32[]{:S(2)}) collective-permute-start(bf16[12,48,128]{2,1,0:T(8,128)(2,1)S(1)} %get-tuple-element.113.value.earlier), channel_id=1, source_target_pairs={{1,2},{3,4},{5,6},{7,0},{2,1},{4,3},{6,5},{0,7},{9,10},{11,12},{13... | collective-permute-start | bytes 442376 | tf_op jit(solution)/shard_map/while/body/eval_jaxpr/ppermute | solution.py:206
  50.7 1.9 %eval_jaxpr.5.part = f32[12,48,128]{2,1,0:T(8,128)S(1)} custom-call(bf16[12,48,128]{2,1,0:T(8,128)(2,1)S(1)} %get-tuple-element.121.rhs, bf16[12,48,128]{2,1,0:T(8,128)(2,1)S(1)} %get-tuple-element.113.value.earlier, bf16[12,128,128]{2,1,0:T(8,128)(2,1)S(1)} %get-tuple-element.122.kept, bf16[9,12,128,128]{3,2,1,0:T(8,128)(2,1)} %get-tuple-element.123.links), custom_call_target="tpu_custom_call" | custom-call | flops 94371840 | tf_op jit(solution)/shard_map/while/body/eval_jaxpr/pallas_call | solution.py:28
  52.7 1.1 collective-permute-done.2.arrived.c
  54.2 2.1 %collective-permute-start = (bf16[12,48,128]{2,1,0:T(8,128)(2,1)S(1)}, bf16[12,48,128]{2,1,0:T(8,128)(2,1)S(1)}, u32[]{:S(2)}, u32[]{:S(2)}) collective-permute-start(bf16[12,48,128]{2,1,0:T(8,128)(2,1)S(1)} %get-tuple-element.113.value.earlier), channel_id=1, source_target_pairs={{8,16},{24,32},{40,48},{56,64},{72,80},{88,96},{104,112},{120,128}... | collective-permute-start | bytes 442376 | tf_op jit(solution)/shard_map/while/body/eval_jaxpr/ppermute | solution.py:208
  56.4 3.4 %collective-permute-start.2 = (bf16[12,48,128]{2,1,0:T(8,128)(2,1)S(1)}, bf16[12,48,128]{2,1,0:T(8,128)(2,1)S(1)}, u32[]{:S(2)}, u32[]{:S(2)}) collective-permute-start(bf16[12,48,128]{2,1,0:T(8,128)(2,1)S(1)} %get-tuple-element.113.value.earlier), channel_id=1, source_target_pairs={{1,2},{3,4},{5,6},{7,0},{2,1},{4,3},{6,5},{0,7},{9,10},{11,12},{13... | collective-permute-start | bytes 442376 | tf_op jit(solution)/shard_map/while/body/eval_jaxpr/ppermute | solution.py:206
  59.7 1.9 %eval_jaxpr.5.part = f32[12,48,128]{2,1,0:T(8,128)S(1)} custom-call(bf16[12,48,128]{2,1,0:T(8,128)(2,1)S(1)} %get-tuple-element.121.rhs, bf16[12,48,128]{2,1,0:T(8,128)(2,1)S(1)} %get-tuple-element.113.value.earlier, bf16[12,128,128]{2,1,0:T(8,128)(2,1)S(1)} %get-tuple-element.122.kept, bf16[9,12,128,128]{3,2,1,0:T(8,128)(2,1)} %get-tuple-element.123.links), custom_call_target="tpu_custom_call" | custom-call | flops 94371840 | tf_op jit(solution)/shard_map/while/body/eval_jaxpr/pallas_call | solution.py:28
  61.7 1.1 collective-permute-done.2.arrived.c
  63.2 2.1 %collective-permute-start = (bf16[12,48,128]{2,1,0:T(8,128)(2,1)S(1)}, bf16[12,48,128]{2,1,0:T(8,128)(2,1)S(1)}, u32[]{:S(2)}, u32[]{:S(2)}) collective-permute-start(bf16[12,48,128]{2,1,0:T(8,128)(2,1)S(1)} %get-tuple-element.113.value.earlier), channel_id=1, source_target_pairs={{8,16},{24,32},{40,48},{56,64},{72,80},{88,96},{104,112},{120,128}... | collective-permute-start | bytes 442376 | tf_op jit(solution)/shard_map/while/body/eval_jaxpr/ppermute | solution.py:208
  65.3 3.4 %collective-permute-start.2 = (bf16[12,48,128]{2,1,0:T(8,128)(2,1)S(1)}, bf16[12,48,128]{2,1,0:T(8,128)(2,1)S(1)}, u32[]{:S(2)}, u32[]{:S(2)}) collective-permute-start(bf16[12,48,128]{2,1,0:T(8,128)(2,1)S(1)} %get-tuple-element.113.value.earlier), channel_id=1, source_target_pairs={{1,2},{3,4},{5,6},{7,0},{2,1},{4,3},{6,5},{0,7},{9,10},{11,12},{13... | collective-permute-start | bytes 442376 | tf_op jit(solution)/shard_map/while/body/eval_jaxpr/ppermute | solution.py:206
  68.7 1.9 %eval_jaxpr.5.part = f32[12,48,128]{2,1,0:T(8,128)S(1)} custom-call(bf16[12,48,128]{2,1,0:T(8,128)(2,1)S(1)} %get-tuple-element.121.rhs, bf16[12,48,128]{2,1,0:T(8,128)(2,1)S(1)} %get-tuple-element.113.value.earlier, bf16[12,128,128]{2,1,0:T(8,128)(2,1)S(1)} %get-tuple-element.122.kept, bf16[9,12,128,128]{3,2,1,0:T(8,128)(2,1)} %get-tuple-element.123.links), custom_call_target="tpu_custom_call" | custom-call | flops 94371840 | tf_op jit(solution)/shard_map/while/body/eval_jaxpr/pallas_call | solution.py:28
  70.7 1.1 collective-permute-done.2.arrived.c
  72.2 2.1 %collective-permute-start = (bf16[12,48,128]{2,1,0:T(8,128)(2,1)S(1)}, bf16[12,48,128]{2,1,0:T(8,128)(2,1)S(1)}, u32[]{:S(2)}, u32[]{:S(2)}) collective-permute-start(bf16[12,48,128]{2,1,0:T(8,128)(2,1)S(1)} %get-tuple-element.113.value.earlier), channel_id=1, source_target_pairs={{8,16},{24,32},{40,48},{56,64},{72,80},{88,96},{104,112},{120,128}... | collective-permute-start | bytes 442376 | tf_op jit(solution)/shard_map/while/body/eval_jaxpr/ppermute | solution.py:208
  74.3 3.4 %collective-permute-start.2 = (bf16[12,48,128]{2,1,0:T(8,128)(2,1)S(1)}, bf16[12,48,128]{2,1,0:T(8,128)(2,1)S(1)}, u32[]{:S(2)}, u32[]{:S(2)}) collective-permute-start(bf16[12,48,128]{2,1,0:T(8,128)(2,1)S(1)} %get-tuple-element.113.value.earlier), channel_id=1, source_target_pairs={{1,2},{3,4},{5,6},{7,0},{2,1},{4,3},{6,5},{0,7},{9,10},{11,12},{13... | collective-permute-start | bytes 442376 | tf_op jit(solution)/shard_map/while/body/eval_jaxpr/ppermute | solution.py:206
  77.7 1.9 %eval_jaxpr.5.part = f32[12,48,128]{2,1,0:T(8,128)S(1)} custom-call(bf16[12,48,128]{2,1,0:T(8,128)(2,1)S(1)} %get-tuple-element.121.rhs, bf16[12,48,128]{2,1,0:T(8,128)(2,1)S(1)} %get-tuple-element.113.value.earlier, bf16[12,128,128]{2,1,0:T(8,128)(2,1)S(1)} %get-tuple-element.122.kept, bf16[9,12,128,128]{3,2,1,0:T(8,128)(2,1)} %get-tuple-element.123.links), custom_call_target="tpu_custom_call" | custom-call | flops 94371840 | tf_op jit(solution)/shard_map/while/body/eval_jaxpr/pallas_call | solution.py:28
  79.7 1.1 collective-permute-done.2.arrived.c
  81.2 2.1 %collective-permute-start = (bf16[12,48,128]{2,1,0:T(8,128)(2,1)S(1)}, bf16[12,48,128]{2,1,0:T(8,128)(2,1)S(1)}, u32[]{:S(2)}, u32[]{:S(2)}) collective-permute-start(bf16[12,48,128]{2,1,0:T(8,128)(2,1)S(1)} %get-tuple-element.113.value.earlier), channel_id=1, source_target_pairs={{8,16},{24,32},{40,48},{56,64},{72,80},{88,96},{104,112},{120,128}... | collective-permute-start | bytes 442376 | tf_op jit(solution)/shard_map/while/body/eval_jaxpr/ppermute | solution.py:208
  83.3 3.3 %collective-permute-start.2 = (bf16[12,48,128]{2,1,0:T(8,128)(2,1)S(1)}, bf16[12,48,128]{2,1,0:T(8,128)(2,1)S(1)}, u32[]{:S(2)}, u32[]{:S(2)}) collective-permute-start(bf16[12,48,128]{2,1,0:T(8,128)(2,1)S(1)} %get-tuple-element.113.value.earlier), channel_id=1, source_target_pairs={{1,2},{3,4},{5,6},{7,0},{2,1},{4,3},{6,5},{0,7},{9,10},{11,12},{13... | collective-permute-start | bytes 442376 | tf_op jit(solution)/shard_map/while/body/eval_jaxpr/ppermute | solution.py:206
  86.7 1.9 %eval_jaxpr.5.part = f32[12,48,128]{2,1,0:T(8,128)S(1)} custom-call(bf16[12,48,128]{2,1,0:T(8,128)(2,1)S(1)} %get-tuple-element.121.rhs, bf16[12,48,128]{2,1,0:T(8,128)(2,1)S(1)} %get-tuple-element.113.value.earlier, bf16[12,128,128]{2,1,0:T(8,128)(2,1)S(1)} %get-tuple-element.122.kept, bf16[9,12,128,128]{3,2,1,0:T(8,128)(2,1)} %get-tuple-element.123.links), custom_call_target="tpu_custom_call" | custom-call | flops 94371840 | tf_op jit(solution)/shard_map/while/body/eval_jaxpr/pallas_call | solution.py:28
  88.7 1.1 collective-permute-done.2.arrived.c
  90.2 2.1 %collective-permute-start = (bf16[12,48,128]{2,1,0:T(8,128)(2,1)S(1)}, bf16[12,48,128]{2,1,0:T(8,128)(2,1)S(1)}, u32[]{:S(2)}, u32[]{:S(2)}) collective-permute-start(bf16[12,48,128]{2,1,0:T(8,128)(2,1)S(1)} %get-tuple-element.113.value.earlier), channel_id=1, source_target_pairs={{8,16},{24,32},{40,48},{56,64},{72,80},{88,96},{104,112},{120,128}... | collective-permute-start | bytes 442376 | tf_op jit(solution)/shard_map/while/body/eval_jaxpr/ppermute | solution.py:208
  92.3 3.3 %collective-permute-start.2 = (bf16[12,48,128]{2,1,0:T(8,128)(2,1)S(1)}, bf16[12,48,128]{2,1,0:T(8,128)(2,1)S(1)}, u32[]{:S(2)}, u32[]{:S(2)}) collective-permute-start(bf16[12,48,128]{2,1,0:T(8,128)(2,1)S(1)} %get-tuple-element.113.value.earlier), channel_id=1, source_target_pairs={{1,2},{3,4},{5,6},{7,0},{2,1},{4,3},{6,5},{0,7},{9,10},{11,12},{13... | collective-permute-start | bytes 442376 | tf_op jit(solution)/shard_map/while/body/eval_jaxpr/ppermute | solution.py:206
  95.7 1.9 %eval_jaxpr.5.part = f32[12,48,128]{2,1,0:T(8,128)S(1)} custom-call(bf16[12,48,128]{2,1,0:T(8,128)(2,1)S(1)} %get-tuple-element.121.rhs, bf16[12,48,128]{2,1,0:T(8,128)(2,1)S(1)} %get-tuple-element.113.value.earlier, bf16[12,128,128]{2,1,0:T(8,128)(2,1)S(1)} %get-tuple-element.122.kept, bf16[9,12,128,128]{3,2,1,0:T(8,128)(2,1)} %get-tuple-element.123.links), custom_call_target="tpu_custom_call" | custom-call | flops 94371840 | tf_op jit(solution)/shard_map/while/body/eval_jaxpr/pallas_call | solution.py:28
  97.6 1.1 collective-permute-done.2.arrived.c
  99.2 2.1 %collective-permute-start = (bf16[12,48,128]{2,1,0:T(8,128)(2,1)S(1)}, bf16[12,48,128]{2,1,0:T(8,128)(2,1)S(1)}, u32[]{:S(2)}, u32[]{:S(2)}) collective-permute-start(bf16[12,48,128]{2,1,0:T(8,128)(2,1)S(1)} %get-tuple-element.113.value.earlier), channel_id=1, source_target_pairs={{8,16},{24,32},{40,48},{56,64},{72,80},{88,96},{104,112},{120,128}... | collective-permute-start | bytes 442376 | tf_op jit(solution)/shard_map/while/body/eval_jaxpr/ppermute | solution.py:208
  101.3 3.3 %collective-permute-start.2 = (bf16[12,48,128]{2,1,0:T(8,128)(2,1)S(1)}, bf16[12,48,128]{2,1,0:T(8,128)(2,1)S(1)}, u32[]{:S(2)}, u32[]{:S(2)}) collective-permute-start(bf16[12,48,128]{2,1,0:T(8,128)(2,1)S(1)} %get-tuple-element.113.value.earlier), channel_id=1, source_target_pairs={{1,2},{3,4},{5,6},{7,0},{2,1},{4,3},{6,5},{0,7},{9,10},{11,12},{13... | collective-permute-start | bytes 442376 | tf_op jit(solution)/shard_map/while/body/eval_jaxpr/ppermute | solution.py:206
  104.6 1.9 %eval_jaxpr.5.part = f32[12,48,128]{2,1,0:T(8,128)S(1)} custom-call(bf16[12,48,128]{2,1,0:T(8,128)(2,1)S(1)} %get-tuple-element.121.rhs, bf16[12,48,128]{2,1,0:T(8,128)(2,1)S(1)} %get-tuple-element.113.value.earlier, bf16[12,128,128]{2,1,0:T(8,128)(2,1)S(1)} %get-tuple-element.122.kept, bf16[9,12,128,128]{3,2,1,0:T(8,128)(2,1)} %get-tuple-element.123.links), custom_call_target="tpu_custom_call" | custom-call | flops 94371840 | tf_op jit(solution)/shard_map/while/body/eval_jaxpr/pallas_call | solution.py:28
  106.6 1.1 collective-permute-done.2.arrived.c
  108.2 2.1 %collective-permute-start = (bf16[12,48,128]{2,1,0:T(8,128)(2,1)S(1)}, bf16[12,48,128]{2,1,0:T(8,128)(2,1)S(1)}, u32[]{:S(2)}, u32[]{:S(2)}) collective-permute-start(bf16[12,48,128]{2,1,0:T(8,128)(2,1)S(1)} %get-tuple-element.113.value.earlier), channel_id=1, source_target_pairs={{8,16},{24,32},{40,48},{56,64},{72,80},{88,96},{104,112},{120,128}... | collective-permute-start | bytes 442376 | tf_op jit(solution)/shard_map/while/body/eval_jaxpr/ppermute | solution.py:208
  110.3 3.3 %collective-permute-start.2 = (bf16[12,48,128]{2,1,0:T(8,128)(2,1)S(1)}, bf16[12,48,128]{2,1,0:T(8,128)(2,1)S(1)}, u32[]{:S(2)}, u32[]{:S(2)}) collective-permute-start(bf16[12,48,128]{2,1,0:T(8,128)(2,1)S(1)} %get-tuple-element.113.value.earlier), channel_id=1, source_target_pairs={{1,2},{3,4},{5,6},{7,0},{2,1},{4,3},{6,5},{0,7},{9,10},{11,12},{13... | collective-permute-start | bytes 442376 | tf_op jit(solution)/shard_map/while/body/eval_jaxpr/ppermute | solution.py:206
  113.6 1.9 %eval_jaxpr.5.part = f32[12,48,128]{2,1,0:T(8,128)S(1)} custom-call(bf16[12,48,128]{2,1,0:T(8,128)(2,1)S(1)} %get-tuple-element.121.rhs, bf16[12,48,128]{2,1,0:T(8,128)(2,1)S(1)} %get-tuple-element.113.value.earlier, bf16[12,128,128]{2,1,0:T(8,128)(2,1)S(1)} %get-tuple-element.122.kept, bf16[9,12,128,128]{3,2,1,0:T(8,128)(2,1)} %get-tuple-element.123.links), custom_call_target="tpu_custom_call" | custom-call | flops 94371840 | tf_op jit(solution)/shard_map/while/body/eval_jaxpr/pallas_call | solution.py:28
  115.6 1.1 collective-permute-done.2.arrived.c
  117.2 2.1 %collective-permute-start = (bf16[12,48,128]{2,1,0:T(8,128)(2,1)S(1)}, bf16[12,48,128]{2,1,0:T(8,128)(2,1)S(1)}, u32[]{:S(2)}, u32[]{:S(2)}) collective-permute-start(bf16[12,48,128]{2,1,0:T(8,128)(2,1)S(1)} %get-tuple-element.113.value.earlier), channel_id=1, source_target_pairs={{8,16},{24,32},{40,48},{56,64},{72,80},{88,96},{104,112},{120,128}... | collective-permute-start | bytes 442376 | tf_op jit(solution)/shard_map/while/body/eval_jaxpr/ppermute | solution.py:208
  119.3 3.3 %collective-permute-start.2 = (bf16[12,48,128]{2,1,0:T(8,128)(2,1)S(1)}, bf16[12,48,128]{2,1,0:T(8,128)(2,1)S(1)}, u32[]{:S(2)}, u32[]{:S(2)}) collective-permute-start(bf16[12,48,128]{2,1,0:T(8,128)(2,1)S(1)} %get-tuple-element.113.value.earlier), channel_id=1, source_target_pairs={{1,2},{3,4},{5,6},{7,0},{2,1},{4,3},{6,5},{0,7},{9,10},{11,12},{13... | collective-permute-start | bytes 442376 | tf_op jit(solution)/shard_map/while/body/eval_jaxpr/ppermute | solution.py:206
  122.6 1.9 %eval_jaxpr.5.part = f32[12,48,128]{2,1,0:T(8,128)S(1)} custom-call(bf16[12,48,128]{2,1,0:T(8,128)(2,1)S(1)} %get-tuple-element.121.rhs, bf16[12,48,128]{2,1,0:T(8,128)(2,1)S(1)} %get-tuple-element.113.value.earlier, bf16[12,128,128]{2,1,0:T(8,128)(2,1)S(1)} %get-tuple-element.122.kept, bf16[9,12,128,128]{3,2,1,0:T(8,128)(2,1)} %get-tuple-element.123.links), custom_call_target="tpu_custom_call" | custom-call | flops 94371840 | tf_op jit(solution)/shard_map/while/body/eval_jaxpr/pallas_call | solution.py:28
  124.6 1.1 collective-permute-done.2.arrived.c
  126.1 2.1 %collective-permute-start.8 = (bf16[12,48,128]{2,1,0:T(8,128)(2,1)S(1)}, bf16[12,48,128]{2,1,0:T(8,128)(2,1)S(1)}, u32[]{:S(2)}, u32[]{:S(2)}) collective-permute-start(bf16[12,48,128]{2,1,0:T(8,128)(2,1)S(1)} %get-tuple-element.49.value.earlier), channel_id=1, source_target_pairs={{8,16},{24,32},{40,48},{56,64},{72,80},{88,96},{104,112},{120,128}... | collective-permute-start | bytes 442376 | tf_op jit(solution)/shard_map/ppermute | solution.py:208
  128.3 3.3 %collective-permute-start.10 = (bf16[12,48,128]{2,1,0:T(8,128)(2,1)S(1)}, bf16[12,48,128]{2,1,0:T(8,128)(2,1)S(1)}, u32[]{:S(2)}, u32[]{:S(2)}) collective-permute-start(bf16[12,48,128]{2,1,0:T(8,128)(2,1)S(1)} %get-tuple-element.49.value.earlier), channel_id=1, source_target_pairs={{1,2},{3,4},{5,6},{7,0},{2,1},{4,3},{6,5},{0,7},{9,10},{11,12},{13... | collective-permute-start | bytes 442376 | tf_op jit(solution)/shard_map/ppermute | solution.py:206
  131.6 2.8 %shard_map.43 = (f32[12,48,128]{2,1,0:T(8,128)S(1)}, bf16[4,128,1536]{2,1,0:T(8,128)(2,1)S(1)}) custom-call(bf16[12,48,128]{2,1,0:T(8,128)(2,1)S(1)} %get-tuple-element.140, bf16[12,48,128]{2,1,0:T(8,128)(2,1)S(1)} %get-tuple-element.49.value.earlier, bf16[12,128,128]{2,1,0:T(8,128)(2,1)S(1)} %get-tuple-element.127, ...), custom_call_target="tpu_custom_call" | custom-call | flops 94371840 | tf_op jit(solution)/shard_map/pallas_call | solution.py:28
  135.1 2.3 %collective-permute-start.12 = (bf16[12,48,128]{2,1,0:T(8,128)(2,1)S(1)}, bf16[12,48,128]{2,1,0:T(8,128)(2,1)S(1)}, u32[]{:S(2)}, u32[]{:S(2)}) collective-permute-start(bf16[12,48,128]{2,1,0:T(8,128)(2,1)S(1)} %shard_map.47.value.earlier), channel_id=1, source_target_pairs={{8,16},{24,32},{40,48},{56,64},{72,80},{88,96},{104,112},{120,128}... | collective-permute-start | bytes 442376 | tf_op jit(solution)/shard_map/ppermute | solution.py:208
  137.4 3.3 %collective-permute-start.14 = (bf16[12,48,128]{2,1,0:T(8,128)(2,1)S(1)}, bf16[12,48,128]{2,1,0:T(8,128)(2,1)S(1)}, u32[]{:S(2)}, u32[]{:S(2)}) collective-permute-start(bf16[12,48,128]{2,1,0:T(8,128)(2,1)S(1)} %shard_map.47.value.earlier), channel_id=1, source_target_pairs={{1,2},{3,4},{5,6},{7,0},{2,1},{4,3},{6,5},{0,7},{9,10},{11,12},{13... | collective-permute-start | bytes 442376 | tf_op jit(solution)/shard_map/ppermute | solution.py:206
  140.8 2.6 %shard_map.48 = (f32[12,48,128]{2,1,0:T(8,128)S(1)}, bf16[4,128,1536]{2,1,0:T(8,128)(2,1)S(1)}) custom-call(bf16[12,48,128]{2,1,0:T(8,128)(2,1)S(1)} %get-tuple-element.140, bf16[12,48,128]{2,1,0:T(8,128)(2,1)S(1)} %shard_map.47.value.earlier, bf16[12,128,128]{2,1,0:T(8,128)(2,1)S(1)} %get-tuple-element.127, bf16[9,12,128,128]{3,2,1,0:T(8,128)(2,1)} %get-tuple-element.169, ...), custom_call_target="tpu_custom_call" | custom-call | flops 94371840 | tf_op jit(solution)/shard_map/pallas_call | solution.py:28
  144.3 2.1 %collective-permute-start.16 = (bf16[12,48,128]{2,1,0:T(8,128)(2,1)S(1)}, bf16[12,48,128]{2,1,0:T(8,128)(2,1)S(1)}, u32[]{:S(2)}, u32[]{:S(2)}) collective-permute-start(bf16[12,48,128]{2,1,0:T(8,128)(2,1)S(1)} %shard_map.52.value.earlier), channel_id=1, source_target_pairs={{8,16},{24,32},{40,48},{56,64},{72,80},{88,96},{104,112},{120,128}... | collective-permute-start | bytes 442376 | tf_op jit(solution)/shard_map/ppermute | solution.py:208
  146.4 3.3 %collective-permute-start.18 = (bf16[12,48,128]{2,1,0:T(8,128)(2,1)S(1)}, bf16[12,48,128]{2,1,0:T(8,128)(2,1)S(1)}, u32[]{:S(2)}, u32[]{:S(2)}) collective-permute-start(bf16[12,48,128]{2,1,0:T(8,128)(2,1)S(1)} %shard_map.52.value.earlier), channel_id=1, source_target_pairs={{1,2},{3,4},{5,6},{7,0},{2,1},{4,3},{6,5},{0,7},{9,10},{11,12},{13... | collective-permute-start | bytes 442376 | tf_op jit(solution)/shard_map/ppermute | solution.py:206
  149.7 2.6 %shard_map.53 = (f32[12,48,128]{2,1,0:T(8,128)S(1)}, bf16[4,128,1536]{2,1,0:T(8,128)(2,1)S(1)}) custom-call(bf16[12,48,128]{2,1,0:T(8,128)(2,1)S(1)} %get-tuple-element.140, bf16[12,48,128]{2,1,0:T(8,128)(2,1)S(1)} %shard_map.52.value.earlier, bf16[12,128,128]{2,1,0:T(8,128)(2,1)S(1)} %get-tuple-element.127, bf16[9,12,128,128]{3,2,1,0:T(8,128)(2,1)} %get-tuple-element.169, ...), custom_call_target="tpu_custom_call" | custom-call | flops 94371840 | tf_op jit(solution)/shard_map/pallas_call | solution.py:28
  153.2 1.5 shard_map.58
  (148 shorter events, 7.9 us)
Async XLA Ops:
  3.3 15.4 %collective-permute-start.4 = (bf16[12,48,128]{2,1,0:T(8,128)(2,1)S(1)}, bf16[12,48,128]{2,1,0:T(8,128)(2,1)S(1)}, u32[]{:S(2)}, u32[]{:S(2)}) collective-permute-start(bf16[12,48,128]{2,1,0:T(8,128)(2,1)S(1)} %shard_map.37.rhs.earlier), channel_id=1, source_target_pairs={{8,16},{24,32},{40,48},{56,64},{72,80},{88,96},{104,112},{120,128}... | collective-permute-start | bytes 442376 | tf_op jit(solution)/shard_map/ppermute | solution.py:208
  12.3 6.5 %collective-permute-start.5 = (bf16[12,48,128]{2,1,0:T(8,128)(2,1)S(1)}, bf16[12,48,128]{2,1,0:T(8,128)(2,1)S(1)}, u32[]{:S(2)}, u32[]{:S(2)}) collective-permute-start(bf16[12,48,128]{2,1,0:T(8,128)(2,1)S(1)} %shard_map.37.rhs.earlier), channel_id=1, source_target_pairs={{0,8},{16,24},{32,40},{48,56},{64,72},{80,88},{96,104},{112,120},{... | collective-permute-start | bytes 442376 | tf_op jit(solution)/shard_map/ppermute | solution.py:207
  12.3 6.5 %collective-permute-start.6 = (bf16[12,48,128]{2,1,0:T(8,128)(2,1)S(1)}, bf16[12,48,128]{2,1,0:T(8,128)(2,1)S(1)}, u32[]{:S(2)}, u32[]{:S(2)}) collective-permute-start(bf16[12,48,128]{2,1,0:T(8,128)(2,1)S(1)} %shard_map.37.rhs.earlier), channel_id=1, source_target_pairs={{1,2},{3,4},{5,6},{7,0},{2,1},{4,3},{6,5},{0,7},{9,10},{11,12},{13... | collective-permute-start | bytes 442376 | tf_op jit(solution)/shard_map/ppermute | solution.py:206
  14.3 4.5 %collective-permute-start.7 = (bf16[12,48,128]{2,1,0:T(8,128)(2,1)S(1)}, bf16[12,48,128]{2,1,0:T(8,128)(2,1)S(1)}, u32[]{:S(2)}, u32[]{:S(2)}) collective-permute-start(bf16[12,48,128]{2,1,0:T(8,128)(2,1)S(1)} %shard_map.37.rhs.earlier), channel_id=1, source_target_pairs={{0,1},{2,3},{4,5},{6,7},{1,0},{3,2},{5,4},{7,6},{8,9},{10,11},{12,... | collective-permute-start | bytes 442376 | tf_op jit(solution)/shard_map/ppermute | solution.py:205
  19.2 8.7 %collective-permute-start = (bf16[12,48,128]{2,1,0:T(8,128)(2,1)S(1)}, bf16[12,48,128]{2,1,0:T(8,128)(2,1)S(1)}, u32[]{:S(2)}, u32[]{:S(2)}) collective-permute-start(bf16[12,48,128]{2,1,0:T(8,128)(2,1)S(1)} %get-tuple-element.113.value.earlier), channel_id=1, source_target_pairs={{8,16},{24,32},{40,48},{56,64},{72,80},{88,96},{104,112},{120,128}... | collective-permute-start | bytes 442376 | tf_op jit(solution)/shard_map/while/body/eval_jaxpr/ppermute | solution.py:208
  20.8 7.0 %collective-permute-start.1 = (bf16[12,48,128]{2,1,0:T(8,128)(2,1)S(1)}, bf16[12,48,128]{2,1,0:T(8,128)(2,1)S(1)}, u32[]{:S(2)}, u32[]{:S(2)}) collective-permute-start(bf16[12,48,128]{2,1,0:T(8,128)(2,1)S(1)} %get-tuple-element.113.value.earlier), channel_id=1, source_target_pairs={{0,8},{16,24},{32,40},{48,56},{64,72},{80,88},{96,104},{112,120},{... | collective-permute-start | bytes 442376 | tf_op jit(solution)/shard_map/while/body/eval_jaxpr/ppermute | solution.py:207
  20.8 7.0 %collective-permute-start.2 = (bf16[12,48,128]{2,1,0:T(8,128)(2,1)S(1)}, bf16[12,48,128]{2,1,0:T(8,128)(2,1)S(1)}, u32[]{:S(2)}, u32[]{:S(2)}) collective-permute-start(bf16[12,48,128]{2,1,0:T(8,128)(2,1)S(1)} %get-tuple-element.113.value.earlier), channel_id=1, source_target_pairs={{1,2},{3,4},{5,6},{7,0},{2,1},{4,3},{6,5},{0,7},{9,10},{11,12},{13... | collective-permute-start | bytes 442376 | tf_op jit(solution)/shard_map/while/body/eval_jaxpr/ppermute | solution.py:206
  23.8 4.1 %collective-permute-start.3 = (bf16[12,48,128]{2,1,0:T(8,128)(2,1)S(1)}, bf16[12,48,128]{2,1,0:T(8,128)(2,1)S(1)}, u32[]{:S(2)}, u32[]{:S(2)}) collective-permute-start(bf16[12,48,128]{2,1,0:T(8,128)(2,1)S(1)} %get-tuple-element.113.value.earlier), channel_id=1, source_target_pairs={{0,1},{2,3},{4,5},{6,7},{1,0},{3,2},{5,4},{7,6},{8,9},{10,11},{12,... | collective-permute-start | bytes 442376 | tf_op jit(solution)/shard_map/while/body/eval_jaxpr/ppermute | solution.py:205
  28.3 7.7 %collective-permute-start = (bf16[12,48,128]{2,1,0:T(8,128)(2,1)S(1)}, bf16[12,48,128]{2,1,0:T(8,128)(2,1)S(1)}, u32[]{:S(2)}, u32[]{:S(2)}) collective-permute-start(bf16[12,48,128]{2,1,0:T(8,128)(2,1)S(1)} %get-tuple-element.113.value.earlier), channel_id=1, source_target_pairs={{8,16},{24,32},{40,48},{56,64},{72,80},{88,96},{104,112},{120,128}... | collective-permute-start | bytes 442376 | tf_op jit(solution)/shard_map/while/body/eval_jaxpr/ppermute | solution.py:208
  29.5 6.5 %collective-permute-start.1 = (bf16[12,48,128]{2,1,0:T(8,128)(2,1)S(1)}, bf16[12,48,128]{2,1,0:T(8,128)(2,1)S(1)}, u32[]{:S(2)}, u32[]{:S(2)}) collective-permute-start(bf16[12,48,128]{2,1,0:T(8,128)(2,1)S(1)} %get-tuple-element.113.value.earlier), channel_id=1, source_target_pairs={{0,8},{16,24},{32,40},{48,56},{64,72},{80,88},{96,104},{112,120},{... | collective-permute-start | bytes 442376 | tf_op jit(solution)/shard_map/while/body/eval_jaxpr/ppermute | solution.py:207
  29.5 6.5 %collective-permute-start.2 = (bf16[12,48,128]{2,1,0:T(8,128)(2,1)S(1)}, bf16[12,48,128]{2,1,0:T(8,128)(2,1)S(1)}, u32[]{:S(2)}, u32[]{:S(2)}) collective-permute-start(bf16[12,48,128]{2,1,0:T(8,128)(2,1)S(1)} %get-tuple-element.113.value.earlier), channel_id=1, source_target_pairs={{1,2},{3,4},{5,6},{7,0},{2,1},{4,3},{6,5},{0,7},{9,10},{11,12},{13... | collective-permute-start | bytes 442376 | tf_op jit(solution)/shard_map/while/body/eval_jaxpr/ppermute | solution.py:206
  32.7 3.3 %collective-permute-start.3 = (bf16[12,48,128]{2,1,0:T(8,128)(2,1)S(1)}, bf16[12,48,128]{2,1,0:T(8,128)(2,1)S(1)}, u32[]{:S(2)}, u32[]{:S(2)}) collective-permute-start(bf16[12,48,128]{2,1,0:T(8,128)(2,1)S(1)} %get-tuple-element.113.value.earlier), channel_id=1, source_target_pairs={{0,1},{2,3},{4,5},{6,7},{1,0},{3,2},{5,4},{7,6},{8,9},{10,11},{12,... | collective-permute-start | bytes 442376 | tf_op jit(solution)/shard_map/while/body/eval_jaxpr/ppermute | solution.py:205
  36.5 7.4 %collective-permute-start = (bf16[12,48,128]{2,1,0:T(8,128)(2,1)S(1)}, bf16[12,48,128]{2,1,0:T(8,128)(2,1)S(1)}, u32[]{:S(2)}, u32[]{:S(2)}) collective-permute-start(bf16[12,48,128]{2,1,0:T(8,128)(2,1)S(1)} %get-tuple-element.113.value.earlier), channel_id=1, source_target_pairs={{8,16},{24,32},{40,48},{56,64},{72,80},{88,96},{104,112},{120,128}... | collective-permute-start | bytes 442376 | tf_op jit(solution)/shard_map/while/body/eval_jaxpr/ppermute | solution.py:208
  38.5 5.3 %collective-permute-start.1 = (bf16[12,48,128]{2,1,0:T(8,128)(2,1)S(1)}, bf16[12,48,128]{2,1,0:T(8,128)(2,1)S(1)}, u32[]{:S(2)}, u32[]{:S(2)}) collective-permute-start(bf16[12,48,128]{2,1,0:T(8,128)(2,1)S(1)} %get-tuple-element.113.value.earlier), channel_id=1, source_target_pairs={{0,8},{16,24},{32,40},{48,56},{64,72},{80,88},{96,104},{112,120},{... | collective-permute-start | bytes 442376 | tf_op jit(solution)/shard_map/while/body/eval_jaxpr/ppermute | solution.py:207
  38.5 6.3 %collective-permute-start.2 = (bf16[12,48,128]{2,1,0:T(8,128)(2,1)S(1)}, bf16[12,48,128]{2,1,0:T(8,128)(2,1)S(1)}, u32[]{:S(2)}, u32[]{:S(2)}) collective-permute-start(bf16[12,48,128]{2,1,0:T(8,128)(2,1)S(1)} %get-tuple-element.113.value.earlier), channel_id=1, source_target_pairs={{1,2},{3,4},{5,6},{7,0},{2,1},{4,3},{6,5},{0,7},{9,10},{11,12},{13... | collective-permute-start | bytes 442376 | tf_op jit(solution)/shard_map/while/body/eval_jaxpr/ppermute | solution.py:206
  41.7 3.1 %collective-permute-start.3 = (bf16[12,48,128]{2,1,0:T(8,128)(2,1)S(1)}, bf16[12,48,128]{2,1,0:T(8,128)(2,1)S(1)}, u32[]{:S(2)}, u32[]{:S(2)}) collective-permute-start(bf16[12,48,128]{2,1,0:T(8,128)(2,1)S(1)} %get-tuple-element.113.value.earlier), channel_id=1, source_target_pairs={{0,1},{2,3},{4,5},{6,7},{1,0},{3,2},{5,4},{7,6},{8,9},{10,11},{12,... | collective-permute-start | bytes 442376 | tf_op jit(solution)/shard_map/while/body/eval_jaxpr/ppermute | solution.py:205
  45.3 7.4 %collective-permute-start = (bf16[12,48,128]{2,1,0:T(8,128)(2,1)S(1)}, bf16[12,48,128]{2,1,0:T(8,128)(2,1)S(1)}, u32[]{:S(2)}, u32[]{:S(2)}) collective-permute-start(bf16[12,48,128]{2,1,0:T(8,128)(2,1)S(1)} %get-tuple-element.113.value.earlier), channel_id=1, source_target_pairs={{8,16},{24,32},{40,48},{56,64},{72,80},{88,96},{104,112},{120,128}... | collective-permute-start | bytes 442376 | tf_op jit(solution)/shard_map/while/body/eval_jaxpr/ppermute | solution.py:208
  47.4 5.3 %collective-permute-start.1 = (bf16[12,48,128]{2,1,0:T(8,128)(2,1)S(1)}, bf16[12,48,128]{2,1,0:T(8,128)(2,1)S(1)}, u32[]{:S(2)}, u32[]{:S(2)}) collective-permute-start(bf16[12,48,128]{2,1,0:T(8,128)(2,1)S(1)} %get-tuple-element.113.value.earlier), channel_id=1, source_target_pairs={{0,8},{16,24},{32,40},{48,56},{64,72},{80,88},{96,104},{112,120},{... | collective-permute-start | bytes 442376 | tf_op jit(solution)/shard_map/while/body/eval_jaxpr/ppermute | solution.py:207
  47.4 6.5 %collective-permute-start.2 = (bf16[12,48,128]{2,1,0:T(8,128)(2,1)S(1)}, bf16[12,48,128]{2,1,0:T(8,128)(2,1)S(1)}, u32[]{:S(2)}, u32[]{:S(2)}) collective-permute-start(bf16[12,48,128]{2,1,0:T(8,128)(2,1)S(1)} %get-tuple-element.113.value.earlier), channel_id=1, source_target_pairs={{1,2},{3,4},{5,6},{7,0},{2,1},{4,3},{6,5},{0,7},{9,10},{11,12},{13... | collective-permute-start | bytes 442376 | tf_op jit(solution)/shard_map/while/body/eval_jaxpr/ppermute | solution.py:206
  50.7 3.1 %collective-permute-start.3 = (bf16[12,48,128]{2,1,0:T(8,128)(2,1)S(1)}, bf16[12,48,128]{2,1,0:T(8,128)(2,1)S(1)}, u32[]{:S(2)}, u32[]{:S(2)}) collective-permute-start(bf16[12,48,128]{2,1,0:T(8,128)(2,1)S(1)} %get-tuple-element.113.value.earlier), channel_id=1, source_target_pairs={{0,1},{2,3},{4,5},{6,7},{1,0},{3,2},{5,4},{7,6},{8,9},{10,11},{12,... | collective-permute-start | bytes 442376 | tf_op jit(solution)/shard_map/while/body/eval_jaxpr/ppermute | solution.py:205
  54.2 7.4 %collective-permute-start = (bf16[12,48,128]{2,1,0:T(8,128)(2,1)S(1)}, bf16[12,48,128]{2,1,0:T(8,128)(2,1)S(1)}, u32[]{:S(2)}, u32[]{:S(2)}) collective-permute-start(bf16[12,48,128]{2,1,0:T(8,128)(2,1)S(1)} %get-tuple-element.113.value.earlier), channel_id=1, source_target_pairs={{8,16},{24,32},{40,48},{56,64},{72,80},{88,96},{104,112},{120,128}... | collective-permute-start | bytes 442376 | tf_op jit(solution)/shard_map/while/body/eval_jaxpr/ppermute | solution.py:208
  56.3 5.3 %collective-permute-start.1 = (bf16[12,48,128]{2,1,0:T(8,128)(2,1)S(1)}, bf16[12,48,128]{2,1,0:T(8,128)(2,1)S(1)}, u32[]{:S(2)}, u32[]{:S(2)}) collective-permute-start(bf16[12,48,128]{2,1,0:T(8,128)(2,1)S(1)} %get-tuple-element.113.value.earlier), channel_id=1, source_target_pairs={{0,8},{16,24},{32,40},{48,56},{64,72},{80,88},{96,104},{112,120},{... | collective-permute-start | bytes 442376 | tf_op jit(solution)/shard_map/while/body/eval_jaxpr/ppermute | solution.py:207
  56.4 6.5 %collective-permute-start.2 = (bf16[12,48,128]{2,1,0:T(8,128)(2,1)S(1)}, bf16[12,48,128]{2,1,0:T(8,128)(2,1)S(1)}, u32[]{:S(2)}, u32[]{:S(2)}) collective-permute-start(bf16[12,48,128]{2,1,0:T(8,128)(2,1)S(1)} %get-tuple-element.113.value.earlier), channel_id=1, source_target_pairs={{1,2},{3,4},{5,6},{7,0},{2,1},{4,3},{6,5},{0,7},{9,10},{11,12},{13... | collective-permute-start | bytes 442376 | tf_op jit(solution)/shard_map/while/body/eval_jaxpr/ppermute | solution.py:206
  59.7 3.1 %collective-permute-start.3 = (bf16[12,48,128]{2,1,0:T(8,128)(2,1)S(1)}, bf16[12,48,128]{2,1,0:T(8,128)(2,1)S(1)}, u32[]{:S(2)}, u32[]{:S(2)}) collective-permute-start(bf16[12,48,128]{2,1,0:T(8,128)(2,1)S(1)} %get-tuple-element.113.value.earlier), channel_id=1, source_target_pairs={{0,1},{2,3},{4,5},{6,7},{1,0},{3,2},{5,4},{7,6},{8,9},{10,11},{12,... | collective-permute-start | bytes 442376 | tf_op jit(solution)/shard_map/while/body/eval_jaxpr/ppermute | solution.py:205
  63.2 7.4 %collective-permute-start = (bf16[12,48,128]{2,1,0:T(8,128)(2,1)S(1)}, bf16[12,48,128]{2,1,0:T(8,128)(2,1)S(1)}, u32[]{:S(2)}, u32[]{:S(2)}) collective-permute-start(bf16[12,48,128]{2,1,0:T(8,128)(2,1)S(1)} %get-tuple-element.113.value.earlier), channel_id=1, source_target_pairs={{8,16},{24,32},{40,48},{56,64},{72,80},{88,96},{104,112},{120,128}... | collective-permute-start | bytes 442376 | tf_op jit(solution)/shard_map/while/body/eval_jaxpr/ppermute | solution.py:208
  65.3 5.3 %collective-permute-start.1 = (bf16[12,48,128]{2,1,0:T(8,128)(2,1)S(1)}, bf16[12,48,128]{2,1,0:T(8,128)(2,1)S(1)}, u32[]{:S(2)}, u32[]{:S(2)}) collective-permute-start(bf16[12,48,128]{2,1,0:T(8,128)(2,1)S(1)} %get-tuple-element.113.value.earlier), channel_id=1, source_target_pairs={{0,8},{16,24},{32,40},{48,56},{64,72},{80,88},{96,104},{112,120},{... | collective-permute-start | bytes 442376 | tf_op jit(solution)/shard_map/while/body/eval_jaxpr/ppermute | solution.py:207
  65.3 6.5 %collective-permute-start.2 = (bf16[12,48,128]{2,1,0:T(8,128)(2,1)S(1)}, bf16[12,48,128]{2,1,0:T(8,128)(2,1)S(1)}, u32[]{:S(2)}, u32[]{:S(2)}) collective-permute-start(bf16[12,48,128]{2,1,0:T(8,128)(2,1)S(1)} %get-tuple-element.113.value.earlier), channel_id=1, source_target_pairs={{1,2},{3,4},{5,6},{7,0},{2,1},{4,3},{6,5},{0,7},{9,10},{11,12},{13... | collective-permute-start | bytes 442376 | tf_op jit(solution)/shard_map/while/body/eval_jaxpr/ppermute | solution.py:206
  68.7 3.1 %collective-permute-start.3 = (bf16[12,48,128]{2,1,0:T(8,128)(2,1)S(1)}, bf16[12,48,128]{2,1,0:T(8,128)(2,1)S(1)}, u32[]{:S(2)}, u32[]{:S(2)}) collective-permute-start(bf16[12,48,128]{2,1,0:T(8,128)(2,1)S(1)} %get-tuple-element.113.value.earlier), channel_id=1, source_target_pairs={{0,1},{2,3},{4,5},{6,7},{1,0},{3,2},{5,4},{7,6},{8,9},{10,11},{12,... | collective-permute-start | bytes 442376 | tf_op jit(solution)/shard_map/while/body/eval_jaxpr/ppermute | solution.py:205
  72.2 7.4 %collective-permute-start = (bf16[12,48,128]{2,1,0:T(8,128)(2,1)S(1)}, bf16[12,48,128]{2,1,0:T(8,128)(2,1)S(1)}, u32[]{:S(2)}, u32[]{:S(2)}) collective-permute-start(bf16[12,48,128]{2,1,0:T(8,128)(2,1)S(1)} %get-tuple-element.113.value.earlier), channel_id=1, source_target_pairs={{8,16},{24,32},{40,48},{56,64},{72,80},{88,96},{104,112},{120,128}... | collective-permute-start | bytes 442376 | tf_op jit(solution)/shard_map/while/body/eval_jaxpr/ppermute | solution.py:208
  74.3 5.3 %collective-permute-start.1 = (bf16[12,48,128]{2,1,0:T(8,128)(2,1)S(1)}, bf16[12,48,128]{2,1,0:T(8,128)(2,1)S(1)}, u32[]{:S(2)}, u32[]{:S(2)}) collective-permute-start(bf16[12,48,128]{2,1,0:T(8,128)(2,1)S(1)} %get-tuple-element.113.value.earlier), channel_id=1, source_target_pairs={{0,8},{16,24},{32,40},{48,56},{64,72},{80,88},{96,104},{112,120},{... | collective-permute-start | bytes 442376 | tf_op jit(solution)/shard_map/while/body/eval_jaxpr/ppermute | solution.py:207
  74.3 6.5 %collective-permute-start.2 = (bf16[12,48,128]{2,1,0:T(8,128)(2,1)S(1)}, bf16[12,48,128]{2,1,0:T(8,128)(2,1)S(1)}, u32[]{:S(2)}, u32[]{:S(2)}) collective-permute-start(bf16[12,48,128]{2,1,0:T(8,128)(2,1)S(1)} %get-tuple-element.113.value.earlier), channel_id=1, source_target_pairs={{1,2},{3,4},{5,6},{7,0},{2,1},{4,3},{6,5},{0,7},{9,10},{11,12},{13... | collective-permute-start | bytes 442376 | tf_op jit(solution)/shard_map/while/body/eval_jaxpr/ppermute | solution.py:206
  77.7 3.1 %collective-permute-start.3 = (bf16[12,48,128]{2,1,0:T(8,128)(2,1)S(1)}, bf16[12,48,128]{2,1,0:T(8,128)(2,1)S(1)}, u32[]{:S(2)}, u32[]{:S(2)}) collective-permute-start(bf16[12,48,128]{2,1,0:T(8,128)(2,1)S(1)} %get-tuple-element.113.value.earlier), channel_id=1, source_target_pairs={{0,1},{2,3},{4,5},{6,7},{1,0},{3,2},{5,4},{7,6},{8,9},{10,11},{12,... | collective-permute-start | bytes 442376 | tf_op jit(solution)/shard_map/while/body/eval_jaxpr/ppermute | solution.py:205
  81.2 7.4 %collective-permute-start = (bf16[12,48,128]{2,1,0:T(8,128)(2,1)S(1)}, bf16[12,48,128]{2,1,0:T(8,128)(2,1)S(1)}, u32[]{:S(2)}, u32[]{:S(2)}) collective-permute-start(bf16[12,48,128]{2,1,0:T(8,128)(2,1)S(1)} %get-tuple-element.113.value.earlier), channel_id=1, source_target_pairs={{8,16},{24,32},{40,48},{56,64},{72,80},{88,96},{104,112},{120,128}... | collective-permute-start | bytes 442376 | tf_op jit(solution)/shard_map/while/body/eval_jaxpr/ppermute | solution.py:208
  83.3 5.3 %collective-permute-start.1 = (bf16[12,48,128]{2,1,0:T(8,128)(2,1)S(1)}, bf16[12,48,128]{2,1,0:T(8,128)(2,1)S(1)}, u32[]{:S(2)}, u32[]{:S(2)}) collective-permute-start(bf16[12,48,128]{2,1,0:T(8,128)(2,1)S(1)} %get-tuple-element.113.value.earlier), channel_id=1, source_target_pairs={{0,8},{16,24},{32,40},{48,56},{64,72},{80,88},{96,104},{112,120},{... | collective-permute-start | bytes 442376 | tf_op jit(solution)/shard_map/while/body/eval_jaxpr/ppermute | solution.py:207
  83.3 6.5 %collective-permute-start.2 = (bf16[12,48,128]{2,1,0:T(8,128)(2,1)S(1)}, bf16[12,48,128]{2,1,0:T(8,128)(2,1)S(1)}, u32[]{:S(2)}, u32[]{:S(2)}) collective-permute-start(bf16[12,48,128]{2,1,0:T(8,128)(2,1)S(1)} %get-tuple-element.113.value.earlier), channel_id=1, source_target_pairs={{1,2},{3,4},{5,6},{7,0},{2,1},{4,3},{6,5},{0,7},{9,10},{11,12},{13... | collective-permute-start | bytes 442376 | tf_op jit(solution)/shard_map/while/body/eval_jaxpr/ppermute | solution.py:206
  86.7 3.1 %collective-permute-start.3 = (bf16[12,48,128]{2,1,0:T(8,128)(2,1)S(1)}, bf16[12,48,128]{2,1,0:T(8,128)(2,1)S(1)}, u32[]{:S(2)}, u32[]{:S(2)}) collective-permute-start(bf16[12,48,128]{2,1,0:T(8,128)(2,1)S(1)} %get-tuple-element.113.value.earlier), channel_id=1, source_target_pairs={{0,1},{2,3},{4,5},{6,7},{1,0},{3,2},{5,4},{7,6},{8,9},{10,11},{12,... | collective-permute-start | bytes 442376 | tf_op jit(solution)/shard_map/while/body/eval_jaxpr/ppermute | solution.py:205
  90.2 7.4 %collective-permute-start = (bf16[12,48,128]{2,1,0:T(8,128)(2,1)S(1)}, bf16[12,48,128]{2,1,0:T(8,128)(2,1)S(1)}, u32[]{:S(2)}, u32[]{:S(2)}) collective-permute-start(bf16[12,48,128]{2,1,0:T(8,128)(2,1)S(1)} %get-tuple-element.113.value.earlier), channel_id=1, source_target_pairs={{8,16},{24,32},{40,48},{56,64},{72,80},{88,96},{104,112},{120,128}... | collective-permute-start | bytes 442376 | tf_op jit(solution)/shard_map/while/body/eval_jaxpr/ppermute | solution.py:208
  92.3 5.3 %collective-permute-start.1 = (bf16[12,48,128]{2,1,0:T(8,128)(2,1)S(1)}, bf16[12,48,128]{2,1,0:T(8,128)(2,1)S(1)}, u32[]{:S(2)}, u32[]{:S(2)}) collective-permute-start(bf16[12,48,128]{2,1,0:T(8,128)(2,1)S(1)} %get-tuple-element.113.value.earlier), channel_id=1, source_target_pairs={{0,8},{16,24},{32,40},{48,56},{64,72},{80,88},{96,104},{112,120},{... | collective-permute-start | bytes 442376 | tf_op jit(solution)/shard_map/while/body/eval_jaxpr/ppermute | solution.py:207
  92.3 6.5 %collective-permute-start.2 = (bf16[12,48,128]{2,1,0:T(8,128)(2,1)S(1)}, bf16[12,48,128]{2,1,0:T(8,128)(2,1)S(1)}, u32[]{:S(2)}, u32[]{:S(2)}) collective-permute-start(bf16[12,48,128]{2,1,0:T(8,128)(2,1)S(1)} %get-tuple-element.113.value.earlier), channel_id=1, source_target_pairs={{1,2},{3,4},{5,6},{7,0},{2,1},{4,3},{6,5},{0,7},{9,10},{11,12},{13... | collective-permute-start | bytes 442376 | tf_op jit(solution)/shard_map/while/body/eval_jaxpr/ppermute | solution.py:206
  95.7 3.1 %collective-permute-start.3 = (bf16[12,48,128]{2,1,0:T(8,128)(2,1)S(1)}, bf16[12,48,128]{2,1,0:T(8,128)(2,1)S(1)}, u32[]{:S(2)}, u32[]{:S(2)}) collective-permute-start(bf16[12,48,128]{2,1,0:T(8,128)(2,1)S(1)} %get-tuple-element.113.value.earlier), channel_id=1, source_target_pairs={{0,1},{2,3},{4,5},{6,7},{1,0},{3,2},{5,4},{7,6},{8,9},{10,11},{12,... | collective-permute-start | bytes 442376 | tf_op jit(solution)/shard_map/while/body/eval_jaxpr/ppermute | solution.py:205
  99.2 7.4 %collective-permute-start = (bf16[12,48,128]{2,1,0:T(8,128)(2,1)S(1)}, bf16[12,48,128]{2,1,0:T(8,128)(2,1)S(1)}, u32[]{:S(2)}, u32[]{:S(2)}) collective-permute-start(bf16[12,48,128]{2,1,0:T(8,128)(2,1)S(1)} %get-tuple-element.113.value.earlier), channel_id=1, source_target_pairs={{8,16},{24,32},{40,48},{56,64},{72,80},{88,96},{104,112},{120,128}... | collective-permute-start | bytes 442376 | tf_op jit(solution)/shard_map/while/body/eval_jaxpr/ppermute | solution.py:208
  101.3 5.3 %collective-permute-start.1 = (bf16[12,48,128]{2,1,0:T(8,128)(2,1)S(1)}, bf16[12,48,128]{2,1,0:T(8,128)(2,1)S(1)}, u32[]{:S(2)}, u32[]{:S(2)}) collective-permute-start(bf16[12,48,128]{2,1,0:T(8,128)(2,1)S(1)} %get-tuple-element.113.value.earlier), channel_id=1, source_target_pairs={{0,8},{16,24},{32,40},{48,56},{64,72},{80,88},{96,104},{112,120},{... | collective-permute-start | bytes 442376 | tf_op jit(solution)/shard_map/while/body/eval_jaxpr/ppermute | solution.py:207
  101.3 6.5 %collective-permute-start.2 = (bf16[12,48,128]{2,1,0:T(8,128)(2,1)S(1)}, bf16[12,48,128]{2,1,0:T(8,128)(2,1)S(1)}, u32[]{:S(2)}, u32[]{:S(2)}) collective-permute-start(bf16[12,48,128]{2,1,0:T(8,128)(2,1)S(1)} %get-tuple-element.113.value.earlier), channel_id=1, source_target_pairs={{1,2},{3,4},{5,6},{7,0},{2,1},{4,3},{6,5},{0,7},{9,10},{11,12},{13... | collective-permute-start | bytes 442376 | tf_op jit(solution)/shard_map/while/body/eval_jaxpr/ppermute | solution.py:206
  104.6 3.1 %collective-permute-start.3 = (bf16[12,48,128]{2,1,0:T(8,128)(2,1)S(1)}, bf16[12,48,128]{2,1,0:T(8,128)(2,1)S(1)}, u32[]{:S(2)}, u32[]{:S(2)}) collective-permute-start(bf16[12,48,128]{2,1,0:T(8,128)(2,1)S(1)} %get-tuple-element.113.value.earlier), channel_id=1, source_target_pairs={{0,1},{2,3},{4,5},{6,7},{1,0},{3,2},{5,4},{7,6},{8,9},{10,11},{12,... | collective-permute-start | bytes 442376 | tf_op jit(solution)/shard_map/while/body/eval_jaxpr/ppermute | solution.py:205
  108.2 7.4 %collective-permute-start = (bf16[12,48,128]{2,1,0:T(8,128)(2,1)S(1)}, bf16[12,48,128]{2,1,0:T(8,128)(2,1)S(1)}, u32[]{:S(2)}, u32[]{:S(2)}) collective-permute-start(bf16[12,48,128]{2,1,0:T(8,128)(2,1)S(1)} %get-tuple-element.113.value.earlier), channel_id=1, source_target_pairs={{8,16},{24,32},{40,48},{56,64},{72,80},{88,96},{104,112},{120,128}... | collective-permute-start | bytes 442376 | tf_op jit(solution)/shard_map/while/body/eval_jaxpr/ppermute | solution.py:208
  110.3 5.3 %collective-permute-start.1 = (bf16[12,48,128]{2,1,0:T(8,128)(2,1)S(1)}, bf16[12,48,128]{2,1,0:T(8,128)(2,1)S(1)}, u32[]{:S(2)}, u32[]{:S(2)}) collective-permute-start(bf16[12,48,128]{2,1,0:T(8,128)(2,1)S(1)} %get-tuple-element.113.value.earlier), channel_id=1, source_target_pairs={{0,8},{16,24},{32,40},{48,56},{64,72},{80,88},{96,104},{112,120},{... | collective-permute-start | bytes 442376 | tf_op jit(solution)/shard_map/while/body/eval_jaxpr/ppermute | solution.py:207
  110.3 6.5 %collective-permute-start.2 = (bf16[12,48,128]{2,1,0:T(8,128)(2,1)S(1)}, bf16[12,48,128]{2,1,0:T(8,128)(2,1)S(1)}, u32[]{:S(2)}, u32[]{:S(2)}) collective-permute-start(bf16[12,48,128]{2,1,0:T(8,128)(2,1)S(1)} %get-tuple-element.113.value.earlier), channel_id=1, source_target_pairs={{1,2},{3,4},{5,6},{7,0},{2,1},{4,3},{6,5},{0,7},{9,10},{11,12},{13... | collective-permute-start | bytes 442376 | tf_op jit(solution)/shard_map/while/body/eval_jaxpr/ppermute | solution.py:206
  113.6 3.1 %collective-permute-start.3 = (bf16[12,48,128]{2,1,0:T(8,128)(2,1)S(1)}, bf16[12,48,128]{2,1,0:T(8,128)(2,1)S(1)}, u32[]{:S(2)}, u32[]{:S(2)}) collective-permute-start(bf16[12,48,128]{2,1,0:T(8,128)(2,1)S(1)} %get-tuple-element.113.value.earlier), channel_id=1, source_target_pairs={{0,1},{2,3},{4,5},{6,7},{1,0},{3,2},{5,4},{7,6},{8,9},{10,11},{12,... | collective-permute-start | bytes 442376 | tf_op jit(solution)/shard_map/while/body/eval_jaxpr/ppermute | solution.py:205
  117.2 7.4 %collective-permute-start = (bf16[12,48,128]{2,1,0:T(8,128)(2,1)S(1)}, bf16[12,48,128]{2,1,0:T(8,128)(2,1)S(1)}, u32[]{:S(2)}, u32[]{:S(2)}) collective-permute-start(bf16[12,48,128]{2,1,0:T(8,128)(2,1)S(1)} %get-tuple-element.113.value.earlier), channel_id=1, source_target_pairs={{8,16},{24,32},{40,48},{56,64},{72,80},{88,96},{104,112},{120,128}... | collective-permute-start | bytes 442376 | tf_op jit(solution)/shard_map/while/body/eval_jaxpr/ppermute | solution.py:208
  119.3 5.3 %collective-permute-start.1 = (bf16[12,48,128]{2,1,0:T(8,128)(2,1)S(1)}, bf16[12,48,128]{2,1,0:T(8,128)(2,1)S(1)}, u32[]{:S(2)}, u32[]{:S(2)}) collective-permute-start(bf16[12,48,128]{2,1,0:T(8,128)(2,1)S(1)} %get-tuple-element.113.value.earlier), channel_id=1, source_target_pairs={{0,8},{16,24},{32,40},{48,56},{64,72},{80,88},{96,104},{112,120},{... | collective-permute-start | bytes 442376 | tf_op jit(solution)/shard_map/while/body/eval_jaxpr/ppermute | solution.py:207
  119.3 6.5 %collective-permute-start.2 = (bf16[12,48,128]{2,1,0:T(8,128)(2,1)S(1)}, bf16[12,48,128]{2,1,0:T(8,128)(2,1)S(1)}, u32[]{:S(2)}, u32[]{:S(2)}) collective-permute-start(bf16[12,48,128]{2,1,0:T(8,128)(2,1)S(1)} %get-tuple-element.113.value.earlier), channel_id=1, source_target_pairs={{1,2},{3,4},{5,6},{7,0},{2,1},{4,3},{6,5},{0,7},{9,10},{11,12},{13... | collective-permute-start | bytes 442376 | tf_op jit(solution)/shard_map/while/body/eval_jaxpr/ppermute | solution.py:206
  122.6 3.1 %collective-permute-start.3 = (bf16[12,48,128]{2,1,0:T(8,128)(2,1)S(1)}, bf16[12,48,128]{2,1,0:T(8,128)(2,1)S(1)}, u32[]{:S(2)}, u32[]{:S(2)}) collective-permute-start(bf16[12,48,128]{2,1,0:T(8,128)(2,1)S(1)} %get-tuple-element.113.value.earlier), channel_id=1, source_target_pairs={{0,1},{2,3},{4,5},{6,7},{1,0},{3,2},{5,4},{7,6},{8,9},{10,11},{12,... | collective-permute-start | bytes 442376 | tf_op jit(solution)/shard_map/while/body/eval_jaxpr/ppermute | solution.py:205
  126.1 8.3 %collective-permute-start.8 = (bf16[12,48,128]{2,1,0:T(8,128)(2,1)S(1)}, bf16[12,48,128]{2,1,0:T(8,128)(2,1)S(1)}, u32[]{:S(2)}, u32[]{:S(2)}) collective-permute-start(bf16[12,48,128]{2,1,0:T(8,128)(2,1)S(1)} %get-tuple-element.49.value.earlier), channel_id=1, source_target_pairs={{8,16},{24,32},{40,48},{56,64},{72,80},{88,96},{104,112},{120,128}... | collective-permute-start | bytes 442376 | tf_op jit(solution)/shard_map/ppermute | solution.py:208
  128.3 6.2 %collective-permute-start.9 = (bf16[12,48,128]{2,1,0:T(8,128)(2,1)S(1)}, bf16[12,48,128]{2,1,0:T(8,128)(2,1)S(1)}, u32[]{:S(2)}, u32[]{:S(2)}) collective-permute-start(bf16[12,48,128]{2,1,0:T(8,128)(2,1)S(1)} %get-tuple-element.49.value.earlier), channel_id=1, source_target_pairs={{0,8},{16,24},{32,40},{48,56},{64,72},{80,88},{96,104},{112,120},{... | collective-permute-start | bytes 442376 | tf_op jit(solution)/shard_map/ppermute | solution.py:207
  128.3 6.5 %collective-permute-start.10 = (bf16[12,48,128]{2,1,0:T(8,128)(2,1)S(1)}, bf16[12,48,128]{2,1,0:T(8,128)(2,1)S(1)}, u32[]{:S(2)}, u32[]{:S(2)}) collective-permute-start(bf16[12,48,128]{2,1,0:T(8,128)(2,1)S(1)} %get-tuple-element.49.value.earlier), channel_id=1, source_target_pairs={{1,2},{3,4},{5,6},{7,0},{2,1},{4,3},{6,5},{0,7},{9,10},{11,12},{13... | collective-permute-start | bytes 442376 | tf_op jit(solution)/shard_map/ppermute | solution.py:206
  131.6 3.1 %collective-permute-start.11 = (bf16[12,48,128]{2,1,0:T(8,128)(2,1)S(1)}, bf16[12,48,128]{2,1,0:T(8,128)(2,1)S(1)}, u32[]{:S(2)}, u32[]{:S(2)}) collective-permute-start(bf16[12,48,128]{2,1,0:T(8,128)(2,1)S(1)} %get-tuple-element.49.value.earlier), channel_id=1, source_target_pairs={{0,1},{2,3},{4,5},{6,7},{1,0},{3,2},{5,4},{7,6},{8,9},{10,11},{12,... | collective-permute-start | bytes 442376 | tf_op jit(solution)/shard_map/ppermute | solution.py:205
  135.1 8.3 %collective-permute-start.12 = (bf16[12,48,128]{2,1,0:T(8,128)(2,1)S(1)}, bf16[12,48,128]{2,1,0:T(8,128)(2,1)S(1)}, u32[]{:S(2)}, u32[]{:S(2)}) collective-permute-start(bf16[12,48,128]{2,1,0:T(8,128)(2,1)S(1)} %shard_map.47.value.earlier), channel_id=1, source_target_pairs={{8,16},{24,32},{40,48},{56,64},{72,80},{88,96},{104,112},{120,128}... | collective-permute-start | bytes 442376 | tf_op jit(solution)/shard_map/ppermute | solution.py:208
  137.4 6.0 %collective-permute-start.13 = (bf16[12,48,128]{2,1,0:T(8,128)(2,1)S(1)}, bf16[12,48,128]{2,1,0:T(8,128)(2,1)S(1)}, u32[]{:S(2)}, u32[]{:S(2)}) collective-permute-start(bf16[12,48,128]{2,1,0:T(8,128)(2,1)S(1)} %shard_map.47.value.earlier), channel_id=1, source_target_pairs={{0,8},{16,24},{32,40},{48,56},{64,72},{80,88},{96,104},{112,120},{... | collective-permute-start | bytes 442376 | tf_op jit(solution)/shard_map/ppermute | solution.py:207
  137.4 6.5 %collective-permute-start.14 = (bf16[12,48,128]{2,1,0:T(8,128)(2,1)S(1)}, bf16[12,48,128]{2,1,0:T(8,128)(2,1)S(1)}, u32[]{:S(2)}, u32[]{:S(2)}) collective-permute-start(bf16[12,48,128]{2,1,0:T(8,128)(2,1)S(1)} %shard_map.47.value.earlier), channel_id=1, source_target_pairs={{1,2},{3,4},{5,6},{7,0},{2,1},{4,3},{6,5},{0,7},{9,10},{11,12},{13... | collective-permute-start | bytes 442376 | tf_op jit(solution)/shard_map/ppermute | solution.py:206
  140.8 3.1 %collective-permute-start.15 = (bf16[12,48,128]{2,1,0:T(8,128)(2,1)S(1)}, bf16[12,48,128]{2,1,0:T(8,128)(2,1)S(1)}, u32[]{:S(2)}, u32[]{:S(2)}) collective-permute-start(bf16[12,48,128]{2,1,0:T(8,128)(2,1)S(1)} %shard_map.47.value.earlier), channel_id=1, source_target_pairs={{0,1},{2,3},{4,5},{6,7},{1,0},{3,2},{5,4},{7,6},{8,9},{10,11},{12,... | collective-permute-start | bytes 442376 | tf_op jit(solution)/shard_map/ppermute | solution.py:205
  144.3 8.1 %collective-permute-start.16 = (bf16[12,48,128]{2,1,0:T(8,128)(2,1)S(1)}, bf16[12,48,128]{2,1,0:T(8,128)(2,1)S(1)}, u32[]{:S(2)}, u32[]{:S(2)}) collective-permute-start(bf16[12,48,128]{2,1,0:T(8,128)(2,1)S(1)} %shard_map.52.value.earlier), channel_id=1, source_target_pairs={{8,16},{24,32},{40,48},{56,64},{72,80},{88,96},{104,112},{120,128}... | collective-permute-start | bytes 442376 | tf_op jit(solution)/shard_map/ppermute | solution.py:208
  146.4 6.0 %collective-permute-start.17 = (bf16[12,48,128]{2,1,0:T(8,128)(2,1)S(1)}, bf16[12,48,128]{2,1,0:T(8,128)(2,1)S(1)}, u32[]{:S(2)}, u32[]{:S(2)}) collective-permute-start(bf16[12,48,128]{2,1,0:T(8,128)(2,1)S(1)} %shard_map.52.value.earlier), channel_id=1, source_target_pairs={{0,8},{16,24},{32,40},{48,56},{64,72},{80,88},{96,104},{112,120},{... | collective-permute-start | bytes 442376 | tf_op jit(solution)/shard_map/ppermute | solution.py:207
  146.4 6.5 %collective-permute-start.18 = (bf16[12,48,128]{2,1,0:T(8,128)(2,1)S(1)}, bf16[12,48,128]{2,1,0:T(8,128)(2,1)S(1)}, u32[]{:S(2)}, u32[]{:S(2)}) collective-permute-start(bf16[12,48,128]{2,1,0:T(8,128)(2,1)S(1)} %shard_map.52.value.earlier), channel_id=1, source_target_pairs={{1,2},{3,4},{5,6},{7,0},{2,1},{4,3},{6,5},{0,7},{9,10},{11,12},{13... | collective-permute-start | bytes 442376 | tf_op jit(solution)/shard_map/ppermute | solution.py:206
  149.7 3.1 %collective-permute-start.19 = (bf16[12,48,128]{2,1,0:T(8,128)(2,1)S(1)}, bf16[12,48,128]{2,1,0:T(8,128)(2,1)S(1)}, u32[]{:S(2)}, u32[]{:S(2)}) collective-permute-start(bf16[12,48,128]{2,1,0:T(8,128)(2,1)S(1)} %shard_map.52.value.earlier), channel_id=1, source_target_pairs={{0,1},{2,3},{4,5},{6,7},{1,0},{3,2},{5,4},{7,6},{8,9},{10,11},{12,... | collective-permute-start | bytes 442376 | tf_op jit(solution)/shard_map/ppermute | solution.py:205

commit v4 on v3

--- a/solution.py
+++ b/solution.py
@@ -9,7 +9,7 @@
 
 ITERS = 16
 KEPT = 1
-LATE = 3
+LATE = 4
 LIMIT = 16 * 2**20
 VMEM = pl.BlockSpec(memory_space=pltpu.VMEM)
 HBM = pl.BlockSpec(memory_space=pltpu.HBM)

time: 156 us -> 156 us (level)
  no operation moved by 1% of the time
where the time goes in v4:
time: 156 us; the launch traced here: 155 us
  starting transfers between devices  91.6 us (59%)
  Pallas kernels  46.4 us (30%)
  waiting for transfers between devices  15.5 us (10%)
    ppermute x16, starting transfers between devices, swaps(): z_far = lax.ppermute(value, 'gz', swap(nz, 1))  51.5 us
    pallas_call x82, Pallas kernels, call(): pl.pallas_call(kernel, in_specs=in_specs, out_specs=out_specs, out_shape=...  46.4 us
    ppermute x16, starting transfers between devices, swaps(): t_far = lax.ppermute(value, 'ta', swap(nt, 1))  39.2 us
    ppermute x16, waiting for transfers between devices, swaps(): z_far = lax.ppermute(value, 'gz', swap(nz, 1))  11.7 us
    ppermute x16, waiting for transfers between devices, swaps(): t_far = lax.ppermute(value, 'ta', swap(nt, 1))  3.72 us
  transfers between devices with their start and end apart: 64, of which 16 were waited for; matrix products, arithmetic and copies ran while one was open for 0% of the time, Pallas kernels for 23%

profile of v4, /device:TPU:1, one launch (start us, length us, event | category | flops | bytes accessed | tf_op | source)
XLA Modules:
  0.0 154.7 jit_solution(14931092389238503857)
XLA Ops:
  0.0 3.3 %shard_map.37.rhs.earlier = bf16[12,48,128]{2,1,0:T(8,128)(2,1)S(1)} custom-call(bf16[12,48,1536]{2,1,0:T(8,128)(2,1)} %bitcast.16, bf16[12,1536,128]{2,1,0:T(8,128)(2,1)} %bitcast.11), custom_call_target="tpu_custom_call" | custom-call | tf_op jit(solution)/shard_map/pallas_call | solution.py:28
  3.3 8.9 %collective-permute-start.4 = (bf16[12,48,128]{2,1,0:T(8,128)(2,1)S(1)}, bf16[12,48,128]{2,1,0:T(8,128)(2,1)S(1)}, u32[]{:S(2)}, u32[]{:S(2)}) collective-permute-start(bf16[12,48,128]{2,1,0:T(8,128)(2,1)S(1)} %shard_map.37.rhs.earlier), channel_id=1, source_target_pairs={{8,16},{24,32},{40,48},{56,64},{72,80},{88,96},{104,112},{120,128}... | collective-permute-start | bytes 442376 | tf_op jit(solution)/shard_map/ppermute | solution.py:208
  12.3 2.1 %collective-permute-start.6 = (bf16[12,48,128]{2,1,0:T(8,128)(2,1)S(1)}, bf16[12,48,128]{2,1,0:T(8,128)(2,1)S(1)}, u32[]{:S(2)}, u32[]{:S(2)}) collective-permute-start(bf16[12,48,128]{2,1,0:T(8,128)(2,1)S(1)} %shard_map.37.rhs.earlier), channel_id=1, source_target_pairs={{1,2},{3,4},{5,6},{7,0},{2,1},{4,3},{6,5},{0,7},{9,10},{11,12},{13... | collective-permute-start | bytes 442376 | tf_op jit(solution)/shard_map/ppermute | solution.py:206
  14.3 0.8 collective-permute-start.7
  15.2 3.5 %shard_map.38 = (f32[12,48,128]{2,1,0:T(8,128)S(1)}, bf16[12,512,128]{2,1,0:T(8,128)(2,1)S(1)}, bf16[12,128,128]{2,1,0:T(8,128)(2,1)S(1)}) custom-call(s32[5]{0:T(128)S(1)} %stack.23.slots, bf16[12,48,128]{2,1,0:T(8,128)(2,1)S(1)} %shard_map.37.rhs.earlier, bf16[9,12,128,128]{3,2,1,0:T(8,128)(2,1)} %bitcast.9), custom_call_target="tpu_custom_call" | custom-call | flops 94371840 | tf_op jit(solution)/shard_map/pallas_call | solution.py:28
  19.2 97.9 %while.10 = (s32[]{:T(128)}, bf16[12,48,128]{2,1,0:T(8,128)(2,1)S(1)}, bf16[12,48,128]{2,1,0:T(8,128)(2,1)S(1)}, bf16[12,128,128]{2,1,0:T(8,128)(2,1)S(1)}, bf16...) while((s32[]{:T(128)}, bf16[12,48,128]{2,1,0:T(8,128)(2,1)S(1)}, ...), condition=%wide.region_1.2_spmd, body=%wide.region_0.1_spmd.sunk | while | flops 169869312 | bytes 2359533 | solution.py:254
  19.2 1.6 %collective-permute-start = (bf16[12,48,128]{2,1,0:T(8,128)(2,1)S(1)}, bf16[12,48,128]{2,1,0:T(8,128)(2,1)S(1)}, u32[]{:S(2)}, u32[]{:S(2)}) collective-permute-start(bf16[12,48,128]{2,1,0:T(8,128)(2,1)S(1)} %get-tuple-element.117.value.earlier), channel_id=1, source_target_pairs={{8,16},{24,32},{40,48},{56,64},{72,80},{88,96},{104,112},{120,128}... | collective-permute-start | bytes 442376 | tf_op jit(solution)/shard_map/while/body/eval_jaxpr/ppermute | solution.py:208
  20.8 2.9 %collective-permute-start.2 = (bf16[12,48,128]{2,1,0:T(8,128)(2,1)S(1)}, bf16[12,48,128]{2,1,0:T(8,128)(2,1)S(1)}, u32[]{:S(2)}, u32[]{:S(2)}) collective-permute-start(bf16[12,48,128]{2,1,0:T(8,128)(2,1)S(1)} %get-tuple-element.117.value.earlier), channel_id=1, source_target_pairs={{1,2},{3,4},{5,6},{7,0},{2,1},{4,3},{6,5},{0,7},{9,10},{11,12},{13... | collective-permute-start | bytes 442376 | tf_op jit(solution)/shard_map/while/body/eval_jaxpr/ppermute | solution.py:206
  23.8 1.9 %eval_jaxpr.5.part = f32[12,48,128]{2,1,0:T(8,128)S(1)} custom-call(bf16[12,48,128]{2,1,0:T(8,128)(2,1)S(1)} %get-tuple-element.125.rhs, bf16[12,48,128]{2,1,0:T(8,128)(2,1)S(1)} %get-tuple-element.117.value.earlier, bf16[12,128,128]{2,1,0:T(8,128)(2,1)S(1)} %get-tuple-element.126.kept, bf16[9,12,128,128]{3,2,1,0:T(8,128)(2,1)} %get-tuple-element.127.links), custom_call_target="tpu_custom_call" | custom-call | flops 94371840 | tf_op jit(solution)/shard_map/while/body/eval_jaxpr/pallas_call | solution.py:28
  25.7 2.2 %collective-permute-done.arrived.a = bf16[12,48,128]{2,1,0:T(8,128)(2,1)S(1)} collective-permute-done((bf16[12,48,128]{2,1,0:T(8,128)(2,1)S(1)}, bf16[12,48,128]{2,1,0:T(8,128)(2,1)S(1)}, u32[]{:S(2)}, u32[]{:S(2)}) %collective-permute-start) | collective-permute-done | bytes 147488 | tf_op jit(solution)/shard_map/while/body/eval_jaxpr/ppermute | solution.py:208
  28.3 1.2 collective-permute-start
  29.5 3.2 %collective-permute-start.2 = (bf16[12,48,128]{2,1,0:T(8,128)(2,1)S(1)}, bf16[12,48,128]{2,1,0:T(8,128)(2,1)S(1)}, u32[]{:S(2)}, u32[]{:S(2)}) collective-permute-start(bf16[12,48,128]{2,1,0:T(8,128)(2,1)S(1)} %get-tuple-element.117.value.earlier), channel_id=1, source_target_pairs={{1,2},{3,4},{5,6},{7,0},{2,1},{4,3},{6,5},{0,7},{9,10},{11,12},{13... | collective-permute-start | bytes 442376 | tf_op jit(solution)/shard_map/while/body/eval_jaxpr/ppermute | solution.py:206
  32.8 1.9 %eval_jaxpr.5.part = f32[12,48,128]{2,1,0:T(8,128)S(1)} custom-call(bf16[12,48,128]{2,1,0:T(8,128)(2,1)S(1)} %get-tuple-element.125.rhs, bf16[12,48,128]{2,1,0:T(8,128)(2,1)S(1)} %get-tuple-element.117.value.earlier, bf16[12,128,128]{2,1,0:T(8,128)(2,1)S(1)} %get-tuple-element.126.kept, bf16[9,12,128,128]{3,2,1,0:T(8,128)(2,1)} %get-tuple-element.127.links), custom_call_target="tpu_custom_call" | custom-call | flops 94371840 | tf_op jit(solution)/shard_map/while/body/eval_jaxpr/pallas_call | solution.py:28
  34.7 1.3 collective-permute-done.arrived.a
  36.5 2.1 %collective-permute-start = (bf16[12,48,128]{2,1,0:T(8,128)(2,1)S(1)}, bf16[12,48,128]{2,1,0:T(8,128)(2,1)S(1)}, u32[]{:S(2)}, u32[]{:S(2)}) collective-permute-start(bf16[12,48,128]{2,1,0:T(8,128)(2,1)S(1)} %get-tuple-element.117.value.earlier), channel_id=1, source_target_pairs={{8,16},{24,32},{40,48},{56,64},{72,80},{88,96},{104,112},{120,128}... | collective-permute-start | bytes 442376 | tf_op jit(solution)/shard_map/while/body/eval_jaxpr/ppermute | solution.py:208
  38.5 3.2 %collective-permute-start.2 = (bf16[12,48,128]{2,1,0:T(8,128)(2,1)S(1)}, bf16[12,48,128]{2,1,0:T(8,128)(2,1)S(1)}, u32[]{:S(2)}, u32[]{:S(2)}) collective-permute-start(bf16[12,48,128]{2,1,0:T(8,128)(2,1)S(1)} %get-tuple-element.117.value.earlier), channel_id=1, source_target_pairs={{1,2},{3,4},{5,6},{7,0},{2,1},{4,3},{6,5},{0,7},{9,10},{11,12},{13... | collective-permute-start | bytes 442376 | tf_op jit(solution)/shard_map/while/body/eval_jaxpr/ppermute | solution.py:206
  41.7 1.9 %eval_jaxpr.5.part = f32[12,48,128]{2,1,0:T(8,128)S(1)} custom-call(bf16[12,48,128]{2,1,0:T(8,128)(2,1)S(1)} %get-tuple-element.125.rhs, bf16[12,48,128]{2,1,0:T(8,128)(2,1)S(1)} %get-tuple-element.117.value.earlier, bf16[12,128,128]{2,1,0:T(8,128)(2,1)S(1)} %get-tuple-element.126.kept, bf16[9,12,128,128]{3,2,1,0:T(8,128)(2,1)} %get-tuple-element.127.links), custom_call_target="tpu_custom_call" | custom-call | flops 94371840 | tf_op jit(solution)/shard_map/while/body/eval_jaxpr/pallas_call | solution.py:28
  43.9 1.0 collective-permute-done.2.arrived.c
  45.3 2.1 %collective-permute-start = (bf16[12,48,128]{2,1,0:T(8,128)(2,1)S(1)}, bf16[12,48,128]{2,1,0:T(8,128)(2,1)S(1)}, u32[]{:S(2)}, u32[]{:S(2)}) collective-permute-start(bf16[12,48,128]{2,1,0:T(8,128)(2,1)S(1)} %get-tuple-element.117.value.earlier), channel_id=1, source_target_pairs={{8,16},{24,32},{40,48},{56,64},{72,80},{88,96},{104,112},{120,128}... | collective-permute-start | bytes 442376 | tf_op jit(solution)/shard_map/while/body/eval_jaxpr/ppermute | solution.py:208
  47.4 3.4 %collective-permute-start.2 = (bf16[12,48,128]{2,1,0:T(8,128)(2,1)S(1)}, bf16[12,48,128]{2,1,0:T(8,128)(2,1)S(1)}, u32[]{:S(2)}, u32[]{:S(2)}) collective-permute-start(bf16[12,48,128]{2,1,0:T(8,128)(2,1)S(1)} %get-tuple-element.117.value.earlier), channel_id=1, source_target_pairs={{1,2},{3,4},{5,6},{7,0},{2,1},{4,3},{6,5},{0,7},{9,10},{11,12},{13... | collective-permute-start | bytes 442376 | tf_op jit(solution)/shard_map/while/body/eval_jaxpr/ppermute | solution.py:206
  50.7 1.9 %eval_jaxpr.5.part = f32[12,48,128]{2,1,0:T(8,128)S(1)} custom-call(bf16[12,48,128]{2,1,0:T(8,128)(2,1)S(1)} %get-tuple-element.125.rhs, bf16[12,48,128]{2,1,0:T(8,128)(2,1)S(1)} %get-tuple-element.117.value.earlier, bf16[12,128,128]{2,1,0:T(8,128)(2,1)S(1)} %get-tuple-element.126.kept, bf16[9,12,128,128]{3,2,1,0:T(8,128)(2,1)} %get-tuple-element.127.links), custom_call_target="tpu_custom_call" | custom-call | flops 94371840 | tf_op jit(solution)/shard_map/while/body/eval_jaxpr/pallas_call | solution.py:28
  52.7 1.1 collective-permute-done.2.arrived.c
  54.2 2.1 %collective-permute-start = (bf16[12,48,128]{2,1,0:T(8,128)(2,1)S(1)}, bf16[12,48,128]{2,1,0:T(8,128)(2,1)S(1)}, u32[]{:S(2)}, u32[]{:S(2)}) collective-permute-start(bf16[12,48,128]{2,1,0:T(8,128)(2,1)S(1)} %get-tuple-element.117.value.earlier), channel_id=1, source_target_pairs={{8,16},{24,32},{40,48},{56,64},{72,80},{88,96},{104,112},{120,128}... | collective-permute-start | bytes 442376 | tf_op jit(solution)/shard_map/while/body/eval_jaxpr/ppermute | solution.py:208
  56.4 3.4 %collective-permute-start.2 = (bf16[12,48,128]{2,1,0:T(8,128)(2,1)S(1)}, bf16[12,48,128]{2,1,0:T(8,128)(2,1)S(1)}, u32[]{:S(2)}, u32[]{:S(2)}) collective-permute-start(bf16[12,48,128]{2,1,0:T(8,128)(2,1)S(1)} %get-tuple-element.117.value.earlier), channel_id=1, source_target_pairs={{1,2},{3,4},{5,6},{7,0},{2,1},{4,3},{6,5},{0,7},{9,10},{11,12},{13... | collective-permute-start | bytes 442376 | tf_op jit(solution)/shard_map/while/body/eval_jaxpr/ppermute | solution.py:206
  59.7 1.9 %eval_jaxpr.5.part = f32[12,48,128]{2,1,0:T(8,128)S(1)} custom-call(bf16[12,48,128]{2,1,0:T(8,128)(2,1)S(1)} %get-tuple-element.125.rhs, bf16[12,48,128]{2,1,0:T(8,128)(2,1)S(1)} %get-tuple-element.117.value.earlier, bf16[12,128,128]{2,1,0:T(8,128)(2,1)S(1)} %get-tuple-element.126.kept, bf16[9,12,128,128]{3,2,1,0:T(8,128)(2,1)} %get-tuple-element.127.links), custom_call_target="tpu_custom_call" | custom-call | flops 94371840 | tf_op jit(solution)/shard_map/while/body/eval_jaxpr/pallas_call | solution.py:28
  61.7 1.1 collective-permute-done.2.arrived.c
  63.2 2.1 %collective-permute-start = (bf16[12,48,128]{2,1,0:T(8,128)(2,1)S(1)}, bf16[12,48,128]{2,1,0:T(8,128)(2,1)S(1)}, u32[]{:S(2)}, u32[]{:S(2)}) collective-permute-start(bf16[12,48,128]{2,1,0:T(8,128)(2,1)S(1)} %get-tuple-element.117.value.earlier), channel_id=1, source_target_pairs={{8,16},{24,32},{40,48},{56,64},{72,80},{88,96},{104,112},{120,128}... | collective-permute-start | bytes 442376 | tf_op jit(solution)/shard_map/while/body/eval_jaxpr/ppermute | solution.py:208
  65.3 3.4 %collective-permute-start.2 = (bf16[12,48,128]{2,1,0:T(8,128)(2,1)S(1)}, bf16[12,48,128]{2,1,0:T(8,128)(2,1)S(1)}, u32[]{:S(2)}, u32[]{:S(2)}) collective-permute-start(bf16[12,48,128]{2,1,0:T(8,128)(2,1)S(1)} %get-tuple-element.117.value.earlier), channel_id=1, source_target_pairs={{1,2},{3,4},{5,6},{7,0},{2,1},{4,3},{6,5},{0,7},{9,10},{11,12},{13... | collective-permute-start | bytes 442376 | tf_op jit(solution)/shard_map/while/body/eval_jaxpr/ppermute | solution.py:206
  68.7 1.9 %eval_jaxpr.5.part = f32[12,48,128]{2,1,0:T(8,128)S(1)} custom-call(bf16[12,48,128]{2,1,0:T(8,128)(2,1)S(1)} %get-tuple-element.125.rhs, bf16[12,48,128]{2,1,0:T(8,128)(2,1)S(1)} %get-tuple-element.117.value.earlier, bf16[12,128,128]{2,1,0:T(8,128)(2,1)S(1)} %get-tuple-element.126.kept, bf16[9,12,128,128]{3,2,1,0:T(8,128)(2,1)} %get-tuple-element.127.links), custom_call_target="tpu_custom_call" | custom-call | flops 94371840 | tf_op jit(solution)/shard_map/while/body/eval_jaxpr/pallas_call | solution.py:28
  70.7 1.1 collective-permute-done.2.arrived.c
  72.2 2.1 %collective-permute-start = (bf16[12,48,128]{2,1,0:T(8,128)(2,1)S(1)}, bf16[12,48,128]{2,1,0:T(8,128)(2,1)S(1)}, u32[]{:S(2)}, u32[]{:S(2)}) collective-permute-start(bf16[12,48,128]{2,1,0:T(8,128)(2,1)S(1)} %get-tuple-element.117.value.earlier), channel_id=1, source_target_pairs={{8,16},{24,32},{40,48},{56,64},{72,80},{88,96},{104,112},{120,128}... | collective-permute-start | bytes 442376 | tf_op jit(solution)/shard_map/while/body/eval_jaxpr/ppermute | solution.py:208
  74.3 3.4 %collective-permute-start.2 = (bf16[12,48,128]{2,1,0:T(8,128)(2,1)S(1)}, bf16[12,48,128]{2,1,0:T(8,128)(2,1)S(1)}, u32[]{:S(2)}, u32[]{:S(2)}) collective-permute-start(bf16[12,48,128]{2,1,0:T(8,128)(2,1)S(1)} %get-tuple-element.117.value.earlier), channel_id=1, source_target_pairs={{1,2},{3,4},{5,6},{7,0},{2,1},{4,3},{6,5},{0,7},{9,10},{11,12},{13... | collective-permute-start | bytes 442376 | tf_op jit(solution)/shard_map/while/body/eval_jaxpr/ppermute | solution.py:206
  77.7 1.9 %eval_jaxpr.5.part = f32[12,48,128]{2,1,0:T(8,128)S(1)} custom-call(bf16[12,48,128]{2,1,0:T(8,128)(2,1)S(1)} %get-tuple-element.125.rhs, bf16[12,48,128]{2,1,0:T(8,128)(2,1)S(1)} %get-tuple-element.117.value.earlier, bf16[12,128,128]{2,1,0:T(8,128)(2,1)S(1)} %get-tuple-element.126.kept, bf16[9,12,128,128]{3,2,1,0:T(8,128)(2,1)} %get-tuple-element.127.links), custom_call_target="tpu_custom_call" | custom-call | flops 94371840 | tf_op jit(solution)/shard_map/while/body/eval_jaxpr/pallas_call | solution.py:28
  79.7 1.1 collective-permute-done.2.arrived.c
  81.2 2.1 %collective-permute-start = (bf16[12,48,128]{2,1,0:T(8,128)(2,1)S(1)}, bf16[12,48,128]{2,1,0:T(8,128)(2,1)S(1)}, u32[]{:S(2)}, u32[]{:S(2)}) collective-permute-start(bf16[12,48,128]{2,1,0:T(8,128)(2,1)S(1)} %get-tuple-element.117.value.earlier), channel_id=1, source_target_pairs={{8,16},{24,32},{40,48},{56,64},{72,80},{88,96},{104,112},{120,128}... | collective-permute-start | bytes 442376 | tf_op jit(solution)/shard_map/while/body/eval_jaxpr/ppermute | solution.py:208
  83.3 3.3 %collective-permute-start.2 = (bf16[12,48,128]{2,1,0:T(8,128)(2,1)S(1)}, bf16[12,48,128]{2,1,0:T(8,128)(2,1)S(1)}, u32[]{:S(2)}, u32[]{:S(2)}) collective-permute-start(bf16[12,48,128]{2,1,0:T(8,128)(2,1)S(1)} %get-tuple-element.117.value.earlier), channel_id=1, source_target_pairs={{1,2},{3,4},{5,6},{7,0},{2,1},{4,3},{6,5},{0,7},{9,10},{11,12},{13... | collective-permute-start | bytes 442376 | tf_op jit(solution)/shard_map/while/body/eval_jaxpr/ppermute | solution.py:206
  86.7 1.9 %eval_jaxpr.5.part = f32[12,48,128]{2,1,0:T(8,128)S(1)} custom-call(bf16[12,48,128]{2,1,0:T(8,128)(2,1)S(1)} %get-tuple-element.125.rhs, bf16[12,48,128]{2,1,0:T(8,128)(2,1)S(1)} %get-tuple-element.117.value.earlier, bf16[12,128,128]{2,1,0:T(8,128)(2,1)S(1)} %get-tuple-element.126.kept, bf16[9,12,128,128]{3,2,1,0:T(8,128)(2,1)} %get-tuple-element.127.links), custom_call_target="tpu_custom_call" | custom-call | flops 94371840 | tf_op jit(solution)/shard_map/while/body/eval_jaxpr/pallas_call | solution.py:28
  88.7 1.1 collective-permute-done.2.arrived.c
  90.2 2.1 %collective-permute-start = (bf16[12,48,128]{2,1,0:T(8,128)(2,1)S(1)}, bf16[12,48,128]{2,1,0:T(8,128)(2,1)S(1)}, u32[]{:S(2)}, u32[]{:S(2)}) collective-permute-start(bf16[12,48,128]{2,1,0:T(8,128)(2,1)S(1)} %get-tuple-element.117.value.earlier), channel_id=1, source_target_pairs={{8,16},{24,32},{40,48},{56,64},{72,80},{88,96},{104,112},{120,128}... | collective-permute-start | bytes 442376 | tf_op jit(solution)/shard_map/while/body/eval_jaxpr/ppermute | solution.py:208
  92.3 3.3 %collective-permute-start.2 = (bf16[12,48,128]{2,1,0:T(8,128)(2,1)S(1)}, bf16[12,48,128]{2,1,0:T(8,128)(2,1)S(1)}, u32[]{:S(2)}, u32[]{:S(2)}) collective-permute-start(bf16[12,48,128]{2,1,0:T(8,128)(2,1)S(1)} %get-tuple-element.117.value.earlier), channel_id=1, source_target_pairs={{1,2},{3,4},{5,6},{7,0},{2,1},{4,3},{6,5},{0,7},{9,10},{11,12},{13... | collective-permute-start | bytes 442376 | tf_op jit(solution)/shard_map/while/body/eval_jaxpr/ppermute | solution.py:206
  95.7 1.9 %eval_jaxpr.5.part = f32[12,48,128]{2,1,0:T(8,128)S(1)} custom-call(bf16[12,48,128]{2,1,0:T(8,128)(2,1)S(1)} %get-tuple-element.125.rhs, bf16[12,48,128]{2,1,0:T(8,128)(2,1)S(1)} %get-tuple-element.117.value.earlier, bf16[12,128,128]{2,1,0:T(8,128)(2,1)S(1)} %get-tuple-element.126.kept, bf16[9,12,128,128]{3,2,1,0:T(8,128)(2,1)} %get-tuple-element.127.links), custom_call_target="tpu_custom_call" | custom-call | flops 94371840 | tf_op jit(solution)/shard_map/while/body/eval_jaxpr/pallas_call | solution.py:28
  97.6 1.1 collective-permute-done.2.arrived.c
  99.2 2.1 %collective-permute-start = (bf16[12,48,128]{2,1,0:T(8,128)(2,1)S(1)}, bf16[12,48,128]{2,1,0:T(8,128)(2,1)S(1)}, u32[]{:S(2)}, u32[]{:S(2)}) collective-permute-start(bf16[12,48,128]{2,1,0:T(8,128)(2,1)S(1)} %get-tuple-element.117.value.earlier), channel_id=1, source_target_pairs={{8,16},{24,32},{40,48},{56,64},{72,80},{88,96},{104,112},{120,128}... | collective-permute-start | bytes 442376 | tf_op jit(solution)/shard_map/while/body/eval_jaxpr/ppermute | solution.py:208
  101.3 3.3 %collective-permute-start.2 = (bf16[12,48,128]{2,1,0:T(8,128)(2,1)S(1)}, bf16[12,48,128]{2,1,0:T(8,128)(2,1)S(1)}, u32[]{:S(2)}, u32[]{:S(2)}) collective-permute-start(bf16[12,48,128]{2,1,0:T(8,128)(2,1)S(1)} %get-tuple-element.117.value.earlier), channel_id=1, source_target_pairs={{1,2},{3,4},{5,6},{7,0},{2,1},{4,3},{6,5},{0,7},{9,10},{11,12},{13... | collective-permute-start | bytes 442376 | tf_op jit(solution)/shard_map/while/body/eval_jaxpr/ppermute | solution.py:206
  104.6 1.9 %eval_jaxpr.5.part = f32[12,48,128]{2,1,0:T(8,128)S(1)} custom-call(bf16[12,48,128]{2,1,0:T(8,128)(2,1)S(1)} %get-tuple-element.125.rhs, bf16[12,48,128]{2,1,0:T(8,128)(2,1)S(1)} %get-tuple-element.117.value.earlier, bf16[12,128,128]{2,1,0:T(8,128)(2,1)S(1)} %get-tuple-element.126.kept, bf16[9,12,128,128]{3,2,1,0:T(8,128)(2,1)} %get-tuple-element.127.links), custom_call_target="tpu_custom_call" | custom-call | flops 94371840 | tf_op jit(solution)/shard_map/while/body/eval_jaxpr/pallas_call | solution.py:28
  106.6 1.1 collective-permute-done.2.arrived.c
  108.2 2.1 %collective-permute-start = (bf16[12,48,128]{2,1,0:T(8,128)(2,1)S(1)}, bf16[12,48,128]{2,1,0:T(8,128)(2,1)S(1)}, u32[]{:S(2)}, u32[]{:S(2)}) collective-permute-start(bf16[12,48,128]{2,1,0:T(8,128)(2,1)S(1)} %get-tuple-element.117.value.earlier), channel_id=1, source_target_pairs={{8,16},{24,32},{40,48},{56,64},{72,80},{88,96},{104,112},{120,128}... | collective-permute-start | bytes 442376 | tf_op jit(solution)/shard_map/while/body/eval_jaxpr/ppermute | solution.py:208
  110.3 3.3 %collective-permute-start.2 = (bf16[12,48,128]{2,1,0:T(8,128)(2,1)S(1)}, bf16[12,48,128]{2,1,0:T(8,128)(2,1)S(1)}, u32[]{:S(2)}, u32[]{:S(2)}) collective-permute-start(bf16[12,48,128]{2,1,0:T(8,128)(2,1)S(1)} %get-tuple-element.117.value.earlier), channel_id=1, source_target_pairs={{1,2},{3,4},{5,6},{7,0},{2,1},{4,3},{6,5},{0,7},{9,10},{11,12},{13... | collective-permute-start | bytes 442376 | tf_op jit(solution)/shard_map/while/body/eval_jaxpr/ppermute | solution.py:206
  113.6 1.9 %eval_jaxpr.5.part = f32[12,48,128]{2,1,0:T(8,128)S(1)} custom-call(bf16[12,48,128]{2,1,0:T(8,128)(2,1)S(1)} %get-tuple-element.125.rhs, bf16[12,48,128]{2,1,0:T(8,128)(2,1)S(1)} %get-tuple-element.117.value.earlier, bf16[12,128,128]{2,1,0:T(8,128)(2,1)S(1)} %get-tuple-element.126.kept, bf16[9,12,128,128]{3,2,1,0:T(8,128)(2,1)} %get-tuple-element.127.links), custom_call_target="tpu_custom_call" | custom-call | flops 94371840 | tf_op jit(solution)/shard_map/while/body/eval_jaxpr/pallas_call | solution.py:28
  115.6 1.1 collective-permute-done.2.arrived.c
  117.2 2.1 %collective-permute-start.8 = (bf16[12,48,128]{2,1,0:T(8,128)(2,1)S(1)}, bf16[12,48,128]{2,1,0:T(8,128)(2,1)S(1)}, u32[]{:S(2)}, u32[]{:S(2)}) collective-permute-start(bf16[12,48,128]{2,1,0:T(8,128)(2,1)S(1)} %get-tuple-element.51.value.earlier), channel_id=1, source_target_pairs={{8,16},{24,32},{40,48},{56,64},{72,80},{88,96},{104,112},{120,128}... | collective-permute-start | bytes 442376 | tf_op jit(solution)/shard_map/ppermute | solution.py:208
  119.3 3.3 %collective-permute-start.10 = (bf16[12,48,128]{2,1,0:T(8,128)(2,1)S(1)}, bf16[12,48,128]{2,1,0:T(8,128)(2,1)S(1)}, u32[]{:S(2)}, u32[]{:S(2)}) collective-permute-start(bf16[12,48,128]{2,1,0:T(8,128)(2,1)S(1)} %get-tuple-element.51.value.earlier), channel_id=1, source_target_pairs={{1,2},{3,4},{5,6},{7,0},{2,1},{4,3},{6,5},{0,7},{9,10},{11,12},{13... | collective-permute-start | bytes 442376 | tf_op jit(solution)/shard_map/ppermute | solution.py:206
  122.6 2.6 %shard_map.43 = (f32[12,48,128]{2,1,0:T(8,128)S(1)}, bf16[3,128,1536]{2,1,0:T(8,128)(2,1)S(1)}) custom-call(bf16[12,48,128]{2,1,0:T(8,128)(2,1)S(1)} %get-tuple-element.144, bf16[12,48,128]{2,1,0:T(8,128)(2,1)S(1)} %get-tuple-element.51.value.earlier, bf16[12,128,128]{2,1,0:T(8,128)(2,1)S(1)} %get-tuple-element.131, ...), custom_call_target="tpu_custom_call" | custom-call | flops 94371840 | tf_op jit(solution)/shard_map/pallas_call | solution.py:28
  125.2 0.5 collective-permute-done.10.arrived.c
  126.1 2.1 %collective-permute-start.12 = (bf16[12,48,128]{2,1,0:T(8,128)(2,1)S(1)}, bf16[12,48,128]{2,1,0:T(8,128)(2,1)S(1)}, u32[]{:S(2)}, u32[]{:S(2)}) collective-permute-start(bf16[12,48,128]{2,1,0:T(8,128)(2,1)S(1)} %shard_map.47.value.earlier), channel_id=1, source_target_pairs={{8,16},{24,32},{40,48},{56,64},{72,80},{88,96},{104,112},{120,128}... | collective-permute-start | bytes 442376 | tf_op jit(solution)/shard_map/ppermute | solution.py:208
  128.2 3.3 %collective-permute-start.14 = (bf16[12,48,128]{2,1,0:T(8,128)(2,1)S(1)}, bf16[12,48,128]{2,1,0:T(8,128)(2,1)S(1)}, u32[]{:S(2)}, u32[]{:S(2)}) collective-permute-start(bf16[12,48,128]{2,1,0:T(8,128)(2,1)S(1)} %shard_map.47.value.earlier), channel_id=1, source_target_pairs={{1,2},{3,4},{5,6},{7,0},{2,1},{4,3},{6,5},{0,7},{9,10},{11,12},{13... | collective-permute-start | bytes 442376 | tf_op jit(solution)/shard_map/ppermute | solution.py:206
  131.6 2.7 %shard_map.48 = (f32[12,48,128]{2,1,0:T(8,128)S(1)}, bf16[3,128,1536]{2,1,0:T(8,128)(2,1)S(1)}) custom-call(bf16[12,48,128]{2,1,0:T(8,128)(2,1)S(1)} %get-tuple-element.144, bf16[12,48,128]{2,1,0:T(8,128)(2,1)S(1)} %shard_map.47.value.earlier, bf16[12,128,128]{2,1,0:T(8,128)(2,1)S(1)} %get-tuple-element.131, bf16[9,12,128,128]{3,2,1,0:T(8,128)(2,1)} %get-tuple-element.181, ...), custom_call_target="tpu_custom_call" | custom-call | flops 94371840 | tf_op jit(solution)/shard_map/pallas_call | solution.py:28
  135.1 2.1 %collective-permute-start.16 = (bf16[12,48,128]{2,1,0:T(8,128)(2,1)S(1)}, bf16[12,48,128]{2,1,0:T(8,128)(2,1)S(1)}, u32[]{:S(2)}, u32[]{:S(2)}) collective-permute-start(bf16[12,48,128]{2,1,0:T(8,128)(2,1)S(1)} %shard_map.52.value.earlier), channel_id=1, source_target_pairs={{8,16},{24,32},{40,48},{56,64},{72,80},{88,96},{104,112},{120,128}... | collective-permute-start | bytes 442376 | tf_op jit(solution)/shard_map/ppermute | solution.py:208
  137.2 3.3 %collective-permute-start.18 = (bf16[12,48,128]{2,1,0:T(8,128)(2,1)S(1)}, bf16[12,48,128]{2,1,0:T(8,128)(2,1)S(1)}, u32[]{:S(2)}, u32[]{:S(2)}) collective-permute-start(bf16[12,48,128]{2,1,0:T(8,128)(2,1)S(1)} %shard_map.52.value.earlier), channel_id=1, source_target_pairs={{1,2},{3,4},{5,6},{7,0},{2,1},{4,3},{6,5},{0,7},{9,10},{11,12},{13... | collective-permute-start | bytes 442376 | tf_op jit(solution)/shard_map/ppermute | solution.py:206
  140.6 2.7 %shard_map.53 = (f32[12,48,128]{2,1,0:T(8,128)S(1)}, bf16[3,128,1536]{2,1,0:T(8,128)(2,1)S(1)}) custom-call(bf16[12,48,128]{2,1,0:T(8,128)(2,1)S(1)} %get-tuple-element.144, bf16[12,48,128]{2,1,0:T(8,128)(2,1)S(1)} %shard_map.52.value.earlier, bf16[12,128,128]{2,1,0:T(8,128)(2,1)S(1)} %get-tuple-element.131, bf16[9,12,128,128]{3,2,1,0:T(8,128)(2,1)} %get-tuple-element.181, ...), custom_call_target="tpu_custom_call" | custom-call | flops 94371840 | tf_op jit(solution)/shard_map/pallas_call | solution.py:28
  144.1 2.1 %collective-permute-start.20 = (bf16[12,48,128]{2,1,0:T(8,128)(2,1)S(1)}, bf16[12,48,128]{2,1,0:T(8,128)(2,1)S(1)}, u32[]{:S(2)}, u32[]{:S(2)}) collective-permute-start(bf16[12,48,128]{2,1,0:T(8,128)(2,1)S(1)} %shard_map.57.value.earlier), channel_id=1, source_target_pairs={{8,16},{24,32},{40,48},{56,64},{72,80},{88,96},{104,112},{120,128}... | collective-permute-start | bytes 442376 | tf_op jit(solution)/shard_map/ppermute | solution.py:208
  146.2 3.3 %collective-permute-start.22 = (bf16[12,48,128]{2,1,0:T(8,128)(2,1)S(1)}, bf16[12,48,128]{2,1,0:T(8,128)(2,1)S(1)}, u32[]{:S(2)}, u32[]{:S(2)}) collective-permute-start(bf16[12,48,128]{2,1,0:T(8,128)(2,1)S(1)} %shard_map.57.value.earlier), channel_id=1, source_target_pairs={{1,2},{3,4},{5,6},{7,0},{2,1},{4,3},{6,5},{0,7},{9,10},{11,12},{13... | collective-permute-start | bytes 442376 | tf_op jit(solution)/shard_map/ppermute | solution.py:206
  149.5 2.7 %shard_map.58 = (f32[12,48,128]{2,1,0:T(8,128)S(1)}, bf16[3,128,1536]{2,1,0:T(8,128)(2,1)S(1)}) custom-call(bf16[12,48,128]{2,1,0:T(8,128)(2,1)S(1)} %get-tuple-element.144, bf16[12,48,128]{2,1,0:T(8,128)(2,1)S(1)} %shard_map.57.value.earlier, bf16[12,128,128]{2,1,0:T(8,128)(2,1)S(1)} %get-tuple-element.131, bf16[9,12,128,128]{3,2,1,0:T(8,128)(2,1)} %get-tuple-element.181, ...), custom_call_target="tpu_custom_call" | custom-call | flops 94371840 | tf_op jit(solution)/shard_map/pallas_call | solution.py:28
  153.0 1.5 shard_map.63
  (148 shorter events, 7.9 us)
Async XLA Ops:
  3.3 15.4 %collective-permute-start.4 = (bf16[12,48,128]{2,1,0:T(8,128)(2,1)S(1)}, bf16[12,48,128]{2,1,0:T(8,128)(2,1)S(1)}, u32[]{:S(2)}, u32[]{:S(2)}) collective-permute-start(bf16[12,48,128]{2,1,0:T(8,128)(2,1)S(1)} %shard_map.37.rhs.earlier), channel_id=1, source_target_pairs={{8,16},{24,32},{40,48},{56,64},{72,80},{88,96},{104,112},{120,128}... | collective-permute-start | bytes 442376 | tf_op jit(solution)/shard_map/ppermute | solution.py:208
  12.3 6.5 %collective-permute-start.5 = (bf16[12,48,128]{2,1,0:T(8,128)(2,1)S(1)}, bf16[12,48,128]{2,1,0:T(8,128)(2,1)S(1)}, u32[]{:S(2)}, u32[]{:S(2)}) collective-permute-start(bf16[12,48,128]{2,1,0:T(8,128)(2,1)S(1)} %shard_map.37.rhs.earlier), channel_id=1, source_target_pairs={{0,8},{16,24},{32,40},{48,56},{64,72},{80,88},{96,104},{112,120},{... | collective-permute-start | bytes 442376 | tf_op jit(solution)/shard_map/ppermute | solution.py:207
  12.3 6.5 %collective-permute-start.6 = (bf16[12,48,128]{2,1,0:T(8,128)(2,1)S(1)}, bf16[12,48,128]{2,1,0:T(8,128)(2,1)S(1)}, u32[]{:S(2)}, u32[]{:S(2)}) collective-permute-start(bf16[12,48,128]{2,1,0:T(8,128)(2,1)S(1)} %shard_map.37.rhs.earlier), channel_id=1, source_target_pairs={{1,2},{3,4},{5,6},{7,0},{2,1},{4,3},{6,5},{0,7},{9,10},{11,12},{13... | collective-permute-start | bytes 442376 | tf_op jit(solution)/shard_map/ppermute | solution.py:206
  14.3 4.5 %collective-permute-start.7 = (bf16[12,48,128]{2,1,0:T(8,128)(2,1)S(1)}, bf16[12,48,128]{2,1,0:T(8,128)(2,1)S(1)}, u32[]{:S(2)}, u32[]{:S(2)}) collective-permute-start(bf16[12,48,128]{2,1,0:T(8,128)(2,1)S(1)} %shard_map.37.rhs.earlier), channel_id=1, source_target_pairs={{0,1},{2,3},{4,5},{6,7},{1,0},{3,2},{5,4},{7,6},{8,9},{10,11},{12,... | collective-permute-start | bytes 442376 | tf_op jit(solution)/shard_map/ppermute | solution.py:205
  19.2 8.7 %collective-permute-start = (bf16[12,48,128]{2,1,0:T(8,128)(2,1)S(1)}, bf16[12,48,128]{2,1,0:T(8,128)(2,1)S(1)}, u32[]{:S(2)}, u32[]{:S(2)}) collective-permute-start(bf16[12,48,128]{2,1,0:T(8,128)(2,1)S(1)} %get-tuple-element.117.value.earlier), channel_id=1, source_target_pairs={{8,16},{24,32},{40,48},{56,64},{72,80},{88,96},{104,112},{120,128}... | collective-permute-start | bytes 442376 | tf_op jit(solution)/shard_map/while/body/eval_jaxpr/ppermute | solution.py:208
  20.8 7.0 %collective-permute-start.1 = (bf16[12,48,128]{2,1,0:T(8,128)(2,1)S(1)}, bf16[12,48,128]{2,1,0:T(8,128)(2,1)S(1)}, u32[]{:S(2)}, u32[]{:S(2)}) collective-permute-start(bf16[12,48,128]{2,1,0:T(8,128)(2,1)S(1)} %get-tuple-element.117.value.earlier), channel_id=1, source_target_pairs={{0,8},{16,24},{32,40},{48,56},{64,72},{80,88},{96,104},{112,120},{... | collective-permute-start | bytes 442376 | tf_op jit(solution)/shard_map/while/body/eval_jaxpr/ppermute | solution.py:207
  20.8 7.0 %collective-permute-start.2 = (bf16[12,48,128]{2,1,0:T(8,128)(2,1)S(1)}, bf16[12,48,128]{2,1,0:T(8,128)(2,1)S(1)}, u32[]{:S(2)}, u32[]{:S(2)}) collective-permute-start(bf16[12,48,128]{2,1,0:T(8,128)(2,1)S(1)} %get-tuple-element.117.value.earlier), channel_id=1, source_target_pairs={{1,2},{3,4},{5,6},{7,0},{2,1},{4,3},{6,5},{0,7},{9,10},{11,12},{13... | collective-permute-start | bytes 442376 | tf_op jit(solution)/shard_map/while/body/eval_jaxpr/ppermute | solution.py:206
  23.8 4.1 %collective-permute-start.3 = (bf16[12,48,128]{2,1,0:T(8,128)(2,1)S(1)}, bf16[12,48,128]{2,1,0:T(8,128)(2,1)S(1)}, u32[]{:S(2)}, u32[]{:S(2)}) collective-permute-start(bf16[12,48,128]{2,1,0:T(8,128)(2,1)S(1)} %get-tuple-element.117.value.earlier), channel_id=1, source_target_pairs={{0,1},{2,3},{4,5},{6,7},{1,0},{3,2},{5,4},{7,6},{8,9},{10,11},{12,... | collective-permute-start | bytes 442376 | tf_op jit(solution)/shard_map/while/body/eval_jaxpr/ppermute | solution.py:205
  28.3 7.7 %collective-permute-start = (bf16[12,48,128]{2,1,0:T(8,128)(2,1)S(1)}, bf16[12,48,128]{2,1,0:T(8,128)(2,1)S(1)}, u32[]{:S(2)}, u32[]{:S(2)}) collective-permute-start(bf16[12,48,128]{2,1,0:T(8,128)(2,1)S(1)} %get-tuple-element.117.value.earlier), channel_id=1, source_target_pairs={{8,16},{24,32},{40,48},{56,64},{72,80},{88,96},{104,112},{120,128}... | collective-permute-start | bytes 442376 | tf_op jit(solution)/shard_map/while/body/eval_jaxpr/ppermute | solution.py:208
  29.5 6.5 %collective-permute-start.1 = (bf16[12,48,128]{2,1,0:T(8,128)(2,1)S(1)}, bf16[12,48,128]{2,1,0:T(8,128)(2,1)S(1)}, u32[]{:S(2)}, u32[]{:S(2)}) collective-permute-start(bf16[12,48,128]{2,1,0:T(8,128)(2,1)S(1)} %get-tuple-element.117.value.earlier), channel_id=1, source_target_pairs={{0,8},{16,24},{32,40},{48,56},{64,72},{80,88},{96,104},{112,120},{... | collective-permute-start | bytes 442376 | tf_op jit(solution)/shard_map/while/body/eval_jaxpr/ppermute | solution.py:207
  29.5 6.5 %collective-permute-start.2 = (bf16[12,48,128]{2,1,0:T(8,128)(2,1)S(1)}, bf16[12,48,128]{2,1,0:T(8,128)(2,1)S(1)}, u32[]{:S(2)}, u32[]{:S(2)}) collective-permute-start(bf16[12,48,128]{2,1,0:T(8,128)(2,1)S(1)} %get-tuple-element.117.value.earlier), channel_id=1, source_target_pairs={{1,2},{3,4},{5,6},{7,0},{2,1},{4,3},{6,5},{0,7},{9,10},{11,12},{13... | collective-permute-start | bytes 442376 | tf_op jit(solution)/shard_map/while/body/eval_jaxpr/ppermute | solution.py:206
  32.7 3.3 %collective-permute-start.3 = (bf16[12,48,128]{2,1,0:T(8,128)(2,1)S(1)}, bf16[12,48,128]{2,1,0:T(8,128)(2,1)S(1)}, u32[]{:S(2)}, u32[]{:S(2)}) collective-permute-start(bf16[12,48,128]{2,1,0:T(8,128)(2,1)S(1)} %get-tuple-element.117.value.earlier), channel_id=1, source_target_pairs={{0,1},{2,3},{4,5},{6,7},{1,0},{3,2},{5,4},{7,6},{8,9},{10,11},{12,... | collective-permute-start | bytes 442376 | tf_op jit(solution)/shard_map/while/body/eval_jaxpr/ppermute | solution.py:205
  36.5 7.4 %collective-permute-start = (bf16[12,48,128]{2,1,0:T(8,128)(2,1)S(1)}, bf16[12,48,128]{2,1,0:T(8,128)(2,1)S(1)}, u32[]{:S(2)}, u32[]{:S(2)}) collective-permute-start(bf16[12,48,128]{2,1,0:T(8,128)(2,1)S(1)} %get-tuple-element.117.value.earlier), channel_id=1, source_target_pairs={{8,16},{24,32},{40,48},{56,64},{72,80},{88,96},{104,112},{120,128}... | collective-permute-start | bytes 442376 | tf_op jit(solution)/shard_map/while/body/eval_jaxpr/ppermute | solution.py:208
  38.5 5.3 %collective-permute-start.1 = (bf16[12,48,128]{2,1,0:T(8,128)(2,1)S(1)}, bf16[12,48,128]{2,1,0:T(8,128)(2,1)S(1)}, u32[]{:S(2)}, u32[]{:S(2)}) collective-permute-start(bf16[12,48,128]{2,1,0:T(8,128)(2,1)S(1)} %get-tuple-element.117.value.earlier), channel_id=1, source_target_pairs={{0,8},{16,24},{32,40},{48,56},{64,72},{80,88},{96,104},{112,120},{... | collective-permute-start | bytes 442376 | tf_op jit(solution)/shard_map/while/body/eval_jaxpr/ppermute | solution.py:207
  38.5 6.3 %collective-permute-start.2 = (bf16[12,48,128]{2,1,0:T(8,128)(2,1)S(1)}, bf16[12,48,128]{2,1,0:T(8,128)(2,1)S(1)}, u32[]{:S(2)}, u32[]{:S(2)}) collective-permute-start(bf16[12,48,128]{2,1,0:T(8,128)(2,1)S(1)} %get-tuple-element.117.value.earlier), channel_id=1, source_target_pairs={{1,2},{3,4},{5,6},{7,0},{2,1},{4,3},{6,5},{0,7},{9,10},{11,12},{13... | collective-permute-start | bytes 442376 | tf_op jit(solution)/shard_map/while/body/eval_jaxpr/ppermute | solution.py:206
  41.7 3.1 %collective-permute-start.3 = (bf16[12,48,128]{2,1,0:T(8,128)(2,1)S(1)}, bf16[12,48,128]{2,1,0:T(8,128)(2,1)S(1)}, u32[]{:S(2)}, u32[]{:S(2)}) collective-permute-start(bf16[12,48,128]{2,1,0:T(8,128)(2,1)S(1)} %get-tuple-element.117.value.earlier), channel_id=1, source_target_pairs={{0,1},{2,3},{4,5},{6,7},{1,0},{3,2},{5,4},{7,6},{8,9},{10,11},{12,... | collective-permute-start | bytes 442376 | tf_op jit(solution)/shard_map/while/body/eval_jaxpr/ppermute | solution.py:205
  45.3 7.4 %collective-permute-start = (bf16[12,48,128]{2,1,0:T(8,128)(2,1)S(1)}, bf16[12,48,128]{2,1,0:T(8,128)(2,1)S(1)}, u32[]{:S(2)}, u32[]{:S(2)}) collective-permute-start(bf16[12,48,128]{2,1,0:T(8,128)(2,1)S(1)} %get-tuple-element.117.value.earlier), channel_id=1, source_target_pairs={{8,16},{24,32},{40,48},{56,64},{72,80},{88,96},{104,112},{120,128}... | collective-permute-start | bytes 442376 | tf_op jit(solution)/shard_map/while/body/eval_jaxpr/ppermute | solution.py:208
  47.4 5.3 %collective-permute-start.1 = (bf16[12,48,128]{2,1,0:T(8,128)(2,1)S(1)}, bf16[12,48,128]{2,1,0:T(8,128)(2,1)S(1)}, u32[]{:S(2)}, u32[]{:S(2)}) collective-permute-start(bf16[12,48,128]{2,1,0:T(8,128)(2,1)S(1)} %get-tuple-element.117.value.earlier), channel_id=1, source_target_pairs={{0,8},{16,24},{32,40},{48,56},{64,72},{80,88},{96,104},{112,120},{... | collective-permute-start | bytes 442376 | tf_op jit(solution)/shard_map/while/body/eval_jaxpr/ppermute | solution.py:207
  47.4 6.5 %collective-permute-start.2 = (bf16[12,48,128]{2,1,0:T(8,128)(2,1)S(1)}, bf16[12,48,128]{2,1,0:T(8,128)(2,1)S(1)}, u32[]{:S(2)}, u32[]{:S(2)}) collective-permute-start(bf16[12,48,128]{2,1,0:T(8,128)(2,1)S(1)} %get-tuple-element.117.value.earlier), channel_id=1, source_target_pairs={{1,2},{3,4},{5,6},{7,0},{2,1},{4,3},{6,5},{0,7},{9,10},{11,12},{13... | collective-permute-start | bytes 442376 | tf_op jit(solution)/shard_map/while/body/eval_jaxpr/ppermute | solution.py:206
  50.7 3.1 %collective-permute-start.3 = (bf16[12,48,128]{2,1,0:T(8,128)(2,1)S(1)}, bf16[12,48,128]{2,1,0:T(8,128)(2,1)S(1)}, u32[]{:S(2)}, u32[]{:S(2)}) collective-permute-start(bf16[12,48,128]{2,1,0:T(8,128)(2,1)S(1)} %get-tuple-element.117.value.earlier), channel_id=1, source_target_pairs={{0,1},{2,3},{4,5},{6,7},{1,0},{3,2},{5,4},{7,6},{8,9},{10,11},{12,... | collective-permute-start | bytes 442376 | tf_op jit(solution)/shard_map/while/body/eval_jaxpr/ppermute | solution.py:205
  54.2 7.4 %collective-permute-start = (bf16[12,48,128]{2,1,0:T(8,128)(2,1)S(1)}, bf16[12,48,128]{2,1,0:T(8,128)(2,1)S(1)}, u32[]{:S(2)}, u32[]{:S(2)}) collective-permute-start(bf16[12,48,128]{2,1,0:T(8,128)(2,1)S(1)} %get-tuple-element.117.value.earlier), channel_id=1, source_target_pairs={{8,16},{24,32},{40,48},{56,64},{72,80},{88,96},{104,112},{120,128}... | collective-permute-start | bytes 442376 | tf_op jit(solution)/shard_map/while/body/eval_jaxpr/ppermute | solution.py:208
  56.3 5.3 %collective-permute-start.1 = (bf16[12,48,128]{2,1,0:T(8,128)(2,1)S(1)}, bf16[12,48,128]{2,1,0:T(8,128)(2,1)S(1)}, u32[]{:S(2)}, u32[]{:S(2)}) collective-permute-start(bf16[12,48,128]{2,1,0:T(8,128)(2,1)S(1)} %get-tuple-element.117.value.earlier), channel_id=1, source_target_pairs={{0,8},{16,24},{32,40},{48,56},{64,72},{80,88},{96,104},{112,120},{... | collective-permute-start | bytes 442376 | tf_op jit(solution)/shard_map/while/body/eval_jaxpr/ppermute | solution.py:207
  56.4 6.5 %collective-permute-start.2 = (bf16[12,48,128]{2,1,0:T(8,128)(2,1)S(1)}, bf16[12,48,128]{2,1,0:T(8,128)(2,1)S(1)}, u32[]{:S(2)}, u32[]{:S(2)}) collective-permute-start(bf16[12,48,128]{2,1,0:T(8,128)(2,1)S(1)} %get-tuple-element.117.value.earlier), channel_id=1, source_target_pairs={{1,2},{3,4},{5,6},{7,0},{2,1},{4,3},{6,5},{0,7},{9,10},{11,12},{13... | collective-permute-start | bytes 442376 | tf_op jit(solution)/shard_map/while/body/eval_jaxpr/ppermute | solution.py:206
  59.7 3.1 %collective-permute-start.3 = (bf16[12,48,128]{2,1,0:T(8,128)(2,1)S(1)}, bf16[12,48,128]{2,1,0:T(8,128)(2,1)S(1)}, u32[]{:S(2)}, u32[]{:S(2)}) collective-permute-start(bf16[12,48,128]{2,1,0:T(8,128)(2,1)S(1)} %get-tuple-element.117.value.earlier), channel_id=1, source_target_pairs={{0,1},{2,3},{4,5},{6,7},{1,0},{3,2},{5,4},{7,6},{8,9},{10,11},{12,... | collective-permute-start | bytes 442376 | tf_op jit(solution)/shard_map/while/body/eval_jaxpr/ppermute | solution.py:205
  63.2 7.4 %collective-permute-start = (bf16[12,48,128]{2,1,0:T(8,128)(2,1)S(1)}, bf16[12,48,128]{2,1,0:T(8,128)(2,1)S(1)}, u32[]{:S(2)}, u32[]{:S(2)}) collective-permute-start(bf16[12,48,128]{2,1,0:T(8,128)(2,1)S(1)} %get-tuple-element.117.value.earlier), channel_id=1, source_target_pairs={{8,16},{24,32},{40,48},{56,64},{72,80},{88,96},{104,112},{120,128}... | collective-permute-start | bytes 442376 | tf_op jit(solution)/shard_map/while/body/eval_jaxpr/ppermute | solution.py:208
  65.3 5.3 %collective-permute-start.1 = (bf16[12,48,128]{2,1,0:T(8,128)(2,1)S(1)}, bf16[12,48,128]{2,1,0:T(8,128)(2,1)S(1)}, u32[]{:S(2)}, u32[]{:S(2)}) collective-permute-start(bf16[12,48,128]{2,1,0:T(8,128)(2,1)S(1)} %get-tuple-element.117.value.earlier), channel_id=1, source_target_pairs={{0,8},{16,24},{32,40},{48,56},{64,72},{80,88},{96,104},{112,120},{... | collective-permute-start | bytes 442376 | tf_op jit(solution)/shard_map/while/body/eval_jaxpr/ppermute | solution.py:207
  65.3 6.5 %collective-permute-start.2 = (bf16[12,48,128]{2,1,0:T(8,128)(2,1)S(1)}, bf16[12,48,128]{2,1,0:T(8,128)(2,1)S(1)}, u32[]{:S(2)}, u32[]{:S(2)}) collective-permute-start(bf16[12,48,128]{2,1,0:T(8,128)(2,1)S(1)} %get-tuple-element.117.value.earlier), channel_id=1, source_target_pairs={{1,2},{3,4},{5,6},{7,0},{2,1},{4,3},{6,5},{0,7},{9,10},{11,12},{13... | collective-permute-start | bytes 442376 | tf_op jit(solution)/shard_map/while/body/eval_jaxpr/ppermute | solution.py:206
  68.7 3.1 %collective-permute-start.3 = (bf16[12,48,128]{2,1,0:T(8,128)(2,1)S(1)}, bf16[12,48,128]{2,1,0:T(8,128)(2,1)S(1)}, u32[]{:S(2)}, u32[]{:S(2)}) collective-permute-start(bf16[12,48,128]{2,1,0:T(8,128)(2,1)S(1)} %get-tuple-element.117.value.earlier), channel_id=1, source_target_pairs={{0,1},{2,3},{4,5},{6,7},{1,0},{3,2},{5,4},{7,6},{8,9},{10,11},{12,... | collective-permute-start | bytes 442376 | tf_op jit(solution)/shard_map/while/body/eval_jaxpr/ppermute | solution.py:205
  72.2 7.4 %collective-permute-start = (bf16[12,48,128]{2,1,0:T(8,128)(2,1)S(1)}, bf16[12,48,128]{2,1,0:T(8,128)(2,1)S(1)}, u32[]{:S(2)}, u32[]{:S(2)}) collective-permute-start(bf16[12,48,128]{2,1,0:T(8,128)(2,1)S(1)} %get-tuple-element.117.value.earlier), channel_id=1, source_target_pairs={{8,16},{24,32},{40,48},{56,64},{72,80},{88,96},{104,112},{120,128}... | collective-permute-start | bytes 442376 | tf_op jit(solution)/shard_map/while/body/eval_jaxpr/ppermute | solution.py:208
  74.3 5.3 %collective-permute-start.1 = (bf16[12,48,128]{2,1,0:T(8,128)(2,1)S(1)}, bf16[12,48,128]{2,1,0:T(8,128)(2,1)S(1)}, u32[]{:S(2)}, u32[]{:S(2)}) collective-permute-start(bf16[12,48,128]{2,1,0:T(8,128)(2,1)S(1)} %get-tuple-element.117.value.earlier), channel_id=1, source_target_pairs={{0,8},{16,24},{32,40},{48,56},{64,72},{80,88},{96,104},{112,120},{... | collective-permute-start | bytes 442376 | tf_op jit(solution)/shard_map/while/body/eval_jaxpr/ppermute | solution.py:207
  74.3 6.5 %collective-permute-start.2 = (bf16[12,48,128]{2,1,0:T(8,128)(2,1)S(1)}, bf16[12,48,128]{2,1,0:T(8,128)(2,1)S(1)}, u32[]{:S(2)}, u32[]{:S(2)}) collective-permute-start(bf16[12,48,128]{2,1,0:T(8,128)(2,1)S(1)} %get-tuple-element.117.value.earlier), channel_id=1, source_target_pairs={{1,2},{3,4},{5,6},{7,0},{2,1},{4,3},{6,5},{0,7},{9,10},{11,12},{13... | collective-permute-start | bytes 442376 | tf_op jit(solution)/shard_map/while/body/eval_jaxpr/ppermute | solution.py:206
  77.7 3.1 %collective-permute-start.3 = (bf16[12,48,128]{2,1,0:T(8,128)(2,1)S(1)}, bf16[12,48,128]{2,1,0:T(8,128)(2,1)S(1)}, u32[]{:S(2)}, u32[]{:S(2)}) collective-permute-start(bf16[12,48,128]{2,1,0:T(8,128)(2,1)S(1)} %get-tuple-element.117.value.earlier), channel_id=1, source_target_pairs={{0,1},{2,3},{4,5},{6,7},{1,0},{3,2},{5,4},{7,6},{8,9},{10,11},{12,... | collective-permute-start | bytes 442376 | tf_op jit(solution)/shard_map/while/body/eval_jaxpr/ppermute | solution.py:205
  81.2 7.4 %collective-permute-start = (bf16[12,48,128]{2,1,0:T(8,128)(2,1)S(1)}, bf16[12,48,128]{2,1,0:T(8,128)(2,1)S(1)}, u32[]{:S(2)}, u32[]{:S(2)}) collective-permute-start(bf16[12,48,128]{2,1,0:T(8,128)(2,1)S(1)} %get-tuple-element.117.value.earlier), channel_id=1, source_target_pairs={{8,16},{24,32},{40,48},{56,64},{72,80},{88,96},{104,112},{120,128}... | collective-permute-start | bytes 442376 | tf_op jit(solution)/shard_map/while/body/eval_jaxpr/ppermute | solution.py:208
  83.3 5.3 %collective-permute-start.1 = (bf16[12,48,128]{2,1,0:T(8,128)(2,1)S(1)}, bf16[12,48,128]{2,1,0:T(8,128)(2,1)S(1)}, u32[]{:S(2)}, u32[]{:S(2)}) collective-permute-start(bf16[12,48,128]{2,1,0:T(8,128)(2,1)S(1)} %get-tuple-element.117.value.earlier), channel_id=1, source_target_pairs={{0,8},{16,24},{32,40},{48,56},{64,72},{80,88},{96,104},{112,120},{... | collective-permute-start | bytes 442376 | tf_op jit(solution)/shard_map/while/body/eval_jaxpr/ppermute | solution.py:207
  83.3 6.5 %collective-permute-start.2 = (bf16[12,48,128]{2,1,0:T(8,128)(2,1)S(1)}, bf16[12,48,128]{2,1,0:T(8,128)(2,1)S(1)}, u32[]{:S(2)}, u32[]{:S(2)}) collective-permute-start(bf16[12,48,128]{2,1,0:T(8,128)(2,1)S(1)} %get-tuple-element.117.value.earlier), channel_id=1, source_target_pairs={{1,2},{3,4},{5,6},{7,0},{2,1},{4,3},{6,5},{0,7},{9,10},{11,12},{13... | collective-permute-start | bytes 442376 | tf_op jit(solution)/shard_map/while/body/eval_jaxpr/ppermute | solution.py:206
  86.7 3.1 %collective-permute-start.3 = (bf16[12,48,128]{2,1,0:T(8,128)(2,1)S(1)}, bf16[12,48,128]{2,1,0:T(8,128)(2,1)S(1)}, u32[]{:S(2)}, u32[]{:S(2)}) collective-permute-start(bf16[12,48,128]{2,1,0:T(8,128)(2,1)S(1)} %get-tuple-element.117.value.earlier), channel_id=1, source_target_pairs={{0,1},{2,3},{4,5},{6,7},{1,0},{3,2},{5,4},{7,6},{8,9},{10,11},{12,... | collective-permute-start | bytes 442376 | tf_op jit(solution)/shard_map/while/body/eval_jaxpr/ppermute | solution.py:205
  90.2 7.4 %collective-permute-start = (bf16[12,48,128]{2,1,0:T(8,128)(2,1)S(1)}, bf16[12,48,128]{2,1,0:T(8,128)(2,1)S(1)}, u32[]{:S(2)}, u32[]{:S(2)}) collective-permute-start(bf16[12,48,128]{2,1,0:T(8,128)(2,1)S(1)} %get-tuple-element.117.value.earlier), channel_id=1, source_target_pairs={{8,16},{24,32},{40,48},{56,64},{72,80},{88,96},{104,112},{120,128}... | collective-permute-start | bytes 442376 | tf_op jit(solution)/shard_map/while/body/eval_jaxpr/ppermute | solution.py:208
  92.3 5.3 %collective-permute-start.1 = (bf16[12,48,128]{2,1,0:T(8,128)(2,1)S(1)}, bf16[12,48,128]{2,1,0:T(8,128)(2,1)S(1)}, u32[]{:S(2)}, u32[]{:S(2)}) collective-permute-start(bf16[12,48,128]{2,1,0:T(8,128)(2,1)S(1)} %get-tuple-element.117.value.earlier), channel_id=1, source_target_pairs={{0,8},{16,24},{32,40},{48,56},{64,72},{80,88},{96,104},{112,120},{... | collective-permute-start | bytes 442376 | tf_op jit(solution)/shard_map/while/body/eval_jaxpr/ppermute | solution.py:207
  92.3 6.5 %collective-permute-start.2 = (bf16[12,48,128]{2,1,0:T(8,128)(2,1)S(1)}, bf16[12,48,128]{2,1,0:T(8,128)(2,1)S(1)}, u32[]{:S(2)}, u32[]{:S(2)}) collective-permute-start(bf16[12,48,128]{2,1,0:T(8,128)(2,1)S(1)} %get-tuple-element.117.value.earlier), channel_id=1, source_target_pairs={{1,2},{3,4},{5,6},{7,0},{2,1},{4,3},{6,5},{0,7},{9,10},{11,12},{13... | collective-permute-start | bytes 442376 | tf_op jit(solution)/shard_map/while/body/eval_jaxpr/ppermute | solution.py:206
  95.7 3.1 %collective-permute-start.3 = (bf16[12,48,128]{2,1,0:T(8,128)(2,1)S(1)}, bf16[12,48,128]{2,1,0:T(8,128)(2,1)S(1)}, u32[]{:S(2)}, u32[]{:S(2)}) collective-permute-start(bf16[12,48,128]{2,1,0:T(8,128)(2,1)S(1)} %get-tuple-element.117.value.earlier), channel_id=1, source_target_pairs={{0,1},{2,3},{4,5},{6,7},{1,0},{3,2},{5,4},{7,6},{8,9},{10,11},{12,... | collective-permute-start | bytes 442376 | tf_op jit(solution)/shard_map/while/body/eval_jaxpr/ppermute | solution.py:205
  99.2 7.4 %collective-permute-start = (bf16[12,48,128]{2,1,0:T(8,128)(2,1)S(1)}, bf16[12,48,128]{2,1,0:T(8,128)(2,1)S(1)}, u32[]{:S(2)}, u32[]{:S(2)}) collective-permute-start(bf16[12,48,128]{2,1,0:T(8,128)(2,1)S(1)} %get-tuple-element.117.value.earlier), channel_id=1, source_target_pairs={{8,16},{24,32},{40,48},{56,64},{72,80},{88,96},{104,112},{120,128}... | collective-permute-start | bytes 442376 | tf_op jit(solution)/shard_map/while/body/eval_jaxpr/ppermute | solution.py:208
  101.3 5.3 %collective-permute-start.1 = (bf16[12,48,128]{2,1,0:T(8,128)(2,1)S(1)}, bf16[12,48,128]{2,1,0:T(8,128)(2,1)S(1)}, u32[]{:S(2)}, u32[]{:S(2)}) collective-permute-start(bf16[12,48,128]{2,1,0:T(8,128)(2,1)S(1)} %get-tuple-element.117.value.earlier), channel_id=1, source_target_pairs={{0,8},{16,24},{32,40},{48,56},{64,72},{80,88},{96,104},{112,120},{... | collective-permute-start | bytes 442376 | tf_op jit(solution)/shard_map/while/body/eval_jaxpr/ppermute | solution.py:207
  101.3 6.5 %collective-permute-start.2 = (bf16[12,48,128]{2,1,0:T(8,128)(2,1)S(1)}, bf16[12,48,128]{2,1,0:T(8,128)(2,1)S(1)}, u32[]{:S(2)}, u32[]{:S(2)}) collective-permute-start(bf16[12,48,128]{2,1,0:T(8,128)(2,1)S(1)} %get-tuple-element.117.value.earlier), channel_id=1, source_target_pairs={{1,2},{3,4},{5,6},{7,0},{2,1},{4,3},{6,5},{0,7},{9,10},{11,12},{13... | collective-permute-start | bytes 442376 | tf_op jit(solution)/shard_map/while/body/eval_jaxpr/ppermute | solution.py:206
  104.6 3.1 %collective-permute-start.3 = (bf16[12,48,128]{2,1,0:T(8,128)(2,1)S(1)}, bf16[12,48,128]{2,1,0:T(8,128)(2,1)S(1)}, u32[]{:S(2)}, u32[]{:S(2)}) collective-permute-start(bf16[12,48,128]{2,1,0:T(8,128)(2,1)S(1)} %get-tuple-element.117.value.earlier), channel_id=1, source_target_pairs={{0,1},{2,3},{4,5},{6,7},{1,0},{3,2},{5,4},{7,6},{8,9},{10,11},{12,... | collective-permute-start | bytes 442376 | tf_op jit(solution)/shard_map/while/body/eval_jaxpr/ppermute | solution.py:205
  108.2 7.4 %collective-permute-start = (bf16[12,48,128]{2,1,0:T(8,128)(2,1)S(1)}, bf16[12,48,128]{2,1,0:T(8,128)(2,1)S(1)}, u32[]{:S(2)}, u32[]{:S(2)}) collective-permute-start(bf16[12,48,128]{2,1,0:T(8,128)(2,1)S(1)} %get-tuple-element.117.value.earlier), channel_id=1, source_target_pairs={{8,16},{24,32},{40,48},{56,64},{72,80},{88,96},{104,112},{120,128}... | collective-permute-start | bytes 442376 | tf_op jit(solution)/shard_map/while/body/eval_jaxpr/ppermute | solution.py:208
  110.3 5.3 %collective-permute-start.1 = (bf16[12,48,128]{2,1,0:T(8,128)(2,1)S(1)}, bf16[12,48,128]{2,1,0:T(8,128)(2,1)S(1)}, u32[]{:S(2)}, u32[]{:S(2)}) collective-permute-start(bf16[12,48,128]{2,1,0:T(8,128)(2,1)S(1)} %get-tuple-element.117.value.earlier), channel_id=1, source_target_pairs={{0,8},{16,24},{32,40},{48,56},{64,72},{80,88},{96,104},{112,120},{... | collective-permute-start | bytes 442376 | tf_op jit(solution)/shard_map/while/body/eval_jaxpr/ppermute | solution.py:207
  110.3 6.5 %collective-permute-start.2 = (bf16[12,48,128]{2,1,0:T(8,128)(2,1)S(1)}, bf16[12,48,128]{2,1,0:T(8,128)(2,1)S(1)}, u32[]{:S(2)}, u32[]{:S(2)}) collective-permute-start(bf16[12,48,128]{2,1,0:T(8,128)(2,1)S(1)} %get-tuple-element.117.value.earlier), channel_id=1, source_target_pairs={{1,2},{3,4},{5,6},{7,0},{2,1},{4,3},{6,5},{0,7},{9,10},{11,12},{13... | collective-permute-start | bytes 442376 | tf_op jit(solution)/shard_map/while/body/eval_jaxpr/ppermute | solution.py:206
  113.6 3.1 %collective-permute-start.3 = (bf16[12,48,128]{2,1,0:T(8,128)(2,1)S(1)}, bf16[12,48,128]{2,1,0:T(8,128)(2,1)S(1)}, u32[]{:S(2)}, u32[]{:S(2)}) collective-permute-start(bf16[12,48,128]{2,1,0:T(8,128)(2,1)S(1)} %get-tuple-element.117.value.earlier), channel_id=1, source_target_pairs={{0,1},{2,3},{4,5},{6,7},{1,0},{3,2},{5,4},{7,6},{8,9},{10,11},{12,... | collective-permute-start | bytes 442376 | tf_op jit(solution)/shard_map/while/body/eval_jaxpr/ppermute | solution.py:205
  117.2 8.0 %collective-permute-start.8 = (bf16[12,48,128]{2,1,0:T(8,128)(2,1)S(1)}, bf16[12,48,128]{2,1,0:T(8,128)(2,1)S(1)}, u32[]{:S(2)}, u32[]{:S(2)}) collective-permute-start(bf16[12,48,128]{2,1,0:T(8,128)(2,1)S(1)} %get-tuple-element.51.value.earlier), channel_id=1, source_target_pairs={{8,16},{24,32},{40,48},{56,64},{72,80},{88,96},{104,112},{120,128}... | collective-permute-start | bytes 442376 | tf_op jit(solution)/shard_map/ppermute | solution.py:208
  119.3 5.9 %collective-permute-start.9 = (bf16[12,48,128]{2,1,0:T(8,128)(2,1)S(1)}, bf16[12,48,128]{2,1,0:T(8,128)(2,1)S(1)}, u32[]{:S(2)}, u32[]{:S(2)}) collective-permute-start(bf16[12,48,128]{2,1,0:T(8,128)(2,1)S(1)} %get-tuple-element.51.value.earlier), channel_id=1, source_target_pairs={{0,8},{16,24},{32,40},{48,56},{64,72},{80,88},{96,104},{112,120},{... | collective-permute-start | bytes 442376 | tf_op jit(solution)/shard_map/ppermute | solution.py:207
  119.3 6.5 %collective-permute-start.10 = (bf16[12,48,128]{2,1,0:T(8,128)(2,1)S(1)}, bf16[12,48,128]{2,1,0:T(8,128)(2,1)S(1)}, u32[]{:S(2)}, u32[]{:S(2)}) collective-permute-start(bf16[12,48,128]{2,1,0:T(8,128)(2,1)S(1)} %get-tuple-element.51.value.earlier), channel_id=1, source_target_pairs={{1,2},{3,4},{5,6},{7,0},{2,1},{4,3},{6,5},{0,7},{9,10},{11,12},{13... | collective-permute-start | bytes 442376 | tf_op jit(solution)/shard_map/ppermute | solution.py:206
  122.6 3.1 %collective-permute-start.11 = (bf16[12,48,128]{2,1,0:T(8,128)(2,1)S(1)}, bf16[12,48,128]{2,1,0:T(8,128)(2,1)S(1)}, u32[]{:S(2)}, u32[]{:S(2)}) collective-permute-start(bf16[12,48,128]{2,1,0:T(8,128)(2,1)S(1)} %get-tuple-element.51.value.earlier), channel_id=1, source_target_pairs={{0,1},{2,3},{4,5},{6,7},{1,0},{3,2},{5,4},{7,6},{8,9},{10,11},{12,... | collective-permute-start | bytes 442376 | tf_op jit(solution)/shard_map/ppermute | solution.py:205
  126.1 8.1 %collective-permute-start.12 = (bf16[12,48,128]{2,1,0:T(8,128)(2,1)S(1)}, bf16[12,48,128]{2,1,0:T(8,128)(2,1)S(1)}, u32[]{:S(2)}, u32[]{:S(2)}) collective-permute-start(bf16[12,48,128]{2,1,0:T(8,128)(2,1)S(1)} %shard_map.47.value.earlier), channel_id=1, source_target_pairs={{8,16},{24,32},{40,48},{56,64},{72,80},{88,96},{104,112},{120,128}... | collective-permute-start | bytes 442376 | tf_op jit(solution)/shard_map/ppermute | solution.py:208
  128.2 6.0 %collective-permute-start.13 = (bf16[12,48,128]{2,1,0:T(8,128)(2,1)S(1)}, bf16[12,48,128]{2,1,0:T(8,128)(2,1)S(1)}, u32[]{:S(2)}, u32[]{:S(2)}) collective-permute-start(bf16[12,48,128]{2,1,0:T(8,128)(2,1)S(1)} %shard_map.47.value.earlier), channel_id=1, source_target_pairs={{0,8},{16,24},{32,40},{48,56},{64,72},{80,88},{96,104},{112,120},{... | collective-permute-start | bytes 442376 | tf_op jit(solution)/shard_map/ppermute | solution.py:207
  128.2 6.5 %collective-permute-start.14 = (bf16[12,48,128]{2,1,0:T(8,128)(2,1)S(1)}, bf16[12,48,128]{2,1,0:T(8,128)(2,1)S(1)}, u32[]{:S(2)}, u32[]{:S(2)}) collective-permute-start(bf16[12,48,128]{2,1,0:T(8,128)(2,1)S(1)} %shard_map.47.value.earlier), channel_id=1, source_target_pairs={{1,2},{3,4},{5,6},{7,0},{2,1},{4,3},{6,5},{0,7},{9,10},{11,12},{13... | collective-permute-start | bytes 442376 | tf_op jit(solution)/shard_map/ppermute | solution.py:206
  131.6 3.1 %collective-permute-start.15 = (bf16[12,48,128]{2,1,0:T(8,128)(2,1)S(1)}, bf16[12,48,128]{2,1,0:T(8,128)(2,1)S(1)}, u32[]{:S(2)}, u32[]{:S(2)}) collective-permute-start(bf16[12,48,128]{2,1,0:T(8,128)(2,1)S(1)} %shard_map.47.value.earlier), channel_id=1, source_target_pairs={{0,1},{2,3},{4,5},{6,7},{1,0},{3,2},{5,4},{7,6},{8,9},{10,11},{12,... | collective-permute-start | bytes 442376 | tf_op jit(solution)/shard_map/ppermute | solution.py:205
  135.1 8.1 %collective-permute-start.16 = (bf16[12,48,128]{2,1,0:T(8,128)(2,1)S(1)}, bf16[12,48,128]{2,1,0:T(8,128)(2,1)S(1)}, u32[]{:S(2)}, u32[]{:S(2)}) collective-permute-start(bf16[12,48,128]{2,1,0:T(8,128)(2,1)S(1)} %shard_map.52.value.earlier), channel_id=1, source_target_pairs={{8,16},{24,32},{40,48},{56,64},{72,80},{88,96},{104,112},{120,128}... | collective-permute-start | bytes 442376 | tf_op jit(solution)/shard_map/ppermute | solution.py:208
  137.2 6.0 %collective-permute-start.17 = (bf16[12,48,128]{2,1,0:T(8,128)(2,1)S(1)}, bf16[12,48,128]{2,1,0:T(8,128)(2,1)S(1)}, u32[]{:S(2)}, u32[]{:S(2)}) collective-permute-start(bf16[12,48,128]{2,1,0:T(8,128)(2,1)S(1)} %shard_map.52.value.earlier), channel_id=1, source_target_pairs={{0,8},{16,24},{32,40},{48,56},{64,72},{80,88},{96,104},{112,120},{... | collective-permute-start | bytes 442376 | tf_op jit(solution)/shard_map/ppermute | solution.py:207
  137.2 6.5 %collective-permute-start.18 = (bf16[12,48,128]{2,1,0:T(8,128)(2,1)S(1)}, bf16[12,48,128]{2,1,0:T(8,128)(2,1)S(1)}, u32[]{:S(2)}, u32[]{:S(2)}) collective-permute-start(bf16[12,48,128]{2,1,0:T(8,128)(2,1)S(1)} %shard_map.52.value.earlier), channel_id=1, source_target_pairs={{1,2},{3,4},{5,6},{7,0},{2,1},{4,3},{6,5},{0,7},{9,10},{11,12},{13... | collective-permute-start | bytes 442376 | tf_op jit(solution)/shard_map/ppermute | solution.py:206
  140.6 3.1 %collective-permute-start.19 = (bf16[12,48,128]{2,1,0:T(8,128)(2,1)S(1)}, bf16[12,48,128]{2,1,0:T(8,128)(2,1)S(1)}, u32[]{:S(2)}, u32[]{:S(2)}) collective-permute-start(bf16[12,48,128]{2,1,0:T(8,128)(2,1)S(1)} %shard_map.52.value.earlier), channel_id=1, source_target_pairs={{0,1},{2,3},{4,5},{6,7},{1,0},{3,2},{5,4},{7,6},{8,9},{10,11},{12,... | collective-permute-start | bytes 442376 | tf_op jit(solution)/shard_map/ppermute | solution.py:205
  144.1 8.1 %collective-permute-start.20 = (bf16[12,48,128]{2,1,0:T(8,128)(2,1)S(1)}, bf16[12,48,128]{2,1,0:T(8,128)(2,1)S(1)}, u32[]{:S(2)}, u32[]{:S(2)}) collective-permute-start(bf16[12,48,128]{2,1,0:T(8,128)(2,1)S(1)} %shard_map.57.value.earlier), channel_id=1, source_target_pairs={{8,16},{24,32},{40,48},{56,64},{72,80},{88,96},{104,112},{120,128}... | collective-permute-start | bytes 442376 | tf_op jit(solution)/shard_map/ppermute | solution.py:208
  146.2 6.0 %collective-permute-start.21 = (bf16[12,48,128]{2,1,0:T(8,128)(2,1)S(1)}, bf16[12,48,128]{2,1,0:T(8,128)(2,1)S(1)}, u32[]{:S(2)}, u32[]{:S(2)}) collective-permute-start(bf16[12,48,128]{2,1,0:T(8,128)(2,1)S(1)} %shard_map.57.value.earlier), channel_id=1, source_target_pairs={{0,8},{16,24},{32,40},{48,56},{64,72},{80,88},{96,104},{112,120},{... | collective-permute-start | bytes 442376 | tf_op jit(solution)/shard_map/ppermute | solution.py:207
  146.2 6.5 %collective-permute-start.22 = (bf16[12,48,128]{2,1,0:T(8,128)(2,1)S(1)}, bf16[12,48,128]{2,1,0:T(8,128)(2,1)S(1)}, u32[]{:S(2)}, u32[]{:S(2)}) collective-permute-start(bf16[12,48,128]{2,1,0:T(8,128)(2,1)S(1)} %shard_map.57.value.earlier), channel_id=1, source_target_pairs={{1,2},{3,4},{5,6},{7,0},{2,1},{4,3},{6,5},{0,7},{9,10},{11,12},{13... | collective-permute-start | bytes 442376 | tf_op jit(solution)/shard_map/ppermute | solution.py:206
  149.5 3.1 %collective-permute-start.23 = (bf16[12,48,128]{2,1,0:T(8,128)(2,1)S(1)}, bf16[12,48,128]{2,1,0:T(8,128)(2,1)S(1)}, u32[]{:S(2)}, u32[]{:S(2)}) collective-permute-start(bf16[12,48,128]{2,1,0:T(8,128)(2,1)S(1)} %shard_map.57.value.earlier), channel_id=1, source_target_pairs={{0,1},{2,3},{4,5},{6,7},{1,0},{3,2},{5,4},{7,6},{8,9},{10,11},{12,... | collective-permute-start | bytes 442376 | tf_op jit(solution)/shard_map/ppermute | solution.py:205

commit v5 on v3

--- a/solution.py
+++ b/solution.py
@@ -8,7 +8,7 @@
 from jax.sharding import PartitionSpec as P
 
 ITERS = 16
-KEPT = 1
+KEPT = 2
 LATE = 3
 LIMIT = 16 * 2**20
 VMEM = pl.BlockSpec(memory_space=pltpu.VMEM)

time: 156 us -> 157 us (level)
  waiting for transfers between devices: 16 us -> 17.8 us
    ppermute x16, waiting for transfers between devices: 3.72 us -> 6.11 us  [swaps(): t_far = lax.ppermute(value, 'ta', swap(nt, 1))]
where the time goes in v5:
time: 157 us; the launch traced here: 155 us
  starting transfers between devices  90.3 us (58%)
  Pallas kernels  45.9 us (29%)
  waiting for transfers between devices  17.8 us (11%)
    ppermute x16, starting transfers between devices, swaps(): z_far = lax.ppermute(value, 'gz', swap(nz, 1))  50.1 us
    pallas_call x82, Pallas kernels, call(): pl.pallas_call(kernel, in_specs=in_specs, out_specs=out_specs, out_shape=...  45.9 us
    ppermute x16, starting transfers between devices, swaps(): t_far = lax.ppermute(value, 'ta', swap(nt, 1))  39.1 us
    ppermute x16, waiting for transfers between devices, swaps(): z_far = lax.ppermute(value, 'gz', swap(nz, 1))  11.6 us
    ppermute x16, waiting for transfers between devices, swaps(): t_far = lax.ppermute(value, 'ta', swap(nt, 1))  6.11 us
  transfers between devices with their start and end apart: 64, of which 16 were waited for; matrix products, arithmetic and copies ran while one was open for 0% of the time, Pallas kernels for 23%

profile of v5, /device:TPU:1, one launch (start us, length us, event | category | flops | bytes accessed | tf_op | source)
XLA Modules:
  0.0 154.9 jit_solution(14268078986374052581)
XLA Ops:
  0.0 3.3 %shard_map.37.rhs.earlier = bf16[12,48,128]{2,1,0:T(8,128)(2,1)S(1)} custom-call(bf16[12,48,1536]{2,1,0:T(8,128)(2,1)} %bitcast.15, bf16[12,1536,128]{2,1,0:T(8,128)(2,1)} %bitcast.11), custom_call_target="tpu_custom_call" | custom-call | tf_op jit(solution)/shard_map/pallas_call | solution.py:28
  3.3 8.9 %collective-permute-start.4 = (bf16[12,48,128]{2,1,0:T(8,128)(2,1)S(1)}, bf16[12,48,128]{2,1,0:T(8,128)(2,1)S(1)}, u32[]{:S(2)}, u32[]{:S(2)}) collective-permute-start(bf16[12,48,128]{2,1,0:T(8,128)(2,1)S(1)} %shard_map.37.rhs.earlier), channel_id=1, source_target_pairs={{8,16},{24,32},{40,48},{56,64},{72,80},{88,96},{104,112},{120,128}... | collective-permute-start | bytes 442376 | tf_op jit(solution)/shard_map/ppermute | solution.py:208
  12.3 2.1 %collective-permute-start.6 = (bf16[12,48,128]{2,1,0:T(8,128)(2,1)S(1)}, bf16[12,48,128]{2,1,0:T(8,128)(2,1)S(1)}, u32[]{:S(2)}, u32[]{:S(2)}) collective-permute-start(bf16[12,48,128]{2,1,0:T(8,128)(2,1)S(1)} %shard_map.37.rhs.earlier), channel_id=1, source_target_pairs={{1,2},{3,4},{5,6},{7,0},{2,1},{4,3},{6,5},{0,7},{9,10},{11,12},{13... | collective-permute-start | bytes 442376 | tf_op jit(solution)/shard_map/ppermute | solution.py:206
  14.3 0.8 collective-permute-start.7
  15.2 3.8 %shard_map.38 = (f32[12,48,128]{2,1,0:T(8,128)S(1)}, bf16[12,512,128]{2,1,0:T(8,128)(2,1)S(1)}, bf16[12,256,128]{2,1,0:T(8,128)(2,1)S(1)}) custom-call(s32[5]{0:T(128)S(1)} %stack.23.slots, bf16[12,48,128]{2,1,0:T(8,128)(2,1)S(1)} %shard_map.37.rhs.earlier, bf16[9,12,128,128]{3,2,1,0:T(8,128)(2,1)} %bitcast.9), custom_call_target="tpu_custom_call" | custom-call | flops 94371840 | tf_op jit(solution)/shard_map/pallas_call | solution.py:28
  19.5 106.6 %while.10 = (s32[]{:T(128)}, bf16[12,48,128]{2,1,0:T(8,128)(2,1)S(1)}, bf16[12,48,128]{2,1,0:T(8,128)(2,1)S(1)}, bf16[12,256,128]{2,1,0:T(8,128)(2,1)S(1)}, bf16...) while((s32[]{:T(128)}, bf16[12,48,128]{2,1,0:T(8,128)(2,1)S(1)}, ...), condition=%wide.region_1.2_spmd, body=%wide.region_0.1_spmd.sunk | while | flops 169869312 | bytes 2359533 | solution.py:254
  19.5 1.5 collective-permute-start
  21.1 2.7 %collective-permute-start.2 = (bf16[12,48,128]{2,1,0:T(8,128)(2,1)S(1)}, bf16[12,48,128]{2,1,0:T(8,128)(2,1)S(1)}, u32[]{:S(2)}, u32[]{:S(2)}) collective-permute-start(bf16[12,48,128]{2,1,0:T(8,128)(2,1)S(1)} %get-tuple-element.113.value.earlier), channel_id=1, source_target_pairs={{1,2},{3,4},{5,6},{7,0},{2,1},{4,3},{6,5},{0,7},{9,10},{11,12},{13... | collective-permute-start | bytes 442376 | tf_op jit(solution)/shard_map/while/body/eval_jaxpr/ppermute | solution.py:206
  23.8 1.9 %eval_jaxpr.5.part = f32[12,48,128]{2,1,0:T(8,128)S(1)} custom-call(bf16[12,48,128]{2,1,0:T(8,128)(2,1)S(1)} %get-tuple-element.121.rhs, bf16[12,48,128]{2,1,0:T(8,128)(2,1)S(1)} %get-tuple-element.113.value.earlier, bf16[12,256,128]{2,1,0:T(8,128)(2,1)S(1)} %get-tuple-element.122.kept, bf16[9,12,128,128]{3,2,1,0:T(8,128)(2,1)} %get-tuple-element.123.links), custom_call_target="tpu_custom_call" | custom-call | flops 94371840 | tf_op jit(solution)/shard_map/while/body/eval_jaxpr/pallas_call | solution.py:28
  25.7 2.7 %collective-permute-done.arrived.a = bf16[12,48,128]{2,1,0:T(8,128)(2,1)S(1)} collective-permute-done((bf16[12,48,128]{2,1,0:T(8,128)(2,1)S(1)}, bf16[12,48,128]{2,1,0:T(8,128)(2,1)S(1)}, u32[]{:S(2)}, u32[]{:S(2)}) %collective-permute-start) | collective-permute-done | bytes 147488 | tf_op jit(solution)/shard_map/while/body/eval_jaxpr/ppermute | solution.py:208
  28.8 1.2 collective-permute-start
  30.0 2.7 %collective-permute-start.2 = (bf16[12,48,128]{2,1,0:T(8,128)(2,1)S(1)}, bf16[12,48,128]{2,1,0:T(8,128)(2,1)S(1)}, u32[]{:S(2)}, u32[]{:S(2)}) collective-permute-start(bf16[12,48,128]{2,1,0:T(8,128)(2,1)S(1)} %get-tuple-element.113.value.earlier), channel_id=1, source_target_pairs={{1,2},{3,4},{5,6},{7,0},{2,1},{4,3},{6,5},{0,7},{9,10},{11,12},{13... | collective-permute-start | bytes 442376 | tf_op jit(solution)/shard_map/while/body/eval_jaxpr/ppermute | solution.py:206
  32.8 1.9 %eval_jaxpr.5.part = f32[12,48,128]{2,1,0:T(8,128)S(1)} custom-call(bf16[12,48,128]{2,1,0:T(8,128)(2,1)S(1)} %get-tuple-element.121.rhs, bf16[12,48,128]{2,1,0:T(8,128)(2,1)S(1)} %get-tuple-element.113.value.earlier, bf16[12,256,128]{2,1,0:T(8,128)(2,1)S(1)} %get-tuple-element.122.kept, bf16[9,12,128,128]{3,2,1,0:T(8,128)(2,1)} %get-tuple-element.123.links), custom_call_target="tpu_custom_call" | custom-call | flops 94371840 | tf_op jit(solution)/shard_map/while/body/eval_jaxpr/pallas_call | solution.py:28
  34.7 2.1 %collective-permute-done.arrived.a = bf16[12,48,128]{2,1,0:T(8,128)(2,1)S(1)} collective-permute-done((bf16[12,48,128]{2,1,0:T(8,128)(2,1)S(1)}, bf16[12,48,128]{2,1,0:T(8,128)(2,1)S(1)}, u32[]{:S(2)}, u32[]{:S(2)}) %collective-permute-start) | collective-permute-done | bytes 147488 | tf_op jit(solution)/shard_map/while/body/eval_jaxpr/ppermute | solution.py:208
  37.2 1.8 %collective-permute-start = (bf16[12,48,128]{2,1,0:T(8,128)(2,1)S(1)}, bf16[12,48,128]{2,1,0:T(8,128)(2,1)S(1)}, u32[]{:S(2)}, u32[]{:S(2)}) collective-permute-start(bf16[12,48,128]{2,1,0:T(8,128)(2,1)S(1)} %get-tuple-element.113.value.earlier), channel_id=1, source_target_pairs={{8,16},{24,32},{40,48},{56,64},{72,80},{88,96},{104,112},{120,128}... | collective-permute-start | bytes 442376 | tf_op jit(solution)/shard_map/while/body/eval_jaxpr/ppermute | solution.py:208
  39.1 2.7 %collective-permute-start.2 = (bf16[12,48,128]{2,1,0:T(8,128)(2,1)S(1)}, bf16[12,48,128]{2,1,0:T(8,128)(2,1)S(1)}, u32[]{:S(2)}, u32[]{:S(2)}) collective-permute-start(bf16[12,48,128]{2,1,0:T(8,128)(2,1)S(1)} %get-tuple-element.113.value.earlier), channel_id=1, source_target_pairs={{1,2},{3,4},{5,6},{7,0},{2,1},{4,3},{6,5},{0,7},{9,10},{11,12},{13... | collective-permute-start | bytes 442376 | tf_op jit(solution)/shard_map/while/body/eval_jaxpr/ppermute | solution.py:206
  41.7 1.9 %eval_jaxpr.5.part = f32[12,48,128]{2,1,0:T(8,128)S(1)} custom-call(bf16[12,48,128]{2,1,0:T(8,128)(2,1)S(1)} %get-tuple-element.121.rhs, bf16[12,48,128]{2,1,0:T(8,128)(2,1)S(1)} %get-tuple-element.113.value.earlier, bf16[12,256,128]{2,1,0:T(8,128)(2,1)S(1)} %get-tuple-element.122.kept, bf16[9,12,128,128]{3,2,1,0:T(8,128)(2,1)} %get-tuple-element.123.links), custom_call_target="tpu_custom_call" | custom-call | flops 94371840 | tf_op jit(solution)/shard_map/while/body/eval_jaxpr/pallas_call | solution.py:28
  43.6 1.0 collective-permute-done.arrived.a
  45.3 2.1 %collective-permute-start = (bf16[12,48,128]{2,1,0:T(8,128)(2,1)S(1)}, bf16[12,48,128]{2,1,0:T(8,128)(2,1)S(1)}, u32[]{:S(2)}, u32[]{:S(2)}) collective-permute-start(bf16[12,48,128]{2,1,0:T(8,128)(2,1)S(1)} %get-tuple-element.113.value.earlier), channel_id=1, source_target_pairs={{8,16},{24,32},{40,48},{56,64},{72,80},{88,96},{104,112},{120,128}... | collective-permute-start | bytes 442376 | tf_op jit(solution)/shard_map/while/body/eval_jaxpr/ppermute | solution.py:208
  47.4 3.4 %collective-permute-start.2 = (bf16[12,48,128]{2,1,0:T(8,128)(2,1)S(1)}, bf16[12,48,128]{2,1,0:T(8,128)(2,1)S(1)}, u32[]{:S(2)}, u32[]{:S(2)}) collective-permute-start(bf16[12,48,128]{2,1,0:T(8,128)(2,1)S(1)} %get-tuple-element.113.value.earlier), channel_id=1, source_target_pairs={{1,2},{3,4},{5,6},{7,0},{2,1},{4,3},{6,5},{0,7},{9,10},{11,12},{13... | collective-permute-start | bytes 442376 | tf_op jit(solution)/shard_map/while/body/eval_jaxpr/ppermute | solution.py:206
  50.7 1.9 %eval_jaxpr.5.part = f32[12,48,128]{2,1,0:T(8,128)S(1)} custom-call(bf16[12,48,128]{2,1,0:T(8,128)(2,1)S(1)} %get-tuple-element.121.rhs, bf16[12,48,128]{2,1,0:T(8,128)(2,1)S(1)} %get-tuple-element.113.value.earlier, bf16[12,256,128]{2,1,0:T(8,128)(2,1)S(1)} %get-tuple-element.122.kept, bf16[9,12,128,128]{3,2,1,0:T(8,128)(2,1)} %get-tuple-element.123.links), custom_call_target="tpu_custom_call" | custom-call | flops 94371840 | tf_op jit(solution)/shard_map/while/body/eval_jaxpr/pallas_call | solution.py:28
  52.7 1.2 collective-permute-done.2.arrived.c
  54.2 2.1 %collective-permute-start = (bf16[12,48,128]{2,1,0:T(8,128)(2,1)S(1)}, bf16[12,48,128]{2,1,0:T(8,128)(2,1)S(1)}, u32[]{:S(2)}, u32[]{:S(2)}) collective-permute-start(bf16[12,48,128]{2,1,0:T(8,128)(2,1)S(1)} %get-tuple-element.113.value.earlier), channel_id=1, source_target_pairs={{8,16},{24,32},{40,48},{56,64},{72,80},{88,96},{104,112},{120,128}... | collective-permute-start | bytes 442376 | tf_op jit(solution)/shard_map/while/body/eval_jaxpr/ppermute | solution.py:208
  56.4 3.4 %collective-permute-start.2 = (bf16[12,48,128]{2,1,0:T(8,128)(2,1)S(1)}, bf16[12,48,128]{2,1,0:T(8,128)(2,1)S(1)}, u32[]{:S(2)}, u32[]{:S(2)}) collective-permute-start(bf16[12,48,128]{2,1,0:T(8,128)(2,1)S(1)} %get-tuple-element.113.value.earlier), channel_id=1, source_target_pairs={{1,2},{3,4},{5,6},{7,0},{2,1},{4,3},{6,5},{0,7},{9,10},{11,12},{13... | collective-permute-start | bytes 442376 | tf_op jit(solution)/shard_map/while/body/eval_jaxpr/ppermute | solution.py:206
  59.7 1.9 %eval_jaxpr.5.part = f32[12,48,128]{2,1,0:T(8,128)S(1)} custom-call(bf16[12,48,128]{2,1,0:T(8,128)(2,1)S(1)} %get-tuple-element.121.rhs, bf16[12,48,128]{2,1,0:T(8,128)(2,1)S(1)} %get-tuple-element.113.value.earlier, bf16[12,256,128]{2,1,0:T(8,128)(2,1)S(1)} %get-tuple-element.122.kept, bf16[9,12,128,128]{3,2,1,0:T(8,128)(2,1)} %get-tuple-element.123.links), custom_call_target="tpu_custom_call" | custom-call | flops 94371840 | tf_op jit(solution)/shard_map/while/body/eval_jaxpr/pallas_call | solution.py:28
  61.7 1.2 collective-permute-done.2.arrived.c
  63.2 2.1 %collective-permute-start = (bf16[12,48,128]{2,1,0:T(8,128)(2,1)S(1)}, bf16[12,48,128]{2,1,0:T(8,128)(2,1)S(1)}, u32[]{:S(2)}, u32[]{:S(2)}) collective-permute-start(bf16[12,48,128]{2,1,0:T(8,128)(2,1)S(1)} %get-tuple-element.113.value.earlier), channel_id=1, source_target_pairs={{8,16},{24,32},{40,48},{56,64},{72,80},{88,96},{104,112},{120,128}... | collective-permute-start | bytes 442376 | tf_op jit(solution)/shard_map/while/body/eval_jaxpr/ppermute | solution.py:208
  65.3 3.4 %collective-permute-start.2 = (bf16[12,48,128]{2,1,0:T(8,128)(2,1)S(1)}, bf16[12,48,128]{2,1,0:T(8,128)(2,1)S(1)}, u32[]{:S(2)}, u32[]{:S(2)}) collective-permute-start(bf16[12,48,128]{2,1,0:T(8,128)(2,1)S(1)} %get-tuple-element.113.value.earlier), channel_id=1, source_target_pairs={{1,2},{3,4},{5,6},{7,0},{2,1},{4,3},{6,5},{0,7},{9,10},{11,12},{13... | collective-permute-start | bytes 442376 | tf_op jit(solution)/shard_map/while/body/eval_jaxpr/ppermute | solution.py:206
  68.7 1.9 %eval_jaxpr.5.part = f32[12,48,128]{2,1,0:T(8,128)S(1)} custom-call(bf16[12,48,128]{2,1,0:T(8,128)(2,1)S(1)} %get-tuple-element.121.rhs, bf16[12,48,128]{2,1,0:T(8,128)(2,1)S(1)} %get-tuple-element.113.value.earlier, bf16[12,256,128]{2,1,0:T(8,128)(2,1)S(1)} %get-tuple-element.122.kept, bf16[9,12,128,128]{3,2,1,0:T(8,128)(2,1)} %get-tuple-element.123.links), custom_call_target="tpu_custom_call" | custom-call | flops 94371840 | tf_op jit(solution)/shard_map/while/body/eval_jaxpr/pallas_call | solution.py:28
  70.6 1.2 collective-permute-done.2.arrived.c
  72.2 2.1 %collective-permute-start = (bf16[12,48,128]{2,1,0:T(8,128)(2,1)S(1)}, bf16[12,48,128]{2,1,0:T(8,128)(2,1)S(1)}, u32[]{:S(2)}, u32[]{:S(2)}) collective-permute-start(bf16[12,48,128]{2,1,0:T(8,128)(2,1)S(1)} %get-tuple-element.113.value.earlier), channel_id=1, source_target_pairs={{8,16},{24,32},{40,48},{56,64},{72,80},{88,96},{104,112},{120,128}... | collective-permute-start | bytes 442376 | tf_op jit(solution)/shard_map/while/body/eval_jaxpr/ppermute | solution.py:208
  74.3 3.4 %collective-permute-start.2 = (bf16[12,48,128]{2,1,0:T(8,128)(2,1)S(1)}, bf16[12,48,128]{2,1,0:T(8,128)(2,1)S(1)}, u32[]{:S(2)}, u32[]{:S(2)}) collective-permute-start(bf16[12,48,128]{2,1,0:T(8,128)(2,1)S(1)} %get-tuple-element.113.value.earlier), channel_id=1, source_target_pairs={{1,2},{3,4},{5,6},{7,0},{2,1},{4,3},{6,5},{0,7},{9,10},{11,12},{13... | collective-permute-start | bytes 442376 | tf_op jit(solution)/shard_map/while/body/eval_jaxpr/ppermute | solution.py:206
  77.7 1.9 %eval_jaxpr.5.part = f32[12,48,128]{2,1,0:T(8,128)S(1)} custom-call(bf16[12,48,128]{2,1,0:T(8,128)(2,1)S(1)} %get-tuple-element.121.rhs, bf16[12,48,128]{2,1,0:T(8,128)(2,1)S(1)} %get-tuple-element.113.value.earlier, bf16[12,256,128]{2,1,0:T(8,128)(2,1)S(1)} %get-tuple-element.122.kept, bf16[9,12,128,128]{3,2,1,0:T(8,128)(2,1)} %get-tuple-element.123.links), custom_call_target="tpu_custom_call" | custom-call | flops 94371840 | tf_op jit(solution)/shard_map/while/body/eval_jaxpr/pallas_call | solution.py:28
  79.6 1.2 collective-permute-done.2.arrived.c
  81.2 2.1 %collective-permute-start = (bf16[12,48,128]{2,1,0:T(8,128)(2,1)S(1)}, bf16[12,48,128]{2,1,0:T(8,128)(2,1)S(1)}, u32[]{:S(2)}, u32[]{:S(2)}) collective-permute-start(bf16[12,48,128]{2,1,0:T(8,128)(2,1)S(1)} %get-tuple-element.113.value.earlier), channel_id=1, source_target_pairs={{8,16},{24,32},{40,48},{56,64},{72,80},{88,96},{104,112},{120,128}... | collective-permute-start | bytes 442376 | tf_op jit(solution)/shard_map/while/body/eval_jaxpr/ppermute | solution.py:208
  83.3 3.3 %collective-permute-start.2 = (bf16[12,48,128]{2,1,0:T(8,128)(2,1)S(1)}, bf16[12,48,128]{2,1,0:T(8,128)(2,1)S(1)}, u32[]{:S(2)}, u32[]{:S(2)}) collective-permute-start(bf16[12,48,128]{2,1,0:T(8,128)(2,1)S(1)} %get-tuple-element.113.value.earlier), channel_id=1, source_target_pairs={{1,2},{3,4},{5,6},{7,0},{2,1},{4,3},{6,5},{0,7},{9,10},{11,12},{13... | collective-permute-start | bytes 442376 | tf_op jit(solution)/shard_map/while/body/eval_jaxpr/ppermute | solution.py:206
  86.7 1.9 %eval_jaxpr.5.part = f32[12,48,128]{2,1,0:T(8,128)S(1)} custom-call(bf16[12,48,128]{2,1,0:T(8,128)(2,1)S(1)} %get-tuple-element.121.rhs, bf16[12,48,128]{2,1,0:T(8,128)(2,1)S(1)} %get-tuple-element.113.value.earlier, bf16[12,256,128]{2,1,0:T(8,128)(2,1)S(1)} %get-tuple-element.122.kept, bf16[9,12,128,128]{3,2,1,0:T(8,128)(2,1)} %get-tuple-element.123.links), custom_call_target="tpu_custom_call" | custom-call | flops 94371840 | tf_op jit(solution)/shard_map/while/body/eval_jaxpr/pallas_call | solution.py:28
  88.6 1.2 collective-permute-done.2.arrived.c
  90.2 2.1 %collective-permute-start = (bf16[12,48,128]{2,1,0:T(8,128)(2,1)S(1)}, bf16[12,48,128]{2,1,0:T(8,128)(2,1)S(1)}, u32[]{:S(2)}, u32[]{:S(2)}) collective-permute-start(bf16[12,48,128]{2,1,0:T(8,128)(2,1)S(1)} %get-tuple-element.113.value.earlier), channel_id=1, source_target_pairs={{8,16},{24,32},{40,48},{56,64},{72,80},{88,96},{104,112},{120,128}... | collective-permute-start | bytes 442376 | tf_op jit(solution)/shard_map/while/body/eval_jaxpr/ppermute | solution.py:208
  92.3 3.3 %collective-permute-start.2 = (bf16[12,48,128]{2,1,0:T(8,128)(2,1)S(1)}, bf16[12,48,128]{2,1,0:T(8,128)(2,1)S(1)}, u32[]{:S(2)}, u32[]{:S(2)}) collective-permute-start(bf16[12,48,128]{2,1,0:T(8,128)(2,1)S(1)} %get-tuple-element.113.value.earlier), channel_id=1, source_target_pairs={{1,2},{3,4},{5,6},{7,0},{2,1},{4,3},{6,5},{0,7},{9,10},{11,12},{13... | collective-permute-start | bytes 442376 | tf_op jit(solution)/shard_map/while/body/eval_jaxpr/ppermute | solution.py:206
  95.7 1.9 %eval_jaxpr.5.part = f32[12,48,128]{2,1,0:T(8,128)S(1)} custom-call(bf16[12,48,128]{2,1,0:T(8,128)(2,1)S(1)} %get-tuple-element.121.rhs, bf16[12,48,128]{2,1,0:T(8,128)(2,1)S(1)} %get-tuple-element.113.value.earlier, bf16[12,256,128]{2,1,0:T(8,128)(2,1)S(1)} %get-tuple-element.122.kept, bf16[9,12,128,128]{3,2,1,0:T(8,128)(2,1)} %get-tuple-element.123.links), custom_call_target="tpu_custom_call" | custom-call | flops 94371840 | tf_op jit(solution)/shard_map/while/body/eval_jaxpr/pallas_call | solution.py:28
  97.6 1.2 collective-permute-done.2.arrived.c
  99.2 2.1 %collective-permute-start = (bf16[12,48,128]{2,1,0:T(8,128)(2,1)S(1)}, bf16[12,48,128]{2,1,0:T(8,128)(2,1)S(1)}, u32[]{:S(2)}, u32[]{:S(2)}) collective-permute-start(bf16[12,48,128]{2,1,0:T(8,128)(2,1)S(1)} %get-tuple-element.113.value.earlier), channel_id=1, source_target_pairs={{8,16},{24,32},{40,48},{56,64},{72,80},{88,96},{104,112},{120,128}... | collective-permute-start | bytes 442376 | tf_op jit(solution)/shard_map/while/body/eval_jaxpr/ppermute | solution.py:208
  101.3 3.3 %collective-permute-start.2 = (bf16[12,48,128]{2,1,0:T(8,128)(2,1)S(1)}, bf16[12,48,128]{2,1,0:T(8,128)(2,1)S(1)}, u32[]{:S(2)}, u32[]{:S(2)}) collective-permute-start(bf16[12,48,128]{2,1,0:T(8,128)(2,1)S(1)} %get-tuple-element.113.value.earlier), channel_id=1, source_target_pairs={{1,2},{3,4},{5,6},{7,0},{2,1},{4,3},{6,5},{0,7},{9,10},{11,12},{13... | collective-permute-start | bytes 442376 | tf_op jit(solution)/shard_map/while/body/eval_jaxpr/ppermute | solution.py:206
  104.6 1.9 %eval_jaxpr.5.part = f32[12,48,128]{2,1,0:T(8,128)S(1)} custom-call(bf16[12,48,128]{2,1,0:T(8,128)(2,1)S(1)} %get-tuple-element.121.rhs, bf16[12,48,128]{2,1,0:T(8,128)(2,1)S(1)} %get-tuple-element.113.value.earlier, bf16[12,256,128]{2,1,0:T(8,128)(2,1)S(1)} %get-tuple-element.122.kept, bf16[9,12,128,128]{3,2,1,0:T(8,128)(2,1)} %get-tuple-element.123.links), custom_call_target="tpu_custom_call" | custom-call | flops 94371840 | tf_op jit(solution)/shard_map/while/body/eval_jaxpr/pallas_call | solution.py:28
  106.6 1.2 collective-permute-done.2.arrived.c
  108.2 2.1 %collective-permute-start = (bf16[12,48,128]{2,1,0:T(8,128)(2,1)S(1)}, bf16[12,48,128]{2,1,0:T(8,128)(2,1)S(1)}, u32[]{:S(2)}, u32[]{:S(2)}) collective-permute-start(bf16[12,48,128]{2,1,0:T(8,128)(2,1)S(1)} %get-tuple-element.113.value.earlier), channel_id=1, source_target_pairs={{8,16},{24,32},{40,48},{56,64},{72,80},{88,96},{104,112},{120,128}... | collective-permute-start | bytes 442376 | tf_op jit(solution)/shard_map/while/body/eval_jaxpr/ppermute | solution.py:208
  110.3 3.3 %collective-permute-start.2 = (bf16[12,48,128]{2,1,0:T(8,128)(2,1)S(1)}, bf16[12,48,128]{2,1,0:T(8,128)(2,1)S(1)}, u32[]{:S(2)}, u32[]{:S(2)}) collective-permute-start(bf16[12,48,128]{2,1,0:T(8,128)(2,1)S(1)} %get-tuple-element.113.value.earlier), channel_id=1, source_target_pairs={{1,2},{3,4},{5,6},{7,0},{2,1},{4,3},{6,5},{0,7},{9,10},{11,12},{13... | collective-permute-start | bytes 442376 | tf_op jit(solution)/shard_map/while/body/eval_jaxpr/ppermute | solution.py:206
  113.6 1.9 %eval_jaxpr.5.part = f32[12,48,128]{2,1,0:T(8,128)S(1)} custom-call(bf16[12,48,128]{2,1,0:T(8,128)(2,1)S(1)} %get-tuple-element.121.rhs, bf16[12,48,128]{2,1,0:T(8,128)(2,1)S(1)} %get-tuple-element.113.value.earlier, bf16[12,256,128]{2,1,0:T(8,128)(2,1)S(1)} %get-tuple-element.122.kept, bf16[9,12,128,128]{3,2,1,0:T(8,128)(2,1)} %get-tuple-element.123.links), custom_call_target="tpu_custom_call" | custom-call | flops 94371840 | tf_op jit(solution)/shard_map/while/body/eval_jaxpr/pallas_call | solution.py:28
  115.6 1.2 collective-permute-done.2.arrived.c
  117.2 2.1 %collective-permute-start = (bf16[12,48,128]{2,1,0:T(8,128)(2,1)S(1)}, bf16[12,48,128]{2,1,0:T(8,128)(2,1)S(1)}, u32[]{:S(2)}, u32[]{:S(2)}) collective-permute-start(bf16[12,48,128]{2,1,0:T(8,128)(2,1)S(1)} %get-tuple-element.113.value.earlier), channel_id=1, source_target_pairs={{8,16},{24,32},{40,48},{56,64},{72,80},{88,96},{104,112},{120,128}... | collective-permute-start | bytes 442376 | tf_op jit(solution)/shard_map/while/body/eval_jaxpr/ppermute | solution.py:208
  119.3 3.3 %collective-permute-start.2 = (bf16[12,48,128]{2,1,0:T(8,128)(2,1)S(1)}, bf16[12,48,128]{2,1,0:T(8,128)(2,1)S(1)}, u32[]{:S(2)}, u32[]{:S(2)}) collective-permute-start(bf16[12,48,128]{2,1,0:T(8,128)(2,1)S(1)} %get-tuple-element.113.value.earlier), channel_id=1, source_target_pairs={{1,2},{3,4},{5,6},{7,0},{2,1},{4,3},{6,5},{0,7},{9,10},{11,12},{13... | collective-permute-start | bytes 442376 | tf_op jit(solution)/shard_map/while/body/eval_jaxpr/ppermute | solution.py:206
  122.6 1.9 %eval_jaxpr.5.part = f32[12,48,128]{2,1,0:T(8,128)S(1)} custom-call(bf16[12,48,128]{2,1,0:T(8,128)(2,1)S(1)} %get-tuple-element.121.rhs, bf16[12,48,128]{2,1,0:T(8,128)(2,1)S(1)} %get-tuple-element.113.value.earlier, bf16[12,256,128]{2,1,0:T(8,128)(2,1)S(1)} %get-tuple-element.122.kept, bf16[9,12,128,128]{3,2,1,0:T(8,128)(2,1)} %get-tuple-element.123.links), custom_call_target="tpu_custom_call" | custom-call | flops 94371840 | tf_op jit(solution)/shard_map/while/body/eval_jaxpr/pallas_call | solution.py:28
  124.6 1.2 collective-permute-done.2.arrived.c
  126.1 2.1 %collective-permute-start.8 = (bf16[12,48,128]{2,1,0:T(8,128)(2,1)S(1)}, bf16[12,48,128]{2,1,0:T(8,128)(2,1)S(1)}, u32[]{:S(2)}, u32[]{:S(2)}) collective-permute-start(bf16[12,48,128]{2,1,0:T(8,128)(2,1)S(1)} %get-tuple-element.49.value.earlier), channel_id=1, source_target_pairs={{8,16},{24,32},{40,48},{56,64},{72,80},{88,96},{104,112},{120,128}... | collective-permute-start | bytes 442376 | tf_op jit(solution)/shard_map/ppermute | solution.py:208
  128.3 3.3 %collective-permute-start.10 = (bf16[12,48,128]{2,1,0:T(8,128)(2,1)S(1)}, bf16[12,48,128]{2,1,0:T(8,128)(2,1)S(1)}, u32[]{:S(2)}, u32[]{:S(2)}) collective-permute-start(bf16[12,48,128]{2,1,0:T(8,128)(2,1)S(1)} %get-tuple-element.49.value.earlier), channel_id=1, source_target_pairs={{1,2},{3,4},{5,6},{7,0},{2,1},{4,3},{6,5},{0,7},{9,10},{11,12},{13... | collective-permute-start | bytes 442376 | tf_op jit(solution)/shard_map/ppermute | solution.py:206
  131.6 2.7 %shard_map.43 = (f32[12,48,128]{2,1,0:T(8,128)S(1)}, bf16[4,128,1536]{2,1,0:T(8,128)(2,1)S(1)}) custom-call(bf16[12,48,128]{2,1,0:T(8,128)(2,1)S(1)} %get-tuple-element.140, bf16[12,48,128]{2,1,0:T(8,128)(2,1)S(1)} %get-tuple-element.49.value.earlier, bf16[12,256,128]{2,1,0:T(8,128)(2,1)S(1)} %get-tuple-element.127, ...), custom_call_target="tpu_custom_call" | custom-call | flops 94371840 | tf_op jit(solution)/shard_map/pallas_call | solution.py:28
  135.1 2.3 %collective-permute-start.12 = (bf16[12,48,128]{2,1,0:T(8,128)(2,1)S(1)}, bf16[12,48,128]{2,1,0:T(8,128)(2,1)S(1)}, u32[]{:S(2)}, u32[]{:S(2)}) collective-permute-start(bf16[12,48,128]{2,1,0:T(8,128)(2,1)S(1)} %shard_map.47.value.earlier), channel_id=1, source_target_pairs={{8,16},{24,32},{40,48},{56,64},{72,80},{88,96},{104,112},{120,128}... | collective-permute-start | bytes 442376 | tf_op jit(solution)/shard_map/ppermute | solution.py:208
  137.4 3.3 %collective-permute-start.14 = (bf16[12,48,128]{2,1,0:T(8,128)(2,1)S(1)}, bf16[12,48,128]{2,1,0:T(8,128)(2,1)S(1)}, u32[]{:S(2)}, u32[]{:S(2)}) collective-permute-start(bf16[12,48,128]{2,1,0:T(8,128)(2,1)S(1)} %shard_map.47.value.earlier), channel_id=1, source_target_pairs={{1,2},{3,4},{5,6},{7,0},{2,1},{4,3},{6,5},{0,7},{9,10},{11,12},{13... | collective-permute-start | bytes 442376 | tf_op jit(solution)/shard_map/ppermute | solution.py:206
  140.8 2.8 %shard_map.48 = (f32[12,48,128]{2,1,0:T(8,128)S(1)}, bf16[4,128,1536]{2,1,0:T(8,128)(2,1)S(1)}) custom-call(bf16[12,48,128]{2,1,0:T(8,128)(2,1)S(1)} %get-tuple-element.140, bf16[12,48,128]{2,1,0:T(8,128)(2,1)S(1)} %shard_map.47.value.earlier, bf16[12,256,128]{2,1,0:T(8,128)(2,1)S(1)} %get-tuple-element.127, bf16[9,12,128,128]{3,2,1,0:T(8,128)(2,1)} %get-tuple-element.169, ...), custom_call_target="tpu_custom_call" | custom-call | flops 94371840 | tf_op jit(solution)/shard_map/pallas_call | solution.py:28
  144.3 2.2 %collective-permute-start.16 = (bf16[12,48,128]{2,1,0:T(8,128)(2,1)S(1)}, bf16[12,48,128]{2,1,0:T(8,128)(2,1)S(1)}, u32[]{:S(2)}, u32[]{:S(2)}) collective-permute-start(bf16[12,48,128]{2,1,0:T(8,128)(2,1)S(1)} %shard_map.52.value.earlier), channel_id=1, source_target_pairs={{8,16},{24,32},{40,48},{56,64},{72,80},{88,96},{104,112},{120,128}... | collective-permute-start | bytes 442376 | tf_op jit(solution)/shard_map/ppermute | solution.py:208
  146.5 3.2 %collective-permute-start.18 = (bf16[12,48,128]{2,1,0:T(8,128)(2,1)S(1)}, bf16[12,48,128]{2,1,0:T(8,128)(2,1)S(1)}, u32[]{:S(2)}, u32[]{:S(2)}) collective-permute-start(bf16[12,48,128]{2,1,0:T(8,128)(2,1)S(1)} %shard_map.52.value.earlier), channel_id=1, source_target_pairs={{1,2},{3,4},{5,6},{7,0},{2,1},{4,3},{6,5},{0,7},{9,10},{11,12},{13... | collective-permute-start | bytes 442376 | tf_op jit(solution)/shard_map/ppermute | solution.py:206
  149.7 2.8 %shard_map.53 = (f32[12,48,128]{2,1,0:T(8,128)S(1)}, bf16[4,128,1536]{2,1,0:T(8,128)(2,1)S(1)}) custom-call(bf16[12,48,128]{2,1,0:T(8,128)(2,1)S(1)} %get-tuple-element.140, bf16[12,48,128]{2,1,0:T(8,128)(2,1)S(1)} %shard_map.52.value.earlier, bf16[12,256,128]{2,1,0:T(8,128)(2,1)S(1)} %get-tuple-element.127, bf16[9,12,128,128]{3,2,1,0:T(8,128)(2,1)} %get-tuple-element.169, ...), custom_call_target="tpu_custom_call" | custom-call | flops 94371840 | tf_op jit(solution)/shard_map/pallas_call | solution.py:28
  153.2 1.5 shard_map.58
  (148 shorter events, 7.9 us)
Async XLA Ops:
  3.3 15.7 %collective-permute-start.4 = (bf16[12,48,128]{2,1,0:T(8,128)(2,1)S(1)}, bf16[12,48,128]{2,1,0:T(8,128)(2,1)S(1)}, u32[]{:S(2)}, u32[]{:S(2)}) collective-permute-start(bf16[12,48,128]{2,1,0:T(8,128)(2,1)S(1)} %shard_map.37.rhs.earlier), channel_id=1, source_target_pairs={{8,16},{24,32},{40,48},{56,64},{72,80},{88,96},{104,112},{120,128}... | collective-permute-start | bytes 442376 | tf_op jit(solution)/shard_map/ppermute | solution.py:208
  12.3 6.8 %collective-permute-start.5 = (bf16[12,48,128]{2,1,0:T(8,128)(2,1)S(1)}, bf16[12,48,128]{2,1,0:T(8,128)(2,1)S(1)}, u32[]{:S(2)}, u32[]{:S(2)}) collective-permute-start(bf16[12,48,128]{2,1,0:T(8,128)(2,1)S(1)} %shard_map.37.rhs.earlier), channel_id=1, source_target_pairs={{0,8},{16,24},{32,40},{48,56},{64,72},{80,88},{96,104},{112,120},{... | collective-permute-start | bytes 442376 | tf_op jit(solution)/shard_map/ppermute | solution.py:207
  12.3 6.8 %collective-permute-start.6 = (bf16[12,48,128]{2,1,0:T(8,128)(2,1)S(1)}, bf16[12,48,128]{2,1,0:T(8,128)(2,1)S(1)}, u32[]{:S(2)}, u32[]{:S(2)}) collective-permute-start(bf16[12,48,128]{2,1,0:T(8,128)(2,1)S(1)} %shard_map.37.rhs.earlier), channel_id=1, source_target_pairs={{1,2},{3,4},{5,6},{7,0},{2,1},{4,3},{6,5},{0,7},{9,10},{11,12},{13... | collective-permute-start | bytes 442376 | tf_op jit(solution)/shard_map/ppermute | solution.py:206
  14.3 4.8 %collective-permute-start.7 = (bf16[12,48,128]{2,1,0:T(8,128)(2,1)S(1)}, bf16[12,48,128]{2,1,0:T(8,128)(2,1)S(1)}, u32[]{:S(2)}, u32[]{:S(2)}) collective-permute-start(bf16[12,48,128]{2,1,0:T(8,128)(2,1)S(1)} %shard_map.37.rhs.earlier), channel_id=1, source_target_pairs={{0,1},{2,3},{4,5},{6,7},{1,0},{3,2},{5,4},{7,6},{8,9},{10,11},{12,... | collective-permute-start | bytes 442376 | tf_op jit(solution)/shard_map/ppermute | solution.py:205
  19.5 8.9 %collective-permute-start = (bf16[12,48,128]{2,1,0:T(8,128)(2,1)S(1)}, bf16[12,48,128]{2,1,0:T(8,128)(2,1)S(1)}, u32[]{:S(2)}, u32[]{:S(2)}) collective-permute-start(bf16[12,48,128]{2,1,0:T(8,128)(2,1)S(1)} %get-tuple-element.113.value.earlier), channel_id=1, source_target_pairs={{8,16},{24,32},{40,48},{56,64},{72,80},{88,96},{104,112},{120,128}... | collective-permute-start | bytes 442376 | tf_op jit(solution)/shard_map/while/body/eval_jaxpr/ppermute | solution.py:208
  21.0 7.3 %collective-permute-start.1 = (bf16[12,48,128]{2,1,0:T(8,128)(2,1)S(1)}, bf16[12,48,128]{2,1,0:T(8,128)(2,1)S(1)}, u32[]{:S(2)}, u32[]{:S(2)}) collective-permute-start(bf16[12,48,128]{2,1,0:T(8,128)(2,1)S(1)} %get-tuple-element.113.value.earlier), channel_id=1, source_target_pairs={{0,8},{16,24},{32,40},{48,56},{64,72},{80,88},{96,104},{112,120},{... | collective-permute-start | bytes 442376 | tf_op jit(solution)/shard_map/while/body/eval_jaxpr/ppermute | solution.py:207
  21.1 7.3 %collective-permute-start.2 = (bf16[12,48,128]{2,1,0:T(8,128)(2,1)S(1)}, bf16[12,48,128]{2,1,0:T(8,128)(2,1)S(1)}, u32[]{:S(2)}, u32[]{:S(2)}) collective-permute-start(bf16[12,48,128]{2,1,0:T(8,128)(2,1)S(1)} %get-tuple-element.113.value.earlier), channel_id=1, source_target_pairs={{1,2},{3,4},{5,6},{7,0},{2,1},{4,3},{6,5},{0,7},{9,10},{11,12},{13... | collective-permute-start | bytes 442376 | tf_op jit(solution)/shard_map/while/body/eval_jaxpr/ppermute | solution.py:206
  23.8 4.7 %collective-permute-start.3 = (bf16[12,48,128]{2,1,0:T(8,128)(2,1)S(1)}, bf16[12,48,128]{2,1,0:T(8,128)(2,1)S(1)}, u32[]{:S(2)}, u32[]{:S(2)}) collective-permute-start(bf16[12,48,128]{2,1,0:T(8,128)(2,1)S(1)} %get-tuple-element.113.value.earlier), channel_id=1, source_target_pairs={{0,1},{2,3},{4,5},{6,7},{1,0},{3,2},{5,4},{7,6},{8,9},{10,11},{12,... | collective-permute-start | bytes 442376 | tf_op jit(solution)/shard_map/while/body/eval_jaxpr/ppermute | solution.py:205
  28.8 8.0 %collective-permute-start = (bf16[12,48,128]{2,1,0:T(8,128)(2,1)S(1)}, bf16[12,48,128]{2,1,0:T(8,128)(2,1)S(1)}, u32[]{:S(2)}, u32[]{:S(2)}) collective-permute-start(bf16[12,48,128]{2,1,0:T(8,128)(2,1)S(1)} %get-tuple-element.113.value.earlier), channel_id=1, source_target_pairs={{8,16},{24,32},{40,48},{56,64},{72,80},{88,96},{104,112},{120,128}... | collective-permute-start | bytes 442376 | tf_op jit(solution)/shard_map/while/body/eval_jaxpr/ppermute | solution.py:208
  30.0 6.8 %collective-permute-start.1 = (bf16[12,48,128]{2,1,0:T(8,128)(2,1)S(1)}, bf16[12,48,128]{2,1,0:T(8,128)(2,1)S(1)}, u32[]{:S(2)}, u32[]{:S(2)}) collective-permute-start(bf16[12,48,128]{2,1,0:T(8,128)(2,1)S(1)} %get-tuple-element.113.value.earlier), channel_id=1, source_target_pairs={{0,8},{16,24},{32,40},{48,56},{64,72},{80,88},{96,104},{112,120},{... | collective-permute-start | bytes 442376 | tf_op jit(solution)/shard_map/while/body/eval_jaxpr/ppermute | solution.py:207
  30.0 6.8 %collective-permute-start.2 = (bf16[12,48,128]{2,1,0:T(8,128)(2,1)S(1)}, bf16[12,48,128]{2,1,0:T(8,128)(2,1)S(1)}, u32[]{:S(2)}, u32[]{:S(2)}) collective-permute-start(bf16[12,48,128]{2,1,0:T(8,128)(2,1)S(1)} %get-tuple-element.113.value.earlier), channel_id=1, source_target_pairs={{1,2},{3,4},{5,6},{7,0},{2,1},{4,3},{6,5},{0,7},{9,10},{11,12},{13... | collective-permute-start | bytes 442376 | tf_op jit(solution)/shard_map/while/body/eval_jaxpr/ppermute | solution.py:206
  32.7 4.1 %collective-permute-start.3 = (bf16[12,48,128]{2,1,0:T(8,128)(2,1)S(1)}, bf16[12,48,128]{2,1,0:T(8,128)(2,1)S(1)}, u32[]{:S(2)}, u32[]{:S(2)}) collective-permute-start(bf16[12,48,128]{2,1,0:T(8,128)(2,1)S(1)} %get-tuple-element.113.value.earlier), channel_id=1, source_target_pairs={{0,1},{2,3},{4,5},{6,7},{1,0},{3,2},{5,4},{7,6},{8,9},{10,11},{12,... | collective-permute-start | bytes 442376 | tf_op jit(solution)/shard_map/while/body/eval_jaxpr/ppermute | solution.py:205
  37.2 7.4 %collective-permute-start = (bf16[12,48,128]{2,1,0:T(8,128)(2,1)S(1)}, bf16[12,48,128]{2,1,0:T(8,128)(2,1)S(1)}, u32[]{:S(2)}, u32[]{:S(2)}) collective-permute-start(bf16[12,48,128]{2,1,0:T(8,128)(2,1)S(1)} %get-tuple-element.113.value.earlier), channel_id=1, source_target_pairs={{8,16},{24,32},{40,48},{56,64},{72,80},{88,96},{104,112},{120,128}... | collective-permute-start | bytes 442376 | tf_op jit(solution)/shard_map/while/body/eval_jaxpr/ppermute | solution.py:208
  39.1 5.6 %collective-permute-start.1 = (bf16[12,48,128]{2,1,0:T(8,128)(2,1)S(1)}, bf16[12,48,128]{2,1,0:T(8,128)(2,1)S(1)}, u32[]{:S(2)}, u32[]{:S(2)}) collective-permute-start(bf16[12,48,128]{2,1,0:T(8,128)(2,1)S(1)} %get-tuple-element.113.value.earlier), channel_id=1, source_target_pairs={{0,8},{16,24},{32,40},{48,56},{64,72},{80,88},{96,104},{112,120},{... | collective-permute-start | bytes 442376 | tf_op jit(solution)/shard_map/while/body/eval_jaxpr/ppermute | solution.py:207
  39.1 5.8 %collective-permute-start.2 = (bf16[12,48,128]{2,1,0:T(8,128)(2,1)S(1)}, bf16[12,48,128]{2,1,0:T(8,128)(2,1)S(1)}, u32[]{:S(2)}, u32[]{:S(2)}) collective-permute-start(bf16[12,48,128]{2,1,0:T(8,128)(2,1)S(1)} %get-tuple-element.113.value.earlier), channel_id=1, source_target_pairs={{1,2},{3,4},{5,6},{7,0},{2,1},{4,3},{6,5},{0,7},{9,10},{11,12},{13... | collective-permute-start | bytes 442376 | tf_op jit(solution)/shard_map/while/body/eval_jaxpr/ppermute | solution.py:206
  41.7 3.1 %collective-permute-start.3 = (bf16[12,48,128]{2,1,0:T(8,128)(2,1)S(1)}, bf16[12,48,128]{2,1,0:T(8,128)(2,1)S(1)}, u32[]{:S(2)}, u32[]{:S(2)}) collective-permute-start(bf16[12,48,128]{2,1,0:T(8,128)(2,1)S(1)} %get-tuple-element.113.value.earlier), channel_id=1, source_target_pairs={{0,1},{2,3},{4,5},{6,7},{1,0},{3,2},{5,4},{7,6},{8,9},{10,11},{12,... | collective-permute-start | bytes 442376 | tf_op jit(solution)/shard_map/while/body/eval_jaxpr/ppermute | solution.py:205
  45.3 7.4 %collective-permute-start = (bf16[12,48,128]{2,1,0:T(8,128)(2,1)S(1)}, bf16[12,48,128]{2,1,0:T(8,128)(2,1)S(1)}, u32[]{:S(2)}, u32[]{:S(2)}) collective-permute-start(bf16[12,48,128]{2,1,0:T(8,128)(2,1)S(1)} %get-tuple-element.113.value.earlier), channel_id=1, source_target_pairs={{8,16},{24,32},{40,48},{56,64},{72,80},{88,96},{104,112},{120,128}... | collective-permute-start | bytes 442376 | tf_op jit(solution)/shard_map/while/body/eval_jaxpr/ppermute | solution.py:208
  47.4 5.3 %collective-permute-start.1 = (bf16[12,48,128]{2,1,0:T(8,128)(2,1)S(1)}, bf16[12,48,128]{2,1,0:T(8,128)(2,1)S(1)}, u32[]{:S(2)}, u32[]{:S(2)}) collective-permute-start(bf16[12,48,128]{2,1,0:T(8,128)(2,1)S(1)} %get-tuple-element.113.value.earlier), channel_id=1, source_target_pairs={{0,8},{16,24},{32,40},{48,56},{64,72},{80,88},{96,104},{112,120},{... | collective-permute-start | bytes 442376 | tf_op jit(solution)/shard_map/while/body/eval_jaxpr/ppermute | solution.py:207
  47.4 6.5 %collective-permute-start.2 = (bf16[12,48,128]{2,1,0:T(8,128)(2,1)S(1)}, bf16[12,48,128]{2,1,0:T(8,128)(2,1)S(1)}, u32[]{:S(2)}, u32[]{:S(2)}) collective-permute-start(bf16[12,48,128]{2,1,0:T(8,128)(2,1)S(1)} %get-tuple-element.113.value.earlier), channel_id=1, source_target_pairs={{1,2},{3,4},{5,6},{7,0},{2,1},{4,3},{6,5},{0,7},{9,10},{11,12},{13... | collective-permute-start | bytes 442376 | tf_op jit(solution)/shard_map/while/body/eval_jaxpr/ppermute | solution.py:206
  50.7 3.1 %collective-permute-start.3 = (bf16[12,48,128]{2,1,0:T(8,128)(2,1)S(1)}, bf16[12,48,128]{2,1,0:T(8,128)(2,1)S(1)}, u32[]{:S(2)}, u32[]{:S(2)}) collective-permute-start(bf16[12,48,128]{2,1,0:T(8,128)(2,1)S(1)} %get-tuple-element.113.value.earlier), channel_id=1, source_target_pairs={{0,1},{2,3},{4,5},{6,7},{1,0},{3,2},{5,4},{7,6},{8,9},{10,11},{12,... | collective-permute-start | bytes 442376 | tf_op jit(solution)/shard_map/while/body/eval_jaxpr/ppermute | solution.py:205
  54.2 7.4 %collective-permute-start = (bf16[12,48,128]{2,1,0:T(8,128)(2,1)S(1)}, bf16[12,48,128]{2,1,0:T(8,128)(2,1)S(1)}, u32[]{:S(2)}, u32[]{:S(2)}) collective-permute-start(bf16[12,48,128]{2,1,0:T(8,128)(2,1)S(1)} %get-tuple-element.113.value.earlier), channel_id=1, source_target_pairs={{8,16},{24,32},{40,48},{56,64},{72,80},{88,96},{104,112},{120,128}... | collective-permute-start | bytes 442376 | tf_op jit(solution)/shard_map/while/body/eval_jaxpr/ppermute | solution.py:208
  56.3 5.3 %collective-permute-start.1 = (bf16[12,48,128]{2,1,0:T(8,128)(2,1)S(1)}, bf16[12,48,128]{2,1,0:T(8,128)(2,1)S(1)}, u32[]{:S(2)}, u32[]{:S(2)}) collective-permute-start(bf16[12,48,128]{2,1,0:T(8,128)(2,1)S(1)} %get-tuple-element.113.value.earlier), channel_id=1, source_target_pairs={{0,8},{16,24},{32,40},{48,56},{64,72},{80,88},{96,104},{112,120},{... | collective-permute-start | bytes 442376 | tf_op jit(solution)/shard_map/while/body/eval_jaxpr/ppermute | solution.py:207
  56.4 6.5 %collective-permute-start.2 = (bf16[12,48,128]{2,1,0:T(8,128)(2,1)S(1)}, bf16[12,48,128]{2,1,0:T(8,128)(2,1)S(1)}, u32[]{:S(2)}, u32[]{:S(2)}) collective-permute-start(bf16[12,48,128]{2,1,0:T(8,128)(2,1)S(1)} %get-tuple-element.113.value.earlier), channel_id=1, source_target_pairs={{1,2},{3,4},{5,6},{7,0},{2,1},{4,3},{6,5},{0,7},{9,10},{11,12},{13... | collective-permute-start | bytes 442376 | tf_op jit(solution)/shard_map/while/body/eval_jaxpr/ppermute | solution.py:206
  59.7 3.1 %collective-permute-start.3 = (bf16[12,48,128]{2,1,0:T(8,128)(2,1)S(1)}, bf16[12,48,128]{2,1,0:T(8,128)(2,1)S(1)}, u32[]{:S(2)}, u32[]{:S(2)}) collective-permute-start(bf16[12,48,128]{2,1,0:T(8,128)(2,1)S(1)} %get-tuple-element.113.value.earlier), channel_id=1, source_target_pairs={{0,1},{2,3},{4,5},{6,7},{1,0},{3,2},{5,4},{7,6},{8,9},{10,11},{12,... | collective-permute-start | bytes 442376 | tf_op jit(solution)/shard_map/while/body/eval_jaxpr/ppermute | solution.py:205
  63.2 7.4 %collective-permute-start = (bf16[12,48,128]{2,1,0:T(8,128)(2,1)S(1)}, bf16[12,48,128]{2,1,0:T(8,128)(2,1)S(1)}, u32[]{:S(2)}, u32[]{:S(2)}) collective-permute-start(bf16[12,48,128]{2,1,0:T(8,128)(2,1)S(1)} %get-tuple-element.113.value.earlier), channel_id=1, source_target_pairs={{8,16},{24,32},{40,48},{56,64},{72,80},{88,96},{104,112},{120,128}... | collective-permute-start | bytes 442376 | tf_op jit(solution)/shard_map/while/body/eval_jaxpr/ppermute | solution.py:208
  65.3 5.3 %collective-permute-start.1 = (bf16[12,48,128]{2,1,0:T(8,128)(2,1)S(1)}, bf16[12,48,128]{2,1,0:T(8,128)(2,1)S(1)}, u32[]{:S(2)}, u32[]{:S(2)}) collective-permute-start(bf16[12,48,128]{2,1,0:T(8,128)(2,1)S(1)} %get-tuple-element.113.value.earlier), channel_id=1, source_target_pairs={{0,8},{16,24},{32,40},{48,56},{64,72},{80,88},{96,104},{112,120},{... | collective-permute-start | bytes 442376 | tf_op jit(solution)/shard_map/while/body/eval_jaxpr/ppermute | solution.py:207
  65.3 6.5 %collective-permute-start.2 = (bf16[12,48,128]{2,1,0:T(8,128)(2,1)S(1)}, bf16[12,48,128]{2,1,0:T(8,128)(2,1)S(1)}, u32[]{:S(2)}, u32[]{:S(2)}) collective-permute-start(bf16[12,48,128]{2,1,0:T(8,128)(2,1)S(1)} %get-tuple-element.113.value.earlier), channel_id=1, source_target_pairs={{1,2},{3,4},{5,6},{7,0},{2,1},{4,3},{6,5},{0,7},{9,10},{11,12},{13... | collective-permute-start | bytes 442376 | tf_op jit(solution)/shard_map/while/body/eval_jaxpr/ppermute | solution.py:206
  68.7 3.1 %collective-permute-start.3 = (bf16[12,48,128]{2,1,0:T(8,128)(2,1)S(1)}, bf16[12,48,128]{2,1,0:T(8,128)(2,1)S(1)}, u32[]{:S(2)}, u32[]{:S(2)}) collective-permute-start(bf16[12,48,128]{2,1,0:T(8,128)(2,1)S(1)} %get-tuple-element.113.value.earlier), channel_id=1, source_target_pairs={{0,1},{2,3},{4,5},{6,7},{1,0},{3,2},{5,4},{7,6},{8,9},{10,11},{12,... | collective-permute-start | bytes 442376 | tf_op jit(solution)/shard_map/while/body/eval_jaxpr/ppermute | solution.py:205
  72.2 7.4 %collective-permute-start = (bf16[12,48,128]{2,1,0:T(8,128)(2,1)S(1)}, bf16[12,48,128]{2,1,0:T(8,128)(2,1)S(1)}, u32[]{:S(2)}, u32[]{:S(2)}) collective-permute-start(bf16[12,48,128]{2,1,0:T(8,128)(2,1)S(1)} %get-tuple-element.113.value.earlier), channel_id=1, source_target_pairs={{8,16},{24,32},{40,48},{56,64},{72,80},{88,96},{104,112},{120,128}... | collective-permute-start | bytes 442376 | tf_op jit(solution)/shard_map/while/body/eval_jaxpr/ppermute | solution.py:208
  74.3 5.3 %collective-permute-start.1 = (bf16[12,48,128]{2,1,0:T(8,128)(2,1)S(1)}, bf16[12,48,128]{2,1,0:T(8,128)(2,1)S(1)}, u32[]{:S(2)}, u32[]{:S(2)}) collective-permute-start(bf16[12,48,128]{2,1,0:T(8,128)(2,1)S(1)} %get-tuple-element.113.value.earlier), channel_id=1, source_target_pairs={{0,8},{16,24},{32,40},{48,56},{64,72},{80,88},{96,104},{112,120},{... | collective-permute-start | bytes 442376 | tf_op jit(solution)/shard_map/while/body/eval_jaxpr/ppermute | solution.py:207
  74.3 6.5 %collective-permute-start.2 = (bf16[12,48,128]{2,1,0:T(8,128)(2,1)S(1)}, bf16[12,48,128]{2,1,0:T(8,128)(2,1)S(1)}, u32[]{:S(2)}, u32[]{:S(2)}) collective-permute-start(bf16[12,48,128]{2,1,0:T(8,128)(2,1)S(1)} %get-tuple-element.113.value.earlier), channel_id=1, source_target_pairs={{1,2},{3,4},{5,6},{7,0},{2,1},{4,3},{6,5},{0,7},{9,10},{11,12},{13... | collective-permute-start | bytes 442376 | tf_op jit(solution)/shard_map/while/body/eval_jaxpr/ppermute | solution.py:206
  77.7 3.1 %collective-permute-start.3 = (bf16[12,48,128]{2,1,0:T(8,128)(2,1)S(1)}, bf16[12,48,128]{2,1,0:T(8,128)(2,1)S(1)}, u32[]{:S(2)}, u32[]{:S(2)}) collective-permute-start(bf16[12,48,128]{2,1,0:T(8,128)(2,1)S(1)} %get-tuple-element.113.value.earlier), channel_id=1, source_target_pairs={{0,1},{2,3},{4,5},{6,7},{1,0},{3,2},{5,4},{7,6},{8,9},{10,11},{12,... | collective-permute-start | bytes 442376 | tf_op jit(solution)/shard_map/while/body/eval_jaxpr/ppermute | solution.py:205
  81.2 7.4 %collective-permute-start = (bf16[12,48,128]{2,1,0:T(8,128)(2,1)S(1)}, bf16[12,48,128]{2,1,0:T(8,128)(2,1)S(1)}, u32[]{:S(2)}, u32[]{:S(2)}) collective-permute-start(bf16[12,48,128]{2,1,0:T(8,128)(2,1)S(1)} %get-tuple-element.113.value.earlier), channel_id=1, source_target_pairs={{8,16},{24,32},{40,48},{56,64},{72,80},{88,96},{104,112},{120,128}... | collective-permute-start | bytes 442376 | tf_op jit(solution)/shard_map/while/body/eval_jaxpr/ppermute | solution.py:208
  83.3 5.3 %collective-permute-start.1 = (bf16[12,48,128]{2,1,0:T(8,128)(2,1)S(1)}, bf16[12,48,128]{2,1,0:T(8,128)(2,1)S(1)}, u32[]{:S(2)}, u32[]{:S(2)}) collective-permute-start(bf16[12,48,128]{2,1,0:T(8,128)(2,1)S(1)} %get-tuple-element.113.value.earlier), channel_id=1, source_target_pairs={{0,8},{16,24},{32,40},{48,56},{64,72},{80,88},{96,104},{112,120},{... | collective-permute-start | bytes 442376 | tf_op jit(solution)/shard_map/while/body/eval_jaxpr/ppermute | solution.py:207
  83.3 6.5 %collective-permute-start.2 = (bf16[12,48,128]{2,1,0:T(8,128)(2,1)S(1)}, bf16[12,48,128]{2,1,0:T(8,128)(2,1)S(1)}, u32[]{:S(2)}, u32[]{:S(2)}) collective-permute-start(bf16[12,48,128]{2,1,0:T(8,128)(2,1)S(1)} %get-tuple-element.113.value.earlier), channel_id=1, source_target_pairs={{1,2},{3,4},{5,6},{7,0},{2,1},{4,3},{6,5},{0,7},{9,10},{11,12},{13... | collective-permute-start | bytes 442376 | tf_op jit(solution)/shard_map/while/body/eval_jaxpr/ppermute | solution.py:206
  86.7 3.1 %collective-permute-start.3 = (bf16[12,48,128]{2,1,0:T(8,128)(2,1)S(1)}, bf16[12,48,128]{2,1,0:T(8,128)(2,1)S(1)}, u32[]{:S(2)}, u32[]{:S(2)}) collective-permute-start(bf16[12,48,128]{2,1,0:T(8,128)(2,1)S(1)} %get-tuple-element.113.value.earlier), channel_id=1, source_target_pairs={{0,1},{2,3},{4,5},{6,7},{1,0},{3,2},{5,4},{7,6},{8,9},{10,11},{12,... | collective-permute-start | bytes 442376 | tf_op jit(solution)/shard_map/while/body/eval_jaxpr/ppermute | solution.py:205
  90.2 7.4 %collective-permute-start = (bf16[12,48,128]{2,1,0:T(8,128)(2,1)S(1)}, bf16[12,48,128]{2,1,0:T(8,128)(2,1)S(1)}, u32[]{:S(2)}, u32[]{:S(2)}) collective-permute-start(bf16[12,48,128]{2,1,0:T(8,128)(2,1)S(1)} %get-tuple-element.113.value.earlier), channel_id=1, source_target_pairs={{8,16},{24,32},{40,48},{56,64},{72,80},{88,96},{104,112},{120,128}... | collective-permute-start | bytes 442376 | tf_op jit(solution)/shard_map/while/body/eval_jaxpr/ppermute | solution.py:208
  92.3 5.3 %collective-permute-start.1 = (bf16[12,48,128]{2,1,0:T(8,128)(2,1)S(1)}, bf16[12,48,128]{2,1,0:T(8,128)(2,1)S(1)}, u32[]{:S(2)}, u32[]{:S(2)}) collective-permute-start(bf16[12,48,128]{2,1,0:T(8,128)(2,1)S(1)} %get-tuple-element.113.value.earlier), channel_id=1, source_target_pairs={{0,8},{16,24},{32,40},{48,56},{64,72},{80,88},{96,104},{112,120},{... | collective-permute-start | bytes 442376 | tf_op jit(solution)/shard_map/while/body/eval_jaxpr/ppermute | solution.py:207
  92.3 6.5 %collective-permute-start.2 = (bf16[12,48,128]{2,1,0:T(8,128)(2,1)S(1)}, bf16[12,48,128]{2,1,0:T(8,128)(2,1)S(1)}, u32[]{:S(2)}, u32[]{:S(2)}) collective-permute-start(bf16[12,48,128]{2,1,0:T(8,128)(2,1)S(1)} %get-tuple-element.113.value.earlier), channel_id=1, source_target_pairs={{1,2},{3,4},{5,6},{7,0},{2,1},{4,3},{6,5},{0,7},{9,10},{11,12},{13... | collective-permute-start | bytes 442376 | tf_op jit(solution)/shard_map/while/body/eval_jaxpr/ppermute | solution.py:206
  95.7 3.1 %collective-permute-start.3 = (bf16[12,48,128]{2,1,0:T(8,128)(2,1)S(1)}, bf16[12,48,128]{2,1,0:T(8,128)(2,1)S(1)}, u32[]{:S(2)}, u32[]{:S(2)}) collective-permute-start(bf16[12,48,128]{2,1,0:T(8,128)(2,1)S(1)} %get-tuple-element.113.value.earlier), channel_id=1, source_target_pairs={{0,1},{2,3},{4,5},{6,7},{1,0},{3,2},{5,4},{7,6},{8,9},{10,11},{12,... | collective-permute-start | bytes 442376 | tf_op jit(solution)/shard_map/while/body/eval_jaxpr/ppermute | solution.py:205
  99.2 7.4 %collective-permute-start = (bf16[12,48,128]{2,1,0:T(8,128)(2,1)S(1)}, bf16[12,48,128]{2,1,0:T(8,128)(2,1)S(1)}, u32[]{:S(2)}, u32[]{:S(2)}) collective-permute-start(bf16[12,48,128]{2,1,0:T(8,128)(2,1)S(1)} %get-tuple-element.113.value.earlier), channel_id=1, source_target_pairs={{8,16},{24,32},{40,48},{56,64},{72,80},{88,96},{104,112},{120,128}... | collective-permute-start | bytes 442376 | tf_op jit(solution)/shard_map/while/body/eval_jaxpr/ppermute | solution.py:208
  101.3 5.3 %collective-permute-start.1 = (bf16[12,48,128]{2,1,0:T(8,128)(2,1)S(1)}, bf16[12,48,128]{2,1,0:T(8,128)(2,1)S(1)}, u32[]{:S(2)}, u32[]{:S(2)}) collective-permute-start(bf16[12,48,128]{2,1,0:T(8,128)(2,1)S(1)} %get-tuple-element.113.value.earlier), channel_id=1, source_target_pairs={{0,8},{16,24},{32,40},{48,56},{64,72},{80,88},{96,104},{112,120},{... | collective-permute-start | bytes 442376 | tf_op jit(solution)/shard_map/while/body/eval_jaxpr/ppermute | solution.py:207
  101.3 6.5 %collective-permute-start.2 = (bf16[12,48,128]{2,1,0:T(8,128)(2,1)S(1)}, bf16[12,48,128]{2,1,0:T(8,128)(2,1)S(1)}, u32[]{:S(2)}, u32[]{:S(2)}) collective-permute-start(bf16[12,48,128]{2,1,0:T(8,128)(2,1)S(1)} %get-tuple-element.113.value.earlier), channel_id=1, source_target_pairs={{1,2},{3,4},{5,6},{7,0},{2,1},{4,3},{6,5},{0,7},{9,10},{11,12},{13... | collective-permute-start | bytes 442376 | tf_op jit(solution)/shard_map/while/body/eval_jaxpr/ppermute | solution.py:206
  104.6 3.1 %collective-permute-start.3 = (bf16[12,48,128]{2,1,0:T(8,128)(2,1)S(1)}, bf16[12,48,128]{2,1,0:T(8,128)(2,1)S(1)}, u32[]{:S(2)}, u32[]{:S(2)}) collective-permute-start(bf16[12,48,128]{2,1,0:T(8,128)(2,1)S(1)} %get-tuple-element.113.value.earlier), channel_id=1, source_target_pairs={{0,1},{2,3},{4,5},{6,7},{1,0},{3,2},{5,4},{7,6},{8,9},{10,11},{12,... | collective-permute-start | bytes 442376 | tf_op jit(solution)/shard_map/while/body/eval_jaxpr/ppermute | solution.py:205
  108.2 7.4 %collective-permute-start = (bf16[12,48,128]{2,1,0:T(8,128)(2,1)S(1)}, bf16[12,48,128]{2,1,0:T(8,128)(2,1)S(1)}, u32[]{:S(2)}, u32[]{:S(2)}) collective-permute-start(bf16[12,48,128]{2,1,0:T(8,128)(2,1)S(1)} %get-tuple-element.113.value.earlier), channel_id=1, source_target_pairs={{8,16},{24,32},{40,48},{56,64},{72,80},{88,96},{104,112},{120,128}... | collective-permute-start | bytes 442376 | tf_op jit(solution)/shard_map/while/body/eval_jaxpr/ppermute | solution.py:208
  110.3 5.3 %collective-permute-start.1 = (bf16[12,48,128]{2,1,0:T(8,128)(2,1)S(1)}, bf16[12,48,128]{2,1,0:T(8,128)(2,1)S(1)}, u32[]{:S(2)}, u32[]{:S(2)}) collective-permute-start(bf16[12,48,128]{2,1,0:T(8,128)(2,1)S(1)} %get-tuple-element.113.value.earlier), channel_id=1, source_target_pairs={{0,8},{16,24},{32,40},{48,56},{64,72},{80,88},{96,104},{112,120},{... | collective-permute-start | bytes 442376 | tf_op jit(solution)/shard_map/while/body/eval_jaxpr/ppermute | solution.py:207
  110.3 6.5 %collective-permute-start.2 = (bf16[12,48,128]{2,1,0:T(8,128)(2,1)S(1)}, bf16[12,48,128]{2,1,0:T(8,128)(2,1)S(1)}, u32[]{:S(2)}, u32[]{:S(2)}) collective-permute-start(bf16[12,48,128]{2,1,0:T(8,128)(2,1)S(1)} %get-tuple-element.113.value.earlier), channel_id=1, source_target_pairs={{1,2},{3,4},{5,6},{7,0},{2,1},{4,3},{6,5},{0,7},{9,10},{11,12},{13... | collective-permute-start | bytes 442376 | tf_op jit(solution)/shard_map/while/body/eval_jaxpr/ppermute | solution.py:206
  113.6 3.1 %collective-permute-start.3 = (bf16[12,48,128]{2,1,0:T(8,128)(2,1)S(1)}, bf16[12,48,128]{2,1,0:T(8,128)(2,1)S(1)}, u32[]{:S(2)}, u32[]{:S(2)}) collective-permute-start(bf16[12,48,128]{2,1,0:T(8,128)(2,1)S(1)} %get-tuple-element.113.value.earlier), channel_id=1, source_target_pairs={{0,1},{2,3},{4,5},{6,7},{1,0},{3,2},{5,4},{7,6},{8,9},{10,11},{12,... | collective-permute-start | bytes 442376 | tf_op jit(solution)/shard_map/while/body/eval_jaxpr/ppermute | solution.py:205
  117.2 7.4 %collective-permute-start = (bf16[12,48,128]{2,1,0:T(8,128)(2,1)S(1)}, bf16[12,48,128]{2,1,0:T(8,128)(2,1)S(1)}, u32[]{:S(2)}, u32[]{:S(2)}) collective-permute-start(bf16[12,48,128]{2,1,0:T(8,128)(2,1)S(1)} %get-tuple-element.113.value.earlier), channel_id=1, source_target_pairs={{8,16},{24,32},{40,48},{56,64},{72,80},{88,96},{104,112},{120,128}... | collective-permute-start | bytes 442376 | tf_op jit(solution)/shard_map/while/body/eval_jaxpr/ppermute | solution.py:208
  119.3 5.3 %collective-permute-start.1 = (bf16[12,48,128]{2,1,0:T(8,128)(2,1)S(1)}, bf16[12,48,128]{2,1,0:T(8,128)(2,1)S(1)}, u32[]{:S(2)}, u32[]{:S(2)}) collective-permute-start(bf16[12,48,128]{2,1,0:T(8,128)(2,1)S(1)} %get-tuple-element.113.value.earlier), channel_id=1, source_target_pairs={{0,8},{16,24},{32,40},{48,56},{64,72},{80,88},{96,104},{112,120},{... | collective-permute-start | bytes 442376 | tf_op jit(solution)/shard_map/while/body/eval_jaxpr/ppermute | solution.py:207
  119.3 6.5 %collective-permute-start.2 = (bf16[12,48,128]{2,1,0:T(8,128)(2,1)S(1)}, bf16[12,48,128]{2,1,0:T(8,128)(2,1)S(1)}, u32[]{:S(2)}, u32[]{:S(2)}) collective-permute-start(bf16[12,48,128]{2,1,0:T(8,128)(2,1)S(1)} %get-tuple-element.113.value.earlier), channel_id=1, source_target_pairs={{1,2},{3,4},{5,6},{7,0},{2,1},{4,3},{6,5},{0,7},{9,10},{11,12},{13... | collective-permute-start | bytes 442376 | tf_op jit(solution)/shard_map/while/body/eval_jaxpr/ppermute | solution.py:206
  122.6 3.1 %collective-permute-start.3 = (bf16[12,48,128]{2,1,0:T(8,128)(2,1)S(1)}, bf16[12,48,128]{2,1,0:T(8,128)(2,1)S(1)}, u32[]{:S(2)}, u32[]{:S(2)}) collective-permute-start(bf16[12,48,128]{2,1,0:T(8,128)(2,1)S(1)} %get-tuple-element.113.value.earlier), channel_id=1, source_target_pairs={{0,1},{2,3},{4,5},{6,7},{1,0},{3,2},{5,4},{7,6},{8,9},{10,11},{12,... | collective-permute-start | bytes 442376 | tf_op jit(solution)/shard_map/while/body/eval_jaxpr/ppermute | solution.py:205
  126.1 8.1 %collective-permute-start.8 = (bf16[12,48,128]{2,1,0:T(8,128)(2,1)S(1)}, bf16[12,48,128]{2,1,0:T(8,128)(2,1)S(1)}, u32[]{:S(2)}, u32[]{:S(2)}) collective-permute-start(bf16[12,48,128]{2,1,0:T(8,128)(2,1)S(1)} %get-tuple-element.49.value.earlier), channel_id=1, source_target_pairs={{8,16},{24,32},{40,48},{56,64},{72,80},{88,96},{104,112},{120,128}... | collective-permute-start | bytes 442376 | tf_op jit(solution)/shard_map/ppermute | solution.py:208
  128.3 6.1 %collective-permute-start.9 = (bf16[12,48,128]{2,1,0:T(8,128)(2,1)S(1)}, bf16[12,48,128]{2,1,0:T(8,128)(2,1)S(1)}, u32[]{:S(2)}, u32[]{:S(2)}) collective-permute-start(bf16[12,48,128]{2,1,0:T(8,128)(2,1)S(1)} %get-tuple-element.49.value.earlier), channel_id=1, source_target_pairs={{0,8},{16,24},{32,40},{48,56},{64,72},{80,88},{96,104},{112,120},{... | collective-permute-start | bytes 442376 | tf_op jit(solution)/shard_map/ppermute | solution.py:207
  128.3 6.5 %collective-permute-start.10 = (bf16[12,48,128]{2,1,0:T(8,128)(2,1)S(1)}, bf16[12,48,128]{2,1,0:T(8,128)(2,1)S(1)}, u32[]{:S(2)}, u32[]{:S(2)}) collective-permute-start(bf16[12,48,128]{2,1,0:T(8,128)(2,1)S(1)} %get-tuple-element.49.value.earlier), channel_id=1, source_target_pairs={{1,2},{3,4},{5,6},{7,0},{2,1},{4,3},{6,5},{0,7},{9,10},{11,12},{13... | collective-permute-start | bytes 442376 | tf_op jit(solution)/shard_map/ppermute | solution.py:206
  131.6 3.1 %collective-permute-start.11 = (bf16[12,48,128]{2,1,0:T(8,128)(2,1)S(1)}, bf16[12,48,128]{2,1,0:T(8,128)(2,1)S(1)}, u32[]{:S(2)}, u32[]{:S(2)}) collective-permute-start(bf16[12,48,128]{2,1,0:T(8,128)(2,1)S(1)} %get-tuple-element.49.value.earlier), channel_id=1, source_target_pairs={{0,1},{2,3},{4,5},{6,7},{1,0},{3,2},{5,4},{7,6},{8,9},{10,11},{12,... | collective-permute-start | bytes 442376 | tf_op jit(solution)/shard_map/ppermute | solution.py:205
  135.1 8.5 %collective-permute-start.12 = (bf16[12,48,128]{2,1,0:T(8,128)(2,1)S(1)}, bf16[12,48,128]{2,1,0:T(8,128)(2,1)S(1)}, u32[]{:S(2)}, u32[]{:S(2)}) collective-permute-start(bf16[12,48,128]{2,1,0:T(8,128)(2,1)S(1)} %shard_map.47.value.earlier), channel_id=1, source_target_pairs={{8,16},{24,32},{40,48},{56,64},{72,80},{88,96},{104,112},{120,128}... | collective-permute-start | bytes 442376 | tf_op jit(solution)/shard_map/ppermute | solution.py:208
  137.4 6.2 %collective-permute-start.13 = (bf16[12,48,128]{2,1,0:T(8,128)(2,1)S(1)}, bf16[12,48,128]{2,1,0:T(8,128)(2,1)S(1)}, u32[]{:S(2)}, u32[]{:S(2)}) collective-permute-start(bf16[12,48,128]{2,1,0:T(8,128)(2,1)S(1)} %shard_map.47.value.earlier), channel_id=1, source_target_pairs={{0,8},{16,24},{32,40},{48,56},{64,72},{80,88},{96,104},{112,120},{... | collective-permute-start | bytes 442376 | tf_op jit(solution)/shard_map/ppermute | solution.py:207
  137.4 6.5 %collective-permute-start.14 = (bf16[12,48,128]{2,1,0:T(8,128)(2,1)S(1)}, bf16[12,48,128]{2,1,0:T(8,128)(2,1)S(1)}, u32[]{:S(2)}, u32[]{:S(2)}) collective-permute-start(bf16[12,48,128]{2,1,0:T(8,128)(2,1)S(1)} %shard_map.47.value.earlier), channel_id=1, source_target_pairs={{1,2},{3,4},{5,6},{7,0},{2,1},{4,3},{6,5},{0,7},{9,10},{11,12},{13... | collective-permute-start | bytes 442376 | tf_op jit(solution)/shard_map/ppermute | solution.py:206
  140.8 3.1 %collective-permute-start.15 = (bf16[12,48,128]{2,1,0:T(8,128)(2,1)S(1)}, bf16[12,48,128]{2,1,0:T(8,128)(2,1)S(1)}, u32[]{:S(2)}, u32[]{:S(2)}) collective-permute-start(bf16[12,48,128]{2,1,0:T(8,128)(2,1)S(1)} %shard_map.47.value.earlier), channel_id=1, source_target_pairs={{0,1},{2,3},{4,5},{6,7},{1,0},{3,2},{5,4},{7,6},{8,9},{10,11},{12,... | collective-permute-start | bytes 442376 | tf_op jit(solution)/shard_map/ppermute | solution.py:205
  144.3 8.3 %collective-permute-start.16 = (bf16[12,48,128]{2,1,0:T(8,128)(2,1)S(1)}, bf16[12,48,128]{2,1,0:T(8,128)(2,1)S(1)}, u32[]{:S(2)}, u32[]{:S(2)}) collective-permute-start(bf16[12,48,128]{2,1,0:T(8,128)(2,1)S(1)} %shard_map.52.value.earlier), channel_id=1, source_target_pairs={{8,16},{24,32},{40,48},{56,64},{72,80},{88,96},{104,112},{120,128}... | collective-permute-start | bytes 442376 | tf_op jit(solution)/shard_map/ppermute | solution.py:208
  146.5 6.1 %collective-permute-start.17 = (bf16[12,48,128]{2,1,0:T(8,128)(2,1)S(1)}, bf16[12,48,128]{2,1,0:T(8,128)(2,1)S(1)}, u32[]{:S(2)}, u32[]{:S(2)}) collective-permute-start(bf16[12,48,128]{2,1,0:T(8,128)(2,1)S(1)} %shard_map.52.value.earlier), channel_id=1, source_target_pairs={{0,8},{16,24},{32,40},{48,56},{64,72},{80,88},{96,104},{112,120},{... | collective-permute-start | bytes 442376 | tf_op jit(solution)/shard_map/ppermute | solution.py:207
  146.5 6.4 %collective-permute-start.18 = (bf16[12,48,128]{2,1,0:T(8,128)(2,1)S(1)}, bf16[12,48,128]{2,1,0:T(8,128)(2,1)S(1)}, u32[]{:S(2)}, u32[]{:S(2)}) collective-permute-start(bf16[12,48,128]{2,1,0:T(8,128)(2,1)S(1)} %shard_map.52.value.earlier), channel_id=1, source_target_pairs={{1,2},{3,4},{5,6},{7,0},{2,1},{4,3},{6,5},{0,7},{9,10},{11,12},{13... | collective-permute-start | bytes 442376 | tf_op jit(solution)/shard_map/ppermute | solution.py:206
  149.7 3.1 %collective-permute-start.19 = (bf16[12,48,128]{2,1,0:T(8,128)(2,1)S(1)}, bf16[12,48,128]{2,1,0:T(8,128)(2,1)S(1)}, u32[]{:S(2)}, u32[]{:S(2)}) collective-permute-start(bf16[12,48,128]{2,1,0:T(8,128)(2,1)S(1)} %shard_map.52.value.earlier), channel_id=1, source_target_pairs={{0,1},{2,3},{4,5},{6,7},{1,0},{3,2},{5,4},{7,6},{8,9},{10,11},{12,... | collective-permute-start | bytes 442376 | tf_op jit(solution)/shard_map/ppermute | solution.py:205
